TPU v7x, 32 devices: a whole 2x2x4 slice. The times are simulated.
32 devices in a mesh: chan: 4 (over z), brow: 2 (over y), bcol: 4 (over x, core).
Axes of the slice: x: 2, y: 2, z: 4, core: 2. Of those that a mesh axis runs over, the one named last changes fastest.
Arguments:
- voltages: int32 [2, 64, 131072], P(None, ('brow', 'bcol'), 'chan'), may hold values from -127 to 127
- antenna_gains: float32 [64, 2, 512], P(('brow', 'bcol'), None, 'chan'), may hold values from -4 to 4
- tile_map: int32 [8, 8], replicated, may hold values from 0 to 1, as said below
Outputs:
- visibilities: float32 [2, 4, 512, 2, 16, 32], P('brow', 'bcol', 'chan')
Inputs may be any that keep to these rules, and one draw needn't show every extreme that they name: For two different antenna blocks i and j exactly one of tile_map[i, j] and tile_map[j, i] is 1; every diagonal entry is 1.
All inputs are finite; a program needn't handle non-finite values.
Results may differ from a plain program's by a relative error of at most 0.0029.
Values may be sent and summed in bfloat16 or wider, within the bound.
No kernel may reach another device: no remote copies, remote signals or barrier semaphores. Data moves between devices by JAX's collectives and lax.ppermute only.
A program may use at most 64 MiB of HBM per device.

v0:
```python
import math

import jax
import jax.numpy as jnp
from jax import lax
from jax.sharding import PartitionSpec as P

NCHAN = 1024
CHANNELS = 512
TAPS = 4
FIRST = 256


def passed_along(block, axis, distance):
    devices = range(lax.axis_size(axis))
    route = [(i - distance, i) for i in devices if i - distance in devices]
    return lax.ppermute(block, axis, route)


def fir_coefficients():
    position = jnp.arange(TAPS * NCHAN, dtype=jnp.int32).astype(jnp.float32) + 0.5
    offsets = position / NCHAN - TAPS / 2.0
    window = 0.5 - 0.5 * jnp.cos(2.0 * math.pi * position / (TAPS * NCHAN))
    return (jnp.sinc(offsets) * window).reshape(TAPS, NCHAN)


def make_dft_table():
    sample_index = jnp.arange(NCHAN, dtype=jnp.int32)[:, None]
    channel_index = FIRST + jnp.arange(CHANNELS, dtype=jnp.int32)[None, :]
    angles = (sample_index * channel_index % NCHAN).astype(jnp.float32) * (2.0 * math.pi / NCHAN)
    cosine = jnp.cos(angles)
    sine_part = jnp.sin(angles)
    upper_half = jnp.concatenate([cosine, -sine_part], axis=1)
    lower_half = jnp.concatenate([sine_part, cosine], axis=1)
    return jnp.stack([upper_half, lower_half], axis=0).astype(jnp.bfloat16)


def rotated(panel):
    return jnp.stack([panel, jnp.stack([-panel[:, 1], panel[:, 0]], axis=1)], axis=1)


def shards(voltages, antenna_gains, tile_map):
    signals = voltages.shape[1]
    spec_dev = voltages.shape[2] // NCHAN
    coefficients = fir_coefficients()
    dft_table = make_dft_table()
    spectrum_scale = 1.0 / (128.0 * jnp.sqrt(jnp.sum(coefficients * coefficients)))
    frames = voltages.astype(jnp.float32).astype(jnp.bfloat16).reshape(2, signals, spec_dev, NCHAN)
    earlier = passed_along(frames[:, :, spec_dev - (TAPS - 1) :, :], "chan", 1)
    padded = jnp.concatenate([earlier, frames], axis=2)
    filtered_sum = jnp.zeros((2, signals, spec_dev, NCHAN), jnp.float32)
    for tap_index in range(TAPS):
        filtered_sum = (
            filtered_sum
            + coefficients[tap_index] * padded[:, :, tap_index : tap_index + spec_dev, :]
        )
    filtered = filtered_sum.astype(jnp.bfloat16)
    raw = jnp.einsum("psmn,pnc->scm", filtered, dft_table, preferred_element_type=jnp.float32)
    spectrum = (raw * spectrum_scale).reshape(signals, 2, CHANNELS, spec_dev).astype(jnp.bfloat16)
    turned = lax.all_to_all(spectrum, "chan", split_axis=2, concat_axis=3, tiled=True)
    spectra = turned.shape[3]
    real_part = turned[:, 0].astype(jnp.float32)
    imag_part = turned[:, 1].astype(jnp.float32)
    gain_real = antenna_gains[:, 0, :, None]
    gain_imag = antenna_gains[:, 1, :, None]
    equalized = jnp.stack(
        [
            real_part * gain_real - imag_part * gain_imag,
            real_part * gain_imag + imag_part * gain_real,
        ],
        axis=1,
    ).astype(jnp.bfloat16)
    row_count = lax.axis_size("brow")
    col_count = lax.axis_size("bcol")
    row_index = lax.axis_index("brow")
    col_index = lax.axis_index("bcol")
    row_panel = lax.all_gather(equalized, "bcol", axis=0, tiled=True)
    col_panel = lax.all_gather(equalized, "brow", axis=0, tiled=True)
    correlated = (
        jnp.einsum(
            "apft,bqpft->fqba", row_panel, rotated(col_panel), preferred_element_type=jnp.float32
        )
        / spectra
    )
    map_rows = lax.dynamic_slice_in_dim(tile_map, row_index * col_count, col_count, 0)
    map_rows = map_rows.reshape(col_count, row_count, col_count)
    owned = lax.dynamic_slice_in_dim(map_rows, col_index, 1, 2)[:, :, 0]
    kept_mask = (
        jnp.broadcast_to(
            owned.T[:, None, :, None], (row_count, signals, col_count, signals)
        ).reshape(row_count * signals, col_count * signals)
        == 1
    )
    result = jnp.where(kept_mask[None, None], correlated, jnp.zeros_like(correlated))
    return result[None, None]


def solution(mesh):
    in_specs = (P(None, ("brow", "bcol"), "chan"), P(("brow", "bcol"), None, "chan"), P())
    out_specs = P("brow", "bcol", "chan", None, None, None)
    return jax.shard_map(shards, mesh=mesh, in_specs=in_specs, out_specs=out_specs, check_vma=False)
```

profile of v0, /device:TPU:0, one launch (start us, length us, event | category | flops | bytes accessed | tf_op | source)
XLA Modules:
  0.0 117.2 jit_solution(2126739697560442705)
XLA Ops:
  6.5 0.0 copy-start
  6.5 1.7 %convert_convert_fusion = bf16[2,8,32768]{2,1,0:T(8,128)(2,1)S(1)} fusion(s32[2,8,32768]{2,1,0:T(8,128)} %param.3), kind=kLoop, calls=%fused_computation.20 | loop fusion | flops 1048576 | bytes 3145728 | tf_op jit(solution)/shard_map/convert_element_type | solution.py:48
  8.2 0.6 copy.36
  8.8 0.1 slice.61
  8.9 4.9 %collective-permute-start = (bf16[2,8,3,1024]{3,2,0,1:T(4,128)(2,1)S(1)}, bf16[2,8,3,1024]{3,2,0,1:T(4,128)(2,1)S(1)}, u32[]{:S(2)}, u32[]{:S(2)}) collective-permute-start(bf16[2,8,3,1024]{3,2,0,1:T(4,128)(2,1)S(1)} %slice.61), channel_id=1, source_target_pairs={{0,8},{8,16},{16,24},{1,9},{9,17},{17,25},{2,10},{10,18},{18,26},{... | collective-permute-start | bytes 294920 | tf_op jit(solution)/shard_map/ppermute | solution.py:17
  13.9 0.1 fusion.39
  14.0 8.7 %negate_convert_fusion = (bf16[1024,512]{1,0:T(8,128)(2,1)S(1)}, bf16[1024,512]{1,0:T(8,128)(2,1)S(1)}, bf16[1024,512]{1,0:T(8,128)(2,1)S(1)}) fusion(s32[512]{0:T(512)S(1)} %iota_add_fusion), kind=kLoop, calls=%fused_computation.21 | loop fusion | flops 9437184 | bytes 3147776 | tf_op jit(solution)/shard_map/convert.9
  22.7 2.0 %maximum_bitcast_fusion.2 = (bf16[1,1024,1024]{2,1,0:T(8,128)(2,1)S(1)}, bf16[1,1024,1024]{2,1,0:T(8,128)(2,1)}) fusion(bf16[1024,512]{1,0:T(8,128)(2,1)S(1)} %get-tuple-element.19, bf16[1024,512]{1,0:T(8,128)(2,1)S(1)} %get-tuple-element.21, bf16[1024,512]{1,0:T(8,128)(2,1)S(1)} %get-tuple-element.20), kind=kLoop, calls=%fused_computation.10 | loop fusion | flops 8388608 | bytes 7340032 | tf_op jit(solution)/shard_map/stack | solution.py:35
  24.7 0.7 multiply_reduce_fusion
  26.1 0.0 collective-permute-done
  26.1 4.1 %fusion.21 = bf16[8,1024,32]{1,2,0:T(8,128)(2,1)} fusion(bf16[1,1024,1024]{2,1,0:T(8,128)(2,1)} %get-tuple-element.8, bf16[1,1024,1024]{2,1,0:T(8,128)(2,1)S(1)} %get-tuple-element.7, bf16[2,8,32,1024]{3,2,0,1:T(8,128)(2,1)S(1)} %copy.36, bf16[2,8,3,1024]{3,2,0,1:T(4,128)(2,1)S(1)} %collective-permute-done, f32[1024]{0:T(1024)S(1)} %get-tuple-element.14, ...), kind=kOutput, calls=%fused_computation.33 | convolution fusion | flops 1093664768 | bytes 5881860 | tf_op jit(solution)/shard_map/psmn,pnc->scm/dot_general | solution.py:58
  30.2 1.4 %convert_element_type.80 = bf16[8,2,512,32]{2,1,3,0:T(2,128)(2,1)S(1)} reshape(bf16[8,1024,32]{1,2,0:T(8,128)(2,1)} %fusion.21) | data formatting | bytes 1048576 | tf_op jit(solution)/shard_map/convert_element_type | solution.py:59
  31.6 2.2 %copy.39 = bf16[8,2,512,32]{3,1,0,2:T(2,128)(2,1)S(1)} copy(bf16[8,2,512,32]{2,1,3,0:T(2,128)(2,1)S(1)} %convert_element_type.80) | data formatting | bytes 1048576 | tf_op jit(solution)/shard_map/convert_element_type | solution.py:59
  33.8 0.0 copy-start.2
  33.9 3.0 %reshape.47 = bf16[4,2,32768]{2,1,0:T(2,128)(2,1)} reshape(bf16[512,8,2,32]{3,2,1,0:T(2,128)(2,1)S(1)} %bitcast.58) | data formatting | bytes 1048576
  36.8 3.9 %all-to-all-start = ((bf16[4,2,32768]{2,1,0:T(2,128)(2,1)}), bf16[4,2,32768]{2,1,0:T(2,128)(2,1)S(1)}, u32[]{:S(2)}, u32[]{:S(2)}) async-start(bf16[4,2,32768]{2,1,0:T(2,128)(2,1)} %reshape.47), calls=%async_computation | async-start | bytes 1048576 | tf_op jit(solution)/shard_map/all_to_all | solution.py:60
  40.7 0.0 all-gather.3.cloned.1.call-start
  40.7 0.0 copy-done.2
  40.7 0.1 copy.43
  40.8 0.1 copy.45
  40.9 14.0 %all-to-all-done = bf16[4,2,32768]{2,1,0:T(2,128)(2,1)S(1)} async-done(((bf16[4,2,32768]{2,1,0:T(2,128)(2,1)}), bf16[4,2,32768]{2,1,0:T(2,128)(2,1)S(1)}, u32[]{:S(2)}, u32[]{:S(2)}) %all-to-all-start) | async-done | bytes 524320 | tf_op jit(solution)/shard_map/all_to_all | solution.py:60
  54.9 1.1 reshape.48
  56.0 2.8 %copy.51 = bf16[8,2,4,128,32]{3,2,4,1,0:T(4,128)(2,1)S(1)} copy(bf16[8,2,4,128,32]{4,1,0,3,2:T(2,128)(2,1)S(1)} %bitcast.59) | data formatting | bytes 1048576 | tf_op jit(solution)/shard_map/all_to_all | solution.py:60
  58.7 0.1 copy.41
  58.9 0.2 copy.52
  59.1 0.2 copy.53
  59.3 0.3 fusion.32
  59.7 0.9 pad_maximum_fusion.3
  60.5 0.0 all-gather.3.cloned.1.call-update
  60.6 0.0 all-gather.5.cloned.1.call-start
  60.6 0.7 all-gather.5.cloned.1.call-update
  61.3 0.0 copy-done
  61.3 0.1 reshape.40
  61.4 0.2 compare_reduce_fusion
  61.7 0.1 copy.35
  61.8 0.1 broadcast_in_dim.28
  61.8 0.1 eq.72
  61.9 19.2 %all-gather.3.cloned.1.call-done = bf16[16,2,128,128]{3,0,1,2:T(8,128)(2,1)} async-done(((bf16[8,2,128,128]{3,0,1,2:T(8,128)(2,1)}), bf16[16,2,128,128]{3,0,1,2:T(8,128)(2,1)}) %all-gather.3.cloned.1.call-update) | async-done | bytes 1048592 | tf_op jit(solution)/shard_map/all_gather | solution.py:78
  81.1 0.0 copy-start.1
  81.1 1.4 %slice_negate_fusion = (bf16[16,1,128,128]{3,0,1,2:T(8,128)(2,1)S(1)}, bf16[16,1,128,128]{3,0,1,2:T(8,128)(2,1)S(1)}) fusion(bf16[16,2,128,128]{3,0,1,2:T(8,128)(2,1)} %all-gather.3.cloned.1.call-done), kind=kLoop, calls=%fused_computation.53 | loop fusion | flops 262144 | bytes 2097152 | tf_op jit(solution)/shard_map/neg | solution.py:39
  82.5 1.1 maximum_bitcast_fusion.12
  83.6 21.9 %all-gather.5.cloned.1.call-done = bf16[32,2,128,128]{3,0,1,2:T(8,128)(2,1)} async-done(((bf16[8,2,128,128]{3,0,1,2:T(8,128)(2,1)}), bf16[32,2,128,128]{3,0,1,2:T(8,128)(2,1)}) %all-gather.5.cloned.1.call-update) | async-done | bytes 2097168 | tf_op jit(solution)/shard_map/all_gather | solution.py:77
  105.5 0.0 copy-done.1
  105.5 2.6 %fusion.9 = f32[1,1,128,2,16,32]{5,4,3,2,1,0:T(8,128)S(1)} fusion(bf16[32,2,128,128]{3,0,1,2:T(8,128)(2,1)} %all-gather.5.cloned.1.call-done, pred[16,32]{1,0:T(8,128)(4,1)S(1)} %eq.72, bf16[16,1,2,128,128]{4,0,2,3,1:T(8,128)(2,1)} %maximum_bitcast_fusion.12, bf16[16,1,2,128,128]{4,0,2,3,1:T(8,128)(2,1)S(1)} %bitcast.63), kind=kOutput, calls=%fused_computation.17 | convolution fusion | flops 68419584 | bytes 4719104 | tf_op jit(solution)/shard_map/apft,bqpft->fqba/dot_general | solution.py:80
  108.2 2.2 %copy.47 = f32[1,1,128,2,16,32]{2,5,4,3,1,0:T(8,128)} copy(f32[1,1,128,2,16,32]{5,4,3,2,1,0:T(8,128)S(1)} %fusion.9) | data formatting | bytes 1048576 | tf_op jit(solution)/shard_map/broadcast_in_dim | solution.py:95
  (5 shorter events, 0.1 us)
Async XLA Ops:
  6.5 54.8 %copy-start = (s32[8,8]{1,0:T(8,128)S(1)}, s32[8,8]{1,0:T(8,128)}, u32[]{:S(2)}) copy-start(s32[8,8]{1,0:T(8,128)} %param.5) | copy-start | bytes 772
  8.9 17.2 %collective-permute-start = (bf16[2,8,3,1024]{3,2,0,1:T(4,128)(2,1)S(1)}, bf16[2,8,3,1024]{3,2,0,1:T(4,128)(2,1)S(1)}, u32[]{:S(2)}, u32[]{:S(2)}) collective-permute-start(bf16[2,8,3,1024]{3,2,0,1:T(4,128)(2,1)S(1)} %slice.61), channel_id=1, source_target_pairs={{0,8},{8,16},{16,24},{1,9},{9,17},{17,25},{2,10},{10,18},{18,26},{... | collective-permute-start | bytes 294920 | tf_op jit(solution)/shard_map/ppermute | solution.py:17
  33.8 6.8 %copy-start.2 = (f32[8,2,128]{2,1,0:T(2,128)S(1)}, f32[8,2,128]{2,1,0:T(2,128)}, u32[]{:S(2)}) copy-start(f32[8,2,128]{2,1,0:T(2,128)} %param.4) | copy-start | bytes 24580
  36.8 18.1 %all-to-all-start = ((bf16[4,2,32768]{2,1,0:T(2,128)(2,1)}), bf16[4,2,32768]{2,1,0:T(2,128)(2,1)S(1)}, u32[]{:S(2)}, u32[]{:S(2)}) async-start(bf16[4,2,32768]{2,1,0:T(2,128)(2,1)} %reshape.47), calls=%async_computation | async-start | bytes 1048576 | tf_op jit(solution)/shard_map/all_to_all | solution.py:60
  40.7 40.4 %all-gather.3.cloned.1.call-start = ((), (), s32[]{:S(2)}) async-start(), calls=%async_computation.1 | async-start | bytes 1572864 | tf_op jit(solution)/shard_map/all_gather | solution.py:78
  60.6 45.0 %all-gather.5.cloned.1.call-start = ((), (), s32[]{:S(2)}) async-start(), calls=%async_computation.2 | async-start | bytes 2621440 | tf_op jit(solution)/shard_map/all_gather | solution.py:77
  81.1 24.4 %copy-start.1 = (bf16[16,2,128,128]{3,0,1,2:T(8,128)(2,1)S(1)}, bf16[16,2,128,128]{3,0,1,2:T(8,128)(2,1)}, u32[]{:S(2)}) copy-start(bf16[16,2,128,128]{3,0,1,2:T(8,128)(2,1)} %all-gather.3.cloned.1.call-done) | copy-start | bytes 3145732
Sparse Core Ops, SparseCore 0:
  60.7 20.3 all-gather.2
  82.7 22.8 all-gather.4
where the time goes:
time: 117 us
  waiting for transfers between devices  55.8 us (48%)
  other arithmetic  17.1 us (15%)
  local copies, waits for them, and re-layouts  14.4 us (12%)
  between operations  14.3 us (12%)
  starting transfers between devices  8.83 us (8%)
  matrix products  6.71 us (6%)
    all_gather x1, waiting for transfers between devices, shards(): row_panel = lax.all_gather(equalized, 'bcol', axis=0, tiled=True)  21.9 us
    all_gather x1, waiting for transfers between devices, shards(): col_panel = lax.all_gather(equalized, 'brow', axis=0, tiled=True)  19.2 us
    all_to_all x1, waiting for transfers between devices, shards(): lax.all_to_all(spectrum, 'chan', split_axis=2, concat_axis=3, tiled=True)  14 us
    another operation x2, other arithmetic  9.02 us
    ppermute x1, starting transfers between devices, passed_along(): return lax.ppermute(block, axis, route)  4.94 us
    unnamed x10, local copies, waits for them, and re-layouts  4.46 us
    dot_general x1, matrix products, shards(): jnp.einsum('psmn,pnc->scm', filtered, dft_table, preferred_element_type=j...  4.1 us
    all_to_all x1, starting transfers between devices, shards(): lax.all_to_all(spectrum, 'chan', split_axis=2, concat_axis=3, tiled=True)  3.85 us
  transfers between devices with their start and end apart: 4, of which 3 were waited for; matrix products, arithmetic and copies ran while one was open for 13% of the time, Pallas kernels for 0%

commit v1 on v0

v1 whole, which is shorter than its diff:
```python
import functools
import math

import jax
import jax.numpy as jnp
import ml_dtypes
import numpy as np
from jax import lax
from jax.experimental import pallas as pl
from jax.experimental.pallas import tpu as pltpu
from jax.sharding import PartitionSpec as P

NCHAN = 1024
HALF = NCHAN // 2
CHANNELS = 512
TAPS = 4
FIRST = 256
SIG = 8
LANES = 128
GROUP = 4
VMEM_BYTES = 48 * 1024 * 1024


def fir_coefficients():
    position = np.arange(TAPS * NCHAN, dtype=np.float64) + 0.5
    offsets = position / NCHAN - TAPS / 2.0
    window = 0.5 - 0.5 * np.cos(2.0 * math.pi * position / (TAPS * NCHAN))
    return (np.sinc(offsets) * window).reshape(TAPS, NCHAN)


def dft_tables(owners):
    width = CHANNELS // owners // 2
    n = np.arange(HALF, dtype=np.int64)[:, None]
    tables = []
    for parity in range(2):
        j = 2 * np.arange(CHANNELS // 2, dtype=np.int64)[None, :] + parity
        angles = (n * (FIRST + j) % NCHAN) * (2.0 * math.pi / NCHAN)
        cosine = np.cos(angles).reshape(HALF, owners, 1, width)
        sine = np.sin(angles).reshape(HALF, owners, 1, width)
        first = np.concatenate([cosine, -sine], axis=2).reshape(HALF, CHANNELS)
        second = np.concatenate([sine, cosine], axis=2).reshape(HALF, CHANNELS)
        tables.append(np.concatenate([first, second], axis=0))
    return np.stack(tables).astype(np.float32).astype(ml_dtypes.bfloat16)


def channelize_kernel(
    frames, pieces, owners, width, scale, volt_hbm, table_hbm, coef_ref, out_ref, volt, table, filt, sems
):
    per = frames // pieces
    lead = TAPS - 1
    copies = []
    for piece in range(pieces):
        copies.append(
            pltpu.make_async_copy(
                volt_hbm.at[:, :, pl.ds(piece * per * NCHAN, per * NCHAN)],
                volt.at[:, :, pl.ds((lead + piece * per) * NCHAN, per * NCHAN)],
                sems.at[piece],
            )
        )
    table_copy = pltpu.make_async_copy(table_hbm, table, sems.at[pieces])
    for copy in copies:
        copy.start()
    table_copy.start()
    tail = volt.shape[2] - (lead + frames) * NCHAN
    volt[:, :, : lead * NCHAN] = jnp.zeros((2, SIG, lead * NCHAN), jnp.int32)
    volt[:, :, (lead + frames) * NCHAN :] = jnp.zeros((2, SIG, tail), jnp.int32)

    def filter_group(group, _):
        base = pl.multiple_of(group * (GROUP * NCHAN), GROUP * NCHAN)
        rows = pl.ds(pl.multiple_of(group * (GROUP * SIG), GROUP * SIG), GROUP * SIG)
        for column in range(HALF // LANES):
            for part in range(2):
                halves = []
                for half in range(2):
                    lane = half * HALF + column * LANES
                    taps = [coef_ref[k : k + 1, lane : lane + LANES] for k in range(TAPS)]
                    near = [
                        volt[part, :, pl.ds(base + f * NCHAN + lane, LANES)].astype(jnp.float32)
                        for f in range(GROUP + TAPS - 1)
                    ]
                    sums = []
                    for m in range(GROUP):
                        total = taps[0] * near[m]
                        for k in range(1, TAPS):
                            total = total + taps[k] * near[m + k]
                        sums.append(total)
                    halves.append(jnp.concatenate(sums, axis=0))
                where = pl.ds(part * HALF + column * LANES, LANES)
                filt[0, rows, where] = (halves[0] + halves[1]).astype(jnp.bfloat16)
                filt[1, rows, where] = (halves[0] - halves[1]).astype(jnp.bfloat16)
        return 0

    groups = per // GROUP
    for piece in range(pieces):
        copies[piece].wait()
        lax.fori_loop(piece * groups, (piece + 1) * groups, filter_group, 0)
    lax.fori_loop(frames // GROUP, frames // GROUP + 1, filter_group, 0)
    table_copy.wait()
    for parity in range(2):
        spectrum = jnp.dot(filt[parity], table[parity], preferred_element_type=jnp.float32) * scale
        for owner in range(owners):
            out_ref[owner, :, parity * width : (parity + 1) * width] = spectrum[
                :, owner * width : (owner + 1) * width
            ].astype(jnp.bfloat16)


def channelize(voltages, owners):
    frames = voltages.shape[2] // NCHAN
    width = CHANNELS // owners
    coefficients = fir_coefficients()
    scale = float(1.0 / (128.0 * np.sqrt(np.sum(coefficients * coefficients))))
    rows = (frames + GROUP) * SIG
    pieces = 4
    kernel = functools.partial(channelize_kernel, frames, pieces, owners, width, scale)
    return pl.pallas_call(
        kernel,
        out_shape=jax.ShapeDtypeStruct((owners, rows, 2 * width), jnp.bfloat16),
        in_specs=[
            pl.BlockSpec(memory_space=pl.ANY),
            pl.BlockSpec(memory_space=pl.ANY),
            pl.BlockSpec(memory_space=pltpu.VMEM),
        ],
        out_specs=pl.BlockSpec(memory_space=pltpu.VMEM),
        scratch_shapes=[
            pltpu.VMEM((2, SIG, (frames + GROUP + TAPS - 1) * NCHAN), jnp.int32),
            pltpu.VMEM((2, NCHAN, CHANNELS), jnp.bfloat16),
            pltpu.VMEM((2, rows, NCHAN), jnp.bfloat16),
            pltpu.SemaphoreType.DMA((pieces + 1,)),
        ],
        compiler_params=pltpu.CompilerParams(vmem_limit_bytes=VMEM_BYTES),
        name="channelize",
    )(voltages, jnp.asarray(dft_tables(owners)), jnp.asarray(coefficients, jnp.float32))


def half_turn(x):
    h = x.shape[1] // 2
    return pltpu.roll(x, h, axis=1) if x.shape[1] == LANES else jnp.concatenate([x[:, h:], x[:, :h]], axis=1)


def equalize_kernel(owners, frames, width, turned_ref, direct_ref, cross_ref, out_ref, by_time, by_channel):
    own_rows = frames * SIG
    over = GROUP * SIG
    times = owners * frames
    tiles = times // LANES
    h = width // 2
    for parity in range(2):
        lanes = slice(parity * width, (parity + 1) * width)
        for source in range(owners):
            by_time[source * own_rows : (source + 1) * own_rows, :width] = turned_ref[source, :own_rows, lanes].astype(
                jnp.float32
            )
            if source > 0:
                start = source * own_rows
                by_time[start : start + over, :width] += turned_ref[source - 1, own_rows:, lanes].astype(jnp.float32)
        for s in range(SIG):
            x = by_time[pl.ds(s, times, stride=SIG), :][:, :width]
            y = x * direct_ref[parity, s : s + 1, :] + half_turn(x) * cross_ref[parity, s : s + 1, :]
            y = y.T
            for q in range(2):
                for tile in range(tiles):
                    by_channel[q * tiles + tile, pl.ds(s, h, stride=SIG), :] = y[
                        q * h : (q + 1) * h, tile * LANES : (tile + 1) * LANES
                    ]
        for tile in range(2 * tiles):
            out_ref[parity, :, tile * LANES : (tile + 1) * LANES] = by_channel[tile].astype(jnp.bfloat16)


def equalize(turned, gains, frames):
    owners = turned.shape[0]
    width = gains.shape[2]
    times = owners * frames
    h = width // 2
    split = jnp.transpose(gains.reshape(SIG, 2, h, 2), (3, 1, 0, 2))
    direct = jnp.concatenate([split[:, 0], split[:, 0]], axis=-1)
    cross = jnp.concatenate([-split[:, 1], split[:, 1]], axis=-1)
    return pl.pallas_call(
        functools.partial(equalize_kernel, owners, frames, width),
        out_shape=jax.ShapeDtypeStruct((2, h * SIG, 2 * times), jnp.bfloat16),
        in_specs=[pl.BlockSpec(memory_space=pltpu.VMEM)] * 3,
        out_specs=pl.BlockSpec(memory_space=pltpu.VMEM),
        scratch_shapes=[
            pltpu.VMEM((times * SIG, LANES), jnp.float32),
            pltpu.VMEM((2 * times // LANES, h * SIG, LANES), jnp.float32),
        ],
        compiler_params=pltpu.CompilerParams(vmem_limit_bytes=VMEM_BYTES),
        name="equalize",
    )(turned, direct, cross)


BATCH = 4


def correlate_kernel(n_row, n_col, h, times, map_ref, place_ref, *refs):
    blocks = refs[: n_col + n_row - 1]
    out_ref, row_panel, col_panel, product, sems = refs[n_col + n_row - 1 :]
    copies = []
    for i in range(n_col):
        copies.append(pltpu.make_async_copy(blocks[i], row_panel.at[place_ref[i]], sems.at[i]))
    for i in range(n_row):
        block = blocks[0] if i == 0 else blocks[n_col + i - 1]
        copies.append(pltpu.make_async_copy(block, col_panel.at[place_ref[n_col + i]], sems.at[n_col + i]))
    for copy in copies:
        copy.start()
    for copy in copies:
        copy.wait()
    rows = BATCH * SIG
    tiles = n_col * rows // LANES

    def batch(step, _):
        parity = step // (h // BATCH)
        inner = step % (h // BATCH)
        here = pl.ds(pl.multiple_of(inner * rows, rows), rows)
        a = jnp.concatenate([row_panel[c, parity, here, :] for c in range(n_col)], axis=0)
        b = jnp.concatenate([col_panel[c, parity, here, :] for c in range(n_row)], axis=0)
        turned = jnp.concatenate([-b[:, times:], b[:, :times]], axis=1)
        both = jnp.concatenate([b, turned], axis=0)
        result = lax.dot_general(both, a, (((1,), (1,)), ((), ())), preferred_element_type=jnp.float32)
        for k in range(2 * n_row):
            for i in range(BATCH):
                channel = 2 * (inner * BATCH + i) + parity
                for tile in range(tiles):
                    product[k * tiles + tile, pl.ds(pl.multiple_of(channel * SIG, SIG), SIG), :] = result[
                        k * rows + i * SIG : k * rows + (i + 1) * SIG, tile * LANES : (tile + 1) * LANES
                    ]
        return 0

    lax.fori_loop(0, 2 * h // BATCH, batch, 0, unroll=4)
    me_row = place_ref[n_col]
    me_col = place_ref[0]
    channels = 2 * h
    lane = lax.broadcasted_iota(jnp.int32, (SIG, channels), 1)
    inner_of = (lane // 2) % BATCH
    for q in range(2):
        for r2 in range(n_row):
            keeps = [
                jnp.where(map_ref[me_row * n_col + c2, r2 * n_col + me_col] == 1, 1.0 / times, 0.0)
                for c2 in range(n_col)
            ]
            for s2 in range(SIG):
                for c2 in range(n_col):
                    if c2 * rows % LANES == 0:
                        tile = (q * n_row + r2) * tiles + c2 * rows // LANES
                        x = product[tile, pl.ds(s2, channels, stride=SIG), :].T
                    start = c2 * rows % LANES
                    kept = x[start : start + SIG]
                    for i in range(1, BATCH):
                        kept = jnp.where(inner_of == i, x[start + i * SIG : start + (i + 1) * SIG], kept)
                    out_ref[q, r2 * SIG + s2, c2 * SIG : (c2 + 1) * SIG, :] = jnp.where(
                        keeps[c2] != 0.0, kept * keeps[c2], 0.0
                    )


def correlate(tile_map, place, blocks, n_row, n_col):
    h = blocks[0].shape[1] // SIG
    times = blocks[0].shape[2] // 2
    return pl.pallas_call(
        functools.partial(correlate_kernel, n_row, n_col, h, times),
        out_shape=jax.ShapeDtypeStruct((2, n_row * SIG, n_col * SIG, 2 * h), jnp.float32),
        in_specs=[pl.BlockSpec(memory_space=pltpu.SMEM)] * 2 + [pl.BlockSpec(memory_space=pl.ANY)] * len(blocks),
        out_specs=pl.BlockSpec(memory_space=pltpu.VMEM),
        scratch_shapes=[
            pltpu.VMEM((n_col,) + blocks[0].shape, jnp.bfloat16),
            pltpu.VMEM((n_row,) + blocks[0].shape, jnp.bfloat16),
            pltpu.VMEM((2 * n_row * n_col * BATCH * SIG // LANES, 2 * h * SIG, LANES), jnp.float32),
            pltpu.SemaphoreType.DMA((n_row + n_col,)),
        ],
        compiler_params=pltpu.CompilerParams(vmem_limit_bytes=VMEM_BYTES),
        name="correlate",
    )(tile_map, place, *blocks)


def shards(voltages, antenna_gains, tile_map):
    owners = lax.axis_size("chan")
    n_row = lax.axis_size("brow")
    n_col = lax.axis_size("bcol")
    frames = voltages.shape[2] // NCHAN
    row = lax.axis_index("brow")
    col = lax.axis_index("bcol")
    spectra = channelize(voltages, owners)
    turned = lax.all_to_all(spectra, "chan", split_axis=0, concat_axis=0, tiled=True)
    own = equalize(turned, antenna_gains, frames)

    chips = n_col // 2
    other_core = [(i, i ^ 1) for i in range(n_col)]
    blocks, places = [own], [col]
    far = []
    for d in range(1, chips):
        route = [(i, (i // 2 + d) % chips * 2 + i % 2) for i in range(n_col)]
        far.append(lax.ppermute(own, "bcol", route))
        places.append((col // 2 + chips - d) % chips * 2 + col % 2)
    blocks += far
    column = []
    for d in range(1, n_row):
        column.append(lax.ppermute(own, "brow", [(i, (i + d) % n_row) for i in range(n_row)]))
    near = [lax.ppermute(own, "bcol", other_core)]
    near += [lax.ppermute(block, "bcol", other_core) for block in far]
    blocks += near
    places += [p + 1 - 2 * (p % 2) for p in places]
    blocks += column
    places += [row] + [(row + n_row - d) % n_row for d in range(1, n_row)]
    place = jnp.stack(places).astype(jnp.int32)
    result = correlate(tile_map, place, blocks, n_row, n_col)
    return jnp.transpose(result, (3, 0, 1, 2))[None, None]


def solution(mesh):
    in_specs = (P(None, ("brow", "bcol"), "chan"), P(("brow", "bcol"), None, "chan"), P())
    out_specs = P("brow", "bcol", "chan", None, None, None)
    return jax.shard_map(shards, mesh=mesh, in_specs=in_specs, out_specs=out_specs, check_vma=False)
```

time: 117 us -> 49.2 us (0.42)
  waiting for transfers between devices: 55.8 us -> 27.3 us
  other arithmetic: 17.1 us -> 0.1 us
  between operations: 14.3 us -> 0.04 us
  local copies, waits for them, and re-layouts: 14.4 us -> 4.2 us
  Pallas kernels: 0 us -> 7.85 us
  matrix products: 6.71 us -> 0 us
    all_gather x2 -> x0, waiting for transfers between devices: 41.1 us -> none  [the longest x1 21.9 us: shards(): row_panel = lax.all_gather(equalized, 'bcol', axis=0, tiled=True)]
    another operation x5 -> x0, other arithmetic: 13 us -> none
    ppermute x1 -> x4, waiting for transfers between devices: 0.01 us -> 11.7 us  [the longest x1 9.88 us: shards(): far.append(lax.ppermute(own, 'bcol', route))]
    pallas_call x0 -> x3, Pallas kernels: none -> 7.85 us  [the longest x1 4.22 us: correlate(): pl.pallas_call(functools.partial(correlate_kernel, n_row, n_col, h, times...]
    dot_general x2 -> x0, matrix products: 6.71 us -> none  [the longest x1 4.1 us: shards(): jnp.einsum('psmn,pnc->scm', filtered, dft_table, preferred_element_type=j...]
    convert_element_type x2 -> x0, local copies, waits for them, and re-layouts: 3.65 us -> none  [shards(): (raw * spectrum_scale).reshape(signals, 2, CHANNELS, spec_dev)]
    all_to_all x2 -> x0, local copies, waits for them, and re-layouts: 2.87 us -> none  [shards(): lax.all_to_all(spectrum, 'chan', split_axis=2, concat_axis=3, tiled=True)]
    all_to_all x1, starting transfers between devices: 3.85 us -> 6.33 us  [shards(): lax.all_to_all(spectra, 'chan', split_axis=0, concat_axis=0, tiled=True)]
  transfers between devices with their start and end apart: 4 -> 5, of which waited for: 3 -> 4; matrix products, arithmetic and copies ran while one was open for 13% -> 1% of each run, Pallas kernels for 0% -> 0%
where the time goes in v1:
time: 49.2 us; the launch traced here: 48.9 us
  waiting for transfers between devices  27.3 us (55%)
  starting transfers between devices  9.41 us (19%)
  Pallas kernels  7.85 us (16%)
  local copies, waits for them, and re-layouts  4.2 us (9%)
    all_to_all x1, waiting for transfers between devices, shards(): lax.all_to_all(spectra, 'chan', split_axis=0, concat_axis=0, tiled=True)  15.6 us
    ppermute x1, waiting for transfers between devices, shards(): far.append(lax.ppermute(own, 'bcol', route))  9.88 us
    all_to_all x1, starting transfers between devices, shards(): lax.all_to_all(spectra, 'chan', split_axis=0, concat_axis=0, tiled=True)  6.33 us
    pallas_call x1, Pallas kernels, correlate(): pl.pallas_call(functools.partial(correlate_kernel, n_row, n_col, h, times...  4.22 us
    unnamed x11, local copies, waits for them, and re-layouts  4.03 us
    pallas_call x1, Pallas kernels, channelize(): pl.pallas_call(kernel, out_shape=jax.ShapeDtypeStruct((owners, rows, 2 *...  2.86 us
    ppermute x1, starting transfers between devices, shards(): far.append(lax.ppermute(own, 'bcol', route))  1.56 us
    ppermute x1, starting transfers between devices, shards(): lax.ppermute(own, 'brow', [(i, (i + d) % n_row) for i in range(n_row)])  1.52 us
  transfers between devices with their start and end apart: 5, of which 4 were waited for; matrix products, arithmetic and copies ran while one was open for 1% of the time, Pallas kernels for 0%

profile of v1, /device:TPU:0, one launch (start us, length us, event | category | flops | bytes accessed | tf_op | source)
XLA Modules:
  0.0 48.9 jit_solution(9260592550012711479)
XLA Ops:
  0.0 0.0 copy-start
  0.0 1.6 %copy-done = s32[2,8,32768]{2,1,0:T(8,128)S(1)} copy-done((s32[2,8,32768]{2,1,0:T(8,128)S(1)}, s32[2,8,32768]{2,1,0:T(8,128)}, u32[]{:S(2)}) %copy-start) | copy-done | bytes 2097176
  1.6 0.0 copy-start.1
  1.6 1.6 %copy-done.1 = bf16[2,1024,512]{2,1,0:T(8,128)(2,1)S(1)} copy-done((bf16[2,1024,512]{2,1,0:T(8,128)(2,1)S(1)}, bf16[2,1024,512]{2,1,0:T(8,128)(2,1)}, u32[]{:S(2)}) %copy-start.1) | copy-done | bytes 2097176
  3.2 0.0 copy-start.2
  3.2 0.7 %copy-done.2 = f32[4,1024]{1,0:T(4,128)S(1)} copy-done((f32[4,1024]{1,0:T(4,128)S(1)}, f32[4,1024]{1,0:T(4,128)}, u32[]{:S(2)}) %copy-start.2) | copy-done | bytes 16408
  3.9 0.0 copy-start.4
  3.9 2.9 %channelize.1 = bf16[4,288,256]{2,1,0:T(8,128)(2,1)} custom-call(s32[2,8,32768]{2,1,0:T(8,128)S(1)} %copy-done, bf16[2,1024,512]{2,1,0:T(8,128)(2,1)S(1)} %copy-done.1, f32[4,1024]{1,0:T(4,128)S(1)} %copy-done.2), custom_call_target="tpu_custom_call" | custom-call | tf_op jit(solution)/shard_map/channelize/pallas_call | solution.py:115
  6.8 0.0 copy-start.3
  6.8 6.3 %all-to-all-start = ((bf16[4,288,256]{2,1,0:T(8,128)(2,1)}), bf16[4,288,256]{2,1,0:T(8,128)(2,1)S(1)}, u32[]{:S(2)}, u32[]{:S(2)}) async-start(bf16[4,288,256]{2,1,0:T(8,128)(2,1)} %channelize.1), calls=%async_computation | async-start | bytes 1179648 | tf_op jit(solution)/shard_map/all_to_all | solution.py:280
  13.1 0.0 copy-done.4
  13.1 0.1 copy.6
  13.2 0.1 copy.7
  13.3 0.1 pad_maximum_fusion
  13.4 15.6 %all-to-all-done.turned_ref = bf16[4,288,256]{2,1,0:T(8,128)(2,1)S(1)} async-done(((bf16[4,288,256]{2,1,0:T(8,128)(2,1)}), bf16[4,288,256]{2,1,0:T(8,128)(2,1)S(1)}, u32[]{:S(2)}, u32[]{:S(2)}) %all-to-all-start) | async-done | bytes 589856 | tf_op jit(solution)/shard_map/all_to_all | solution.py:280
  29.0 0.8 %equalize.1.refs_0_ = bf16[2,512,256]{2,1,0:T(8,128)(2,1)S(1)} custom-call(bf16[4,288,256]{2,1,0:T(8,128)(2,1)S(1)} %all-to-all-done.turned_ref, f32[2,8,128]{2,1,0:T(8,128)S(1)} %get-tuple-element.7.direct_ref, f32[2,8,128]{2,1,0:T(8,128)S(1)} %get-tuple-element.8.cross_ref), custom_call_target="tpu_custom_call" | custom-call | tf_op jit(solution)/shard_map/equalize/pallas_call | solution.py:176
  29.8 1.6 %collective-permute-start = (bf16[2,512,256]{2,1,0:T(8,128)(2,1)S(1)}, bf16[2,512,256]{2,1,0:T(8,128)(2,1)S(1)}, u32[]{:S(2)}, u32[]{:S(2)}) collective-permute-start(bf16[2,512,256]{2,1,0:T(8,128)(2,1)S(1)} %equalize.1.refs_0_), channel_id=1, source_target_pairs={{0,2},{1,3},{2,0},{3,1},{4,6},{5,7},{6,4},{7,5},{8,10},{9,11},{10,... | collective-permute-start | bytes 1572872 | tf_op jit(solution)/shard_map/ppermute | solution.py:289
  31.3 1.5 %collective-permute-start.3 = (bf16[2,512,256]{2,1,0:T(8,128)(2,1)S(1)}, bf16[2,512,256]{2,1,0:T(8,128)(2,1)S(1)}, u32[]{:S(2)}, u32[]{:S(2)}) collective-permute-start(bf16[2,512,256]{2,1,0:T(8,128)(2,1)S(1)} %equalize.1.refs_0_), channel_id=1, source_target_pairs={{0,4},{4,0},{1,5},{5,1},{2,6},{6,2},{3,7},{7,3},{8,12},{12,8},{9,1... | collective-permute-start | bytes 1572872 | tf_op jit(solution)/shard_map/ppermute | solution.py:294
  32.9 0.0 collective-permute-start.1
  32.9 9.9 %collective-permute-done.refs_1_ = bf16[2,512,256]{2,1,0:T(8,128)(2,1)S(1)} collective-permute-done((bf16[2,512,256]{2,1,0:T(8,128)(2,1)S(1)}, bf16[2,512,256]{2,1,0:T(8,128)(2,1)S(1)}, u32[]{:S(2)}, u32[]{:S(2)}) %collective-permute-start) | collective-permute-done | bytes 524320 | tf_op jit(solution)/shard_map/ppermute | solution.py:289
  42.7 0.0 collective-permute-start.2
  42.7 0.1 stack.27.place_ref
  42.8 1.1 %collective-permute-done.3.refs_4_ = bf16[2,512,256]{2,1,0:T(8,128)(2,1)S(1)} collective-permute-done((bf16[2,512,256]{2,1,0:T(8,128)(2,1)S(1)}, bf16[2,512,256]{2,1,0:T(8,128)(2,1)S(1)}, u32[]{:S(2)}, u32[]{:S(2)}) %collective-permute-start.3) | collective-permute-done | bytes 524320 | tf_op jit(solution)/shard_map/ppermute | solution.py:294
  44.0 0.0 collective-permute-done.1.refs_2_
  44.0 0.7 %collective-permute-done.2.refs_3_ = bf16[2,512,256]{2,1,0:T(8,128)(2,1)S(1)} collective-permute-done((bf16[2,512,256]{2,1,0:T(8,128)(2,1)S(1)}, bf16[2,512,256]{2,1,0:T(8,128)(2,1)S(1)}, u32[]{:S(2)}, u32[]{:S(2)}) %collective-permute-start.2) | collective-permute-done | bytes 524320 | tf_op jit(solution)/shard_map/ppermute | solution.py:296
  44.7 0.0 copy-done.3
  44.7 4.2 %correlate.1 = f32[2,16,32,128]{3,2,1,0:T(8,128)} custom-call(s32[8,8]{1,0:T(8,128)S(1)} %copy-done.3, s32[6]{0:T(128)S(1)} %stack.27.place_ref, bf16[2,512,256]{2,1,0:T(8,128)(2,1)S(1)} %equalize.1.refs_0_, bf16[2,512,256]{2,1,0:T(8,128)(2,1)S(1)} %collective-permute-done.refs_1_, bf16[2,512,256]{2,1,0:T(8,128)(2,1)S(1)} %collective-permute-done.1.refs_2_, ...), custom_call_target="tpu_custom_call" | custom-call | tf_op jit(solution)/shard_map/correlate/pallas_call | solution.py:256
  (2 shorter events, 0.0 us)
Async XLA Ops:
  0.0 1.6 %copy-start = (s32[2,8,32768]{2,1,0:T(8,128)S(1)}, s32[2,8,32768]{2,1,0:T(8,128)}, u32[]{:S(2)}) copy-start(s32[2,8,32768]{2,1,0:T(8,128)} %volt_hbm.1) | copy-start | bytes 6291460
  1.6 1.6 %copy-start.1 = (bf16[2,1024,512]{2,1,0:T(8,128)(2,1)S(1)}, bf16[2,1024,512]{2,1,0:T(8,128)(2,1)}, u32[]{:S(2)}) copy-start(bf16[2,1024,512]{2,1,0:T(8,128)(2,1)} %constant.56.clone.table_hbm) | copy-start | bytes 6291460
  3.2 0.7 %copy-start.2 = (f32[4,1024]{1,0:T(4,128)S(1)}, f32[4,1024]{1,0:T(4,128)}, u32[]{:S(2)}) copy-start(f32[4,1024]{1,0:T(4,128)} %constant.57.clone.coef_ref) | copy-start | bytes 49156
  3.9 9.2 %copy-start.4 = (f32[8,2,128]{2,1,0:T(2,128)S(1)}, f32[8,2,128]{2,1,0:T(2,128)}, u32[]{:S(2)}) copy-start(f32[8,2,128]{2,1,0:T(2,128)} %param.6) | copy-start | bytes 24580
  6.8 37.9 %copy-start.3 = (s32[8,8]{1,0:T(8,128)S(1)}, s32[8,8]{1,0:T(8,128)}, u32[]{:S(2)}) copy-start(s32[8,8]{1,0:T(8,128)} %map_ref.1) | copy-start | bytes 772
  6.8 22.2 %all-to-all-start = ((bf16[4,288,256]{2,1,0:T(8,128)(2,1)}), bf16[4,288,256]{2,1,0:T(8,128)(2,1)S(1)}, u32[]{:S(2)}, u32[]{:S(2)}) async-start(bf16[4,288,256]{2,1,0:T(8,128)(2,1)} %channelize.1), calls=%async_computation | async-start | bytes 1179648 | tf_op jit(solution)/shard_map/all_to_all | solution.py:280
  29.8 13.0 %collective-permute-start = (bf16[2,512,256]{2,1,0:T(8,128)(2,1)S(1)}, bf16[2,512,256]{2,1,0:T(8,128)(2,1)S(1)}, u32[]{:S(2)}, u32[]{:S(2)}) collective-permute-start(bf16[2,512,256]{2,1,0:T(8,128)(2,1)S(1)} %equalize.1.refs_0_), channel_id=1, source_target_pairs={{0,2},{1,3},{2,0},{3,1},{4,6},{5,7},{6,4},{7,5},{8,10},{9,11},{10,... | collective-permute-start | bytes 1572872 | tf_op jit(solution)/shard_map/ppermute | solution.py:289
  31.3 12.6 %collective-permute-start.3 = (bf16[2,512,256]{2,1,0:T(8,128)(2,1)S(1)}, bf16[2,512,256]{2,1,0:T(8,128)(2,1)S(1)}, u32[]{:S(2)}, u32[]{:S(2)}) collective-permute-start(bf16[2,512,256]{2,1,0:T(8,128)(2,1)S(1)} %equalize.1.refs_0_), channel_id=1, source_target_pairs={{0,4},{4,0},{1,5},{5,1},{2,6},{6,2},{3,7},{7,3},{8,12},{12,8},{9,1... | collective-permute-start | bytes 1572872 | tf_op jit(solution)/shard_map/ppermute | solution.py:294
  32.9 11.1 %collective-permute-start.1 = (bf16[2,512,256]{2,1,0:T(8,128)(2,1)S(1)}, bf16[2,512,256]{2,1,0:T(8,128)(2,1)S(1)}, u32[]{:S(2)}, u32[]{:S(2)}) collective-permute-start(bf16[2,512,256]{2,1,0:T(8,128)(2,1)S(1)} %equalize.1.refs_0_), channel_id=1, source_target_pairs={{0,1},{1,0},{2,3},{3,2},{4,5},{5,4},{6,7},{7,6},{8,9},{9,8},{10,11... | collective-permute-start | bytes 1572872 | tf_op jit(solution)/shard_map/ppermute | solution.py:295
  42.7 1.9 %collective-permute-start.2 = (bf16[2,512,256]{2,1,0:T(8,128)(2,1)S(1)}, bf16[2,512,256]{2,1,0:T(8,128)(2,1)S(1)}, u32[]{:S(2)}, u32[]{:S(2)}) collective-permute-start(bf16[2,512,256]{2,1,0:T(8,128)(2,1)S(1)} %collective-permute-done.refs_1_), channel_id=1, source_target_pairs={{0,1},{1,0},{2,3},{3,2},{4,5},{5,4},{6,7},{7,6},{8,9},{9,8},{10,11... | collective-permute-start | bytes 1572872 | tf_op jit(solution)/shard_map/ppermute | solution.py:296

commit v2 on v1

v2 whole, which is shorter than its diff:
```python
import functools
import math

import jax
import jax.numpy as jnp
import ml_dtypes
import numpy as np
from jax import lax
from jax.experimental import pallas as pl
from jax.experimental.pallas import tpu as pltpu
from jax.sharding import PartitionSpec as P

NCHAN = 1024
HALF = NCHAN // 2
CHANNELS = 512
TAPS = 4
FIRST = 256
SIG = 8
LANES = 128
GROUP = 4
BATCH = 4
PARTS = 2
VMEM_BYTES = 48 * 1024 * 1024


def fir_coefficients():
    position = np.arange(TAPS * NCHAN, dtype=np.float64) + 0.5
    offsets = position / NCHAN - TAPS / 2.0
    window = 0.5 - 0.5 * np.cos(2.0 * math.pi * position / (TAPS * NCHAN))
    return (np.sinc(offsets) * window).reshape(TAPS, NCHAN)


def dft_tables(owners):
    n = np.arange(HALF, dtype=np.int64)[:, None, None, None, None]
    k = FIRST + np.arange(CHANNELS, dtype=np.int64).reshape(owners, PARTS, -1, 2)
    angles = (n * k % NCHAN) * (2.0 * math.pi / NCHAN)
    cosine, sine = np.cos(angles), np.sin(angles)
    first = np.stack([cosine, -sine], axis=2)
    second = np.stack([sine, cosine], axis=2)
    tables = np.stack([first, second])
    tables = np.transpose(tables, (4, 6, 0, 1, 2, 3, 5))
    return tables.reshape(PARTS, 2, NCHAN, -1).astype(np.float32).astype(ml_dtypes.bfloat16)


def transform(filt, table, scale, stage, out_refs):
    owners = len(out_refs)
    me = lax.axis_index("chan")
    spectra = [jnp.dot(filt[r], table[r], preferred_element_type=jnp.float32) * scale for r in range(2)]
    width = spectra[0].shape[1] // owners
    for owner in range(owners):
        here = slice(owner * width, (owner + 1) * width)
        piece = jnp.concatenate([spectra[0][:, here], spectra[1][:, here]], axis=1)
        stage[jnp.bitwise_xor(me, owner)] = piece.astype(jnp.bfloat16)
    for d in range(owners):
        out_refs[d][...] = stage[d]


def filter_kernel(frames, pieces, scale, volt_hbm, table_hbm, coef_ref, *refs):
    out_refs, filt, volt, table, stage, sems = refs[:-5], refs[-5], refs[-4], refs[-3], refs[-2], refs[-1]
    per = frames // pieces
    lead = TAPS - 1
    copies = []
    for piece in range(pieces):
        copies.append(
            pltpu.make_async_copy(
                volt_hbm.at[:, :, pl.ds(piece * per * NCHAN, per * NCHAN)],
                volt.at[:, :, pl.ds((lead + piece * per) * NCHAN, per * NCHAN)],
                sems.at[piece],
            )
        )
    table_copy = pltpu.make_async_copy(table_hbm, table, sems.at[pieces])
    for copy in copies:
        copy.start()
    table_copy.start()
    tail = volt.shape[2] - (lead + frames) * NCHAN
    volt[:, :, : lead * NCHAN] = jnp.zeros((2, SIG, lead * NCHAN), jnp.int32)
    volt[:, :, (lead + frames) * NCHAN :] = jnp.zeros((2, SIG, tail), jnp.int32)

    def filter_group(group, _):
        base = pl.multiple_of(group * (GROUP * NCHAN), GROUP * NCHAN)
        rows = pl.ds(pl.multiple_of(group * (GROUP * SIG), GROUP * SIG), GROUP * SIG)
        for column in range(HALF // LANES):
            for part in range(2):
                halves = []
                for half in range(2):
                    lane = half * HALF + column * LANES
                    taps = [coef_ref[k : k + 1, lane : lane + LANES] for k in range(TAPS)]
                    near = [
                        volt[part, :, pl.ds(base + f * NCHAN + lane, LANES)].astype(jnp.float32)
                        for f in range(GROUP + TAPS - 1)
                    ]
                    sums = []
                    for m in range(GROUP):
                        total = taps[0] * near[m]
                        for k in range(1, TAPS):
                            total = total + taps[k] * near[m + k]
                        sums.append(total)
                    halves.append(jnp.concatenate(sums, axis=0))
                where = pl.ds(part * HALF + column * LANES, LANES)
                filt[0, rows, where] = (halves[0] + halves[1]).astype(jnp.bfloat16)
                filt[1, rows, where] = (halves[0] - halves[1]).astype(jnp.bfloat16)
        return 0

    groups = per // GROUP
    for piece in range(pieces):
        copies[piece].wait()
        lax.fori_loop(piece * groups, (piece + 1) * groups, filter_group, 0)
    lax.fori_loop(frames // GROUP, frames // GROUP + 1, filter_group, 0)
    table_copy.wait()
    transform(filt, table, scale, stage, out_refs)


def transform_kernel(scale, filt, table_hbm, *refs):
    out_refs, table, stage, sem = refs[:-3], refs[-3], refs[-2], refs[-1]
    copy = pltpu.make_async_copy(table_hbm, table, sem)
    copy.start()
    copy.wait()
    transform(filt, table, scale, stage, out_refs)


IN_VMEM = pl.BlockSpec(memory_space=pltpu.VMEM)
IN_HBM = pl.BlockSpec(memory_space=pltpu.HBM)
IN_SMEM = pl.BlockSpec(memory_space=pltpu.SMEM)


def channelize(voltages, owners):
    frames = voltages.shape[2] // NCHAN
    coefficients = fir_coefficients()
    scale = float(1.0 / (128.0 * np.sqrt(np.sum(coefficients * coefficients))))
    rows = (frames + GROUP) * SIG
    pieces = 4
    tables = dft_tables(owners)
    lanes = 2 * CHANNELS // owners // PARTS
    params = pltpu.CompilerParams(vmem_limit_bytes=VMEM_BYTES)
    piece_shapes = [jax.ShapeDtypeStruct((rows, lanes), jnp.bfloat16)] * owners
    filt_shape = jax.ShapeDtypeStruct((2, rows, NCHAN), jnp.bfloat16)
    common = [pltpu.VMEM(tables.shape[1:], jnp.bfloat16), pltpu.VMEM((owners, rows, lanes), jnp.bfloat16)]
    flops = 2 * 2 * rows * NCHAN * CHANNELS // PARTS * 2
    *first, filt = pl.pallas_call(
        functools.partial(filter_kernel, frames, pieces, scale),
        out_shape=piece_shapes + [filt_shape],
        in_specs=[IN_HBM, IN_HBM, IN_VMEM],
        out_specs=[IN_VMEM] * (owners + 1),
        scratch_shapes=[pltpu.VMEM((2, SIG, (frames + GROUP + TAPS - 1) * NCHAN), jnp.int32)]
        + common
        + [pltpu.SemaphoreType.DMA((pieces + 1,))],
        compiler_params=params,
        cost_estimate=pl.CostEstimate(flops=flops, bytes_accessed=4 << 20, transcendentals=0),
        name="filter_and_transform",
    )(voltages, jnp.asarray(tables[0]), jnp.asarray(coefficients, jnp.float32))
    spectra = [first]
    for part in range(1, PARTS):
        spectra.append(
            pl.pallas_call(
                functools.partial(transform_kernel, scale),
                out_shape=piece_shapes,
                in_specs=[IN_VMEM, IN_HBM],
                out_specs=[IN_VMEM] * owners,
                scratch_shapes=common + [pltpu.SemaphoreType.DMA(())],
                compiler_params=params,
                cost_estimate=pl.CostEstimate(flops=flops, bytes_accessed=2 << 20, transcendentals=0),
                name="transform",
            )(filt, jnp.asarray(tables[part]))
        )
    return spectra


def swap_parts(x, h):
    return jnp.concatenate([x[:, i * h : (i + 1) * h] for i in (1, 0, 3, 2)], axis=1)


def equalize_kernel(owners, frames, h, *refs):
    pieces = refs[:owners]
    direct_ref, cross_ref, out_ref, by_time, by_channel = refs[owners:]
    width = 4 * h
    own_rows = frames * SIG
    over = GROUP * SIG
    times = owners * frames
    tiles = times // LANES
    me = lax.axis_index("chan")
    for d in range(owners):
        source = jnp.bitwise_xor(me, d)
        start = pl.multiple_of(source * own_rows, own_rows)
        by_time[pl.ds(start, own_rows), :width] = pieces[d][:own_rows, :].astype(jnp.float32)
    for d in range(owners):
        source = jnp.bitwise_xor(me, d)

        @pl.when(source < owners - 1)
        def _():
            start = pl.multiple_of((source + 1) * own_rows, own_rows)
            by_time[pl.ds(start, over), :width] += pieces[d][own_rows:, :].astype(jnp.float32)

    for s in range(SIG):
        x = by_time[pl.ds(s, times, stride=SIG), :][:, :width]
        y = x * direct_ref[s : s + 1, :] + swap_parts(x, h) * cross_ref[s : s + 1, :]
        y = y.T
        for r in range(2):
            for q in range(2):
                for tile in range(tiles):
                    by_channel[r * 2 * tiles + q * tiles + tile, pl.ds(s, h, stride=SIG), :] = y[
                        (2 * r + q) * h : (2 * r + q + 1) * h, tile * LANES : (tile + 1) * LANES
                    ]
    for r in range(2):
        for tile in range(2 * tiles):
            out_ref[r, :, tile * LANES : (tile + 1) * LANES] = by_channel[r * 2 * tiles + tile].astype(jnp.bfloat16)


def equalize(pieces, direct, cross, frames):
    owners = len(pieces)
    h = direct.shape[1] // 4
    times = owners * frames
    return pl.pallas_call(
        functools.partial(equalize_kernel, owners, frames, h),
        out_shape=jax.ShapeDtypeStruct((2, h * SIG, 2 * times), jnp.bfloat16),
        in_specs=[IN_VMEM] * (owners + 2),
        out_specs=IN_VMEM,
        scratch_shapes=[
            pltpu.VMEM((times * SIG, LANES), jnp.float32),
            pltpu.VMEM((4 * times // LANES, h * SIG, LANES), jnp.float32),
        ],
        compiler_params=pltpu.CompilerParams(vmem_limit_bytes=VMEM_BYTES),
        cost_estimate=pl.CostEstimate(flops=1 << 20, bytes_accessed=1 << 20, transcendentals=0),
        name="equalize",
    )(*pieces, direct, cross)


def row_places(col, n_col):
    chips = n_col // 2
    chip, core = lax.div(col, 2), lax.rem(col, 2)
    places = [col] + [lax.rem(chip + chips - d, chips) * 2 + core for d in range(1, chips)]
    return places + [jnp.bitwise_xor(p, 1) for p in places]


def column_places(row, n_row):
    return [row] + [lax.rem(row + n_row - d, n_row) for d in range(1, n_row)]


def correlate_kernel(n_row, n_col, h, times, before, map_ref, *refs):
    row_blocks = refs[:n_col]
    col_blocks = (refs[0],) + refs[n_col : n_col + n_row - 1]
    out_ref, product = refs[-2:]
    me_row, me_col = lax.axis_index("brow"), lax.axis_index("bcol")
    row_at, col_at = row_places(me_col, n_col), column_places(me_row, n_row)
    rows = BATCH * SIG
    tiles = n_col * rows // LANES

    def batch(step, _):
        parity = step // (h // BATCH)
        inner = step % (h // BATCH)
        here = pl.ds(pl.multiple_of(inner * rows, rows), rows)
        a = jnp.concatenate([block[parity, here, :] for block in row_blocks], axis=0)
        b = jnp.concatenate([block[parity, here, :] for block in col_blocks], axis=0)
        turned = jnp.concatenate([-b[:, times:], b[:, :times]], axis=1)
        both = jnp.concatenate([b, turned], axis=0)
        result = lax.dot_general(both, a, (((1,), (1,)), ((), ())), preferred_element_type=jnp.float32)
        for k in range(2 * n_row):
            for i in range(BATCH):
                channel = 2 * (inner * BATCH + i) + parity
                for tile in range(tiles):
                    product[k * tiles + tile, pl.ds(pl.multiple_of(channel * SIG, SIG), SIG), :] = result[
                        k * rows + i * SIG : k * rows + (i + 1) * SIG, tile * LANES : (tile + 1) * LANES
                    ]
        return 0

    lax.fori_loop(0, 2 * h // BATCH, batch, 0, unroll=4)
    channels = 2 * h
    lane = lax.broadcasted_iota(jnp.int32, (SIG, channels), 1)
    inner_of = (lane // 2) % BATCH
    for q in range(2):
        for e in range(n_row):
            owned = [map_ref[me_row * n_col + row_at[d], col_at[e] * n_col + me_col] == 1 for d in range(n_col)]
            for s2 in range(SIG):
                b_at = col_at[e] * SIG + s2
                for d in range(n_col):
                    if d * rows % LANES == 0:
                        tile = (q * n_row + e) * tiles + d * rows // LANES
                        x = product[tile, pl.ds(s2, channels, stride=SIG), :].T
                    start = d * rows % LANES
                    kept = x[start : start + SIG]
                    for i in range(1, BATCH):
                        kept = jnp.where(inner_of == i, x[start + i * SIG : start + (i + 1) * SIG], kept)
                    kept = jnp.where(owned[d], kept * (1.0 / times), 0.0)
                    a_at = pl.ds(pl.multiple_of(row_at[d] * SIG, SIG), SIG)
                    if before:
                        kept = jnp.concatenate([refs[-3][q, b_at, a_at, :], kept], axis=1)
                    out_ref[q, b_at, a_at, :] = kept


def correlate(tile_map, blocks, earlier, n_row, n_col):
    h = blocks[0].shape[1] // SIG
    times = blocks[0].shape[2] // 2
    before = earlier.shape[3] if earlier is not None else 0
    operands = list(blocks) + ([earlier] if before else [])
    return pl.pallas_call(
        functools.partial(correlate_kernel, n_row, n_col, h, times, before),
        out_shape=jax.ShapeDtypeStruct((2, n_row * SIG, n_col * SIG, before + 2 * h), jnp.float32),
        in_specs=[IN_SMEM] + [IN_VMEM] * len(operands),
        out_specs=IN_VMEM,
        scratch_shapes=[pltpu.VMEM((2 * n_row * n_col * BATCH * SIG // LANES, 2 * h * SIG, LANES), jnp.float32)],
        compiler_params=pltpu.CompilerParams(vmem_limit_bytes=VMEM_BYTES),
        cost_estimate=pl.CostEstimate(flops=1 << 29, bytes_accessed=4 << 20, transcendentals=0),
        name="correlate",
    )(tile_map, *operands)


def to_owners(pieces):
    owners = len(pieces)
    arrived = [pieces[0]] + [None] * (owners - 1)
    for d in range(owners - 1, 0, -1):
        arrived[d] = lax.ppermute(pieces[d], "chan", [(i, i ^ d) for i in range(owners)])
    return arrived


def gather(own, n_row, n_col):
    chips = n_col // 2
    other_core = [(i, i ^ 1) for i in range(n_col)]
    far = []
    for d in range(1, chips):
        far.append(lax.ppermute(own, "bcol", [(i, (i // 2 + d) % chips * 2 + i % 2) for i in range(n_col)]))
    column = []
    for d in range(1, n_row):
        column.append(lax.ppermute(own, "brow", [(i, (i + d) % n_row) for i in range(n_row)]))
    near = [lax.ppermute(block, "bcol", other_core) for block in [own] + far]
    return [own] + far + near + column


def shards(voltages, antenna_gains, tile_map):
    owners = lax.axis_size("chan")
    n_row = lax.axis_size("brow")
    n_col = lax.axis_size("bcol")
    frames = voltages.shape[2] // NCHAN
    h = antenna_gains.shape[2] // PARTS // 2
    gains = jnp.transpose(antenna_gains.reshape(SIG, 2, PARTS, h, 2), (2, 1, 0, 4, 3))
    direct = jnp.stack([gains[:, 0], gains[:, 0]], axis=3).reshape(PARTS, SIG, 4 * h)
    cross = jnp.stack([-gains[:, 1], gains[:, 1]], axis=3).reshape(PARTS, SIG, 4 * h)
    spectra = channelize(voltages, owners)
    arrived = [to_owners(pieces) for pieces in spectra]
    result = None
    panels = []
    for part in range(PARTS):
        panels.append(gather(equalize(arrived[part], direct[part], cross[part], frames), n_row, n_col))
    for part in range(PARTS):
        result = correlate(tile_map, panels[part], result, n_row, n_col)
    return jnp.transpose(result, (3, 0, 1, 2))[None, None]


def solution(mesh):
    in_specs = (P(None, ("brow", "bcol"), "chan"), P(("brow", "bcol"), None, "chan"), P())
    out_specs = P("brow", "bcol", "chan", None, None, None)
    return jax.shard_map(shards, mesh=mesh, in_specs=in_specs, out_specs=out_specs, check_vma=False)
```

time: 49.2 us -> 45.7 us (0.929)
  waiting for transfers between devices: 27.3 us -> 14 us
  starting transfers between devices: 9.41 us -> 18 us
  Pallas kernels: 7.85 us -> 8.94 us
    all_to_all x1 -> x0, waiting for transfers between devices: 15.6 us -> none  [shards(): lax.all_to_all(spectra, 'chan', split_axis=0, concat_axis=0, tiled=True)]
    ppermute x4 -> x14, starting transfers between devices: 3.08 us -> 18 us  [the longest x6 13.1 us: to_owners(): lax.ppermute(pieces[d], 'chan', [(i, i ^ d) for i in range(owners)])]
    all_to_all x1 -> x0, starting transfers between devices: 6.33 us -> none  [shards(): lax.all_to_all(spectra, 'chan', split_axis=0, concat_axis=0, tiled=True)]
    ppermute x4 -> x14, waiting for transfers between devices: 11.7 us -> 14 us  [the longest x2 6.03 us: gather(): lax.ppermute(own, 'bcol', [(i, (i // 2 + d) % chips * 2 + i % 2) for i in...]
    pallas_call x1 -> x2, Pallas kernels: 4.22 us -> 5.31 us  [correlate(): pl.pallas_call(functools.partial(correlate_kernel, n_row, n_col, h, times...]
    unnamed x11 -> x13, local copies, waits for them, and re-layouts: 4.03 us -> 3.67 us
    pallas_call x2 -> x4, Pallas kernels: 3.63 us -> 3.63 us  [the longest x1 1.78 us: channelize(): pl.pallas_call(functools.partial(filter_kernel, frames, pieces, scale), o...]
  transfers between devices with their start and end apart: 5 -> 14, of which waited for: 4 -> 5; matrix products, arithmetic and copies ran while one was open for 1% -> 2% of each run, Pallas kernels for 0% -> 7%
where the time goes in v2:
time: 45.7 us; the launch traced here: 45.4 us
  starting transfers between devices  18 us (39%)
  waiting for transfers between devices  14 us (31%)
  Pallas kernels  8.94 us (20%)
  local copies, waits for them, and re-layouts  4.3 us (9%)
    ppermute x6, starting transfers between devices, to_owners(): lax.ppermute(pieces[d], 'chan', [(i, i ^ d) for i in range(owners)])  13.1 us
    ppermute x2, waiting for transfers between devices, gather(): lax.ppermute(own, 'bcol', [(i, (i // 2 + d) % chips * 2 + i % 2) for i in...  6.03 us
    pallas_call x2, Pallas kernels, correlate(): pl.pallas_call(functools.partial(correlate_kernel, n_row, n_col, h, times...  5.31 us
    ppermute x6, waiting for transfers between devices, to_owners(): lax.ppermute(pieces[d], 'chan', [(i, i ^ d) for i in range(owners)])  4.22 us
    ppermute x2, waiting for transfers between devices, gather(): lax.ppermute(own, 'brow', [(i, (i + d) % n_row) for i in range(n_row)])  3.71 us
    unnamed x13, local copies, waits for them, and re-layouts  3.67 us
    ppermute x2, starting transfers between devices, gather(): lax.ppermute(own, 'brow', [(i, (i + d) % n_row) for i in range(n_row)])  2.5 us
    ppermute x2, starting transfers between devices, gather(): lax.ppermute(own, 'bcol', [(i, (i // 2 + d) % chips * 2 + i % 2) for i in...  2.19 us
  transfers between devices with their start and end apart: 14, of which 5 were waited for; matrix products, arithmetic and copies ran while one was open for 2% of the time, Pallas kernels for 7%

profile of v2, /device:TPU:0, one launch (start us, length us, event | category | flops | bytes accessed | tf_op | source)
XLA Modules:
  0.0 45.4 jit_solution(5858530603740323693)
XLA Ops:
  0.0 1.6 %copy-done = s32[2,8,32768]{2,1,0:T(8,128)S(1)} copy-done((s32[2,8,32768]{2,1,0:T(8,128)S(1)}, s32[2,8,32768]{2,1,0:T(8,128)}, u32[]{:S(2)}) %copy-start) | copy-done | bytes 2097176
  1.6 1.2 %copy-done.1 = bf16[2,1024,256]{2,1,0:T(8,128)(2,1)S(1)} copy-done((bf16[2,1024,256]{2,1,0:T(8,128)(2,1)S(1)}, bf16[2,1024,256]{2,1,0:T(8,128)(2,1)}, u32[]{:S(2)}) %copy-start.1) | copy-done | bytes 1048600
  2.8 0.7 %copy-done.2 = f32[4,1024]{1,0:T(4,128)S(1)} copy-done((f32[4,1024]{1,0:T(4,128)S(1)}, f32[4,1024]{1,0:T(4,128)}, u32[]{:S(2)}) %copy-start.2) | copy-done | bytes 16408
  3.5 1.8 %filter_and_transform.1 = (bf16[288,128]{1,0:T(8,128)(2,1)S(1)}, bf16[288,128]{1,0:T(8,128)(2,1)S(1)}, bf16[288,128]{1,0:T(8,128)(2,1)S(1)}, bf16[288,128]{1,0:T(8,128)(2,1)S(1)}, bf16[2,288,1024]{2,1,0:T(8,128)(2,1)S(1)}) custom-call(s32[2,8,32768]{2,1,0:T(8,128)S(1)} %copy-done, bf16[2,1024,256]{2,1,0:T(8,128)(2,1)S(1)} %copy-done.1, f32[4,1024]{1,0:T(4,128)S(1)} %copy-done.2), custom_call_target="tpu_custom_call" | custom-call | flops 603979776 | bytes 4194304 | tf_op jit(solution)/shard_map/filter_and_transform/pallas_call | solution.py:139
  5.3 0.0 copy-done.4
  5.3 0.0 copy-start.3
  5.4 0.7 %transform.1 = (bf16[288,128]{1,0:T(8,128)(2,1)S(1)}, bf16[288,128]{1,0:T(8,128)(2,1)S(1)}, bf16[288,128]{1,0:T(8,128)(2,1)S(1)}, bf16[288,128]{1,0:T(8,128)(2,1)S(1)}) custom-call(bf16[2,288,1024]{2,1,0:T(8,128)(2,1)S(1)} %get-tuple-element.14.filt, bf16[2,1024,256]{2,1,0:T(8,128)(2,1)S(1)} %copy-done.4), custom_call_target="tpu_custom_call" | custom-call | flops 603979776 | bytes 2097152 | tf_op jit(solution)/shard_map/transform/pallas_call | solution.py:154
  6.0 3.1 %collective-permute-start = (bf16[288,128]{1,0:T(8,128)(2,1)S(1)}, bf16[288,128]{1,0:T(8,128)(2,1)S(1)}, u32[]{:S(2)}, u32[]{:S(2)}) collective-permute-start(bf16[288,128]{1,0:T(8,128)(2,1)S(1)} %get-tuple-element.16), channel_id=1, source_target_pairs={{0,8},{8,0},{16,24},{24,16},{1,9},{9,1},{17,25},{25,17},{2,10},{10... | collective-permute-start | bytes 221192 | tf_op jit(solution)/shard_map/ppermute | solution.py:310
  9.1 2.6 %collective-permute-start.1 = (bf16[288,128]{1,0:T(8,128)(2,1)S(1)}, bf16[288,128]{1,0:T(8,128)(2,1)S(1)}, u32[]{:S(2)}, u32[]{:S(2)}) collective-permute-start(bf16[288,128]{1,0:T(8,128)(2,1)S(1)} %get-tuple-element.17), channel_id=1, source_target_pairs={{0,16},{8,24},{16,0},{24,8},{1,17},{9,25},{17,1},{25,9},{2,18},{10... | collective-permute-start | bytes 221192 | tf_op jit(solution)/shard_map/ppermute | solution.py:310
  11.7 0.0 collective-permute-start.2
  11.7 0.9 %collective-permute-start.7 = (bf16[288,128]{1,0:T(8,128)(2,1)S(1)}, bf16[288,128]{1,0:T(8,128)(2,1)S(1)}, u32[]{:S(2)}, u32[]{:S(2)}) collective-permute-start(bf16[288,128]{1,0:T(8,128)(2,1)S(1)} %get-tuple-element.20), channel_id=1, source_target_pairs={{0,8},{8,0},{16,24},{24,16},{1,9},{9,1},{17,25},{25,17},{2,10},{10... | collective-permute-start | bytes 221192 | tf_op jit(solution)/shard_map/ppermute | solution.py:310
  12.6 3.5 %collective-permute-start.8 = (bf16[288,128]{1,0:T(8,128)(2,1)S(1)}, bf16[288,128]{1,0:T(8,128)(2,1)S(1)}, u32[]{:S(2)}, u32[]{:S(2)}) collective-permute-start(bf16[288,128]{1,0:T(8,128)(2,1)S(1)} %get-tuple-element.21), channel_id=1, source_target_pairs={{0,16},{8,24},{16,0},{24,8},{1,17},{9,25},{17,1},{25,9},{2,18},{10... | collective-permute-start | bytes 221192 | tf_op jit(solution)/shard_map/ppermute | solution.py:310
  16.1 0.1 copy.15
  16.3 0.1 copy.19
  16.4 0.1 copy.20
  16.5 0.1 copy.16
  16.6 1.1 %collective-permute-done.7.refs_1_ = bf16[288,128]{1,0:T(8,128)(2,1)S(1)} collective-permute-done((bf16[288,128]{1,0:T(8,128)(2,1)S(1)}, bf16[288,128]{1,0:T(8,128)(2,1)S(1)}, u32[]{:S(2)}, u32[]{:S(2)}) %collective-permute-start.7) | collective-permute-done | bytes 73760 | tf_op jit(solution)/shard_map/ppermute | solution.py:310
  17.7 3.1 %collective-permute-start.9 = (bf16[288,128]{1,0:T(8,128)(2,1)S(1)}, bf16[288,128]{1,0:T(8,128)(2,1)S(1)}, u32[]{:S(2)}, u32[]{:S(2)}) collective-permute-start(bf16[288,128]{1,0:T(8,128)(2,1)S(1)} %get-tuple-element.22), channel_id=1, source_target_pairs={{0,24},{8,16},{16,8},{24,0},{1,25},{9,17},{17,9},{25,1},{2,26},{10... | collective-permute-start | bytes 221192 | tf_op jit(solution)/shard_map/ppermute | solution.py:310
  20.8 0.1 squeeze.19.refs_5_
  20.9 0.1 squeeze.18.refs_4_
  20.9 3.1 %collective-permute-done.8.refs_2_ = bf16[288,128]{1,0:T(8,128)(2,1)S(1)} collective-permute-done((bf16[288,128]{1,0:T(8,128)(2,1)S(1)}, bf16[288,128]{1,0:T(8,128)(2,1)S(1)}, u32[]{:S(2)}, u32[]{:S(2)}) %collective-permute-start.8) | collective-permute-done | bytes 73760 | tf_op jit(solution)/shard_map/ppermute | solution.py:310
  24.0 0.0 collective-permute-done.9.refs_3_
  24.0 0.6 %equalize.3.refs_0_ = bf16[2,256,256]{2,1,0:T(8,128)(2,1)S(1)} custom-call(bf16[288,128]{1,0:T(8,128)(2,1)S(1)} %get-tuple-element.19.refs_0_, bf16[288,128]{1,0:T(8,128)(2,1)S(1)} %collective-permute-done.7.refs_1_, bf16[288,128]{1,0:T(8,128)(2,1)S(1)} %collective-permute-done.8.refs_2_, bf16[288,128]{1,0:T(8,128)(2,1)S(1)} %collective-permute-done.9.refs_3_, ...), custom_call_target="tpu_custom_call" | custom-call | flops 1048576 | bytes 1048576 | tf_op jit(solution)/shard_map/equalize/pallas_call | solution.py:212
  24.6 1.6 %collective-permute-start.10 = (bf16[2,256,256]{2,1,0:T(8,128)(2,1)S(1)}, bf16[2,256,256]{2,1,0:T(8,128)(2,1)S(1)}, u32[]{:S(2)}, u32[]{:S(2)}) collective-permute-start(bf16[2,256,256]{2,1,0:T(8,128)(2,1)S(1)} %equalize.3.refs_0_), channel_id=1, source_target_pairs={{0,2},{1,3},{2,0},{3,1},{4,6},{5,7},{6,4},{7,5},{8,10},{9,11},{10,... | collective-permute-start | bytes 786440 | tf_op jit(solution)/shard_map/ppermute | solution.py:319
  26.2 0.1 squeeze.17.refs_5_
  26.3 0.1 squeeze.15.refs_4_
  26.4 1.5 %collective-permute-start.13 = (bf16[2,256,256]{2,1,0:T(8,128)(2,1)S(1)}, bf16[2,256,256]{2,1,0:T(8,128)(2,1)S(1)}, u32[]{:S(2)}, u32[]{:S(2)}) collective-permute-start(bf16[2,256,256]{2,1,0:T(8,128)(2,1)S(1)} %equalize.3.refs_0_), channel_id=1, source_target_pairs={{0,4},{4,0},{1,5},{5,1},{2,6},{6,2},{3,7},{7,3},{8,12},{12,8},{9,1... | collective-permute-start | bytes 786440 | tf_op jit(solution)/shard_map/ppermute | solution.py:322
  27.9 0.0 collective-permute-done.refs_1_
  27.9 0.0 collective-permute-done.1.refs_2_
  27.9 0.0 collective-permute-done.2.refs_3_
  27.9 0.6 %equalize.2.refs_0_ = bf16[2,256,256]{2,1,0:T(8,128)(2,1)S(1)} custom-call(bf16[288,128]{1,0:T(8,128)(2,1)S(1)} %get-tuple-element.15.refs_0_, bf16[288,128]{1,0:T(8,128)(2,1)S(1)} %collective-permute-done.refs_1_, bf16[288,128]{1,0:T(8,128)(2,1)S(1)} %collective-permute-done.1.refs_2_, bf16[288,128]{1,0:T(8,128)(2,1)S(1)} %collective-permute-done.2.refs_3_, ...), custom_call_target="tpu_custom_call" | custom-call | flops 1048576 | bytes 1048576 | tf_op jit(solution)/shard_map/equalize/pallas_call | solution.py:212
  28.5 0.6 %collective-permute-start.3 = (bf16[2,256,256]{2,1,0:T(8,128)(2,1)S(1)}, bf16[2,256,256]{2,1,0:T(8,128)(2,1)S(1)}, u32[]{:S(2)}, u32[]{:S(2)}) collective-permute-start(bf16[2,256,256]{2,1,0:T(8,128)(2,1)S(1)} %equalize.2.refs_0_), channel_id=1, source_target_pairs={{0,2},{1,3},{2,0},{3,1},{4,6},{5,7},{6,4},{7,5},{8,10},{9,11},{10,... | collective-permute-start | bytes 786440 | tf_op jit(solution)/shard_map/ppermute | solution.py:319
  29.1 0.0 collective-permute-start.11
  29.1 4.5 %collective-permute-done.10.refs_1_ = bf16[2,256,256]{2,1,0:T(8,128)(2,1)S(1)} collective-permute-done((bf16[2,256,256]{2,1,0:T(8,128)(2,1)S(1)}, bf16[2,256,256]{2,1,0:T(8,128)(2,1)S(1)}, u32[]{:S(2)}, u32[]{:S(2)}) %collective-permute-start.10) | collective-permute-done | bytes 262176 | tf_op jit(solution)/shard_map/ppermute | solution.py:319
  33.6 0.0 collective-permute-start.12
  33.6 1.0 %collective-permute-start.6 = (bf16[2,256,256]{2,1,0:T(8,128)(2,1)S(1)}, bf16[2,256,256]{2,1,0:T(8,128)(2,1)S(1)}, u32[]{:S(2)}, u32[]{:S(2)}) collective-permute-start(bf16[2,256,256]{2,1,0:T(8,128)(2,1)S(1)} %equalize.2.refs_0_), channel_id=1, source_target_pairs={{0,4},{4,0},{1,5},{5,1},{2,6},{6,2},{3,7},{7,3},{8,12},{12,8},{9,1... | collective-permute-start | bytes 786440 | tf_op jit(solution)/shard_map/ppermute | solution.py:322
  34.6 0.0 collective-permute-done.13.refs_4_
  34.6 0.2 collective-permute-start.4
  34.8 1.6 %collective-permute-done.3.refs_1_ = bf16[2,256,256]{2,1,0:T(8,128)(2,1)S(1)} collective-permute-done((bf16[2,256,256]{2,1,0:T(8,128)(2,1)S(1)}, bf16[2,256,256]{2,1,0:T(8,128)(2,1)S(1)}, u32[]{:S(2)}, u32[]{:S(2)}) %collective-permute-start.3) | collective-permute-done | bytes 262176 | tf_op jit(solution)/shard_map/ppermute | solution.py:319
  36.4 0.0 collective-permute-start.5
  36.4 0.0 collective-permute-done.11.refs_2_
  36.4 0.0 collective-permute-done.12.refs_3_
  36.4 0.0 copy-done.3
  36.4 2.2 %correlate.2.refs_5_ = f32[2,16,32,64]{3,2,1,0:T(8,128)S(1)} custom-call(s32[8,8]{1,0:T(8,128)S(1)} %copy-done.3, bf16[2,256,256]{2,1,0:T(8,128)(2,1)S(1)} %equalize.3.refs_0_, bf16[2,256,256]{2,1,0:T(8,128)(2,1)S(1)} %collective-permute-done.10.refs_1_, bf16[2,256,256]{2,1,0:T(8,128)(2,1)S(1)} %collective-permute-done.11.refs_2_, ...), custom_call_target="tpu_custom_call" | custom-call | flops 536870912 | bytes 4194304 | tf_op jit(solution)/shard_map/correlate/pallas_call | solution.py:294
  38.6 3.7 %collective-permute-done.6.refs_4_ = bf16[2,256,256]{2,1,0:T(8,128)(2,1)S(1)} collective-permute-done((bf16[2,256,256]{2,1,0:T(8,128)(2,1)S(1)}, bf16[2,256,256]{2,1,0:T(8,128)(2,1)S(1)}, u32[]{:S(2)}, u32[]{:S(2)}) %collective-permute-start.6) | collective-permute-done | bytes 262176 | tf_op jit(solution)/shard_map/ppermute | solution.py:322
  42.3 0.0 collective-permute-done.4.refs_2_
  42.3 0.0 collective-permute-done.5.refs_3_
  42.3 3.1 %correlate.3 = f32[2,16,32,128]{3,2,1,0:T(8,128)} custom-call(s32[8,8]{1,0:T(8,128)S(1)} %copy-done.3, bf16[2,256,256]{2,1,0:T(8,128)(2,1)S(1)} %equalize.2.refs_0_, bf16[2,256,256]{2,1,0:T(8,128)(2,1)S(1)} %collective-permute-done.3.refs_1_, bf16[2,256,256]{2,1,0:T(8,128)(2,1)S(1)} %collective-permute-done.4.refs_2_, ...), custom_call_target="tpu_custom_call" | custom-call | flops 536870912 | bytes 4194304 | tf_op jit(solution)/shard_map/correlate/pallas_call | solution.py:294
  (14 shorter events, 0.1 us)
Async XLA Ops:
  0.0 1.6 %copy-start = (s32[2,8,32768]{2,1,0:T(8,128)S(1)}, s32[2,8,32768]{2,1,0:T(8,128)}, u32[]{:S(2)}) copy-start(s32[2,8,32768]{2,1,0:T(8,128)} %volt_hbm.1) | copy-start | bytes 6291460
  1.6 1.2 %copy-start.1 = (bf16[2,1024,256]{2,1,0:T(8,128)(2,1)S(1)}, bf16[2,1024,256]{2,1,0:T(8,128)(2,1)}, u32[]{:S(2)}) copy-start(bf16[2,1024,256]{2,1,0:T(8,128)(2,1)} %constant.6.clone.table_hbm) | copy-start | bytes 3145732
  2.8 0.7 %copy-start.2 = (f32[4,1024]{1,0:T(4,128)S(1)}, f32[4,1024]{1,0:T(4,128)}, u32[]{:S(2)}) copy-start(f32[4,1024]{1,0:T(4,128)} %constant.7.clone.coef_ref) | copy-start | bytes 49156
  3.5 1.8 %copy-start.4 = (bf16[2,1024,256]{2,1,0:T(8,128)(2,1)S(1)}, bf16[2,1024,256]{2,1,0:T(8,128)(2,1)}, u32[]{:S(2)}) copy-start(bf16[2,1024,256]{2,1,0:T(8,128)(2,1)} %constant.8.clone.table_hbm) | copy-start | bytes 3145732
  3.5 12.6 %copy-start.5 = (f32[8,2,128]{2,1,0:T(2,128)S(1)}, f32[8,2,128]{2,1,0:T(2,128)}, u32[]{:S(2)}) copy-start(f32[8,2,128]{2,1,0:T(2,128)} %param.7) | copy-start | bytes 24580
  5.3 31.1 %copy-start.3 = (s32[8,8]{1,0:T(8,128)S(1)}, s32[8,8]{1,0:T(8,128)}, u32[]{:S(2)}) copy-start(s32[8,8]{1,0:T(8,128)} %map_ref.3) | copy-start | bytes 772
  6.0 21.9 %collective-permute-start = (bf16[288,128]{1,0:T(8,128)(2,1)S(1)}, bf16[288,128]{1,0:T(8,128)(2,1)S(1)}, u32[]{:S(2)}, u32[]{:S(2)}) collective-permute-start(bf16[288,128]{1,0:T(8,128)(2,1)S(1)} %get-tuple-element.16), channel_id=1, source_target_pairs={{0,8},{8,0},{16,24},{24,16},{1,9},{9,1},{17,25},{25,17},{2,10},{10... | collective-permute-start | bytes 221192 | tf_op jit(solution)/shard_map/ppermute | solution.py:310
  9.1 18.8 %collective-permute-start.1 = (bf16[288,128]{1,0:T(8,128)(2,1)S(1)}, bf16[288,128]{1,0:T(8,128)(2,1)S(1)}, u32[]{:S(2)}, u32[]{:S(2)}) collective-permute-start(bf16[288,128]{1,0:T(8,128)(2,1)S(1)} %get-tuple-element.17), channel_id=1, source_target_pairs={{0,16},{8,24},{16,0},{24,8},{1,17},{9,25},{17,1},{25,9},{2,18},{10... | collective-permute-start | bytes 221192 | tf_op jit(solution)/shard_map/ppermute | solution.py:310
  11.7 16.2 %collective-permute-start.2 = (bf16[288,128]{1,0:T(8,128)(2,1)S(1)}, bf16[288,128]{1,0:T(8,128)(2,1)S(1)}, u32[]{:S(2)}, u32[]{:S(2)}) collective-permute-start(bf16[288,128]{1,0:T(8,128)(2,1)S(1)} %get-tuple-element.18), channel_id=1, source_target_pairs={{0,24},{8,16},{16,8},{24,0},{1,25},{9,17},{17,9},{25,1},{2,26},{10... | collective-permute-start | bytes 221192 | tf_op jit(solution)/shard_map/ppermute | solution.py:310
  11.7 5.9 %collective-permute-start.7 = (bf16[288,128]{1,0:T(8,128)(2,1)S(1)}, bf16[288,128]{1,0:T(8,128)(2,1)S(1)}, u32[]{:S(2)}, u32[]{:S(2)}) collective-permute-start(bf16[288,128]{1,0:T(8,128)(2,1)S(1)} %get-tuple-element.20), channel_id=1, source_target_pairs={{0,8},{8,0},{16,24},{24,16},{1,9},{9,1},{17,25},{25,17},{2,10},{10... | collective-permute-start | bytes 221192 | tf_op jit(solution)/shard_map/ppermute | solution.py:310
  12.6 11.4 %collective-permute-start.8 = (bf16[288,128]{1,0:T(8,128)(2,1)S(1)}, bf16[288,128]{1,0:T(8,128)(2,1)S(1)}, u32[]{:S(2)}, u32[]{:S(2)}) collective-permute-start(bf16[288,128]{1,0:T(8,128)(2,1)S(1)} %get-tuple-element.21), channel_id=1, source_target_pairs={{0,16},{8,24},{16,0},{24,8},{1,17},{9,25},{17,1},{25,9},{2,18},{10... | collective-permute-start | bytes 221192 | tf_op jit(solution)/shard_map/ppermute | solution.py:310
  17.7 6.4 %collective-permute-start.9 = (bf16[288,128]{1,0:T(8,128)(2,1)S(1)}, bf16[288,128]{1,0:T(8,128)(2,1)S(1)}, u32[]{:S(2)}, u32[]{:S(2)}) collective-permute-start(bf16[288,128]{1,0:T(8,128)(2,1)S(1)} %get-tuple-element.22), channel_id=1, source_target_pairs={{0,24},{8,16},{16,8},{24,0},{1,25},{9,17},{17,9},{25,1},{2,26},{10... | collective-permute-start | bytes 221192 | tf_op jit(solution)/shard_map/ppermute | solution.py:310
  24.6 8.9 %collective-permute-start.10 = (bf16[2,256,256]{2,1,0:T(8,128)(2,1)S(1)}, bf16[2,256,256]{2,1,0:T(8,128)(2,1)S(1)}, u32[]{:S(2)}, u32[]{:S(2)}) collective-permute-start(bf16[2,256,256]{2,1,0:T(8,128)(2,1)S(1)} %equalize.3.refs_0_), channel_id=1, source_target_pairs={{0,2},{1,3},{2,0},{3,1},{4,6},{5,7},{6,4},{7,5},{8,10},{9,11},{10,... | collective-permute-start | bytes 786440 | tf_op jit(solution)/shard_map/ppermute | solution.py:319
  26.4 8.2 %collective-permute-start.13 = (bf16[2,256,256]{2,1,0:T(8,128)(2,1)S(1)}, bf16[2,256,256]{2,1,0:T(8,128)(2,1)S(1)}, u32[]{:S(2)}, u32[]{:S(2)}) collective-permute-start(bf16[2,256,256]{2,1,0:T(8,128)(2,1)S(1)} %equalize.3.refs_0_), channel_id=1, source_target_pairs={{0,4},{4,0},{1,5},{5,1},{2,6},{6,2},{3,7},{7,3},{8,12},{12,8},{9,1... | collective-permute-start | bytes 786440 | tf_op jit(solution)/shard_map/ppermute | solution.py:322
  28.5 7.9 %collective-permute-start.3 = (bf16[2,256,256]{2,1,0:T(8,128)(2,1)S(1)}, bf16[2,256,256]{2,1,0:T(8,128)(2,1)S(1)}, u32[]{:S(2)}, u32[]{:S(2)}) collective-permute-start(bf16[2,256,256]{2,1,0:T(8,128)(2,1)S(1)} %equalize.2.refs_0_), channel_id=1, source_target_pairs={{0,2},{1,3},{2,0},{3,1},{4,6},{5,7},{6,4},{7,5},{8,10},{9,11},{10,... | collective-permute-start | bytes 786440 | tf_op jit(solution)/shard_map/ppermute | solution.py:319
  29.1 7.3 %collective-permute-start.11 = (bf16[2,256,256]{2,1,0:T(8,128)(2,1)S(1)}, bf16[2,256,256]{2,1,0:T(8,128)(2,1)S(1)}, u32[]{:S(2)}, u32[]{:S(2)}) collective-permute-start(bf16[2,256,256]{2,1,0:T(8,128)(2,1)S(1)} %equalize.3.refs_0_), channel_id=1, source_target_pairs={{0,1},{1,0},{2,3},{3,2},{4,5},{5,4},{6,7},{7,6},{8,9},{9,8},{10,11... | collective-permute-start | bytes 786440 | tf_op jit(solution)/shard_map/ppermute | solution.py:323
  33.6 2.8 %collective-permute-start.12 = (bf16[2,256,256]{2,1,0:T(8,128)(2,1)S(1)}, bf16[2,256,256]{2,1,0:T(8,128)(2,1)S(1)}, u32[]{:S(2)}, u32[]{:S(2)}) collective-permute-start(bf16[2,256,256]{2,1,0:T(8,128)(2,1)S(1)} %collective-permute-done.10.refs_1_), channel_id=1, source_target_pairs={{0,1},{1,0},{2,3},{3,2},{4,5},{5,4},{6,7},{7,6},{8,9},{9,8},{10,11... | collective-permute-start | bytes 786440 | tf_op jit(solution)/shard_map/ppermute | solution.py:323
  33.6 8.7 %collective-permute-start.6 = (bf16[2,256,256]{2,1,0:T(8,128)(2,1)S(1)}, bf16[2,256,256]{2,1,0:T(8,128)(2,1)S(1)}, u32[]{:S(2)}, u32[]{:S(2)}) collective-permute-start(bf16[2,256,256]{2,1,0:T(8,128)(2,1)S(1)} %equalize.2.refs_0_), channel_id=1, source_target_pairs={{0,4},{4,0},{1,5},{5,1},{2,6},{6,2},{3,7},{7,3},{8,12},{12,8},{9,1... | collective-permute-start | bytes 786440 | tf_op jit(solution)/shard_map/ppermute | solution.py:322
  34.6 7.7 %collective-permute-start.4 = (bf16[2,256,256]{2,1,0:T(8,128)(2,1)S(1)}, bf16[2,256,256]{2,1,0:T(8,128)(2,1)S(1)}, u32[]{:S(2)}, u32[]{:S(2)}) collective-permute-start(bf16[2,256,256]{2,1,0:T(8,128)(2,1)S(1)} %equalize.2.refs_0_), channel_id=1, source_target_pairs={{0,1},{1,0},{2,3},{3,2},{4,5},{5,4},{6,7},{7,6},{8,9},{9,8},{10,11... | collective-permute-start | bytes 786440 | tf_op jit(solution)/shard_map/ppermute | solution.py:323
  36.4 5.9 %collective-permute-start.5 = (bf16[2,256,256]{2,1,0:T(8,128)(2,1)S(1)}, bf16[2,256,256]{2,1,0:T(8,128)(2,1)S(1)}, u32[]{:S(2)}, u32[]{:S(2)}) collective-permute-start(bf16[2,256,256]{2,1,0:T(8,128)(2,1)S(1)} %collective-permute-done.3.refs_1_), channel_id=1, source_target_pairs={{0,1},{1,0},{2,3},{3,2},{4,5},{5,4},{6,7},{7,6},{8,9},{9,8},{10,11... | collective-permute-start | bytes 786440 | tf_op jit(solution)/shard_map/ppermute | solution.py:323

commit v3 on v2

v3 whole, which is shorter than its diff:
```python
import functools
import math

import jax
import jax.numpy as jnp
import ml_dtypes
import numpy as np
from jax import lax
from jax.experimental import pallas as pl
from jax.experimental.pallas import tpu as pltpu
from jax.sharding import PartitionSpec as P

NCHAN = 1024
HALF = NCHAN // 2
CHANNELS = 512
TAPS = 4
FIRST = 256
SIG = 8
LANES = 128
GROUP = 4
BATCH = 4
PARTS = 2
VMEM_BYTES = 48 * 1024 * 1024
FILTER_VMEM_BYTES = 52 * 1024 * 1024
COEF_ROWS = 64


def fir_coefficients():
    position = np.arange(TAPS * NCHAN, dtype=np.float64) + 0.5
    offsets = position / NCHAN - TAPS / 2.0
    window = 0.5 - 0.5 * np.cos(2.0 * math.pi * position / (TAPS * NCHAN))
    return (np.sinc(offsets) * window).reshape(TAPS, NCHAN)


def spectrum_scale():
    return float(1.0 / (128.0 * np.sqrt(np.sum(fir_coefficients() ** 2))))


def dft_tables(owners):
    n = np.arange(HALF, dtype=np.int64)[:, None, None, None, None]
    k = FIRST + np.arange(CHANNELS, dtype=np.int64).reshape(owners, PARTS, -1, 2)
    angles = (n * k % NCHAN) * (2.0 * math.pi / NCHAN)
    cosine, sine = np.cos(angles), np.sin(angles)
    first = np.stack([cosine, -sine], axis=2)
    second = np.stack([sine, cosine], axis=2)
    tables = np.stack([first, second])
    tables = np.transpose(tables, (4, 6, 0, 1, 2, 3, 5))
    return tables.reshape(PARTS, 2 * NCHAN, -1).astype(np.float32).astype(ml_dtypes.bfloat16)


def constants(owners):
    tables = dft_tables(owners)
    lanes = tables.shape[2]
    left = fir_coefficients().astype(np.float32)
    terms = []
    for _ in range(3):
        terms.append(left.astype(ml_dtypes.bfloat16))
        left = left - terms[-1].astype(np.float32)
    terms = np.stack(terms).reshape(-1, lanes)
    pad = np.zeros((-terms.shape[0] % COEF_ROWS, lanes), ml_dtypes.bfloat16)
    return np.concatenate([tables.reshape(-1, lanes), terms, pad])


def transform(filt, table, scale, stage, out_refs):
    owners = len(out_refs)
    me = lax.axis_index("chan")
    spectra = [
        jnp.dot(filt[r], table[r * NCHAN : (r + 1) * NCHAN], preferred_element_type=jnp.float32) * scale
        for r in range(2)
    ]
    width = spectra[0].shape[1] // owners
    for owner in range(owners):
        here = slice(owner * width, (owner + 1) * width)
        piece = jnp.concatenate([spectra[0][:, here], spectra[1][:, here]], axis=1)
        stage[jnp.bitwise_xor(me, owner)] = piece.astype(jnp.bfloat16)
    for d in range(owners):
        out_refs[d][...] = stage[d]


def filter_kernel(frames, pieces, scale, volt_hbm, table_hbm, *refs):
    out_refs, (filt, volt, table, terms, coef, stage, sems) = refs[:-7], refs[-7:]
    per = frames // pieces
    lead = TAPS - 1
    copies = []
    for piece in range(pieces):
        copies.append(
            pltpu.make_async_copy(
                volt_hbm.at[:, :, pl.ds(piece * per * NCHAN, per * NCHAN)],
                volt.at[:, :, pl.ds((lead + piece * per) * NCHAN, per * NCHAN)],
                sems.at[piece],
            )
        )
    table_copy = pltpu.make_async_copy(table_hbm.at[pl.ds(0, 2 * NCHAN)], table, sems.at[pieces])
    coef_copy = pltpu.make_async_copy(
        table_hbm.at[pl.ds(PARTS * 2 * NCHAN, terms.shape[0])], terms, sems.at[pieces + 1]
    )
    coef_copy.start()
    for copy in copies:
        copy.start()
    table_copy.start()
    tail = volt.shape[2] - (lead + frames) * NCHAN
    volt[:, :, : lead * NCHAN] = jnp.zeros((2, SIG, lead * NCHAN), jnp.int32)
    volt[:, :, (lead + frames) * NCHAN :] = jnp.zeros((2, SIG, tail), jnp.int32)
    coef_copy.wait()
    across = coef.shape[1]
    per_term = TAPS * NCHAN // across
    coef[...] = sum(terms[t * per_term : (t + 1) * per_term, :].astype(jnp.float32) for t in range(3))

    def filter_group(group, _):
        base = pl.multiple_of(group * (GROUP * NCHAN), GROUP * NCHAN)
        rows = pl.ds(pl.multiple_of(group * (GROUP * SIG), GROUP * SIG), GROUP * SIG)
        for column in range(HALF // LANES):
            for part in range(2):
                halves = []
                for half in range(2):
                    lane = half * HALF + column * LANES
                    at = [k * (NCHAN // across) + lane // across for k in range(TAPS)]
                    taps = [coef[i : i + 1, lane % across : lane % across + LANES] for i in at]
                    near = [
                        volt[part, :, pl.ds(base + f * NCHAN + lane, LANES)].astype(jnp.float32)
                        for f in range(GROUP + TAPS - 1)
                    ]
                    sums = []
                    for m in range(GROUP):
                        total = taps[0] * near[m]
                        for k in range(1, TAPS):
                            total = total + taps[k] * near[m + k]
                        sums.append(total)
                    halves.append(jnp.concatenate(sums, axis=0))
                where = pl.ds(part * HALF + column * LANES, LANES)
                filt[0, rows, where] = (halves[0] + halves[1]).astype(jnp.bfloat16)
                filt[1, rows, where] = (halves[0] - halves[1]).astype(jnp.bfloat16)
        return 0

    groups = per // GROUP
    for piece in range(pieces):
        copies[piece].wait()
        lax.fori_loop(piece * groups, (piece + 1) * groups, filter_group, 0)
    lax.fori_loop(frames // GROUP, frames // GROUP + 1, filter_group, 0)
    table_copy.wait()
    transform(filt, table, scale, stage, out_refs)


def transform_kernel(part, scale, filt, table_hbm, *refs):
    out_refs, table, stage, sem = refs[:-3], refs[-3], refs[-2], refs[-1]
    copy = pltpu.make_async_copy(table_hbm.at[pl.ds(part * 2 * NCHAN, 2 * NCHAN)], table, sem)
    copy.start()
    copy.wait()
    transform(filt, table, scale, stage, out_refs)


IN_VMEM = pl.BlockSpec(memory_space=pltpu.VMEM)
IN_HBM = pl.BlockSpec(memory_space=pl.ANY)
IN_SMEM = pl.BlockSpec(memory_space=pltpu.SMEM)


def filtered_and_first(voltages, owners, table):
    frames = voltages.shape[2] // NCHAN
    rows = (frames + GROUP) * SIG
    pieces = 4
    across = table.shape[1]
    terms = table.shape[0] - PARTS * 2 * NCHAN
    lanes = 2 * CHANNELS // owners // PARTS
    *first, filt = pl.pallas_call(
        functools.partial(filter_kernel, frames, pieces, spectrum_scale()),
        out_shape=[jax.ShapeDtypeStruct((rows, lanes), jnp.bfloat16)] * owners
        + [jax.ShapeDtypeStruct((2, rows, NCHAN), jnp.bfloat16)],
        in_specs=[IN_HBM, IN_HBM],
        out_specs=[IN_VMEM] * (owners + 1),
        scratch_shapes=[
            pltpu.VMEM((2, SIG, (frames + GROUP + TAPS - 1) * NCHAN), jnp.int32),
            pltpu.VMEM((2 * NCHAN, across), jnp.bfloat16),
            pltpu.VMEM((terms, across), jnp.bfloat16),
            pltpu.VMEM((TAPS * NCHAN // across, across), jnp.float32),
            pltpu.VMEM((owners, rows, lanes), jnp.bfloat16),
            pltpu.SemaphoreType.DMA((pieces + 2,)),
        ],
        compiler_params=pltpu.CompilerParams(vmem_limit_bytes=FILTER_VMEM_BYTES),
        cost_estimate=pl.CostEstimate(flops=1 << 29, bytes_accessed=4 << 20, transcendentals=0),
        name="filter_and_transform",
    )(voltages, table)
    return filt, first


def next_part(part, filt, table, owners):
    rows = filt.shape[1]
    lanes = 2 * CHANNELS // owners // PARTS
    return pl.pallas_call(
        functools.partial(transform_kernel, part, spectrum_scale()),
        out_shape=[jax.ShapeDtypeStruct((rows, lanes), jnp.bfloat16)] * owners,
        in_specs=[IN_VMEM, IN_HBM],
        out_specs=[IN_VMEM] * owners,
        scratch_shapes=[
            pltpu.VMEM((2 * NCHAN, table.shape[1]), jnp.bfloat16),
            pltpu.VMEM((owners, rows, lanes), jnp.bfloat16),
            pltpu.SemaphoreType.DMA(()),
        ],
        compiler_params=pltpu.CompilerParams(vmem_limit_bytes=FILTER_VMEM_BYTES),
        cost_estimate=pl.CostEstimate(flops=1 << 29, bytes_accessed=2 << 20, transcendentals=0),
        name="transform",
    )(filt, table)


def equalize_kernel(owners, frames, h, part, before, *refs):
    pieces = refs[:owners]
    gains_ref, by_time, by_channel = refs[owners], refs[-2], refs[-1]
    earlier = refs[owners + 1 : owners + 1 + before]
    out_ref = refs[owners + 1 + before]
    if before:
        together = refs[owners + 2 + before]
        for i in range(before):
            together[i] = earlier[i][...]
    width = 4 * h
    own_rows = frames * SIG
    over = GROUP * SIG
    times = owners * frames
    tiles = times // LANES
    me = lax.axis_index("chan")
    for d in range(owners):
        source = jnp.bitwise_xor(me, d)
        start = pl.multiple_of(source * own_rows, own_rows)
        by_time[pl.ds(start, own_rows), :width] = pieces[d][:own_rows, :].astype(jnp.float32)
    for d in range(owners):
        source = jnp.bitwise_xor(me, d)

        @pl.when(source < owners - 1)
        def _():
            start = pl.multiple_of((source + 1) * own_rows, own_rows)
            by_time[pl.ds(start, over), :width] += pieces[d][own_rows:, :].astype(jnp.float32)

    gains = [gains_ref[pl.ds(part * 2 * h + r, h, stride=2), :] for r in range(2)]
    for s in range(SIG):
        x = by_time[pl.ds(s, times, stride=SIG), :][:, :width].T
        for r in range(2):
            real, imag = x[2 * r * h : (2 * r + 1) * h], x[(2 * r + 1) * h : (2 * r + 2) * h]
            gain_real, gain_imag = gains[r][:, 2 * s : 2 * s + 1], gains[r][:, 2 * s + 1 : 2 * s + 2]
            both = [real * gain_real - imag * gain_imag, real * gain_imag + imag * gain_real]
            for q in range(2):
                for tile in range(tiles):
                    by_channel[(2 * r + q) * tiles + tile, pl.ds(s, h, stride=SIG), :] = both[q][
                        :, tile * LANES : (tile + 1) * LANES
                    ]
    for r in range(2):
        for tile in range(2 * tiles):
            ready = by_channel[r * 2 * tiles + tile].astype(jnp.bfloat16)
            out_ref[r, :, tile * LANES : (tile + 1) * LANES] = ready
            if before:
                together[before, r, :, tile * LANES : (tile + 1) * LANES] = ready


def equalize(pieces, gains, earlier, part, frames):
    owners = len(pieces)
    h = gains.shape[0] // PARTS // 2
    times = owners * frames
    before = len(earlier)
    shape = (2, h * SIG, 2 * times)
    shapes = [jax.ShapeDtypeStruct(shape, jnp.bfloat16)]
    if before:
        shapes.append(jax.ShapeDtypeStruct((before + 1,) + shape, jnp.bfloat16))
    return pl.pallas_call(
        functools.partial(equalize_kernel, owners, frames, h, part, before),
        out_shape=shapes,
        in_specs=[IN_VMEM] * (owners + 1 + before),
        out_specs=[IN_VMEM] * len(shapes),
        scratch_shapes=[
            pltpu.VMEM((times * SIG, LANES), jnp.float32),
            pltpu.VMEM((4 * times // LANES, h * SIG, LANES), jnp.float32),
        ],
        compiler_params=pltpu.CompilerParams(vmem_limit_bytes=VMEM_BYTES),
        cost_estimate=pl.CostEstimate(flops=1 << 20, bytes_accessed=1 << 20, transcendentals=0),
        name="equalize",
    )(*pieces, gains, *earlier)


def row_places(col, n_col):
    chips = n_col // 2
    chip, core = lax.div(col, 2), lax.rem(col, 2)
    places = [col] + [lax.rem(chip + chips - d, chips) * 2 + core for d in range(1, chips)]
    return places + [jnp.bitwise_xor(p, 1) for p in places]


def column_places(row, n_row):
    return [row] + [lax.rem(row + n_row - d, n_row) for d in range(1, n_row)]


def correlate_kernel(n_row, n_col, h, times, part, before, map_ref, *refs):
    row_blocks = [ref.at[part] if i == n_col // 2 else ref for i, ref in enumerate(refs[:n_col])]
    col_blocks = (refs[0],) + refs[n_col : n_col + n_row - 1]
    last = part == PARTS - 1
    if last:
        out_hbm, product, out_ref, sems = refs[-4:]
        earlier = refs[-5]
    else:
        out_ref, product = refs[-2:]
        earlier = refs[-3]
    copies = []
    me_row, me_col = lax.axis_index("brow"), lax.axis_index("bcol")
    row_at, col_at = row_places(me_col, n_col), column_places(me_row, n_row)
    rows = BATCH * SIG
    tiles = n_col * rows // LANES

    def batch(step, _):
        parity = step // (h // BATCH)
        inner = step % (h // BATCH)
        here = pl.ds(pl.multiple_of(inner * rows, rows), rows)
        a = jnp.concatenate([block[parity, here, :] for block in row_blocks], axis=0)
        b = jnp.concatenate([block[parity, here, :] for block in col_blocks], axis=0)
        turned = jnp.concatenate([-b[:, times:], b[:, :times]], axis=1)
        both = jnp.concatenate([b, turned], axis=0)
        result = lax.dot_general(both, a, (((1,), (1,)), ((), ())), preferred_element_type=jnp.float32)
        for k in range(2 * n_row):
            for i in range(BATCH):
                channel = 2 * (inner * BATCH + i) + parity
                for tile in range(tiles):
                    product[k * tiles + tile, pl.ds(pl.multiple_of(channel * SIG, SIG), SIG), :] = result[
                        k * rows + i * SIG : k * rows + (i + 1) * SIG, tile * LANES : (tile + 1) * LANES
                    ]
        return 0

    lax.fori_loop(0, 2 * h // BATCH, batch, 0, unroll=4)
    channels = 2 * h
    lane = lax.broadcasted_iota(jnp.int32, (SIG, channels), 1)
    inner_of = (lane // 2) % BATCH
    for q in range(2):
        for e in range(n_row):
            owned = [map_ref[me_row * n_col + row_at[d], col_at[e] * n_col + me_col] == 1 for d in range(n_col)]
            for s2 in range(SIG):
                b_at = col_at[e] * SIG + s2
                for d in range(n_col):
                    if d * rows % LANES == 0:
                        tile = (q * n_row + e) * tiles + d * rows // LANES
                        x = product[tile, pl.ds(s2, channels, stride=SIG), :].T
                    start = d * rows % LANES
                    kept = x[start : start + SIG]
                    for i in range(1, BATCH):
                        kept = jnp.where(inner_of == i, x[start + i * SIG : start + (i + 1) * SIG], kept)
                    kept = jnp.where(owned[d], kept * (1.0 / times), 0.0)
                    a_at = pl.ds(pl.multiple_of(row_at[d] * SIG, SIG), SIG)
                    if before:
                        kept = jnp.concatenate([earlier[q, b_at, a_at, :], kept], axis=1)
                    out_ref[q, b_at, a_at, :] = kept
            if last:
                where = pl.ds(pl.multiple_of(col_at[e] * SIG, SIG), SIG)
                copy = pltpu.make_async_copy(out_ref.at[q, where], out_hbm.at[q, where], sems.at[q * n_row + e])
                copy.start()
                copies.append(copy)
    for copy in copies:
        copy.wait()


def correlate(tile_map, blocks, earlier, part, n_row, n_col):
    h = blocks[0].shape[1] // SIG
    times = blocks[0].shape[2] // 2
    before = earlier.shape[3] if earlier is not None else 0
    operands = list(blocks) + ([earlier] if before else [])
    last = part == PARTS - 1
    out_shape = (2, n_row * SIG, n_col * SIG, before + 2 * h)
    in_last = [pltpu.VMEM(out_shape, jnp.float32), pltpu.SemaphoreType.DMA((2 * n_row,))]
    return pl.pallas_call(
        functools.partial(correlate_kernel, n_row, n_col, h, times, part, before),
        out_shape=jax.ShapeDtypeStruct(out_shape, jnp.float32),
        in_specs=[IN_SMEM] + [IN_VMEM] * len(operands),
        out_specs=IN_HBM if last else IN_VMEM,
        scratch_shapes=[pltpu.VMEM((2 * n_row * n_col * BATCH * SIG // LANES, 2 * h * SIG, LANES), jnp.float32)]
        + (in_last if last else []),
        compiler_params=pltpu.CompilerParams(vmem_limit_bytes=VMEM_BYTES),
        cost_estimate=pl.CostEstimate(flops=1 << 29, bytes_accessed=4 << 20, transcendentals=0),
        name="correlate",
    )(tile_map, *operands)


def to_owners(pieces):
    owners = len(pieces)
    arrived = [pieces[0]] + [None] * (owners - 1)
    for d in range(owners - 1, 0, -1):
        arrived[d] = lax.ppermute(pieces[d], "chan", [(i, i ^ d) for i in range(owners)])
    return arrived


def held_back(blocks, after):
    return pl.pallas_call(
        lambda *refs: None,
        out_shape=[jax.ShapeDtypeStruct(block.shape, block.dtype) for block in blocks],
        in_specs=[IN_HBM] * (len(blocks) + len(after)),
        out_specs=[IN_HBM] * len(blocks),
        input_output_aliases={i: i for i in range(len(blocks))},
        name="held_back",
    )(*blocks, *after)


def shards(voltages, antenna_gains, tile_map):
    owners = lax.axis_size("chan")
    n_row = lax.axis_size("brow")
    n_col = lax.axis_size("bcol")
    chips = n_col // 2
    frames = voltages.shape[2] // NCHAN
    table = jnp.asarray(constants(owners))
    gains = jnp.transpose(antenna_gains, (2, 0, 1)).reshape(-1, 2 * SIG)
    pad = -gains.shape[1] % LANES
    gains = jnp.pad(gains, ((0, 0), (0, pad)))
    across = [[(i, (i // 2 + d) % chips * 2 + i % 2) for i in range(n_col)] for d in range(chips)]
    along = [[(i, (i + d) % n_row) for i in range(n_row)] for d in range(n_row)]
    other_core = [(i, i ^ 1) for i in range(n_col)]

    filt, pieces = filtered_and_first(voltages, owners, table)
    own, far, column = [], [], []
    arrived = to_owners(pieces)
    for part in range(PARTS):
        later = None
        if part < PARTS - 1:
            pieces = next_part(part + 1, filt, table, owners)
            later = to_owners([pieces[0], *held_back(pieces[1:], arrived[-1:])])
        block, *together = equalize(arrived, gains, own if part == PARTS - 1 else [], part, frames)
        own.append(block)
        far.append([lax.ppermute(block, "bcol", across[d]) for d in range(1, chips)])
        column.append([lax.ppermute(block, "brow", along[d]) for d in range(1, n_row)])
        arrived = later
    beside = lax.ppermute(together[0], "bcol", other_core)
    result = None
    for part in range(PARTS):
        if far[part]:
            far[part] = list(held_back(far[part], own[-1:] + column[part]))
        near = [lax.ppermute(block, "bcol", other_core) for block in far[part]]
        blocks = [own[part]] + far[part] + [beside] + near + column[part]
        result = correlate(tile_map, blocks, result, part, n_row, n_col)
    return jnp.transpose(result, (3, 0, 1, 2))[None, None]


def solution(mesh):
    in_specs = (P(None, ("brow", "bcol"), "chan"), P(("brow", "bcol"), None, "chan"), P())
    out_specs = P("brow", "bcol", "chan", None, None, None)
    return jax.shard_map(shards, mesh=mesh, in_specs=in_specs, out_specs=out_specs, check_vma=False)
```

time: 45.7 us -> 43.4 us (0.950)
  waiting for transfers between devices: 14 us -> 7.3 us
  local copies, waits for them, and re-layouts: 4.3 us -> 7.62 us
  Pallas kernels: 8.94 us -> 11.7 us
  starting transfers between devices: 18 us -> 16.4 us
    ppermute x8 -> x7, waiting for transfers between devices: 9.75 us -> 5.7 us  [the longest x2 4.48 us: shards(): lax.ppermute(block, 'bcol', across[d])]
    unnamed x13 -> x30, local copies, waits for them, and re-layouts: 3.67 us -> 7.51 us
    ppermute x6, starting transfers between devices: 13.1 us -> 10.1 us  [to_owners(): lax.ppermute(pieces[d], 'chan', [(i, i ^ d) for i in range(owners)])]
    ppermute x6, waiting for transfers between devices: 4.22 us -> 1.59 us  [to_owners(): lax.ppermute(pieces[d], 'chan', [(i, i ^ d) for i in range(owners)])]
    pallas_call x4 -> x7, Pallas kernels: 3.63 us -> 6.1 us  [the longest x1 2.61 us: filtered_and_first(): pl.pallas_call(functools.partial(filter_kernel, frames, pieces, spectrum_...]
    ppermute x8 -> x7, starting transfers between devices: 4.92 us -> 6.24 us  [the longest x2 3.25 us: shards(): lax.ppermute(block, 'brow', along[d])]
  transfers between devices with their start and end apart: 14 -> 13, of which waited for: 5 -> 3; matrix products, arithmetic and copies ran while one was open for 2% -> 0% of each run, Pallas kernels for 7% -> 13%
where the time goes in v3:
time: 43.4 us; the launch traced here: 43.2 us
  starting transfers between devices  16.4 us (38%)
  Pallas kernels  11.7 us (27%)
  local copies, waits for them, and re-layouts  7.62 us (18%)
  waiting for transfers between devices  7.3 us (17%)
    ppermute x6, starting transfers between devices, to_owners(): lax.ppermute(pieces[d], 'chan', [(i, i ^ d) for i in range(owners)])  10.1 us
    unnamed x30, local copies, waits for them, and re-layouts  7.51 us
    pallas_call x2, Pallas kernels, correlate(): pl.pallas_call(functools.partial(correlate_kernel, n_row, n_col, h, times...  5.61 us
    ppermute x2, waiting for transfers between devices, shards(): lax.ppermute(block, 'bcol', across[d])  4.48 us
    ppermute x2, starting transfers between devices, shards(): lax.ppermute(block, 'brow', along[d])  3.25 us
    ppermute x2, starting transfers between devices, shards(): lax.ppermute(block, 'bcol', across[d])  2.98 us
    pallas_call x1, Pallas kernels, filtered_and_first(): pl.pallas_call(functools.partial(filter_kernel, frames, pieces, spectrum_...  2.61 us
    pallas_call x1, Pallas kernels, next_part(): pl.pallas_call(functools.partial(transform_kernel, part, spectrum_scale()...  1.83 us
  transfers between devices with their start and end apart: 13, of which 3 were waited for; matrix products, arithmetic and copies ran while one was open for 0% of the time, Pallas kernels for 13%

profile of v3, /device:TPU:0, one launch (start us, length us, event | category | flops | bytes accessed | tf_op | source)
XLA Modules:
  0.0 43.2 jit_solution(15547114904521184925)
XLA Ops:
  0.0 2.6 %filter_and_transform.1 = (bf16[288,128]{1,0:T(8,128)(2,1)S(1)}, bf16[288,128]{1,0:T(8,128)(2,1)S(1)}, bf16[288,128]{1,0:T(8,128)(2,1)S(1)}, bf16[288,128]{1,0:T(8,128)(2,1)S(1)}, bf16[2,288,1024]{2,1,0:T(8,128)(2,1)S(1)}) custom-call(s32[2,8,32768]{2,1,0:T(8,128)} %volt_hbm.1, bf16[4160,256]{1,0:T(8,128)(2,1)} %constant.5.clone.table_hbm), custom_call_target="tpu_custom_call" | custom-call | flops 536870912 | bytes 4194304 | tf_op jit(solution)/shard_map/filter_and_transform/pallas_call | solution.py:164
  2.6 0.0 copy-start.14
  2.6 5.1 %collective-permute-start = (bf16[288,128]{1,0:T(8,128)(2,1)S(1)}, bf16[288,128]{1,0:T(8,128)(2,1)S(1)}, u32[]{:S(2)}, u32[]{:S(2)}) collective-permute-start(bf16[288,128]{1,0:T(8,128)(2,1)S(1)} %get-tuple-element.24), channel_id=1, source_target_pairs={{0,24},{8,16},{16,8},{24,0},{1,25},{9,17},{17,9},{25,1},{2,26},{10... | collective-permute-start | bytes 221192 | tf_op jit(solution)/shard_map/ppermute | solution.py:376
  7.8 0.0 collective-permute-start.4
  7.8 0.6 %collective-permute-start.5 = (bf16[288,128]{1,0:T(8,128)(2,1)S(1)}, bf16[288,128]{1,0:T(8,128)(2,1)S(1)}, u32[]{:S(2)}, u32[]{:S(2)}) collective-permute-start(bf16[288,128]{1,0:T(8,128)(2,1)S(1)} %get-tuple-element.30), channel_id=1, source_target_pairs={{0,16},{8,24},{16,0},{24,8},{1,17},{9,25},{17,1},{25,9},{2,18},{10... | collective-permute-start | bytes 221192 | tf_op jit(solution)/shard_map/ppermute | solution.py:376
  8.4 1.8 %transform.1 = (bf16[288,128]{1,0:T(8,128)(2,1)S(1)}, bf16[288,128]{1,0:T(8,128)(2,1)S(1)}, bf16[288,128]{1,0:T(8,128)(2,1)S(1)}, bf16[288,128]{1,0:T(8,128)(2,1)S(1)}) custom-call(bf16[2,288,1024]{2,1,0:T(8,128)(2,1)S(1)} %get-tuple-element.19.filt, bf16[4160,256]{1,0:T(8,128)(2,1)} %constant.5.clone.table_hbm), custom_call_target="tpu_custom_call" | custom-call | flops 536870912 | bytes 2097152 | tf_op jit(solution)/shard_map/transform/pallas_call | solution.py:188
  10.2 0.0 copy-start.10
  10.2 0.6 %copy-done.10 = bf16[288,128]{1,0:T(8,128)(2,1)} copy-done((bf16[288,128]{1,0:T(8,128)(2,1)}, bf16[288,128]{1,0:T(8,128)(2,1)S(1)}, u32[]{:S(2)}) %copy-start.10) | copy-done | bytes 73752
  10.9 0.6 %copy-done.11 = bf16[288,128]{1,0:T(8,128)(2,1)} copy-done((bf16[288,128]{1,0:T(8,128)(2,1)}, bf16[288,128]{1,0:T(8,128)(2,1)S(1)}, u32[]{:S(2)}) %copy-start.11) | copy-done | bytes 73752
  11.5 0.6 %copy-done.12 = bf16[288,128]{1,0:T(8,128)(2,1)} copy-done((bf16[288,128]{1,0:T(8,128)(2,1)}, bf16[288,128]{1,0:T(8,128)(2,1)S(1)}, u32[]{:S(2)}) %copy-start.12) | copy-done | bytes 73752
  12.1 0.0 collective-permute-done.refs_3_
  12.1 0.6 %copy-done.8 = bf16[288,128]{1,0:T(8,128)(2,1)} copy-done((bf16[288,128]{1,0:T(8,128)(2,1)}, bf16[288,128]{1,0:T(8,128)(2,1)S(1)}, u32[]{:S(2)}) %copy-start.8) | copy-done | bytes 73752
  12.8 1.4 %collective-permute-start.1 = (bf16[288,128]{1,0:T(8,128)(2,1)}, bf16[288,128]{1,0:T(8,128)(2,1)S(1)}, u32[]{:S(2)}, u32[]{:S(2)}) collective-permute-start(bf16[288,128]{1,0:T(8,128)(2,1)} %get-tuple-element.25), channel_id=1, source_target_pairs={{0,8},{8,0},{16,24},{24,16},{1,9},{9,1},{17,25},{25,17},{2,10},{10... | collective-permute-start | bytes 221192 | tf_op jit(solution)/shard_map/ppermute | solution.py:376
  14.2 2.9 %collective-permute-start.2 = (bf16[288,128]{1,0:T(8,128)(2,1)}, bf16[288,128]{1,0:T(8,128)(2,1)S(1)}, u32[]{:S(2)}, u32[]{:S(2)}) collective-permute-start(bf16[288,128]{1,0:T(8,128)(2,1)} %get-tuple-element.26), channel_id=1, source_target_pairs={{0,16},{8,24},{16,0},{24,8},{1,17},{9,25},{17,1},{25,9},{2,18},{10... | collective-permute-start | bytes 221192 | tf_op jit(solution)/shard_map/ppermute | solution.py:376
  17.1 0.1 collective-permute-start.3
  17.2 0.1 copy.11
  17.3 0.0 collective-permute-done.4.refs_1_
  17.3 0.0 collective-permute-done.5.refs_2_
  17.3 0.9 %copy-done.9 = bf16[288,128]{1,0:T(8,128)(2,1)S(1)} copy-done((bf16[288,128]{1,0:T(8,128)(2,1)S(1)}, bf16[288,128]{1,0:T(8,128)(2,1)}, u32[]{:S(2)}) %copy-start.9) | copy-done | bytes 73752
  18.2 0.4 %equalize.2.refs_5_.refs_0_ = bf16[2,256,256]{2,1,0:T(8,128)(2,1)S(1)} custom-call(bf16[288,128]{1,0:T(8,128)(2,1)S(1)} %get-tuple-element.28.refs_0_, bf16[288,128]{1,0:T(8,128)(2,1)S(1)} %collective-permute-done.4.refs_1_, bf16[288,128]{1,0:T(8,128)(2,1)S(1)} %collective-permute-done.5.refs_2_, bf16[288,128]{1,0:T(8,128)(2,1)S(1)} %copy-done.9, ...), custom_call_target="tpu_custom_call" | custom-call | flops 1048576 | bytes 1048576 | tf_op jit(solution)/shard_map/equalize/pallas_call | solution.py:260
  18.6 1.7 %collective-permute-start.11 = (bf16[2,256,256]{2,1,0:T(8,128)(2,1)S(1)}, bf16[2,256,256]{2,1,0:T(8,128)(2,1)S(1)}, u32[]{:S(2)}, u32[]{:S(2)}) collective-permute-start(bf16[2,256,256]{2,1,0:T(8,128)(2,1)S(1)} %equalize.2.refs_5_.refs_0_), channel_id=1, source_target_pairs={{0,4},{4,0},{1,5},{5,1},{2,6},{6,2},{3,7},{7,3},{8,12},{12,8},{9,1... | collective-permute-start | bytes 786440 | tf_op jit(solution)/shard_map/ppermute | solution.py:416
  20.4 1.5 %collective-permute-start.10 = (bf16[2,256,256]{2,1,0:T(8,128)(2,1)S(1)}, bf16[2,256,256]{2,1,0:T(8,128)(2,1)S(1)}, u32[]{:S(2)}, u32[]{:S(2)}) collective-permute-start(bf16[2,256,256]{2,1,0:T(8,128)(2,1)S(1)} %equalize.2.refs_5_.refs_0_), channel_id=1, source_target_pairs={{0,2},{1,3},{2,0},{3,1},{4,6},{5,7},{6,4},{7,5},{8,10},{9,11},{10,... | collective-permute-start | bytes 786440 | tf_op jit(solution)/shard_map/ppermute | solution.py:415
  21.9 0.0 collective-permute-done.1.refs_1_
  21.9 0.0 collective-permute-done.2.refs_2_
  21.9 1.6 %collective-permute-done.3.refs_3_ = bf16[288,128]{1,0:T(8,128)(2,1)S(1)} collective-permute-done((bf16[288,128]{1,0:T(8,128)(2,1)}, bf16[288,128]{1,0:T(8,128)(2,1)S(1)}, u32[]{:S(2)}, u32[]{:S(2)}) %collective-permute-start.3) | collective-permute-done | bytes 73760 | tf_op jit(solution)/shard_map/ppermute | solution.py:376
  23.4 1.2 %equalize.3 = (bf16[2,256,256]{2,1,0:T(8,128)(2,1)}, bf16[2,2,256,256]{3,2,1,0:T(8,128)(2,1)S(1)}) custom-call(bf16[288,128]{1,0:T(8,128)(2,1)S(1)} %get-tuple-element.20.refs_0_, bf16[288,128]{1,0:T(8,128)(2,1)S(1)} %collective-permute-done.1.refs_1_, bf16[288,128]{1,0:T(8,128)(2,1)S(1)} %collective-permute-done.2.refs_2_, ...), custom_call_target="tpu_custom_call" | custom-call | flops 1048576 | bytes 1048576 | tf_op jit(solution)/shard_map/equalize/pallas_call | solution.py:260
  24.7 0.0 collective-permute-start.8
  24.7 1.5 %collective-permute-start.6 = (bf16[2,256,256]{2,1,0:T(8,128)(2,1)}, bf16[2,256,256]{2,1,0:T(8,128)(2,1)S(1)}, u32[]{:S(2)}, u32[]{:S(2)}) collective-permute-start(bf16[2,256,256]{2,1,0:T(8,128)(2,1)} %get-tuple-element.31.refs_1_.refs_0_), channel_id=1, source_target_pairs={{0,2},{1,3},{2,0},{3,1},{4,6},{5,7},{6,4},{7,5},{8,10},{9,11},{10,... | collective-permute-start | bytes 786440 | tf_op jit(solution)/shard_map/ppermute | solution.py:415
  26.1 1.5 %collective-permute-start.7 = (bf16[2,256,256]{2,1,0:T(8,128)(2,1)}, bf16[2,256,256]{2,1,0:T(8,128)(2,1)S(1)}, u32[]{:S(2)}, u32[]{:S(2)}) collective-permute-start(bf16[2,256,256]{2,1,0:T(8,128)(2,1)} %get-tuple-element.31.refs_1_.refs_0_), channel_id=1, source_target_pairs={{0,4},{4,0},{1,5},{5,1},{2,6},{6,2},{3,7},{7,3},{8,12},{12,8},{9,1... | collective-permute-start | bytes 786440 | tf_op jit(solution)/shard_map/ppermute | solution.py:416
  27.7 0.0 collective-permute-done.11.refs_2_.refs_4_
  27.7 0.0 collective-permute-done.10.refs_0_
  27.7 0.7 %copy-done.4 = bf16[2,256,256]{2,1,0:T(8,128)(2,1)} copy-done((bf16[2,256,256]{2,1,0:T(8,128)(2,1)}, bf16[2,256,256]{2,1,0:T(8,128)(2,1)S(1)}, u32[]{:S(2)}) %copy-start.4) | copy-done | bytes 262168
  28.4 0.7 %copy-done.6 = bf16[2,256,256]{2,1,0:T(8,128)(2,1)} copy-done((bf16[2,256,256]{2,1,0:T(8,128)(2,1)}, bf16[2,256,256]{2,1,0:T(8,128)(2,1)S(1)}, u32[]{:S(2)}) %copy-start.6) | copy-done | bytes 262168
  29.1 0.0 collective-permute-start.12
  29.1 4.5 %collective-permute-done.6.refs_0_ = bf16[2,256,256]{2,1,0:T(8,128)(2,1)S(1)} collective-permute-done((bf16[2,256,256]{2,1,0:T(8,128)(2,1)}, bf16[2,256,256]{2,1,0:T(8,128)(2,1)S(1)}, u32[]{:S(2)}, u32[]{:S(2)}) %collective-permute-start.6) | collective-permute-done | bytes 262176 | tf_op jit(solution)/shard_map/ppermute | solution.py:415
  33.6 1.2 %collective-permute-done.7.refs_2_.refs_4_ = bf16[2,256,256]{2,1,0:T(8,128)(2,1)S(1)} collective-permute-done((bf16[2,256,256]{2,1,0:T(8,128)(2,1)}, bf16[2,256,256]{2,1,0:T(8,128)(2,1)S(1)}, u32[]{:S(2)}, u32[]{:S(2)}) %collective-permute-start.7) | collective-permute-done | bytes 262176 | tf_op jit(solution)/shard_map/ppermute | solution.py:416
  34.8 0.0 copy-done.2
  34.8 0.7 %copy-done = bf16[2,256,256]{2,1,0:T(8,128)(2,1)} copy-done((bf16[2,256,256]{2,1,0:T(8,128)(2,1)}, bf16[2,256,256]{2,1,0:T(8,128)(2,1)S(1)}, u32[]{:S(2)}) %copy-start) | copy-done | bytes 262168
  35.5 0.0 collective-permute-start.9
  35.5 0.0 collective-permute-done.12.refs_3_
  35.5 0.0 collective-permute-done.8.refs_2_
  35.6 0.0 copy-done.13
  35.6 0.0 copy-start.5
  35.6 1.0 %copy-done.5 = bf16[2,256,256]{2,1,0:T(8,128)(2,1)S(1)} copy-done((bf16[2,256,256]{2,1,0:T(8,128)(2,1)S(1)}, bf16[2,256,256]{2,1,0:T(8,128)(2,1)}, u32[]{:S(2)}) %copy-start.5) | copy-done | bytes 262168
  36.6 0.9 %copy-done.7 = bf16[2,256,256]{2,1,0:T(8,128)(2,1)S(1)} copy-done((bf16[2,256,256]{2,1,0:T(8,128)(2,1)S(1)}, bf16[2,256,256]{2,1,0:T(8,128)(2,1)}, u32[]{:S(2)}) %copy-start.7) | copy-done | bytes 262168
  37.5 2.2 %correlate.2.refs_5_ = f32[2,16,32,64]{3,2,1,0:T(8,128)S(1)} custom-call(s32[8,8]{1,0:T(8,128)S(1)} %copy-done.13, bf16[2,256,256]{2,1,0:T(8,128)(2,1)S(1)} %equalize.2.refs_5_.refs_0_, bf16[2,256,256]{2,1,0:T(8,128)(2,1)S(1)} %copy-done.7, bf16[2,2,256,256]{3,2,1,0:T(8,128)(2,1)S(1)} %collective-permute-done.8.refs_2_, ...), custom_call_target="tpu_custom_call" | custom-call | flops 536870912 | bytes 4194304 | tf_op jit(solution)/shard_map/correlate/pallas_call | solution.py:359
  39.7 0.0 collective-permute-done.9.refs_3_
  39.7 3.4 %correlate.3 = f32[2,16,32,128]{3,2,1,0:T(8,128)} custom-call(s32[8,8]{1,0:T(8,128)S(1)} %copy-done.13, bf16[2,256,256]{2,1,0:T(8,128)(2,1)} %get-tuple-element.31.refs_1_.refs_0_, bf16[2,256,256]{2,1,0:T(8,128)(2,1)S(1)} %copy-done.3, bf16[2,2,256,256]{3,2,1,0:T(8,128)(2,1)S(1)} %collective-permute-done.8.refs_2_, ...), custom_call_target="tpu_custom_call" | custom-call | flops 536870912 | bytes 4194304 | tf_op jit(solution)/shard_map/correlate/pallas_call | solution.py:359
  (19 shorter events, 0.0 us)
Async XLA Ops:
  2.6 14.5 %copy-start.14 = (f32[8,2,128]{2,1,0:T(2,128)S(1)}, f32[8,2,128]{2,1,0:T(2,128)}, u32[]{:S(2)}) copy-start(f32[8,2,128]{2,1,0:T(2,128)} %param.5) | copy-start | bytes 24580
  2.6 9.5 %collective-permute-start = (bf16[288,128]{1,0:T(8,128)(2,1)S(1)}, bf16[288,128]{1,0:T(8,128)(2,1)S(1)}, u32[]{:S(2)}, u32[]{:S(2)}) collective-permute-start(bf16[288,128]{1,0:T(8,128)(2,1)S(1)} %get-tuple-element.24), channel_id=1, source_target_pairs={{0,24},{8,16},{16,8},{24,0},{1,25},{9,17},{17,9},{25,1},{2,26},{10... | collective-permute-start | bytes 221192 | tf_op jit(solution)/shard_map/ppermute | solution.py:376
  7.8 9.5 %collective-permute-start.4 = (bf16[288,128]{1,0:T(8,128)(2,1)S(1)}, bf16[288,128]{1,0:T(8,128)(2,1)S(1)}, u32[]{:S(2)}, u32[]{:S(2)}) collective-permute-start(bf16[288,128]{1,0:T(8,128)(2,1)S(1)} %get-tuple-element.29), channel_id=1, source_target_pairs={{0,8},{8,0},{16,24},{24,16},{1,9},{9,1},{17,25},{25,17},{2,10},{10... | collective-permute-start | bytes 221192 | tf_op jit(solution)/shard_map/ppermute | solution.py:376
  7.8 9.5 %collective-permute-start.5 = (bf16[288,128]{1,0:T(8,128)(2,1)S(1)}, bf16[288,128]{1,0:T(8,128)(2,1)S(1)}, u32[]{:S(2)}, u32[]{:S(2)}) collective-permute-start(bf16[288,128]{1,0:T(8,128)(2,1)S(1)} %get-tuple-element.30), channel_id=1, source_target_pairs={{0,16},{8,24},{16,0},{24,8},{1,17},{9,25},{17,1},{25,9},{2,18},{10... | collective-permute-start | bytes 221192 | tf_op jit(solution)/shard_map/ppermute | solution.py:376
  10.2 0.6 %copy-start.10 = (bf16[288,128]{1,0:T(8,128)(2,1)}, bf16[288,128]{1,0:T(8,128)(2,1)S(1)}, u32[]{:S(2)}) copy-start(bf16[288,128]{1,0:T(8,128)(2,1)S(1)} %get-tuple-element.21.refs_0_) | copy-start | bytes 221188
  10.9 0.6 %copy-start.11 = (bf16[288,128]{1,0:T(8,128)(2,1)}, bf16[288,128]{1,0:T(8,128)(2,1)S(1)}, u32[]{:S(2)}) copy-start(bf16[288,128]{1,0:T(8,128)(2,1)S(1)} %get-tuple-element.22.refs_1_) | copy-start | bytes 221188
  11.5 0.6 %copy-start.12 = (bf16[288,128]{1,0:T(8,128)(2,1)}, bf16[288,128]{1,0:T(8,128)(2,1)S(1)}, u32[]{:S(2)}) copy-start(bf16[288,128]{1,0:T(8,128)(2,1)S(1)} %get-tuple-element.23.refs_2_) | copy-start | bytes 221188
  12.1 23.4 %copy-start.13 = (s32[8,8]{1,0:T(8,128)S(1)}, s32[8,8]{1,0:T(8,128)}, u32[]{:S(2)}) copy-start(s32[8,8]{1,0:T(8,128)} %map_ref.3) | copy-start | bytes 772
  12.1 0.6 %copy-start.8 = (bf16[288,128]{1,0:T(8,128)(2,1)}, bf16[288,128]{1,0:T(8,128)(2,1)S(1)}, u32[]{:S(2)}) copy-start(bf16[288,128]{1,0:T(8,128)(2,1)S(1)} %collective-permute-done.refs_3_) | copy-start | bytes 221188
  12.8 9.1 %collective-permute-start.1 = (bf16[288,128]{1,0:T(8,128)(2,1)}, bf16[288,128]{1,0:T(8,128)(2,1)S(1)}, u32[]{:S(2)}, u32[]{:S(2)}) collective-permute-start(bf16[288,128]{1,0:T(8,128)(2,1)} %get-tuple-element.25), channel_id=1, source_target_pairs={{0,8},{8,0},{16,24},{24,16},{1,9},{9,1},{17,25},{25,17},{2,10},{10... | collective-permute-start | bytes 221192 | tf_op jit(solution)/shard_map/ppermute | solution.py:376
  14.2 7.7 %collective-permute-start.2 = (bf16[288,128]{1,0:T(8,128)(2,1)}, bf16[288,128]{1,0:T(8,128)(2,1)S(1)}, u32[]{:S(2)}, u32[]{:S(2)}) collective-permute-start(bf16[288,128]{1,0:T(8,128)(2,1)} %get-tuple-element.26), channel_id=1, source_target_pairs={{0,16},{8,24},{16,0},{24,8},{1,17},{9,25},{17,1},{25,9},{2,18},{10... | collective-permute-start | bytes 221192 | tf_op jit(solution)/shard_map/ppermute | solution.py:376
  17.1 6.4 %collective-permute-start.3 = (bf16[288,128]{1,0:T(8,128)(2,1)}, bf16[288,128]{1,0:T(8,128)(2,1)S(1)}, u32[]{:S(2)}, u32[]{:S(2)}) collective-permute-start(bf16[288,128]{1,0:T(8,128)(2,1)} %get-tuple-element.27), channel_id=1, source_target_pairs={{0,24},{8,16},{16,8},{24,0},{1,25},{9,17},{17,9},{25,1},{2,26},{10... | collective-permute-start | bytes 221192 | tf_op jit(solution)/shard_map/ppermute | solution.py:376
  17.3 0.9 %copy-start.9 = (bf16[288,128]{1,0:T(8,128)(2,1)S(1)}, bf16[288,128]{1,0:T(8,128)(2,1)}, u32[]{:S(2)}) copy-start(bf16[288,128]{1,0:T(8,128)(2,1)} %copy-done.8) | copy-start | bytes 221188
  18.6 9.0 %collective-permute-start.11 = (bf16[2,256,256]{2,1,0:T(8,128)(2,1)S(1)}, bf16[2,256,256]{2,1,0:T(8,128)(2,1)S(1)}, u32[]{:S(2)}, u32[]{:S(2)}) collective-permute-start(bf16[2,256,256]{2,1,0:T(8,128)(2,1)S(1)} %equalize.2.refs_5_.refs_0_), channel_id=1, source_target_pairs={{0,4},{4,0},{1,5},{5,1},{2,6},{6,2},{3,7},{7,3},{8,12},{12,8},{9,1... | collective-permute-start | bytes 786440 | tf_op jit(solution)/shard_map/ppermute | solution.py:416
  20.4 7.3 %collective-permute-start.10 = (bf16[2,256,256]{2,1,0:T(8,128)(2,1)S(1)}, bf16[2,256,256]{2,1,0:T(8,128)(2,1)S(1)}, u32[]{:S(2)}, u32[]{:S(2)}) collective-permute-start(bf16[2,256,256]{2,1,0:T(8,128)(2,1)S(1)} %equalize.2.refs_5_.refs_0_), channel_id=1, source_target_pairs={{0,2},{1,3},{2,0},{3,1},{4,6},{5,7},{6,4},{7,5},{8,10},{9,11},{10,... | collective-permute-start | bytes 786440 | tf_op jit(solution)/shard_map/ppermute | solution.py:415
  24.7 10.9 %collective-permute-start.8 = (bf16[2,2,256,256]{3,2,1,0:T(8,128)(2,1)S(1)}, bf16[2,2,256,256]{3,2,1,0:T(8,128)(2,1)S(1)}, u32[]{:S(2)}, u32[]{:S(2)}) collective-permute-start(bf16[2,2,256,256]{3,2,1,0:T(8,128)(2,1)S(1)} %get-tuple-element.32), channel_id=1, source_target_pairs={{0,1},{1,0},{2,3},{3,2},{4,5},{5,4},{6,7},{7,6},{8,9},{9,8},{10,11... | collective-permute-start | bytes 1572872 | tf_op jit(solution)/shard_map/ppermute | solution.py:418
  24.7 8.9 %collective-permute-start.6 = (bf16[2,256,256]{2,1,0:T(8,128)(2,1)}, bf16[2,256,256]{2,1,0:T(8,128)(2,1)S(1)}, u32[]{:S(2)}, u32[]{:S(2)}) collective-permute-start(bf16[2,256,256]{2,1,0:T(8,128)(2,1)} %get-tuple-element.31.refs_1_.refs_0_), channel_id=1, source_target_pairs={{0,2},{1,3},{2,0},{3,1},{4,6},{5,7},{6,4},{7,5},{8,10},{9,11},{10,... | collective-permute-start | bytes 786440 | tf_op jit(solution)/shard_map/ppermute | solution.py:415
  26.1 8.6 %collective-permute-start.7 = (bf16[2,256,256]{2,1,0:T(8,128)(2,1)}, bf16[2,256,256]{2,1,0:T(8,128)(2,1)S(1)}, u32[]{:S(2)}, u32[]{:S(2)}) collective-permute-start(bf16[2,256,256]{2,1,0:T(8,128)(2,1)} %get-tuple-element.31.refs_1_.refs_0_), channel_id=1, source_target_pairs={{0,4},{4,0},{1,5},{5,1},{2,6},{6,2},{3,7},{7,3},{8,12},{12,8},{9,1... | collective-permute-start | bytes 786440 | tf_op jit(solution)/shard_map/ppermute | solution.py:416
  27.7 0.7 %copy-start.4 = (bf16[2,256,256]{2,1,0:T(8,128)(2,1)}, bf16[2,256,256]{2,1,0:T(8,128)(2,1)S(1)}, u32[]{:S(2)}) copy-start(bf16[2,256,256]{2,1,0:T(8,128)(2,1)S(1)} %collective-permute-done.11.refs_2_.refs_4_) | copy-start | bytes 786436
  28.4 0.7 %copy-start.6 = (bf16[2,256,256]{2,1,0:T(8,128)(2,1)}, bf16[2,256,256]{2,1,0:T(8,128)(2,1)S(1)}, u32[]{:S(2)}) copy-start(bf16[2,256,256]{2,1,0:T(8,128)(2,1)S(1)} %collective-permute-done.10.refs_0_) | copy-start | bytes 786436
  29.1 6.4 %collective-permute-start.12 = (bf16[2,256,256]{2,1,0:T(8,128)(2,1)}, bf16[2,256,256]{2,1,0:T(8,128)(2,1)S(1)}, u32[]{:S(2)}, u32[]{:S(2)}) collective-permute-start(bf16[2,256,256]{2,1,0:T(8,128)(2,1)} %held_back.5.refs_1_), channel_id=1, source_target_pairs={{0,1},{1,0},{2,3},{3,2},{4,5},{5,4},{6,7},{7,6},{8,9},{9,8},{10,11... | collective-permute-start | bytes 786440 | tf_op jit(solution)/shard_map/ppermute | solution.py:423
  33.6 1.2 %copy-start.2 = (bf16[2,256,256]{2,1,0:T(8,128)(2,1)}, bf16[2,256,256]{2,1,0:T(8,128)(2,1)S(1)}, u32[]{:S(2)}) copy-start(bf16[2,256,256]{2,1,0:T(8,128)(2,1)S(1)} %collective-permute-done.6.refs_0_) | copy-start | bytes 786436
  34.8 0.7 %copy-start = (bf16[2,256,256]{2,1,0:T(8,128)(2,1)}, bf16[2,256,256]{2,1,0:T(8,128)(2,1)S(1)}, u32[]{:S(2)}) copy-start(bf16[2,256,256]{2,1,0:T(8,128)(2,1)S(1)} %collective-permute-done.7.refs_2_.refs_4_) | copy-start | bytes 786436
  35.5 4.2 %copy-start.1 = (bf16[2,256,256]{2,1,0:T(8,128)(2,1)S(1)}, bf16[2,256,256]{2,1,0:T(8,128)(2,1)}, u32[]{:S(2)}) copy-start(bf16[2,256,256]{2,1,0:T(8,128)(2,1)} %copy-done) | copy-start | bytes 786436
  35.5 4.2 %copy-start.3 = (bf16[2,256,256]{2,1,0:T(8,128)(2,1)S(1)}, bf16[2,256,256]{2,1,0:T(8,128)(2,1)}, u32[]{:S(2)}) copy-start(bf16[2,256,256]{2,1,0:T(8,128)(2,1)} %held_back.4.refs_1_) | copy-start | bytes 786436
  35.5 4.2 %collective-permute-start.9 = (bf16[2,256,256]{2,1,0:T(8,128)(2,1)}, bf16[2,256,256]{2,1,0:T(8,128)(2,1)S(1)}, u32[]{:S(2)}, u32[]{:S(2)}) collective-permute-start(bf16[2,256,256]{2,1,0:T(8,128)(2,1)} %held_back.4.refs_1_), channel_id=1, source_target_pairs={{0,1},{1,0},{2,3},{3,2},{4,5},{5,4},{6,7},{7,6},{8,9},{9,8},{10,11... | collective-permute-start | bytes 786440 | tf_op jit(solution)/shard_map/ppermute | solution.py:423
  35.6 1.0 %copy-start.5 = (bf16[2,256,256]{2,1,0:T(8,128)(2,1)S(1)}, bf16[2,256,256]{2,1,0:T(8,128)(2,1)}, u32[]{:S(2)}) copy-start(bf16[2,256,256]{2,1,0:T(8,128)(2,1)} %copy-done.4) | copy-start | bytes 786436
  36.6 0.9 %copy-start.7 = (bf16[2,256,256]{2,1,0:T(8,128)(2,1)S(1)}, bf16[2,256,256]{2,1,0:T(8,128)(2,1)}, u32[]{:S(2)}) copy-start(bf16[2,256,256]{2,1,0:T(8,128)(2,1)} %held_back.5.refs_1_) | copy-start | bytes 786436

commit v4 on v3

--- a/solution.py
+++ b/solution.py
@@ -201,15 +201,10 @@
     )(filt, table)
 
 
-def equalize_kernel(owners, frames, h, part, before, *refs):
+def equalize_kernel(owners, frames, h, part, *refs):
     pieces = refs[:owners]
     gains_ref, by_time, by_channel = refs[owners], refs[-2], refs[-1]
-    earlier = refs[owners + 1 : owners + 1 + before]
-    out_ref = refs[owners + 1 + before]
-    if before:
-        together = refs[owners + 2 + before]
-        for i in range(before):
-            together[i] = earlier[i][...]
+    out_ref = refs[owners + 1]
     width = 4 * h
     own_rows = frames * SIG
     over = GROUP * SIG
@@ -242,34 +237,26 @@
                     ]
     for r in range(2):
         for tile in range(2 * tiles):
-            ready = by_channel[r * 2 * tiles + tile].astype(jnp.bfloat16)
-            out_ref[r, :, tile * LANES : (tile + 1) * LANES] = ready
-            if before:
-                together[before, r, :, tile * LANES : (tile + 1) * LANES] = ready
-
-
-def equalize(pieces, gains, earlier, part, frames):
+            out_ref[r, :, tile * LANES : (tile + 1) * LANES] = by_channel[r * 2 * tiles + tile].astype(jnp.bfloat16)
+
+
+def equalize(pieces, gains, part, frames):
     owners = len(pieces)
     h = gains.shape[0] // PARTS // 2
     times = owners * frames
-    before = len(earlier)
-    shape = (2, h * SIG, 2 * times)
-    shapes = [jax.ShapeDtypeStruct(shape, jnp.bfloat16)]
-    if before:
-        shapes.append(jax.ShapeDtypeStruct((before + 1,) + shape, jnp.bfloat16))
     return pl.pallas_call(
-        functools.partial(equalize_kernel, owners, frames, h, part, before),
-        out_shape=shapes,
-        in_specs=[IN_VMEM] * (owners + 1 + before),
-        out_specs=[IN_VMEM] * len(shapes),
+        functools.partial(equalize_kernel, owners, frames, h, part),
+        out_shape=jax.ShapeDtypeStruct((2, h * SIG, 2 * times), jnp.bfloat16),
+        in_specs=[IN_VMEM] * (owners + 1),
+        out_specs=IN_VMEM,
         scratch_shapes=[
             pltpu.VMEM((times * SIG, LANES), jnp.float32),
             pltpu.VMEM((4 * times // LANES, h * SIG, LANES), jnp.float32),
         ],
         compiler_params=pltpu.CompilerParams(vmem_limit_bytes=VMEM_BYTES),
-        cost_estimate=pl.CostEstimate(flops=1 << 20, bytes_accessed=1 << 20, transcendentals=0),
+        cost_estimate=pl.CostEstimate(flops=0, bytes_accessed=1 << 10, transcendentals=0),
         name="equalize",
-    )(*pieces, gains, *earlier)
+    )(*pieces, gains)
 
 
 def row_places(col, n_col):
@@ -364,7 +351,7 @@
         scratch_shapes=[pltpu.VMEM((2 * n_row * n_col * BATCH * SIG // LANES, 2 * h * SIG, LANES), jnp.float32)]
         + (in_last if last else []),
         compiler_params=pltpu.CompilerParams(vmem_limit_bytes=VMEM_BYTES),
-        cost_estimate=pl.CostEstimate(flops=1 << 29, bytes_accessed=4 << 20, transcendentals=0),
+        cost_estimate=pl.CostEstimate(flops=0, bytes_accessed=1 << 10, transcendentals=0),
         name="correlate",
     )(tile_map, *operands)
 
@@ -378,14 +365,33 @@
 
 
 def held_back(blocks, after):
+    def kernel(*refs):
+        for i in range(len(blocks)):
+            refs[len(blocks) + len(after) + i][...] = refs[i][...]
+
     return pl.pallas_call(
-        lambda *refs: None,
+        kernel,
         out_shape=[jax.ShapeDtypeStruct(block.shape, block.dtype) for block in blocks],
-        in_specs=[IN_HBM] * (len(blocks) + len(after)),
-        out_specs=[IN_HBM] * len(blocks),
-        input_output_aliases={i: i for i in range(len(blocks))},
+        in_specs=[IN_VMEM] * (len(blocks) + len(after)),
+        out_specs=[IN_VMEM] * len(blocks),
+        cost_estimate=pl.CostEstimate(flops=0, bytes_accessed=1 << 10, transcendentals=0),
         name="held_back",
     )(*blocks, *after)
+
+
+def together(blocks):
+    def kernel(*refs):
+        for i in range(len(blocks)):
+            refs[-1][i] = refs[i][...]
+
+    return pl.pallas_call(
+        kernel,
+        out_shape=jax.ShapeDtypeStruct((len(blocks),) + blocks[0].shape, blocks[0].dtype),
+        in_specs=[IN_VMEM] * len(blocks),
+        out_specs=IN_VMEM,
+        cost_estimate=pl.CostEstimate(flops=0, bytes_accessed=1 << 10, transcendentals=0),
+        name="together",
+    )(*blocks)
 
 
 def shards(voltages, antenna_gains, tile_map):
@@ -409,17 +415,16 @@
         later = None
         if part < PARTS - 1:
             pieces = next_part(part + 1, filt, table, owners)
-            later = to_owners([pieces[0], *held_back(pieces[1:], arrived[-1:])])
-        block, *together = equalize(arrived, gains, own if part == PARTS - 1 else [], part, frames)
-        own.append(block)
-        far.append([lax.ppermute(block, "bcol", across[d]) for d in range(1, chips)])
-        column.append([lax.ppermute(block, "brow", along[d]) for d in range(1, n_row)])
+            later = to_owners([pieces[0], *held_back(pieces[1:], arrived[1:2])])
+        own.append(equalize(arrived, gains, part, frames))
+        far.append([lax.ppermute(own[part], "bcol", across[d]) for d in range(1, chips)])
+        column.append([lax.ppermute(own[part], "brow", along[d]) for d in range(1, n_row)])
         arrived = later
-    beside = lax.ppermute(together[0], "bcol", other_core)
+    beside = lax.ppermute(together(own), "bcol", other_core)
     result = None
     for part in range(PARTS):
-        if far[part]:
-            far[part] = list(held_back(far[part], own[-1:] + column[part]))
+        after = own[-1:] + column[part] + ([] if result is None else [result])
+        far[part] = list(held_back(far[part], after))
         near = [lax.ppermute(block, "bcol", other_core) for block in far[part]]
         blocks = [own[part]] + far[part] + [beside] + near + column[part]
         result = correlate(tile_map, blocks, result, part, n_row, n_col)

time: 43.4 us -> 52.5 us (1.21)
  Pallas kernels: 11.7 us -> 18 us
  local copies, waits for them, and re-layouts: 7.62 us -> 12.6 us
  waiting for transfers between devices: 7.3 us -> 4.4 us
    pallas_call x3 -> x4, Pallas kernels: 0.01 us -> 7.38 us  [the longest x3 5.53 us: held_back(): pl.pallas_call(kernel, out_shape=[jax.ShapeDtypeStruct(block.shape, block...]
    unnamed x30 -> x42, local copies, waits for them, and re-layouts: 7.51 us -> 12.5 us
    ppermute x5, waiting for transfers between devices: 5.7 us -> 1.07 us  [the longest x2 0.78 us: shards(): lax.ppermute(own[part], 'brow', along[d])]
    ppermute x2, waiting for transfers between devices: 0.01 us -> 1.75 us  [shards(): near = [lax.ppermute(block, 'bcol', other_core) for block in far[part]]]
    pallas_call x2, Pallas kernels: 1.66 us -> 0.9 us  [equalize(): pl.pallas_call(functools.partial(equalize_kernel, owners, frames, h, part...]
  transfers between devices with their start and end apart: 13 -> 13, of which waited for: 3 -> 4; matrix products, arithmetic and copies ran while one was open for 0% -> 0% of each run, Pallas kernels for 13% -> 20%
where the time goes in v4:
time: 52.5 us; the launch traced here: 52 us
  Pallas kernels  18 us (34%)
  starting transfers between devices  16.9 us (32%)
  local copies, waits for them, and re-layouts  12.6 us (24%)
  waiting for transfers between devices  4.4 us (8%)
    unnamed x42, local copies, waits for them, and re-layouts  12.5 us
    ppermute x6, starting transfers between devices, to_owners(): lax.ppermute(pieces[d], 'chan', [(i, i ^ d) for i in range(owners)])  10.1 us
    pallas_call x3, Pallas kernels, held_back(): pl.pallas_call(kernel, out_shape=[jax.ShapeDtypeStruct(block.shape, block...  5.53 us
    pallas_call x2, Pallas kernels, correlate(): pl.pallas_call(functools.partial(correlate_kernel, n_row, n_col, h, times...  5.24 us
    ppermute x2, starting transfers between devices, shards(): lax.ppermute(own[part], 'brow', along[d])  3.33 us
    ppermute x2, starting transfers between devices, shards(): lax.ppermute(own[part], 'bcol', across[d])  2.97 us
    pallas_call x1, Pallas kernels, filtered_and_first(): pl.pallas_call(functools.partial(filter_kernel, frames, pieces, spectrum_...  2.62 us
    pallas_call x1, Pallas kernels, together(): pl.pallas_call(kernel, out_shape=jax.ShapeDtypeStruct((len(blocks),) + bl...  1.86 us
  transfers between devices with their start and end apart: 13, of which 4 were waited for; matrix products, arithmetic and copies ran while one was open for 0% of the time, Pallas kernels for 20%

profile of v4, /device:TPU:0, one launch (start us, length us, event | category | flops | bytes accessed | tf_op | source)
XLA Modules:
  0.0 52.0 jit_solution(17310572651431444163)
XLA Ops:
  0.0 2.6 %filter_and_transform.1 = (bf16[288,128]{1,0:T(8,128)(2,1)S(1)}, bf16[288,128]{1,0:T(8,128)(2,1)S(1)}, bf16[288,128]{1,0:T(8,128)(2,1)S(1)}, bf16[288,128]{1,0:T(8,128)(2,1)S(1)}, bf16[2,288,1024]{2,1,0:T(8,128)(2,1)S(1)}) custom-call(s32[2,8,32768]{2,1,0:T(8,128)} %volt_hbm.1, bf16[4160,256]{1,0:T(8,128)(2,1)} %constant.5.clone.table_hbm), custom_call_target="tpu_custom_call" | custom-call | flops 536870912 | bytes 4194304 | tf_op jit(solution)/shard_map/filter_and_transform/pallas_call | solution.py:164
  2.6 0.0 copy-start.20
  2.6 3.1 %collective-permute-start = (bf16[288,128]{1,0:T(8,128)(2,1)S(1)}, bf16[288,128]{1,0:T(8,128)(2,1)S(1)}, u32[]{:S(2)}, u32[]{:S(2)}) collective-permute-start(bf16[288,128]{1,0:T(8,128)(2,1)S(1)} %get-tuple-element.22), channel_id=1, source_target_pairs={{0,8},{8,0},{16,24},{24,16},{1,9},{9,1},{17,25},{25,17},{2,10},{10... | collective-permute-start | bytes 221192 | tf_op jit(solution)/shard_map/ppermute | solution.py:363
  5.7 2.6 %collective-permute-start.6 = (bf16[288,128]{1,0:T(8,128)(2,1)S(1)}, bf16[288,128]{1,0:T(8,128)(2,1)S(1)}, u32[]{:S(2)}, u32[]{:S(2)}) collective-permute-start(bf16[288,128]{1,0:T(8,128)(2,1)S(1)} %get-tuple-element.27), channel_id=1, source_target_pairs={{0,16},{8,24},{16,0},{24,8},{1,17},{9,25},{17,1},{25,9},{2,18},{10... | collective-permute-start | bytes 221192 | tf_op jit(solution)/shard_map/ppermute | solution.py:363
  8.3 0.0 collective-permute-start.7
  8.3 1.8 %transform.1 = (bf16[288,128]{1,0:T(8,128)(2,1)S(1)}, bf16[288,128]{1,0:T(8,128)(2,1)S(1)}, bf16[288,128]{1,0:T(8,128)(2,1)S(1)}, bf16[288,128]{1,0:T(8,128)(2,1)S(1)}) custom-call(bf16[2,288,1024]{2,1,0:T(8,128)(2,1)S(1)} %get-tuple-element.17.filt, bf16[4160,256]{1,0:T(8,128)(2,1)} %constant.5.clone.table_hbm), custom_call_target="tpu_custom_call" | custom-call | flops 536870912 | bytes 2097152 | tf_op jit(solution)/shard_map/transform/pallas_call | solution.py:188
  10.2 0.0 copy-start.14
  10.2 0.6 %copy-done.14 = bf16[288,128]{1,0:T(8,128)(2,1)} copy-done((bf16[288,128]{1,0:T(8,128)(2,1)}, bf16[288,128]{1,0:T(8,128)(2,1)S(1)}, u32[]{:S(2)}) %copy-start.14) | copy-done | bytes 73752
  10.8 0.6 %copy-done.15 = bf16[288,128]{1,0:T(8,128)(2,1)} copy-done((bf16[288,128]{1,0:T(8,128)(2,1)}, bf16[288,128]{1,0:T(8,128)(2,1)S(1)}, u32[]{:S(2)}) %copy-start.15) | copy-done | bytes 73752
  11.4 0.6 %copy-done.16 = bf16[288,128]{1,0:T(8,128)(2,1)} copy-done((bf16[288,128]{1,0:T(8,128)(2,1)}, bf16[288,128]{1,0:T(8,128)(2,1)S(1)}, u32[]{:S(2)}) %copy-start.16) | copy-done | bytes 73752
  12.1 0.0 collective-permute-done.refs_3_.refs_1_
  12.1 0.6 %copy-done.12 = bf16[288,128]{1,0:T(8,128)(2,1)} copy-done((bf16[288,128]{1,0:T(8,128)(2,1)}, bf16[288,128]{1,0:T(8,128)(2,1)S(1)}, u32[]{:S(2)}) %copy-start.12) | copy-done | bytes 73752
  12.7 1.7 %held_back.3 = (bf16[288,128]{1,0:T(8,128)(2,1)}, bf16[288,128]{1,0:T(8,128)(2,1)}, bf16[288,128]{1,0:T(8,128)(2,1)}) custom-call(bf16[288,128]{1,0:T(8,128)(2,1)} %copy-done.14, bf16[288,128]{1,0:T(8,128)(2,1)} %copy-done.15, bf16[288,128]{1,0:T(8,128)(2,1)} %copy-done.16, bf16[288,128]{1,0:T(8,128)(2,1)} %copy-done.12), custom_call_target="tpu_custom_call" | custom-call | bytes 1024 | tf_op jit(solution)/shard_map/held_back/pallas_call | solution.py:372
  14.4 0.9 %collective-permute-start.1 = (bf16[288,128]{1,0:T(8,128)(2,1)}, bf16[288,128]{1,0:T(8,128)(2,1)S(1)}, u32[]{:S(2)}, u32[]{:S(2)}) collective-permute-start(bf16[288,128]{1,0:T(8,128)(2,1)} %get-tuple-element.23), channel_id=1, source_target_pairs={{0,8},{8,0},{16,24},{24,16},{1,9},{9,1},{17,25},{25,17},{2,10},{10... | collective-permute-start | bytes 221192 | tf_op jit(solution)/shard_map/ppermute | solution.py:363
  15.3 3.5 %collective-permute-start.2 = (bf16[288,128]{1,0:T(8,128)(2,1)}, bf16[288,128]{1,0:T(8,128)(2,1)S(1)}, u32[]{:S(2)}, u32[]{:S(2)}) collective-permute-start(bf16[288,128]{1,0:T(8,128)(2,1)} %get-tuple-element.24), channel_id=1, source_target_pairs={{0,16},{8,24},{16,0},{24,8},{1,17},{9,25},{17,1},{25,9},{2,18},{10... | collective-permute-start | bytes 221192 | tf_op jit(solution)/shard_map/ppermute | solution.py:363
  18.8 0.0 collective-permute-start.3
  18.8 0.1 copy.6
  18.9 0.0 collective-permute-done.6.refs_2_
  18.9 0.9 %copy-done.13 = bf16[288,128]{1,0:T(8,128)(2,1)S(1)} copy-done((bf16[288,128]{1,0:T(8,128)(2,1)S(1)}, bf16[288,128]{1,0:T(8,128)(2,1)}, u32[]{:S(2)}) %copy-start.13) | copy-done | bytes 73752
  19.8 0.4 equalize.3.refs_0_
  20.3 1.8 %collective-permute-start.9 = (bf16[2,256,256]{2,1,0:T(8,128)(2,1)S(1)}, bf16[2,256,256]{2,1,0:T(8,128)(2,1)S(1)}, u32[]{:S(2)}, u32[]{:S(2)}) collective-permute-start(bf16[2,256,256]{2,1,0:T(8,128)(2,1)S(1)} %equalize.3.refs_0_), channel_id=1, source_target_pairs={{0,4},{4,0},{1,5},{5,1},{2,6},{6,2},{3,7},{7,3},{8,12},{12,8},{9,1... | collective-permute-start | bytes 786440 | tf_op jit(solution)/shard_map/ppermute | solution.py:421
  22.1 1.5 %collective-permute-start.8 = (bf16[2,256,256]{2,1,0:T(8,128)(2,1)S(1)}, bf16[2,256,256]{2,1,0:T(8,128)(2,1)S(1)}, u32[]{:S(2)}, u32[]{:S(2)}) collective-permute-start(bf16[2,256,256]{2,1,0:T(8,128)(2,1)S(1)} %equalize.3.refs_0_), channel_id=1, source_target_pairs={{0,2},{1,3},{2,0},{3,1},{4,6},{5,7},{6,4},{7,5},{8,10},{9,11},{10,... | collective-permute-start | bytes 786440 | tf_op jit(solution)/shard_map/ppermute | solution.py:420
  23.6 1.6 %collective-permute-done.3.refs_3_ = bf16[288,128]{1,0:T(8,128)(2,1)S(1)} collective-permute-done((bf16[288,128]{1,0:T(8,128)(2,1)}, bf16[288,128]{1,0:T(8,128)(2,1)S(1)}, u32[]{:S(2)}, u32[]{:S(2)}) %collective-permute-start.3) | collective-permute-done | bytes 73760 | tf_op jit(solution)/shard_map/ppermute | solution.py:363
  25.1 0.4 equalize.2.refs_1_.refs_0_
  25.6 0.7 %copy-done = bf16[2,256,256]{2,1,0:T(8,128)(2,1)} copy-done((bf16[2,256,256]{2,1,0:T(8,128)(2,1)}, bf16[2,256,256]{2,1,0:T(8,128)(2,1)S(1)}, u32[]{:S(2)}) %copy-start) | copy-done | bytes 262168
  26.3 1.9 %together.1 = bf16[2,2,256,256]{3,2,1,0:T(8,128)(2,1)} custom-call(bf16[2,256,256]{2,1,0:T(8,128)(2,1)} %copy-done.4, bf16[2,256,256]{2,1,0:T(8,128)(2,1)} %copy-done), custom_call_target="tpu_custom_call" | custom-call | bytes 1024 | tf_op jit(solution)/shard_map/together/pallas_call | solution.py:387
  28.2 0.3 collective-permute-done.8.refs_0_
  28.4 0.4 copy-done.9
  28.8 0.7 %copy-done.18 = bf16[2,256,256]{2,1,0:T(8,128)(2,1)} copy-done((bf16[2,256,256]{2,1,0:T(8,128)(2,1)}, bf16[2,256,256]{2,1,0:T(8,128)(2,1)S(1)}, u32[]{:S(2)}) %copy-start.18) | copy-done | bytes 262168
  29.5 1.8 %held_back.4.refs_1_ = bf16[2,256,256]{2,1,0:T(8,128)(2,1)} custom-call(bf16[2,256,256]{2,1,0:T(8,128)(2,1)} %copy-done.18, bf16[2,256,256]{2,1,0:T(8,128)(2,1)} %copy-done, bf16[2,256,256]{2,1,0:T(8,128)(2,1)} %copy-done.9), custom_call_target="tpu_custom_call" | custom-call | bytes 1024 | tf_op jit(solution)/shard_map/held_back/pallas_call | solution.py:372
  31.4 0.5 collective-permute-start.11
  31.9 1.5 %collective-permute-start.4 = (bf16[2,256,256]{2,1,0:T(8,128)(2,1)}, bf16[2,256,256]{2,1,0:T(8,128)(2,1)S(1)}, u32[]{:S(2)}, u32[]{:S(2)}) collective-permute-start(bf16[2,256,256]{2,1,0:T(8,128)(2,1)} %copy-done), channel_id=1, source_target_pairs={{0,2},{1,3},{2,0},{3,1},{4,6},{5,7},{6,4},{7,5},{8,10},{9,11},{10,... | collective-permute-start | bytes 786440 | tf_op jit(solution)/shard_map/ppermute | solution.py:420
  33.4 1.5 %collective-permute-start.5 = (bf16[2,256,256]{2,1,0:T(8,128)(2,1)}, bf16[2,256,256]{2,1,0:T(8,128)(2,1)S(1)}, u32[]{:S(2)}, u32[]{:S(2)}) collective-permute-start(bf16[2,256,256]{2,1,0:T(8,128)(2,1)} %copy-done), channel_id=1, source_target_pairs={{0,4},{4,0},{1,5},{5,1},{2,6},{6,2},{3,7},{7,3},{8,12},{12,8},{9,1... | collective-permute-start | bytes 786440 | tf_op jit(solution)/shard_map/ppermute | solution.py:421
  34.9 0.9 %copy-done.5 = bf16[2,256,256]{2,1,0:T(8,128)(2,1)S(1)} copy-done((bf16[2,256,256]{2,1,0:T(8,128)(2,1)S(1)}, bf16[2,256,256]{2,1,0:T(8,128)(2,1)}, u32[]{:S(2)}) %copy-start.5) | copy-done | bytes 262168
  35.9 0.9 %copy-done.10 = bf16[2,256,256]{2,1,0:T(8,128)(2,1)S(1)} copy-done((bf16[2,256,256]{2,1,0:T(8,128)(2,1)S(1)}, bf16[2,256,256]{2,1,0:T(8,128)(2,1)}, u32[]{:S(2)}) %copy-start.10) | copy-done | bytes 262168
  36.8 0.9 %copy-done.11 = bf16[2,256,256]{2,1,0:T(8,128)(2,1)S(1)} copy-done((bf16[2,256,256]{2,1,0:T(8,128)(2,1)S(1)}, bf16[2,256,256]{2,1,0:T(8,128)(2,1)}, u32[]{:S(2)}) %copy-start.11) | copy-done | bytes 262168
  37.8 2.2 %correlate.2.refs_3_.refs_5_ = f32[2,16,32,64]{3,2,1,0:T(8,128)S(1)} custom-call(s32[8,8]{1,0:T(8,128)S(1)} %copy-done.17, bf16[2,256,256]{2,1,0:T(8,128)(2,1)S(1)} %copy-done.5, bf16[2,256,256]{2,1,0:T(8,128)(2,1)S(1)} %copy-done.11, bf16[2,2,256,256]{3,2,1,0:T(8,128)(2,1)S(1)} %collective-permute-done.10.refs_2_, ...), custom_call_target="tpu_custom_call" | custom-call | bytes 1024 | tf_op jit(solution)/shard_map/correlate/pallas_call | solution.py:346
  40.0 0.0 copy-start.2
  40.0 0.8 %copy-done.2 = f32[2,16,32,64]{3,2,1,0:T(8,128)} copy-done((f32[2,16,32,64]{3,2,1,0:T(8,128)}, f32[2,16,32,64]{3,2,1,0:T(8,128)S(1)}, u32[]{:S(2)}) %copy-start.2) | copy-done | bytes 262168
  40.8 0.0 collective-permute-done.4.refs_0_
  40.8 0.8 %collective-permute-done.5.refs_2_.refs_4_ = bf16[2,256,256]{2,1,0:T(8,128)(2,1)S(1)} collective-permute-done((bf16[2,256,256]{2,1,0:T(8,128)(2,1)}, bf16[2,256,256]{2,1,0:T(8,128)(2,1)S(1)}, u32[]{:S(2)}, u32[]{:S(2)}) %collective-permute-start.5) | collective-permute-done | bytes 262176 | tf_op jit(solution)/shard_map/ppermute | solution.py:421
  41.5 0.7 %copy-done.6 = bf16[2,256,256]{2,1,0:T(8,128)(2,1)} copy-done((bf16[2,256,256]{2,1,0:T(8,128)(2,1)}, bf16[2,256,256]{2,1,0:T(8,128)(2,1)S(1)}, u32[]{:S(2)}) %copy-start.6) | copy-done | bytes 262168
  42.2 2.0 %held_back.5.refs_1_ = bf16[2,256,256]{2,1,0:T(8,128)(2,1)} custom-call(bf16[2,256,256]{2,1,0:T(8,128)(2,1)} %copy-done.19, bf16[2,256,256]{2,1,0:T(8,128)(2,1)} %copy-done, bf16[2,256,256]{2,1,0:T(8,128)(2,1)} %copy-done.6, f32[2,16,32,64]{3,2,1,0:T(8,128)} %copy-done.2), custom_call_target="tpu_custom_call" | custom-call | bytes 1024 | tf_op jit(solution)/shard_map/held_back/pallas_call | solution.py:372
  44.2 1.7 %collective-permute-done.12.refs_3_ = bf16[2,256,256]{2,1,0:T(8,128)(2,1)S(1)} collective-permute-done((bf16[2,256,256]{2,1,0:T(8,128)(2,1)}, bf16[2,256,256]{2,1,0:T(8,128)(2,1)S(1)}, u32[]{:S(2)}, u32[]{:S(2)}) %collective-permute-start.12) | collective-permute-done | bytes 262176 | tf_op jit(solution)/shard_map/ppermute | solution.py:428
  46.0 1.0 %copy-done.3 = f32[2,16,32,64]{3,2,1,0:T(8,128)S(1)} copy-done((f32[2,16,32,64]{3,2,1,0:T(8,128)S(1)}, f32[2,16,32,64]{3,2,1,0:T(8,128)}, u32[]{:S(2)}) %copy-start.3) | copy-done | bytes 262168
  47.0 0.9 %copy-done.7 = bf16[2,256,256]{2,1,0:T(8,128)(2,1)S(1)} copy-done((bf16[2,256,256]{2,1,0:T(8,128)(2,1)S(1)}, bf16[2,256,256]{2,1,0:T(8,128)(2,1)}, u32[]{:S(2)}) %copy-start.7) | copy-done | bytes 262168
  48.0 0.9 %copy-done.8 = bf16[2,256,256]{2,1,0:T(8,128)(2,1)S(1)} copy-done((bf16[2,256,256]{2,1,0:T(8,128)(2,1)S(1)}, bf16[2,256,256]{2,1,0:T(8,128)(2,1)}, u32[]{:S(2)}) %copy-start.8) | copy-done | bytes 262168
  48.9 3.1 %correlate.3 = f32[2,16,32,128]{3,2,1,0:T(8,128)} custom-call(s32[8,8]{1,0:T(8,128)S(1)} %copy-done.17, bf16[2,256,256]{2,1,0:T(8,128)(2,1)S(1)} %copy-done.1, bf16[2,256,256]{2,1,0:T(8,128)(2,1)S(1)} %copy-done.8, bf16[2,2,256,256]{3,2,1,0:T(8,128)(2,1)S(1)} %collective-permute-done.10.refs_2_, bf16[2,256,256]{2,1,0:T(8,128)(2,1)S(1)} %collective-permute-done.12.refs_3_, ...), custom_call_target="tpu_custom_call" | custom-call | bytes 1024 | tf_op jit(solution)/shard_map/correlate/pallas_call | solution.py:346
  (32 shorter events, 0.1 us)
Async XLA Ops:
  2.6 16.1 %copy-start.20 = (f32[8,2,128]{2,1,0:T(2,128)S(1)}, f32[8,2,128]{2,1,0:T(2,128)}, u32[]{:S(2)}) copy-start(f32[8,2,128]{2,1,0:T(2,128)} %param.5) | copy-start | bytes 24580
  2.6 9.4 %collective-permute-start = (bf16[288,128]{1,0:T(8,128)(2,1)S(1)}, bf16[288,128]{1,0:T(8,128)(2,1)S(1)}, u32[]{:S(2)}, u32[]{:S(2)}) collective-permute-start(bf16[288,128]{1,0:T(8,128)(2,1)S(1)} %get-tuple-element.22), channel_id=1, source_target_pairs={{0,8},{8,0},{16,24},{24,16},{1,9},{9,1},{17,25},{25,17},{2,10},{10... | collective-permute-start | bytes 221192 | tf_op jit(solution)/shard_map/ppermute | solution.py:363
  5.7 13.2 %collective-permute-start.6 = (bf16[288,128]{1,0:T(8,128)(2,1)S(1)}, bf16[288,128]{1,0:T(8,128)(2,1)S(1)}, u32[]{:S(2)}, u32[]{:S(2)}) collective-permute-start(bf16[288,128]{1,0:T(8,128)(2,1)S(1)} %get-tuple-element.27), channel_id=1, source_target_pairs={{0,16},{8,24},{16,0},{24,8},{1,17},{9,25},{17,1},{25,9},{2,18},{10... | collective-permute-start | bytes 221192 | tf_op jit(solution)/shard_map/ppermute | solution.py:363
  8.3 10.6 %collective-permute-start.7 = (bf16[288,128]{1,0:T(8,128)(2,1)S(1)}, bf16[288,128]{1,0:T(8,128)(2,1)S(1)}, u32[]{:S(2)}, u32[]{:S(2)}) collective-permute-start(bf16[288,128]{1,0:T(8,128)(2,1)S(1)} %get-tuple-element.28), channel_id=1, source_target_pairs={{0,24},{8,16},{16,8},{24,0},{1,25},{9,17},{17,9},{25,1},{2,26},{10... | collective-permute-start | bytes 221192 | tf_op jit(solution)/shard_map/ppermute | solution.py:363
  10.2 0.6 %copy-start.14 = (bf16[288,128]{1,0:T(8,128)(2,1)}, bf16[288,128]{1,0:T(8,128)(2,1)S(1)}, u32[]{:S(2)}) copy-start(bf16[288,128]{1,0:T(8,128)(2,1)S(1)} %get-tuple-element.19.refs_0_) | copy-start | bytes 221188
  10.8 0.6 %copy-start.15 = (bf16[288,128]{1,0:T(8,128)(2,1)}, bf16[288,128]{1,0:T(8,128)(2,1)S(1)}, u32[]{:S(2)}) copy-start(bf16[288,128]{1,0:T(8,128)(2,1)S(1)} %get-tuple-element.20.refs_1_) | copy-start | bytes 221188
  11.4 0.6 %copy-start.16 = (bf16[288,128]{1,0:T(8,128)(2,1)}, bf16[288,128]{1,0:T(8,128)(2,1)S(1)}, u32[]{:S(2)}) copy-start(bf16[288,128]{1,0:T(8,128)(2,1)S(1)} %get-tuple-element.21.refs_2_) | copy-start | bytes 221188
  12.1 22.9 %copy-start.17 = (s32[8,8]{1,0:T(8,128)S(1)}, s32[8,8]{1,0:T(8,128)}, u32[]{:S(2)}) copy-start(s32[8,8]{1,0:T(8,128)} %map_ref.3) | copy-start | bytes 772
  12.1 0.6 %copy-start.12 = (bf16[288,128]{1,0:T(8,128)(2,1)}, bf16[288,128]{1,0:T(8,128)(2,1)S(1)}, u32[]{:S(2)}) copy-start(bf16[288,128]{1,0:T(8,128)(2,1)S(1)} %collective-permute-done.refs_3_.refs_1_) | copy-start | bytes 221188
  14.4 9.2 %collective-permute-start.1 = (bf16[288,128]{1,0:T(8,128)(2,1)}, bf16[288,128]{1,0:T(8,128)(2,1)S(1)}, u32[]{:S(2)}, u32[]{:S(2)}) collective-permute-start(bf16[288,128]{1,0:T(8,128)(2,1)} %get-tuple-element.23), channel_id=1, source_target_pairs={{0,8},{8,0},{16,24},{24,16},{1,9},{9,1},{17,25},{25,17},{2,10},{10... | collective-permute-start | bytes 221192 | tf_op jit(solution)/shard_map/ppermute | solution.py:363
  15.3 8.3 %collective-permute-start.2 = (bf16[288,128]{1,0:T(8,128)(2,1)}, bf16[288,128]{1,0:T(8,128)(2,1)S(1)}, u32[]{:S(2)}, u32[]{:S(2)}) collective-permute-start(bf16[288,128]{1,0:T(8,128)(2,1)} %get-tuple-element.24), channel_id=1, source_target_pairs={{0,16},{8,24},{16,0},{24,8},{1,17},{9,25},{17,1},{25,9},{2,18},{10... | collective-permute-start | bytes 221192 | tf_op jit(solution)/shard_map/ppermute | solution.py:363
  18.8 6.4 %collective-permute-start.3 = (bf16[288,128]{1,0:T(8,128)(2,1)}, bf16[288,128]{1,0:T(8,128)(2,1)S(1)}, u32[]{:S(2)}, u32[]{:S(2)}) collective-permute-start(bf16[288,128]{1,0:T(8,128)(2,1)} %get-tuple-element.25), channel_id=1, source_target_pairs={{0,24},{8,16},{16,8},{24,0},{1,25},{9,17},{17,9},{25,1},{2,26},{10... | collective-permute-start | bytes 221192 | tf_op jit(solution)/shard_map/ppermute | solution.py:363
  18.9 0.9 %copy-start.13 = (bf16[288,128]{1,0:T(8,128)(2,1)S(1)}, bf16[288,128]{1,0:T(8,128)(2,1)}, u32[]{:S(2)}) copy-start(bf16[288,128]{1,0:T(8,128)(2,1)} %copy-done.12) | copy-start | bytes 221188
  20.2 5.3 %copy-start.4 = (bf16[2,256,256]{2,1,0:T(8,128)(2,1)}, bf16[2,256,256]{2,1,0:T(8,128)(2,1)S(1)}, u32[]{:S(2)}) copy-start(bf16[2,256,256]{2,1,0:T(8,128)(2,1)S(1)} %equalize.3.refs_0_) | copy-start | bytes 786436
  20.3 7.9 %collective-permute-start.9 = (bf16[2,256,256]{2,1,0:T(8,128)(2,1)S(1)}, bf16[2,256,256]{2,1,0:T(8,128)(2,1)S(1)}, u32[]{:S(2)}, u32[]{:S(2)}) collective-permute-start(bf16[2,256,256]{2,1,0:T(8,128)(2,1)S(1)} %equalize.3.refs_0_), channel_id=1, source_target_pairs={{0,4},{4,0},{1,5},{5,1},{2,6},{6,2},{3,7},{7,3},{8,12},{12,8},{9,1... | collective-permute-start | bytes 786440 | tf_op jit(solution)/shard_map/ppermute | solution.py:421
  22.1 6.4 %collective-permute-start.8 = (bf16[2,256,256]{2,1,0:T(8,128)(2,1)S(1)}, bf16[2,256,256]{2,1,0:T(8,128)(2,1)S(1)}, u32[]{:S(2)}, u32[]{:S(2)}) collective-permute-start(bf16[2,256,256]{2,1,0:T(8,128)(2,1)S(1)} %equalize.3.refs_0_), channel_id=1, source_target_pairs={{0,2},{1,3},{2,0},{3,1},{4,6},{5,7},{6,4},{7,5},{8,10},{9,11},{10,... | collective-permute-start | bytes 786440 | tf_op jit(solution)/shard_map/ppermute | solution.py:420
  25.6 0.7 %copy-start = (bf16[2,256,256]{2,1,0:T(8,128)(2,1)}, bf16[2,256,256]{2,1,0:T(8,128)(2,1)S(1)}, u32[]{:S(2)}) copy-start(bf16[2,256,256]{2,1,0:T(8,128)(2,1)S(1)} %equalize.2.refs_1_.refs_0_) | copy-start | bytes 786436
  28.1 6.8 %collective-permute-start.10 = (bf16[2,2,256,256]{3,2,1,0:T(8,128)(2,1)}, bf16[2,2,256,256]{3,2,1,0:T(8,128)(2,1)S(1)}, u32[]{:S(2)}, u32[]{:S(2)}) collective-permute-start(bf16[2,2,256,256]{3,2,1,0:T(8,128)(2,1)} %together.1), channel_id=1, source_target_pairs={{0,1},{1,0},{2,3},{3,2},{4,5},{5,4},{6,7},{7,6},{8,9},{9,8},{10,11... | collective-permute-start | bytes 1572872 | tf_op jit(solution)/shard_map/ppermute | solution.py:423
  28.1 0.7 %copy-start.9 = (bf16[2,256,256]{2,1,0:T(8,128)(2,1)}, bf16[2,256,256]{2,1,0:T(8,128)(2,1)S(1)}, u32[]{:S(2)}) copy-start(bf16[2,256,256]{2,1,0:T(8,128)(2,1)S(1)} %collective-permute-done.9.refs_2_.refs_4_) | copy-start | bytes 786436
  28.8 0.7 %copy-start.18 = (bf16[2,256,256]{2,1,0:T(8,128)(2,1)}, bf16[2,256,256]{2,1,0:T(8,128)(2,1)S(1)}, u32[]{:S(2)}) copy-start(bf16[2,256,256]{2,1,0:T(8,128)(2,1)S(1)} %collective-permute-done.8.refs_0_) | copy-start | bytes 786436
  31.4 14.6 %copy-start.1 = (bf16[2,256,256]{2,1,0:T(8,128)(2,1)S(1)}, bf16[2,256,256]{2,1,0:T(8,128)(2,1)}, u32[]{:S(2)}) copy-start(bf16[2,256,256]{2,1,0:T(8,128)(2,1)} %copy-done) | copy-start | bytes 786436
  31.4 3.5 %collective-permute-start.11 = (bf16[2,256,256]{2,1,0:T(8,128)(2,1)}, bf16[2,256,256]{2,1,0:T(8,128)(2,1)S(1)}, u32[]{:S(2)}, u32[]{:S(2)}) collective-permute-start(bf16[2,256,256]{2,1,0:T(8,128)(2,1)} %held_back.4.refs_1_), channel_id=1, source_target_pairs={{0,1},{1,0},{2,3},{3,2},{4,5},{5,4},{6,7},{7,6},{8,9},{9,8},{10,11... | collective-permute-start | bytes 786440 | tf_op jit(solution)/shard_map/ppermute | solution.py:428
  31.9 8.9 %collective-permute-start.4 = (bf16[2,256,256]{2,1,0:T(8,128)(2,1)}, bf16[2,256,256]{2,1,0:T(8,128)(2,1)S(1)}, u32[]{:S(2)}, u32[]{:S(2)}) collective-permute-start(bf16[2,256,256]{2,1,0:T(8,128)(2,1)} %copy-done), channel_id=1, source_target_pairs={{0,2},{1,3},{2,0},{3,1},{4,6},{5,7},{6,4},{7,5},{8,10},{9,11},{10,... | collective-permute-start | bytes 786440 | tf_op jit(solution)/shard_map/ppermute | solution.py:420
  33.4 8.1 %collective-permute-start.5 = (bf16[2,256,256]{2,1,0:T(8,128)(2,1)}, bf16[2,256,256]{2,1,0:T(8,128)(2,1)S(1)}, u32[]{:S(2)}, u32[]{:S(2)}) collective-permute-start(bf16[2,256,256]{2,1,0:T(8,128)(2,1)} %copy-done), channel_id=1, source_target_pairs={{0,4},{4,0},{1,5},{5,1},{2,6},{6,2},{3,7},{7,3},{8,12},{12,8},{9,1... | collective-permute-start | bytes 786440 | tf_op jit(solution)/shard_map/ppermute | solution.py:421
  34.9 1.0 %copy-start.5 = (bf16[2,256,256]{2,1,0:T(8,128)(2,1)S(1)}, bf16[2,256,256]{2,1,0:T(8,128)(2,1)}, u32[]{:S(2)}) copy-start(bf16[2,256,256]{2,1,0:T(8,128)(2,1)} %copy-done.4) | copy-start | bytes 786436
  35.9 0.9 %copy-start.10 = (bf16[2,256,256]{2,1,0:T(8,128)(2,1)S(1)}, bf16[2,256,256]{2,1,0:T(8,128)(2,1)}, u32[]{:S(2)}) copy-start(bf16[2,256,256]{2,1,0:T(8,128)(2,1)} %copy-done.9) | copy-start | bytes 786436
  36.8 0.9 %copy-start.11 = (bf16[2,256,256]{2,1,0:T(8,128)(2,1)S(1)}, bf16[2,256,256]{2,1,0:T(8,128)(2,1)}, u32[]{:S(2)}) copy-start(bf16[2,256,256]{2,1,0:T(8,128)(2,1)} %held_back.4.refs_1_) | copy-start | bytes 786436
  40.0 0.8 %copy-start.2 = (f32[2,16,32,64]{3,2,1,0:T(8,128)}, f32[2,16,32,64]{3,2,1,0:T(8,128)S(1)}, u32[]{:S(2)}) copy-start(f32[2,16,32,64]{3,2,1,0:T(8,128)S(1)} %correlate.2.refs_3_.refs_5_) | copy-start | bytes 786436
  40.8 0.8 %copy-start.19 = (bf16[2,256,256]{2,1,0:T(8,128)(2,1)}, bf16[2,256,256]{2,1,0:T(8,128)(2,1)S(1)}, u32[]{:S(2)}) copy-start(bf16[2,256,256]{2,1,0:T(8,128)(2,1)S(1)} %collective-permute-done.4.refs_0_) | copy-start | bytes 786436
  41.5 0.7 %copy-start.6 = (bf16[2,256,256]{2,1,0:T(8,128)(2,1)}, bf16[2,256,256]{2,1,0:T(8,128)(2,1)S(1)}, u32[]{:S(2)}) copy-start(bf16[2,256,256]{2,1,0:T(8,128)(2,1)S(1)} %collective-permute-done.5.refs_2_.refs_4_) | copy-start | bytes 786436
  44.2 1.7 %collective-permute-start.12 = (bf16[2,256,256]{2,1,0:T(8,128)(2,1)}, bf16[2,256,256]{2,1,0:T(8,128)(2,1)S(1)}, u32[]{:S(2)}, u32[]{:S(2)}) collective-permute-start(bf16[2,256,256]{2,1,0:T(8,128)(2,1)} %held_back.5.refs_1_), channel_id=1, source_target_pairs={{0,1},{1,0},{2,3},{3,2},{4,5},{5,4},{6,7},{7,6},{8,9},{9,8},{10,11... | collective-permute-start | bytes 786440 | tf_op jit(solution)/shard_map/ppermute | solution.py:428
  46.0 1.0 %copy-start.3 = (f32[2,16,32,64]{3,2,1,0:T(8,128)S(1)}, f32[2,16,32,64]{3,2,1,0:T(8,128)}, u32[]{:S(2)}) copy-start(f32[2,16,32,64]{3,2,1,0:T(8,128)} %copy-done.2) | copy-start | bytes 786436
  47.0 0.9 %copy-start.7 = (bf16[2,256,256]{2,1,0:T(8,128)(2,1)S(1)}, bf16[2,256,256]{2,1,0:T(8,128)(2,1)}, u32[]{:S(2)}) copy-start(bf16[2,256,256]{2,1,0:T(8,128)(2,1)} %copy-done.6) | copy-start | bytes 786436
  48.0 0.9 %copy-start.8 = (bf16[2,256,256]{2,1,0:T(8,128)(2,1)S(1)}, bf16[2,256,256]{2,1,0:T(8,128)(2,1)}, u32[]{:S(2)}) copy-start(bf16[2,256,256]{2,1,0:T(8,128)(2,1)} %held_back.5.refs_1_) | copy-start | bytes 786436

commit v5 on v4

--- a/solution.py
+++ b/solution.py
@@ -20,7 +20,7 @@
 GROUP = 4
 BATCH = 4
 PARTS = 2
-VMEM_BYTES = 48 * 1024 * 1024
+VMEM_BYTES = 16 * 1024 * 1024
 FILTER_VMEM_BYTES = 52 * 1024 * 1024
 COEF_ROWS = 64
 
@@ -374,6 +374,7 @@
         out_shape=[jax.ShapeDtypeStruct(block.shape, block.dtype) for block in blocks],
         in_specs=[IN_VMEM] * (len(blocks) + len(after)),
         out_specs=[IN_VMEM] * len(blocks),
+        compiler_params=pltpu.CompilerParams(vmem_limit_bytes=VMEM_BYTES),
         cost_estimate=pl.CostEstimate(flops=0, bytes_accessed=1 << 10, transcendentals=0),
         name="held_back",
     )(*blocks, *after)
@@ -389,6 +390,7 @@
         out_shape=jax.ShapeDtypeStruct((len(blocks),) + blocks[0].shape, blocks[0].dtype),
         in_specs=[IN_VMEM] * len(blocks),
         out_specs=IN_VMEM,
+        compiler_params=pltpu.CompilerParams(vmem_limit_bytes=VMEM_BYTES),
         cost_estimate=pl.CostEstimate(flops=0, bytes_accessed=1 << 10, transcendentals=0),
         name="together",
     )(*blocks)

time: 52.5 us -> 38.6 us (0.74)
  local copies, waits for them, and re-layouts: 12.6 us -> 0.12 us
  Pallas kernels: 18 us -> 10.7 us
  waiting for transfers between devices: 4.4 us -> 11.7 us
  starting transfers between devices: 16.9 us -> 15.5 us
    unnamed x42 -> x4, local copies, waits for them, and re-layouts: 12.5 us -> 0.01 us
    ppermute x2, waiting for transfers between devices: 0.29 us -> 5.93 us  [shards(): lax.ppermute(own[part], 'bcol', across[d])]
    pallas_call x3, Pallas kernels: 5.53 us -> 0.05 us  [held_back(): pl.pallas_call(kernel, out_shape=[jax.ShapeDtypeStruct(block.shape, block...]
    pallas_call x1, Pallas kernels: 1.86 us -> 0.04 us  [together(): pl.pallas_call(kernel, out_shape=jax.ShapeDtypeStruct((len(blocks),) + bl...]
    ppermute x2, starting transfers between devices: 3.33 us -> 2.11 us  [shards(): lax.ppermute(own[part], 'brow', along[d])]
    ppermute x6, waiting for transfers between devices: 1.58 us -> 2.58 us  [to_owners(): lax.ppermute(pieces[d], 'chan', [(i, i ^ d) for i in range(owners)])]
    ppermute x2, waiting for transfers between devices: 0.78 us -> 1.68 us  [shards(): lax.ppermute(own[part], 'brow', along[d])]
  transfers between devices with their start and end apart: 13 -> 13, of which waited for: 4 -> 8; matrix products, arithmetic and copies ran while one was open for 0% -> 0% of each run, Pallas kernels for 20% -> 13%
where the time goes in v5:
time: 38.6 us; the launch traced here: 38.2 us
  starting transfers between devices  15.5 us (40%)
  waiting for transfers between devices  11.7 us (30%)
  Pallas kernels  10.7 us (28%)
    ppermute x6, starting transfers between devices, to_owners(): lax.ppermute(pieces[d], 'chan', [(i, i ^ d) for i in range(owners)])  10.1 us
    ppermute x2, waiting for transfers between devices, shards(): lax.ppermute(own[part], 'bcol', across[d])  5.93 us
    pallas_call x2, Pallas kernels, correlate(): pl.pallas_call(functools.partial(correlate_kernel, n_row, n_col, h, times...  5.25 us
    ppermute x2, starting transfers between devices, shards(): lax.ppermute(own[part], 'bcol', across[d])  3.05 us
    pallas_call x1, Pallas kernels, filtered_and_first(): pl.pallas_call(functools.partial(filter_kernel, frames, pieces, spectrum_...  2.61 us
    ppermute x6, waiting for transfers between devices, to_owners(): lax.ppermute(pieces[d], 'chan', [(i, i ^ d) for i in range(owners)])  2.58 us
    ppermute x2, starting transfers between devices, shards(): lax.ppermute(own[part], 'brow', along[d])  2.11 us
    pallas_call x1, Pallas kernels, next_part(): pl.pallas_call(functools.partial(transform_kernel, part, spectrum_scale()...  1.83 us
  transfers between devices with their start and end apart: 13, of which 8 were waited for; matrix products, arithmetic and copies ran while one was open for 0% of the time, Pallas kernels for 13%

profile of v5, /device:TPU:0, one launch (start us, length us, event | category | flops | bytes accessed | tf_op | source)
XLA Modules:
  0.0 38.2 jit_solution(1888374348675215799)
XLA Ops:
  0.0 2.6 %filter_and_transform.1 = (bf16[288,128]{1,0:T(8,128)(2,1)S(1)}, bf16[288,128]{1,0:T(8,128)(2,1)S(1)}, bf16[288,128]{1,0:T(8,128)(2,1)S(1)}, bf16[288,128]{1,0:T(8,128)(2,1)S(1)}, bf16[2,288,1024]{2,1,0:T(8,128)(2,1)S(1)}) custom-call(s32[2,8,32768]{2,1,0:T(8,128)} %volt_hbm.1, bf16[4160,256]{1,0:T(8,128)(2,1)} %constant.5.clone.table_hbm), custom_call_target="tpu_custom_call" | custom-call | flops 536870912 | bytes 4194304 | tf_op jit(solution)/shard_map/filter_and_transform/pallas_call | solution.py:164
  2.6 0.0 copy-start.1
  2.6 3.1 %collective-permute-start = (bf16[288,128]{1,0:T(8,128)(2,1)S(1)}, bf16[288,128]{1,0:T(8,128)(2,1)S(1)}, u32[]{:S(2)}, u32[]{:S(2)}) collective-permute-start(bf16[288,128]{1,0:T(8,128)(2,1)S(1)} %get-tuple-element.22), channel_id=1, source_target_pairs={{0,8},{8,0},{16,24},{24,16},{1,9},{9,1},{17,25},{25,17},{2,10},{10... | collective-permute-start | bytes 221192 | tf_op jit(solution)/shard_map/ppermute | solution.py:363
  5.7 2.6 %collective-permute-start.6 = (bf16[288,128]{1,0:T(8,128)(2,1)S(1)}, bf16[288,128]{1,0:T(8,128)(2,1)S(1)}, u32[]{:S(2)}, u32[]{:S(2)}) collective-permute-start(bf16[288,128]{1,0:T(8,128)(2,1)S(1)} %get-tuple-element.27), channel_id=1, source_target_pairs={{0,16},{8,24},{16,0},{24,8},{1,17},{9,25},{17,1},{25,9},{2,18},{10... | collective-permute-start | bytes 221192 | tf_op jit(solution)/shard_map/ppermute | solution.py:363
  8.3 0.0 collective-permute-start.7
  8.3 1.8 %transform.1 = (bf16[288,128]{1,0:T(8,128)(2,1)S(1)}, bf16[288,128]{1,0:T(8,128)(2,1)S(1)}, bf16[288,128]{1,0:T(8,128)(2,1)S(1)}, bf16[288,128]{1,0:T(8,128)(2,1)S(1)}) custom-call(bf16[2,288,1024]{2,1,0:T(8,128)(2,1)S(1)} %get-tuple-element.17.filt, bf16[4160,256]{1,0:T(8,128)(2,1)} %constant.5.clone.table_hbm), custom_call_target="tpu_custom_call" | custom-call | flops 536870912 | bytes 2097152 | tf_op jit(solution)/shard_map/transform/pallas_call | solution.py:188
  10.2 0.0 copy-start
  10.2 0.0 collective-permute-done.refs_3_.refs_1_
  10.2 1.0 %collective-permute-start.1 = (bf16[288,128]{1,0:T(8,128)(2,1)S(1)}, bf16[288,128]{1,0:T(8,128)(2,1)S(1)}, u32[]{:S(2)}, u32[]{:S(2)}) collective-permute-start(bf16[288,128]{1,0:T(8,128)(2,1)S(1)} %get-tuple-element.23), channel_id=1, source_target_pairs={{0,8},{8,0},{16,24},{24,16},{1,9},{9,1},{17,25},{25,17},{2,10},{10... | collective-permute-start | bytes 221192 | tf_op jit(solution)/shard_map/ppermute | solution.py:363
  11.2 3.5 %collective-permute-start.2 = (bf16[288,128]{1,0:T(8,128)(2,1)S(1)}, bf16[288,128]{1,0:T(8,128)(2,1)S(1)}, u32[]{:S(2)}, u32[]{:S(2)}) collective-permute-start(bf16[288,128]{1,0:T(8,128)(2,1)S(1)} %get-tuple-element.24), channel_id=1, source_target_pairs={{0,16},{8,24},{16,0},{24,8},{1,17},{9,25},{17,1},{25,9},{2,18},{10... | collective-permute-start | bytes 221192 | tf_op jit(solution)/shard_map/ppermute | solution.py:363
  14.7 0.0 collective-permute-start.3
  14.7 0.0 copy-done.1
  14.7 0.1 copy.6
  14.8 0.0 collective-permute-done.6.refs_2_
  14.8 0.2 collective-permute-done.7.refs_3_
  15.0 0.4 %equalize.3.refs_0_ = bf16[2,256,256]{2,1,0:T(8,128)(2,1)S(1)} custom-call(bf16[288,128]{1,0:T(8,128)(2,1)S(1)} %get-tuple-element.26.refs_0_, bf16[288,128]{1,0:T(8,128)(2,1)S(1)} %collective-permute-done.refs_3_.refs_1_, bf16[288,128]{1,0:T(8,128)(2,1)S(1)} %collective-permute-done.6.refs_2_, bf16[288,128]{1,0:T(8,128)(2,1)S(1)} %collective-permute-done.7.refs_3_, ...), custom_call_target="tpu_custom_call" | custom-call | bytes 1024 | tf_op jit(solution)/shard_map/equalize/pallas_call | solution.py:247
  15.5 1.6 %collective-permute-start.9 = (bf16[2,256,256]{2,1,0:T(8,128)(2,1)S(1)}, bf16[2,256,256]{2,1,0:T(8,128)(2,1)S(1)}, u32[]{:S(2)}, u32[]{:S(2)}) collective-permute-start(bf16[2,256,256]{2,1,0:T(8,128)(2,1)S(1)} %equalize.3.refs_0_), channel_id=1, source_target_pairs={{0,4},{4,0},{1,5},{5,1},{2,6},{6,2},{3,7},{7,3},{8,12},{12,8},{9,1... | collective-permute-start | bytes 786440 | tf_op jit(solution)/shard_map/ppermute | solution.py:423
  17.1 1.5 %collective-permute-start.8 = (bf16[2,256,256]{2,1,0:T(8,128)(2,1)S(1)}, bf16[2,256,256]{2,1,0:T(8,128)(2,1)S(1)}, u32[]{:S(2)}, u32[]{:S(2)}) collective-permute-start(bf16[2,256,256]{2,1,0:T(8,128)(2,1)S(1)} %equalize.3.refs_0_), channel_id=1, source_target_pairs={{0,2},{1,3},{2,0},{3,1},{4,6},{5,7},{6,4},{7,5},{8,10},{9,11},{10,... | collective-permute-start | bytes 786440 | tf_op jit(solution)/shard_map/ppermute | solution.py:422
  18.5 0.0 collective-permute-done.1.refs_1_
  18.6 0.9 %collective-permute-done.2.refs_2_ = bf16[288,128]{1,0:T(8,128)(2,1)S(1)} collective-permute-done((bf16[288,128]{1,0:T(8,128)(2,1)S(1)}, bf16[288,128]{1,0:T(8,128)(2,1)S(1)}, u32[]{:S(2)}, u32[]{:S(2)}) %collective-permute-start.2) | collective-permute-done | bytes 73760 | tf_op jit(solution)/shard_map/ppermute | solution.py:363
  19.5 1.5 %collective-permute-done.3.refs_3_ = bf16[288,128]{1,0:T(8,128)(2,1)S(1)} collective-permute-done((bf16[288,128]{1,0:T(8,128)(2,1)S(1)}, bf16[288,128]{1,0:T(8,128)(2,1)S(1)}, u32[]{:S(2)}, u32[]{:S(2)}) %collective-permute-start.3) | collective-permute-done | bytes 73760 | tf_op jit(solution)/shard_map/ppermute | solution.py:363
  20.9 0.4 %equalize.2.refs_1_.refs_0_ = bf16[2,256,256]{2,1,0:T(8,128)(2,1)S(1)} custom-call(bf16[288,128]{1,0:T(8,128)(2,1)S(1)} %get-tuple-element.18.refs_0_, bf16[288,128]{1,0:T(8,128)(2,1)S(1)} %collective-permute-done.1.refs_1_, bf16[288,128]{1,0:T(8,128)(2,1)S(1)} %collective-permute-done.2.refs_2_, bf16[288,128]{1,0:T(8,128)(2,1)S(1)} %collective-permute-done.3.refs_3_, ...), custom_call_target="tpu_custom_call" | custom-call | bytes 1024 | tf_op jit(solution)/shard_map/equalize/pallas_call | solution.py:247
  21.4 0.1 collective-permute-start.10
  21.5 0.5 %collective-permute-done.9.refs_2_.refs_4_ = bf16[2,256,256]{2,1,0:T(8,128)(2,1)S(1)} collective-permute-done((bf16[2,256,256]{2,1,0:T(8,128)(2,1)S(1)}, bf16[2,256,256]{2,1,0:T(8,128)(2,1)S(1)}, u32[]{:S(2)}, u32[]{:S(2)}) %collective-permute-start.9) | collective-permute-done | bytes 262176 | tf_op jit(solution)/shard_map/ppermute | solution.py:423
  22.0 1.5 %collective-permute-done.8.refs_0_ = bf16[2,256,256]{2,1,0:T(8,128)(2,1)S(1)} collective-permute-done((bf16[2,256,256]{2,1,0:T(8,128)(2,1)S(1)}, bf16[2,256,256]{2,1,0:T(8,128)(2,1)S(1)}, u32[]{:S(2)}, u32[]{:S(2)}) %collective-permute-start.8) | collective-permute-done | bytes 262176 | tf_op jit(solution)/shard_map/ppermute | solution.py:422
  23.5 0.1 collective-permute-start.11
  23.5 1.6 %collective-permute-start.4 = (bf16[2,256,256]{2,1,0:T(8,128)(2,1)S(1)}, bf16[2,256,256]{2,1,0:T(8,128)(2,1)S(1)}, u32[]{:S(2)}, u32[]{:S(2)}) collective-permute-start(bf16[2,256,256]{2,1,0:T(8,128)(2,1)S(1)} %equalize.2.refs_1_.refs_0_), channel_id=1, source_target_pairs={{0,2},{1,3},{2,0},{3,1},{4,6},{5,7},{6,4},{7,5},{8,10},{9,11},{10,... | collective-permute-start | bytes 786440 | tf_op jit(solution)/shard_map/ppermute | solution.py:422
  25.1 0.5 %collective-permute-start.5 = (bf16[2,256,256]{2,1,0:T(8,128)(2,1)S(1)}, bf16[2,256,256]{2,1,0:T(8,128)(2,1)S(1)}, u32[]{:S(2)}, u32[]{:S(2)}) collective-permute-start(bf16[2,256,256]{2,1,0:T(8,128)(2,1)S(1)} %equalize.2.refs_1_.refs_0_), channel_id=1, source_target_pairs={{0,4},{4,0},{1,5},{5,1},{2,6},{6,2},{3,7},{7,3},{8,12},{12,8},{9,1... | collective-permute-start | bytes 786440 | tf_op jit(solution)/shard_map/ppermute | solution.py:423
  25.6 0.0 collective-permute-done.11.refs_3_
  25.6 0.0 collective-permute-done.10.refs_2_
  25.6 0.0 copy-done
  25.6 2.2 %correlate.2.refs_3_.refs_5_ = f32[2,16,32,64]{3,2,1,0:T(8,128)S(1)} custom-call(s32[8,8]{1,0:T(8,128)S(1)} %copy-done, bf16[2,256,256]{2,1,0:T(8,128)(2,1)S(1)} %equalize.3.refs_0_, bf16[2,256,256]{2,1,0:T(8,128)(2,1)S(1)} %held_back.4.refs_1_, bf16[2,2,256,256]{3,2,1,0:T(8,128)(2,1)S(1)} %collective-permute-done.10.refs_2_, ...), custom_call_target="tpu_custom_call" | custom-call | bytes 1024 | tf_op jit(solution)/shard_map/correlate/pallas_call | solution.py:346
  27.8 4.5 %collective-permute-done.4.refs_0_ = bf16[2,256,256]{2,1,0:T(8,128)(2,1)S(1)} collective-permute-done((bf16[2,256,256]{2,1,0:T(8,128)(2,1)S(1)}, bf16[2,256,256]{2,1,0:T(8,128)(2,1)S(1)}, u32[]{:S(2)}, u32[]{:S(2)}) %collective-permute-start.4) | collective-permute-done | bytes 262176 | tf_op jit(solution)/shard_map/ppermute | solution.py:422
  32.3 1.2 %collective-permute-done.5.refs_2_.refs_4_ = bf16[2,256,256]{2,1,0:T(8,128)(2,1)S(1)} collective-permute-done((bf16[2,256,256]{2,1,0:T(8,128)(2,1)S(1)}, bf16[2,256,256]{2,1,0:T(8,128)(2,1)S(1)}, u32[]{:S(2)}, u32[]{:S(2)}) %collective-permute-start.5) | collective-permute-done | bytes 262176 | tf_op jit(solution)/shard_map/ppermute | solution.py:423
  33.5 0.1 collective-permute-start.12
  33.6 1.5 %collective-permute-done.12.refs_3_ = bf16[2,256,256]{2,1,0:T(8,128)(2,1)S(1)} collective-permute-done((bf16[2,256,256]{2,1,0:T(8,128)(2,1)S(1)}, bf16[2,256,256]{2,1,0:T(8,128)(2,1)S(1)}, u32[]{:S(2)}, u32[]{:S(2)}) %collective-permute-start.12) | collective-permute-done | bytes 262176 | tf_op jit(solution)/shard_map/ppermute | solution.py:430
  35.1 3.1 %correlate.3 = f32[2,16,32,128]{3,2,1,0:T(8,128)} custom-call(s32[8,8]{1,0:T(8,128)S(1)} %copy-done, bf16[2,256,256]{2,1,0:T(8,128)(2,1)S(1)} %equalize.2.refs_1_.refs_0_, bf16[2,256,256]{2,1,0:T(8,128)(2,1)S(1)} %held_back.5.refs_1_, bf16[2,2,256,256]{3,2,1,0:T(8,128)(2,1)S(1)} %collective-permute-done.10.refs_2_, ...), custom_call_target="tpu_custom_call" | custom-call | bytes 1024 | tf_op jit(solution)/shard_map/correlate/pallas_call | solution.py:346
  (5 shorter events, 0.1 us)
Async XLA Ops:
  2.6 12.0 %copy-start.1 = (f32[8,2,128]{2,1,0:T(2,128)S(1)}, f32[8,2,128]{2,1,0:T(2,128)}, u32[]{:S(2)}) copy-start(f32[8,2,128]{2,1,0:T(2,128)} %param.5) | copy-start | bytes 24580
  2.6 7.5 %collective-permute-start = (bf16[288,128]{1,0:T(8,128)(2,1)S(1)}, bf16[288,128]{1,0:T(8,128)(2,1)S(1)}, u32[]{:S(2)}, u32[]{:S(2)}) collective-permute-start(bf16[288,128]{1,0:T(8,128)(2,1)S(1)} %get-tuple-element.22), channel_id=1, source_target_pairs={{0,8},{8,0},{16,24},{24,16},{1,9},{9,1},{17,25},{25,17},{2,10},{10... | collective-permute-start | bytes 221192 | tf_op jit(solution)/shard_map/ppermute | solution.py:363
  5.7 9.0 %collective-permute-start.6 = (bf16[288,128]{1,0:T(8,128)(2,1)S(1)}, bf16[288,128]{1,0:T(8,128)(2,1)S(1)}, u32[]{:S(2)}, u32[]{:S(2)}) collective-permute-start(bf16[288,128]{1,0:T(8,128)(2,1)S(1)} %get-tuple-element.27), channel_id=1, source_target_pairs={{0,16},{8,24},{16,0},{24,8},{1,17},{9,25},{17,1},{25,9},{2,18},{10... | collective-permute-start | bytes 221192 | tf_op jit(solution)/shard_map/ppermute | solution.py:363
  8.3 6.7 %collective-permute-start.7 = (bf16[288,128]{1,0:T(8,128)(2,1)S(1)}, bf16[288,128]{1,0:T(8,128)(2,1)S(1)}, u32[]{:S(2)}, u32[]{:S(2)}) collective-permute-start(bf16[288,128]{1,0:T(8,128)(2,1)S(1)} %get-tuple-element.28), channel_id=1, source_target_pairs={{0,24},{8,16},{16,8},{24,0},{1,25},{9,17},{17,9},{25,1},{2,26},{10... | collective-permute-start | bytes 221192 | tf_op jit(solution)/shard_map/ppermute | solution.py:363
  10.2 15.4 %copy-start = (s32[8,8]{1,0:T(8,128)S(1)}, s32[8,8]{1,0:T(8,128)}, u32[]{:S(2)}) copy-start(s32[8,8]{1,0:T(8,128)} %map_ref.3) | copy-start | bytes 772
  10.2 8.3 %collective-permute-start.1 = (bf16[288,128]{1,0:T(8,128)(2,1)S(1)}, bf16[288,128]{1,0:T(8,128)(2,1)S(1)}, u32[]{:S(2)}, u32[]{:S(2)}) collective-permute-start(bf16[288,128]{1,0:T(8,128)(2,1)S(1)} %get-tuple-element.23), channel_id=1, source_target_pairs={{0,8},{8,0},{16,24},{24,16},{1,9},{9,1},{17,25},{25,17},{2,10},{10... | collective-permute-start | bytes 221192 | tf_op jit(solution)/shard_map/ppermute | solution.py:363
  11.2 8.3 %collective-permute-start.2 = (bf16[288,128]{1,0:T(8,128)(2,1)S(1)}, bf16[288,128]{1,0:T(8,128)(2,1)S(1)}, u32[]{:S(2)}, u32[]{:S(2)}) collective-permute-start(bf16[288,128]{1,0:T(8,128)(2,1)S(1)} %get-tuple-element.24), channel_id=1, source_target_pairs={{0,16},{8,24},{16,0},{24,8},{1,17},{9,25},{17,1},{25,9},{2,18},{10... | collective-permute-start | bytes 221192 | tf_op jit(solution)/shard_map/ppermute | solution.py:363
  14.7 6.3 %collective-permute-start.3 = (bf16[288,128]{1,0:T(8,128)(2,1)S(1)}, bf16[288,128]{1,0:T(8,128)(2,1)S(1)}, u32[]{:S(2)}, u32[]{:S(2)}) collective-permute-start(bf16[288,128]{1,0:T(8,128)(2,1)S(1)} %get-tuple-element.25), channel_id=1, source_target_pairs={{0,24},{8,16},{16,8},{24,0},{1,25},{9,17},{17,9},{25,1},{2,26},{10... | collective-permute-start | bytes 221192 | tf_op jit(solution)/shard_map/ppermute | solution.py:363
  15.5 6.5 %collective-permute-start.9 = (bf16[2,256,256]{2,1,0:T(8,128)(2,1)S(1)}, bf16[2,256,256]{2,1,0:T(8,128)(2,1)S(1)}, u32[]{:S(2)}, u32[]{:S(2)}) collective-permute-start(bf16[2,256,256]{2,1,0:T(8,128)(2,1)S(1)} %equalize.3.refs_0_), channel_id=1, source_target_pairs={{0,4},{4,0},{1,5},{5,1},{2,6},{6,2},{3,7},{7,3},{8,12},{12,8},{9,1... | collective-permute-start | bytes 786440 | tf_op jit(solution)/shard_map/ppermute | solution.py:423
  17.1 6.4 %collective-permute-start.8 = (bf16[2,256,256]{2,1,0:T(8,128)(2,1)S(1)}, bf16[2,256,256]{2,1,0:T(8,128)(2,1)S(1)}, u32[]{:S(2)}, u32[]{:S(2)}) collective-permute-start(bf16[2,256,256]{2,1,0:T(8,128)(2,1)S(1)} %equalize.3.refs_0_), channel_id=1, source_target_pairs={{0,2},{1,3},{2,0},{3,1},{4,6},{5,7},{6,4},{7,5},{8,10},{9,11},{10,... | collective-permute-start | bytes 786440 | tf_op jit(solution)/shard_map/ppermute | solution.py:422
  21.4 4.2 %collective-permute-start.10 = (bf16[2,2,256,256]{3,2,1,0:T(8,128)(2,1)S(1)}, bf16[2,2,256,256]{3,2,1,0:T(8,128)(2,1)S(1)}, u32[]{:S(2)}, u32[]{:S(2)}) collective-permute-start(bf16[2,2,256,256]{3,2,1,0:T(8,128)(2,1)S(1)} %together.1), channel_id=1, source_target_pairs={{0,1},{1,0},{2,3},{3,2},{4,5},{5,4},{6,7},{7,6},{8,9},{9,8},{10,11... | collective-permute-start | bytes 1572872 | tf_op jit(solution)/shard_map/ppermute | solution.py:425
  23.5 2.1 %collective-permute-start.11 = (bf16[2,256,256]{2,1,0:T(8,128)(2,1)S(1)}, bf16[2,256,256]{2,1,0:T(8,128)(2,1)S(1)}, u32[]{:S(2)}, u32[]{:S(2)}) collective-permute-start(bf16[2,256,256]{2,1,0:T(8,128)(2,1)S(1)} %held_back.4.refs_1_), channel_id=1, source_target_pairs={{0,1},{1,0},{2,3},{3,2},{4,5},{5,4},{6,7},{7,6},{8,9},{9,8},{10,11... | collective-permute-start | bytes 786440 | tf_op jit(solution)/shard_map/ppermute | solution.py:430
  23.5 8.7 %collective-permute-start.4 = (bf16[2,256,256]{2,1,0:T(8,128)(2,1)S(1)}, bf16[2,256,256]{2,1,0:T(8,128)(2,1)S(1)}, u32[]{:S(2)}, u32[]{:S(2)}) collective-permute-start(bf16[2,256,256]{2,1,0:T(8,128)(2,1)S(1)} %equalize.2.refs_1_.refs_0_), channel_id=1, source_target_pairs={{0,2},{1,3},{2,0},{3,1},{4,6},{5,7},{6,4},{7,5},{8,10},{9,11},{10,... | collective-permute-start | bytes 786440 | tf_op jit(solution)/shard_map/ppermute | solution.py:422
  25.1 8.4 %collective-permute-start.5 = (bf16[2,256,256]{2,1,0:T(8,128)(2,1)S(1)}, bf16[2,256,256]{2,1,0:T(8,128)(2,1)S(1)}, u32[]{:S(2)}, u32[]{:S(2)}) collective-permute-start(bf16[2,256,256]{2,1,0:T(8,128)(2,1)S(1)} %equalize.2.refs_1_.refs_0_), channel_id=1, source_target_pairs={{0,4},{4,0},{1,5},{5,1},{2,6},{6,2},{3,7},{7,3},{8,12},{12,8},{9,1... | collective-permute-start | bytes 786440 | tf_op jit(solution)/shard_map/ppermute | solution.py:423
  33.5 1.6 %collective-permute-start.12 = (bf16[2,256,256]{2,1,0:T(8,128)(2,1)S(1)}, bf16[2,256,256]{2,1,0:T(8,128)(2,1)S(1)}, u32[]{:S(2)}, u32[]{:S(2)}) collective-permute-start(bf16[2,256,256]{2,1,0:T(8,128)(2,1)S(1)} %held_back.5.refs_1_), channel_id=1, source_target_pairs={{0,1},{1,0},{2,3},{3,2},{4,5},{5,4},{6,7},{7,6},{8,9},{9,8},{10,11... | collective-permute-start | bytes 786440 | tf_op jit(solution)/shard_map/ppermute | solution.py:430

commit v6 on v5

--- a/solution.py
+++ b/solution.py
@@ -21,7 +21,7 @@
 BATCH = 4
 PARTS = 2
 VMEM_BYTES = 16 * 1024 * 1024
-FILTER_VMEM_BYTES = 52 * 1024 * 1024
+FILTER_VMEM_BYTES = 101 * 512 * 1024
 COEF_ROWS = 64
 
 
@@ -72,13 +72,13 @@
     for owner in range(owners):
         here = slice(owner * width, (owner + 1) * width)
         piece = jnp.concatenate([spectra[0][:, here], spectra[1][:, here]], axis=1)
-        stage[jnp.bitwise_xor(me, owner)] = piece.astype(jnp.bfloat16)
+        stage[jnp.bitwise_xor(me, owner)] = piece[: stage.shape[1]].astype(jnp.bfloat16)
     for d in range(owners):
         out_refs[d][...] = stage[d]
 
 
 def filter_kernel(frames, pieces, scale, volt_hbm, table_hbm, *refs):
-    out_refs, (filt, volt, table, terms, coef, stage, sems) = refs[:-7], refs[-7:]
+    out_refs, (filt, later, volt, table, terms, coef, stage, sems) = refs[:-8], refs[-8:]
     per = frames // pieces
     lead = TAPS - 1
     copies = []
@@ -98,6 +98,10 @@
     for copy in copies:
         copy.start()
     table_copy.start()
+    later_copy = pltpu.make_async_copy(
+        table_hbm.at[pl.ds(2 * NCHAN, (PARTS - 1) * 2 * NCHAN)], later, sems.at[pieces + 2]
+    )
+    later_copy.start()
     tail = volt.shape[2] - (lead + frames) * NCHAN
     volt[:, :, : lead * NCHAN] = jnp.zeros((2, SIG, lead * NCHAN), jnp.int32)
     volt[:, :, (lead + frames) * NCHAN :] = jnp.zeros((2, SIG, tail), jnp.int32)
@@ -139,14 +143,12 @@
     lax.fori_loop(frames // GROUP, frames // GROUP + 1, filter_group, 0)
     table_copy.wait()
     transform(filt, table, scale, stage, out_refs)
-
-
-def transform_kernel(part, scale, filt, table_hbm, *refs):
-    out_refs, table, stage, sem = refs[:-3], refs[-3], refs[-2], refs[-1]
-    copy = pltpu.make_async_copy(table_hbm.at[pl.ds(part * 2 * NCHAN, 2 * NCHAN)], table, sem)
-    copy.start()
-    copy.wait()
-    transform(filt, table, scale, stage, out_refs)
+    later_copy.wait()
+
+
+def transform_kernel(part, scale, filt, later, *refs):
+    table = later.at[pl.ds((part - 1) * 2 * NCHAN, 2 * NCHAN)]
+    transform(filt, table, scale, refs[-1], refs[:-1])
 
 
 IN_VMEM = pl.BlockSpec(memory_space=pltpu.VMEM)
@@ -157,57 +159,57 @@
 def filtered_and_first(voltages, owners, table):
     frames = voltages.shape[2] // NCHAN
     rows = (frames + GROUP) * SIG
+    sent = (frames + TAPS - 1) * SIG
     pieces = 4
     across = table.shape[1]
     terms = table.shape[0] - PARTS * 2 * NCHAN
     lanes = 2 * CHANNELS // owners // PARTS
-    *first, filt = pl.pallas_call(
+    *first, filt, later = pl.pallas_call(
         functools.partial(filter_kernel, frames, pieces, spectrum_scale()),
-        out_shape=[jax.ShapeDtypeStruct((rows, lanes), jnp.bfloat16)] * owners
-        + [jax.ShapeDtypeStruct((2, rows, NCHAN), jnp.bfloat16)],
+        out_shape=[jax.ShapeDtypeStruct((sent, lanes), jnp.bfloat16)] * owners
+        + [
+            jax.ShapeDtypeStruct((2, rows, NCHAN), jnp.bfloat16),
+            jax.ShapeDtypeStruct(((PARTS - 1) * 2 * NCHAN, across), jnp.bfloat16),
+        ],
         in_specs=[IN_HBM, IN_HBM],
-        out_specs=[IN_VMEM] * (owners + 1),
+        out_specs=[IN_VMEM] * (owners + 2),
         scratch_shapes=[
             pltpu.VMEM((2, SIG, (frames + GROUP + TAPS - 1) * NCHAN), jnp.int32),
             pltpu.VMEM((2 * NCHAN, across), jnp.bfloat16),
             pltpu.VMEM((terms, across), jnp.bfloat16),
             pltpu.VMEM((TAPS * NCHAN // across, across), jnp.float32),
-            pltpu.VMEM((owners, rows, lanes), jnp.bfloat16),
-            pltpu.SemaphoreType.DMA((pieces + 2,)),
+            pltpu.VMEM((owners, sent, lanes), jnp.bfloat16),
+            pltpu.SemaphoreType.DMA((pieces + 3,)),
         ],
         compiler_params=pltpu.CompilerParams(vmem_limit_bytes=FILTER_VMEM_BYTES),
         cost_estimate=pl.CostEstimate(flops=1 << 29, bytes_accessed=4 << 20, transcendentals=0),
         name="filter_and_transform",
     )(voltages, table)
-    return filt, first
-
-
-def next_part(part, filt, table, owners):
-    rows = filt.shape[1]
+    return filt, later, first
+
+
+def next_part(part, filt, later, owners):
+    rows = filt.shape[1] - (GROUP - TAPS + 1) * SIG
     lanes = 2 * CHANNELS // owners // PARTS
     return pl.pallas_call(
         functools.partial(transform_kernel, part, spectrum_scale()),
         out_shape=[jax.ShapeDtypeStruct((rows, lanes), jnp.bfloat16)] * owners,
-        in_specs=[IN_VMEM, IN_HBM],
+        in_specs=[IN_VMEM, IN_VMEM],
         out_specs=[IN_VMEM] * owners,
-        scratch_shapes=[
-            pltpu.VMEM((2 * NCHAN, table.shape[1]), jnp.bfloat16),
-            pltpu.VMEM((owners, rows, lanes), jnp.bfloat16),
-            pltpu.SemaphoreType.DMA(()),
-        ],
-        compiler_params=pltpu.CompilerParams(vmem_limit_bytes=FILTER_VMEM_BYTES),
+        scratch_shapes=[pltpu.VMEM((owners, rows, lanes), jnp.bfloat16)],
+        compiler_params=pltpu.CompilerParams(vmem_limit_bytes=VMEM_BYTES),
         cost_estimate=pl.CostEstimate(flops=1 << 29, bytes_accessed=2 << 20, transcendentals=0),
         name="transform",
-    )(filt, table)
+    )(filt, later)
 
 
 def equalize_kernel(owners, frames, h, part, *refs):
-    pieces = refs[:owners]
+    pieces = refs[owners - 1 :: -1]
     gains_ref, by_time, by_channel = refs[owners], refs[-2], refs[-1]
     out_ref = refs[owners + 1]
     width = 4 * h
     own_rows = frames * SIG
-    over = GROUP * SIG
+    over = (TAPS - 1) * SIG
     times = owners * frames
     tiles = times // LANES
     me = lax.axis_index("chan")
@@ -256,7 +258,7 @@
         compiler_params=pltpu.CompilerParams(vmem_limit_bytes=VMEM_BYTES),
         cost_estimate=pl.CostEstimate(flops=0, bytes_accessed=1 << 10, transcendentals=0),
         name="equalize",
-    )(*pieces, gains)
+    )(*pieces[::-1], gains)
 
 
 def row_places(col, n_col):
@@ -271,7 +273,7 @@
 
 
 def correlate_kernel(n_row, n_col, h, times, part, before, map_ref, *refs):
-    row_blocks = [ref.at[part] if i == n_col // 2 else ref for i, ref in enumerate(refs[:n_col])]
+    row_blocks = [ref for ref in refs[:n_col]]
     col_blocks = (refs[0],) + refs[n_col : n_col + n_row - 1]
     last = part == PARTS - 1
     if last:
@@ -410,25 +412,25 @@
     along = [[(i, (i + d) % n_row) for i in range(n_row)] for d in range(n_row)]
     other_core = [(i, i ^ 1) for i in range(n_col)]
 
-    filt, pieces = filtered_and_first(voltages, owners, table)
+    filt, tables, pieces = filtered_and_first(voltages, owners, table)
     own, far, column = [], [], []
     arrived = to_owners(pieces)
     for part in range(PARTS):
         later = None
         if part < PARTS - 1:
-            pieces = next_part(part + 1, filt, table, owners)
-            later = to_owners([pieces[0], *held_back(pieces[1:], arrived[1:2])])
+            pieces = next_part(part + 1, filt, tables, owners)
+            later = to_owners([pieces[0], *held_back(pieces[1:], arrived[-1:])])
         own.append(equalize(arrived, gains, part, frames))
         far.append([lax.ppermute(own[part], "bcol", across[d]) for d in range(1, chips)])
         column.append([lax.ppermute(own[part], "brow", along[d]) for d in range(1, n_row)])
         arrived = later
-    beside = lax.ppermute(together(own), "bcol", other_core)
+    beside = [lax.ppermute(block, "bcol", other_core) for block in own]
     result = None
     for part in range(PARTS):
-        after = own[-1:] + column[part] + ([] if result is None else [result])
+        after = own[-1:] + column[part]
         far[part] = list(held_back(far[part], after))
         near = [lax.ppermute(block, "bcol", other_core) for block in far[part]]
-        blocks = [own[part]] + far[part] + [beside] + near + column[part]
+        blocks = [own[part]] + far[part] + [beside[part]] + near + column[part]
         result = correlate(tile_map, blocks, result, part, n_row, n_col)
     return jnp.transpose(result, (3, 0, 1, 2))[None, None]
 

time: 38.6 us -> 35.1 us (0.909)
  waiting for transfers between devices: 11.7 us -> 8.29 us
  starting transfers between devices: 15.5 us -> 17 us
  Pallas kernels: 10.7 us -> 9.4 us
    ppermute x2, waiting for transfers between devices: 1.68 us -> 0.01 us  [shards(): lax.ppermute(own[part], 'brow', along[d])]
    ppermute x2, waiting for transfers between devices: 1.52 us -> 0.01 us  [shards(): near = [lax.ppermute(block, 'bcol', other_core) for block in far[part]]]
    pallas_call x1, Pallas kernels: 1.83 us -> 0.58 us  [next_part(): pl.pallas_call(functools.partial(transform_kernel, part, spectrum_scale()...]
    ppermute x2, waiting for transfers between devices: 5.93 us -> 4.81 us  [shards(): lax.ppermute(own[part], 'bcol', across[d])]
    ppermute x6, waiting for transfers between devices: 2.58 us -> 3.47 us  [to_owners(): lax.ppermute(pieces[d], 'chan', [(i, i ^ d) for i in range(owners)])]
    ppermute x2, starting transfers between devices: 2.11 us -> 2.65 us  [shards(): lax.ppermute(own[part], 'brow', along[d])]
    ppermute x6, starting transfers between devices: 10.1 us -> 10.7 us  [to_owners(): lax.ppermute(pieces[d], 'chan', [(i, i ^ d) for i in range(owners)])]
    ppermute x1 -> x2, starting transfers between devices: 0.07 us -> 0.51 us  [shards(): beside = [lax.ppermute(block, 'bcol', other_core) for block in own]]
  transfers between devices with their start and end apart: 13 -> 14, of which waited for: 8 -> 5; matrix products, arithmetic and copies ran while one was open for 0% -> 0% of each run, Pallas kernels for 13% -> 11%
where the time goes in v6:
time: 35.1 us; the launch traced here: 35 us
  starting transfers between devices  17 us (48%)
  Pallas kernels  9.4 us (27%)
  waiting for transfers between devices  8.29 us (24%)
    ppermute x6, starting transfers between devices, to_owners(): lax.ppermute(pieces[d], 'chan', [(i, i ^ d) for i in range(owners)])  10.7 us
    pallas_call x2, Pallas kernels, correlate(): pl.pallas_call(functools.partial(correlate_kernel, n_row, n_col, h, times...  5.25 us
    ppermute x2, waiting for transfers between devices, shards(): lax.ppermute(own[part], 'bcol', across[d])  4.81 us
    ppermute x6, waiting for transfers between devices, to_owners(): lax.ppermute(pieces[d], 'chan', [(i, i ^ d) for i in range(owners)])  3.47 us
    ppermute x2, starting transfers between devices, shards(): lax.ppermute(own[part], 'bcol', across[d])  3.05 us
    ppermute x2, starting transfers between devices, shards(): lax.ppermute(own[part], 'brow', along[d])  2.65 us
    pallas_call x1, Pallas kernels, filtered_and_first(): pl.pallas_call(functools.partial(filter_kernel, frames, pieces, spectrum_...  2.62 us
    pallas_call x2, Pallas kernels, equalize(): pl.pallas_call(functools.partial(equalize_kernel, owners, frames, h, part...  0.9 us
  transfers between devices with their start and end apart: 14, of which 5 were waited for; matrix products, arithmetic and copies ran while one was open for 0% of the time, Pallas kernels for 11%

profile of v6, /device:TPU:0, one launch (start us, length us, event | category | flops | bytes accessed | tf_op | source)
XLA Modules:
  0.0 35.0 jit_solution(4122689428619965369)
XLA Ops:
  0.0 2.6 %filter_and_transform.1 = (bf16[280,128]{1,0:T(8,128)(2,1)S(1)}, bf16[280,128]{1,0:T(8,128)(2,1)S(1)}, bf16[280,128]{1,0:T(8,128)(2,1)S(1)}, bf16[280,128]{1,0:T...) custom-call(s32[2,8,32768]{2,1,0:T(8,128)} %volt_hbm.1, ...), custom_call_target="tpu_custom_call" | custom-call | flops 536870912 | bytes 4194304 | tf_op jit(solution)/shard_map/filter_and_transform/pallas_call | solution.py:167
  2.6 0.0 copy-start.1
  2.6 5.1 %collective-permute-start = (bf16[280,128]{1,0:T(8,128)(2,1)S(1)}, bf16[280,128]{1,0:T(8,128)(2,1)S(1)}, u32[]{:S(2)}, u32[]{:S(2)}) collective-permute-start(bf16[280,128]{1,0:T(8,128)(2,1)S(1)} %get-tuple-element.23), channel_id=1, source_target_pairs={{0,24},{8,16},{16,8},{24,0},{1,25},{9,17},{17,9},{25,1},{2,26},{10... | collective-permute-start | bytes 215048 | tf_op jit(solution)/shard_map/ppermute | solution.py:365
  7.8 0.0 collective-permute-start.8
  7.8 0.6 %collective-permute-start.9 = (bf16[280,128]{1,0:T(8,128)(2,1)S(1)}, bf16[280,128]{1,0:T(8,128)(2,1)S(1)}, u32[]{:S(2)}, u32[]{:S(2)}) collective-permute-start(bf16[280,128]{1,0:T(8,128)(2,1)S(1)} %get-tuple-element.29), channel_id=1, source_target_pairs={{0,8},{8,0},{16,24},{24,16},{1,9},{9,1},{17,25},{25,17},{2,10},{10... | collective-permute-start | bytes 215048 | tf_op jit(solution)/shard_map/ppermute | solution.py:365
  8.4 0.6 %transform.1 = (bf16[280,128]{1,0:T(8,128)(2,1)S(1)}, bf16[280,128]{1,0:T(8,128)(2,1)S(1)}, bf16[280,128]{1,0:T(8,128)(2,1)S(1)}, bf16[280,128]{1,0:T(8,128)(2,1)S(1)}) custom-call(bf16[2,288,1024]{2,1,0:T(8,128)(2,1)S(1)} %get-tuple-element.18.filt, bf16[2048,256]{1,0:T(8,128)(2,1)S(1)} %get-tuple-element.19.later), custom_call_target="tpu_custom_call" | custom-call | flops 536870912 | bytes 2097152 | tf_op jit(solution)/shard_map/transform/pallas_call | solution.py:194
  9.0 0.0 copy-start
  9.0 1.5 %collective-permute-done.refs_3_.refs_0_ = bf16[280,128]{1,0:T(8,128)(2,1)S(1)} collective-permute-done((bf16[280,128]{1,0:T(8,128)(2,1)S(1)}, bf16[280,128]{1,0:T(8,128)(2,1)S(1)}, u32[]{:S(2)}, u32[]{:S(2)}) %collective-permute-start) | collective-permute-done | bytes 71712 | tf_op jit(solution)/shard_map/ppermute | solution.py:365
  10.5 4.3 %collective-permute-start.1 = (bf16[280,128]{1,0:T(8,128)(2,1)S(1)}, bf16[280,128]{1,0:T(8,128)(2,1)S(1)}, u32[]{:S(2)}, u32[]{:S(2)}) collective-permute-start(bf16[280,128]{1,0:T(8,128)(2,1)S(1)} %get-tuple-element.24), channel_id=1, source_target_pairs={{0,24},{8,16},{16,8},{24,0},{1,25},{9,17},{17,9},{25,1},{2,26},{10... | collective-permute-start | bytes 215048 | tf_op jit(solution)/shard_map/ppermute | solution.py:365
  14.7 0.3 collective-permute-start.2
  15.0 0.4 %collective-permute-start.3 = (bf16[280,128]{1,0:T(8,128)(2,1)S(1)}, bf16[280,128]{1,0:T(8,128)(2,1)S(1)}, u32[]{:S(2)}, u32[]{:S(2)}) collective-permute-start(bf16[280,128]{1,0:T(8,128)(2,1)S(1)} %get-tuple-element.26), channel_id=1, source_target_pairs={{0,8},{8,0},{16,24},{24,16},{1,9},{9,1},{17,25},{25,17},{2,10},{10... | collective-permute-start | bytes 215048 | tf_op jit(solution)/shard_map/ppermute | solution.py:365
  15.4 0.0 copy-done.1
  15.4 0.1 copy.6
  15.5 0.5 %collective-permute-done.8.refs_1_ = bf16[280,128]{1,0:T(8,128)(2,1)S(1)} collective-permute-done((bf16[280,128]{1,0:T(8,128)(2,1)S(1)}, bf16[280,128]{1,0:T(8,128)(2,1)S(1)}, u32[]{:S(2)}, u32[]{:S(2)}) %collective-permute-start.8) | collective-permute-done | bytes 71712 | tf_op jit(solution)/shard_map/ppermute | solution.py:365
  16.0 0.0 collective-permute-done.9.refs_2_
  16.0 0.4 %equalize.3.refs_0_ = bf16[2,256,256]{2,1,0:T(8,128)(2,1)S(1)} custom-call(bf16[280,128]{1,0:T(8,128)(2,1)S(1)} %collective-permute-done.refs_3_.refs_0_, bf16[280,128]{1,0:T(8,128)(2,1)S(1)} %collective-permute-done.8.refs_1_, bf16[280,128]{1,0:T(8,128)(2,1)S(1)} %collective-permute-done.9.refs_2_, bf16[280,128]{1,0:T(8,128)(2,1)S(1)} %get-tuple-element.30.refs_3_, ...), custom_call_target="tpu_custom_call" | custom-call | bytes 1024 | tf_op jit(solution)/shard_map/equalize/pallas_call | solution.py:249
  16.4 1.1 %collective-permute-start.11 = (bf16[2,256,256]{2,1,0:T(8,128)(2,1)S(1)}, bf16[2,256,256]{2,1,0:T(8,128)(2,1)S(1)}, u32[]{:S(2)}, u32[]{:S(2)}) collective-permute-start(bf16[2,256,256]{2,1,0:T(8,128)(2,1)S(1)} %equalize.3.refs_0_), channel_id=1, source_target_pairs={{0,4},{4,0},{1,5},{5,1},{2,6},{6,2},{3,7},{7,3},{8,12},{12,8},{9,1... | collective-permute-start | bytes 786440 | tf_op jit(solution)/shard_map/ppermute | solution.py:425
  17.6 1.5 %collective-permute-start.10 = (bf16[2,256,256]{2,1,0:T(8,128)(2,1)S(1)}, bf16[2,256,256]{2,1,0:T(8,128)(2,1)S(1)}, u32[]{:S(2)}, u32[]{:S(2)}) collective-permute-start(bf16[2,256,256]{2,1,0:T(8,128)(2,1)S(1)} %equalize.3.refs_0_), channel_id=1, source_target_pairs={{0,2},{1,3},{2,0},{3,1},{4,6},{5,7},{6,4},{7,5},{8,10},{9,11},{10,... | collective-permute-start | bytes 786440 | tf_op jit(solution)/shard_map/ppermute | solution.py:424
  19.1 0.0 collective-permute-done.1.refs_0_
  19.1 1.5 %collective-permute-done.2.refs_1_ = bf16[280,128]{1,0:T(8,128)(2,1)S(1)} collective-permute-done((bf16[280,128]{1,0:T(8,128)(2,1)S(1)}, bf16[280,128]{1,0:T(8,128)(2,1)S(1)}, u32[]{:S(2)}, u32[]{:S(2)}) %collective-permute-start.2) | collective-permute-done | bytes 71712 | tf_op jit(solution)/shard_map/ppermute | solution.py:365
  20.6 0.0 collective-permute-done.3.refs_2_
  20.6 0.4 %equalize.2.refs_1_.refs_0_ = bf16[2,256,256]{2,1,0:T(8,128)(2,1)S(1)} custom-call(bf16[280,128]{1,0:T(8,128)(2,1)S(1)} %collective-permute-done.1.refs_0_, bf16[280,128]{1,0:T(8,128)(2,1)S(1)} %collective-permute-done.2.refs_1_, bf16[280,128]{1,0:T(8,128)(2,1)S(1)} %collective-permute-done.3.refs_2_, bf16[280,128]{1,0:T(8,128)(2,1)S(1)} %get-tuple-element.27.refs_3_, ...), custom_call_target="tpu_custom_call" | custom-call | bytes 1024 | tf_op jit(solution)/shard_map/equalize/pallas_call | solution.py:249
  21.1 1.6 %collective-permute-start.4 = (bf16[2,256,256]{2,1,0:T(8,128)(2,1)S(1)}, bf16[2,256,256]{2,1,0:T(8,128)(2,1)S(1)}, u32[]{:S(2)}, u32[]{:S(2)}) collective-permute-start(bf16[2,256,256]{2,1,0:T(8,128)(2,1)S(1)} %equalize.2.refs_1_.refs_0_), channel_id=1, source_target_pairs={{0,2},{1,3},{2,0},{3,1},{4,6},{5,7},{6,4},{7,5},{8,10},{9,11},{10,... | collective-permute-start | bytes 786440 | tf_op jit(solution)/shard_map/ppermute | solution.py:424
  22.6 1.5 %collective-permute-start.5 = (bf16[2,256,256]{2,1,0:T(8,128)(2,1)S(1)}, bf16[2,256,256]{2,1,0:T(8,128)(2,1)S(1)}, u32[]{:S(2)}, u32[]{:S(2)}) collective-permute-start(bf16[2,256,256]{2,1,0:T(8,128)(2,1)S(1)} %equalize.2.refs_1_.refs_0_), channel_id=1, source_target_pairs={{0,4},{4,0},{1,5},{5,1},{2,6},{6,2},{3,7},{7,3},{8,12},{12,8},{9,1... | collective-permute-start | bytes 786440 | tf_op jit(solution)/shard_map/ppermute | solution.py:425
  24.1 0.0 collective-permute-start.12
  24.1 0.0 collective-permute-done.11.refs_2_.refs_4_
  24.1 0.5 %collective-permute-start.6 = (bf16[2,256,256]{2,1,0:T(8,128)(2,1)S(1)}, bf16[2,256,256]{2,1,0:T(8,128)(2,1)S(1)}, u32[]{:S(2)}, u32[]{:S(2)}) collective-permute-start(bf16[2,256,256]{2,1,0:T(8,128)(2,1)S(1)} %equalize.2.refs_1_.refs_0_), channel_id=1, source_target_pairs={{0,1},{1,0},{2,3},{3,2},{4,5},{5,4},{6,7},{7,6},{8,9},{9,8},{10,11... | collective-permute-start | bytes 786440 | tf_op jit(solution)/shard_map/ppermute | solution.py:427
  24.6 2.1 %collective-permute-done.10.refs_0_ = bf16[2,256,256]{2,1,0:T(8,128)(2,1)S(1)} collective-permute-done((bf16[2,256,256]{2,1,0:T(8,128)(2,1)S(1)}, bf16[2,256,256]{2,1,0:T(8,128)(2,1)S(1)}, u32[]{:S(2)}, u32[]{:S(2)}) %collective-permute-start.10) | collective-permute-done | bytes 262176 | tf_op jit(solution)/shard_map/ppermute | solution.py:424
  26.8 0.1 collective-permute-start.13
  26.8 2.7 %collective-permute-done.4.refs_0_ = bf16[2,256,256]{2,1,0:T(8,128)(2,1)S(1)} collective-permute-done((bf16[2,256,256]{2,1,0:T(8,128)(2,1)S(1)}, bf16[2,256,256]{2,1,0:T(8,128)(2,1)S(1)}, u32[]{:S(2)}, u32[]{:S(2)}) %collective-permute-start.4) | collective-permute-done | bytes 262176 | tf_op jit(solution)/shard_map/ppermute | solution.py:424
  29.6 0.0 collective-permute-done.5.refs_2_.refs_4_
  29.6 0.1 collective-permute-start.7
  29.7 0.0 collective-permute-done.12.refs_2_
  29.7 0.0 collective-permute-done.13.refs_3_
  29.7 0.0 copy-done
  29.7 2.2 %correlate.2.refs_5_ = f32[2,16,32,64]{3,2,1,0:T(8,128)S(1)} custom-call(s32[8,8]{1,0:T(8,128)S(1)} %copy-done, bf16[2,256,256]{2,1,0:T(8,128)(2,1)S(1)} %equalize.3.refs_0_, bf16[2,256,256]{2,1,0:T(8,128)(2,1)S(1)} %held_back.5.refs_1_, bf16[2,256,256]{2,1,0:T(8,128)(2,1)S(1)} %collective-permute-done.12.refs_2_, ...), custom_call_target="tpu_custom_call" | custom-call | bytes 1024 | tf_op jit(solution)/shard_map/correlate/pallas_call | solution.py:348
  31.9 0.0 collective-permute-done.6.refs_2_
  31.9 0.0 collective-permute-done.7.refs_3_
  31.9 3.1 %correlate.3 = f32[2,16,32,128]{3,2,1,0:T(8,128)} custom-call(s32[8,8]{1,0:T(8,128)S(1)} %copy-done, bf16[2,256,256]{2,1,0:T(8,128)(2,1)S(1)} %equalize.2.refs_1_.refs_0_, bf16[2,256,256]{2,1,0:T(8,128)(2,1)S(1)} %held_back.4.refs_1_, bf16[2,256,256]{2,1,0:T(8,128)(2,1)S(1)} %collective-permute-done.6.refs_2_, ...), custom_call_target="tpu_custom_call" | custom-call | bytes 1024 | tf_op jit(solution)/shard_map/correlate/pallas_call | solution.py:348
  (4 shorter events, 0.1 us)
Async XLA Ops:
  2.6 12.8 %copy-start.1 = (f32[8,2,128]{2,1,0:T(2,128)S(1)}, f32[8,2,128]{2,1,0:T(2,128)}, u32[]{:S(2)}) copy-start(f32[8,2,128]{2,1,0:T(2,128)} %param.5) | copy-start | bytes 24580
  2.6 7.8 %collective-permute-start = (bf16[280,128]{1,0:T(8,128)(2,1)S(1)}, bf16[280,128]{1,0:T(8,128)(2,1)S(1)}, u32[]{:S(2)}, u32[]{:S(2)}) collective-permute-start(bf16[280,128]{1,0:T(8,128)(2,1)S(1)} %get-tuple-element.23), channel_id=1, source_target_pairs={{0,24},{8,16},{16,8},{24,0},{1,25},{9,17},{17,9},{25,1},{2,26},{10... | collective-permute-start | bytes 215048 | tf_op jit(solution)/shard_map/ppermute | solution.py:365
  7.8 8.2 %collective-permute-start.8 = (bf16[280,128]{1,0:T(8,128)(2,1)S(1)}, bf16[280,128]{1,0:T(8,128)(2,1)S(1)}, u32[]{:S(2)}, u32[]{:S(2)}) collective-permute-start(bf16[280,128]{1,0:T(8,128)(2,1)S(1)} %get-tuple-element.28), channel_id=1, source_target_pairs={{0,16},{8,24},{16,0},{24,8},{1,17},{9,25},{17,1},{25,9},{2,18},{10... | collective-permute-start | bytes 215048 | tf_op jit(solution)/shard_map/ppermute | solution.py:365
  7.8 8.2 %collective-permute-start.9 = (bf16[280,128]{1,0:T(8,128)(2,1)S(1)}, bf16[280,128]{1,0:T(8,128)(2,1)S(1)}, u32[]{:S(2)}, u32[]{:S(2)}) collective-permute-start(bf16[280,128]{1,0:T(8,128)(2,1)S(1)} %get-tuple-element.29), channel_id=1, source_target_pairs={{0,8},{8,0},{16,24},{24,16},{1,9},{9,1},{17,25},{25,17},{2,10},{10... | collective-permute-start | bytes 215048 | tf_op jit(solution)/shard_map/ppermute | solution.py:365
  9.0 20.7 %copy-start = (s32[8,8]{1,0:T(8,128)S(1)}, s32[8,8]{1,0:T(8,128)}, u32[]{:S(2)}) copy-start(s32[8,8]{1,0:T(8,128)} %map_ref.3) | copy-start | bytes 772
  10.5 8.6 %collective-permute-start.1 = (bf16[280,128]{1,0:T(8,128)(2,1)S(1)}, bf16[280,128]{1,0:T(8,128)(2,1)S(1)}, u32[]{:S(2)}, u32[]{:S(2)}) collective-permute-start(bf16[280,128]{1,0:T(8,128)(2,1)S(1)} %get-tuple-element.24), channel_id=1, source_target_pairs={{0,24},{8,16},{16,8},{24,0},{1,25},{9,17},{17,9},{25,1},{2,26},{10... | collective-permute-start | bytes 215048 | tf_op jit(solution)/shard_map/ppermute | solution.py:365
  14.7 5.8 %collective-permute-start.2 = (bf16[280,128]{1,0:T(8,128)(2,1)S(1)}, bf16[280,128]{1,0:T(8,128)(2,1)S(1)}, u32[]{:S(2)}, u32[]{:S(2)}) collective-permute-start(bf16[280,128]{1,0:T(8,128)(2,1)S(1)} %get-tuple-element.25), channel_id=1, source_target_pairs={{0,16},{8,24},{16,0},{24,8},{1,17},{9,25},{17,1},{25,9},{2,18},{10... | collective-permute-start | bytes 215048 | tf_op jit(solution)/shard_map/ppermute | solution.py:365
  15.0 5.6 %collective-permute-start.3 = (bf16[280,128]{1,0:T(8,128)(2,1)S(1)}, bf16[280,128]{1,0:T(8,128)(2,1)S(1)}, u32[]{:S(2)}, u32[]{:S(2)}) collective-permute-start(bf16[280,128]{1,0:T(8,128)(2,1)S(1)} %get-tuple-element.26), channel_id=1, source_target_pairs={{0,8},{8,0},{16,24},{24,16},{1,9},{9,1},{17,25},{25,17},{2,10},{10... | collective-permute-start | bytes 215048 | tf_op jit(solution)/shard_map/ppermute | solution.py:365
  16.4 7.7 %collective-permute-start.11 = (bf16[2,256,256]{2,1,0:T(8,128)(2,1)S(1)}, bf16[2,256,256]{2,1,0:T(8,128)(2,1)S(1)}, u32[]{:S(2)}, u32[]{:S(2)}) collective-permute-start(bf16[2,256,256]{2,1,0:T(8,128)(2,1)S(1)} %equalize.3.refs_0_), channel_id=1, source_target_pairs={{0,4},{4,0},{1,5},{5,1},{2,6},{6,2},{3,7},{7,3},{8,12},{12,8},{9,1... | collective-permute-start | bytes 786440 | tf_op jit(solution)/shard_map/ppermute | solution.py:425
  17.6 9.2 %collective-permute-start.10 = (bf16[2,256,256]{2,1,0:T(8,128)(2,1)S(1)}, bf16[2,256,256]{2,1,0:T(8,128)(2,1)S(1)}, u32[]{:S(2)}, u32[]{:S(2)}) collective-permute-start(bf16[2,256,256]{2,1,0:T(8,128)(2,1)S(1)} %equalize.3.refs_0_), channel_id=1, source_target_pairs={{0,2},{1,3},{2,0},{3,1},{4,6},{5,7},{6,4},{7,5},{8,10},{9,11},{10,... | collective-permute-start | bytes 786440 | tf_op jit(solution)/shard_map/ppermute | solution.py:424
  21.1 8.5 %collective-permute-start.4 = (bf16[2,256,256]{2,1,0:T(8,128)(2,1)S(1)}, bf16[2,256,256]{2,1,0:T(8,128)(2,1)S(1)}, u32[]{:S(2)}, u32[]{:S(2)}) collective-permute-start(bf16[2,256,256]{2,1,0:T(8,128)(2,1)S(1)} %equalize.2.refs_1_.refs_0_), channel_id=1, source_target_pairs={{0,2},{1,3},{2,0},{3,1},{4,6},{5,7},{6,4},{7,5},{8,10},{9,11},{10,... | collective-permute-start | bytes 786440 | tf_op jit(solution)/shard_map/ppermute | solution.py:424
  22.6 6.9 %collective-permute-start.5 = (bf16[2,256,256]{2,1,0:T(8,128)(2,1)S(1)}, bf16[2,256,256]{2,1,0:T(8,128)(2,1)S(1)}, u32[]{:S(2)}, u32[]{:S(2)}) collective-permute-start(bf16[2,256,256]{2,1,0:T(8,128)(2,1)S(1)} %equalize.2.refs_1_.refs_0_), channel_id=1, source_target_pairs={{0,4},{4,0},{1,5},{5,1},{2,6},{6,2},{3,7},{7,3},{8,12},{12,8},{9,1... | collective-permute-start | bytes 786440 | tf_op jit(solution)/shard_map/ppermute | solution.py:425
  24.1 5.5 %collective-permute-start.12 = (bf16[2,256,256]{2,1,0:T(8,128)(2,1)S(1)}, bf16[2,256,256]{2,1,0:T(8,128)(2,1)S(1)}, u32[]{:S(2)}, u32[]{:S(2)}) collective-permute-start(bf16[2,256,256]{2,1,0:T(8,128)(2,1)S(1)} %equalize.3.refs_0_), channel_id=1, source_target_pairs={{0,1},{1,0},{2,3},{3,2},{4,5},{5,4},{6,7},{7,6},{8,9},{9,8},{10,11... | collective-permute-start | bytes 786440 | tf_op jit(solution)/shard_map/ppermute | solution.py:427
  24.1 7.7 %collective-permute-start.6 = (bf16[2,256,256]{2,1,0:T(8,128)(2,1)S(1)}, bf16[2,256,256]{2,1,0:T(8,128)(2,1)S(1)}, u32[]{:S(2)}, u32[]{:S(2)}) collective-permute-start(bf16[2,256,256]{2,1,0:T(8,128)(2,1)S(1)} %equalize.2.refs_1_.refs_0_), channel_id=1, source_target_pairs={{0,1},{1,0},{2,3},{3,2},{4,5},{5,4},{6,7},{7,6},{8,9},{9,8},{10,11... | collective-permute-start | bytes 786440 | tf_op jit(solution)/shard_map/ppermute | solution.py:427
  26.8 2.9 %collective-permute-start.13 = (bf16[2,256,256]{2,1,0:T(8,128)(2,1)S(1)}, bf16[2,256,256]{2,1,0:T(8,128)(2,1)S(1)}, u32[]{:S(2)}, u32[]{:S(2)}) collective-permute-start(bf16[2,256,256]{2,1,0:T(8,128)(2,1)S(1)} %held_back.5.refs_1_), channel_id=1, source_target_pairs={{0,1},{1,0},{2,3},{3,2},{4,5},{5,4},{6,7},{7,6},{8,9},{9,8},{10,11... | collective-permute-start | bytes 786440 | tf_op jit(solution)/shard_map/ppermute | solution.py:432
  29.6 2.3 %collective-permute-start.7 = (bf16[2,256,256]{2,1,0:T(8,128)(2,1)S(1)}, bf16[2,256,256]{2,1,0:T(8,128)(2,1)S(1)}, u32[]{:S(2)}, u32[]{:S(2)}) collective-permute-start(bf16[2,256,256]{2,1,0:T(8,128)(2,1)S(1)} %held_back.4.refs_1_), channel_id=1, source_target_pairs={{0,1},{1,0},{2,3},{3,2},{4,5},{5,4},{6,7},{7,6},{8,9},{9,8},{10,11... | collective-permute-start | bytes 786440 | tf_op jit(solution)/shard_map/ppermute | solution.py:432

commit v7 on v6

--- a/solution.py
+++ b/solution.py
@@ -234,9 +234,11 @@
             both = [real * gain_real - imag * gain_imag, real * gain_imag + imag * gain_real]
             for q in range(2):
                 for tile in range(tiles):
-                    by_channel[(2 * r + q) * tiles + tile, pl.ds(s, h, stride=SIG), :] = both[q][
-                        :, tile * LANES : (tile + 1) * LANES
-                    ]
+                    for i in range(BATCH):
+                        where = pl.ds(i * SIG + s, h // BATCH, stride=BATCH * SIG)
+                        by_channel[(2 * r + q) * tiles + tile, where, :] = both[q][
+                            i * h // BATCH : (i + 1) * h // BATCH, tile * LANES : (tile + 1) * LANES
+                        ]
     for r in range(2):
         for tile in range(2 * tiles):
             out_ref[r, :, tile * LANES : (tile + 1) * LANES] = by_channel[r * 2 * tiles + tile].astype(jnp.bfloat16)
@@ -272,62 +274,88 @@
     return [row] + [lax.rem(row + n_row - d, n_row) for d in range(1, n_row)]
 
 
-def correlate_kernel(n_row, n_col, h, times, part, before, map_ref, *refs):
-    row_blocks = [ref for ref in refs[:n_col]]
+def regroup(v):
+    lane = lax.broadcasted_iota(jnp.int32, v[0].shape, 1)
+    v = list(v)
+    for bit in (2, 1):
+        width = bit * LANES // 8
+        low = (lane // width) % 2 == 0
+        for i in range(4):
+            if i & bit == 0:
+                a, b = v[i], v[i + bit]
+                v[i] = jnp.where(low, a, pltpu.roll(b, width, axis=1))
+                v[i + bit] = jnp.where(low, pltpu.roll(a, LANES - width, axis=1), b)
+    return v
+
+
+def correlate_kernel(n_row, n_col, h, times, part, dense, map_ref, *refs):
+    row_blocks = refs[:n_col]
     col_blocks = (refs[0],) + refs[n_col : n_col + n_row - 1]
     last = part == PARTS - 1
     if last:
-        out_hbm, product, out_ref, sems = refs[-4:]
-        earlier = refs[-5]
+        out_hbm, chosen, out_ref, sems = refs[-4:]
     else:
-        out_ref, product = refs[-2:]
-        earlier = refs[-3]
-    copies = []
+        out_ref, chosen = refs[-2:]
+    earlier = refs[n_col + n_row - 1]
     me_row, me_col = lax.axis_index("brow"), lax.axis_index("bcol")
     row_at, col_at = row_places(me_col, n_col), column_places(me_row, n_row)
     rows = BATCH * SIG
     tiles = n_col * rows // LANES
-
-    def batch(step, _):
-        parity = step // (h // BATCH)
-        inner = step % (h // BATCH)
-        here = pl.ds(pl.multiple_of(inner * rows, rows), rows)
+    steps = 2 * h // BATCH
+    index_in_batch = (lax.broadcasted_iota(jnp.int32, (SIG, LANES), 1) // SIG) % BATCH
+
+    for step in range(steps):
+        inner, parity = step // 2, step % 2
+        here = slice(inner * rows, (inner + 1) * rows)
         a = jnp.concatenate([block[parity, here, :] for block in row_blocks], axis=0)
         b = jnp.concatenate([block[parity, here, :] for block in col_blocks], axis=0)
         turned = jnp.concatenate([-b[:, times:], b[:, :times]], axis=1)
         both = jnp.concatenate([b, turned], axis=0)
         result = lax.dot_general(both, a, (((1,), (1,)), ((), ())), preferred_element_type=jnp.float32)
         for k in range(2 * n_row):
-            for i in range(BATCH):
-                channel = 2 * (inner * BATCH + i) + parity
-                for tile in range(tiles):
-                    product[k * tiles + tile, pl.ds(pl.multiple_of(channel * SIG, SIG), SIG), :] = result[
-                        k * rows + i * SIG : k * rows + (i + 1) * SIG, tile * LANES : (tile + 1) * LANES
-                    ]
-        return 0
-
-    lax.fori_loop(0, 2 * h // BATCH, batch, 0, unroll=4)
-    channels = 2 * h
-    lane = lax.broadcasted_iota(jnp.int32, (SIG, channels), 1)
-    inner_of = (lane // 2) % BATCH
+            for tile in range(tiles):
+                lanes = slice(tile * LANES, (tile + 1) * LANES)
+                own = [result[k * rows + i * SIG : k * rows + (i + 1) * SIG, lanes] for i in range(BATCH)]
+                kept = own[0]
+                for i in range(1, BATCH):
+                    kept = jnp.where(index_in_batch == i, own[i], kept)
+                chosen[k * tiles + tile, pl.ds(step, SIG, stride=steps), :] = kept
+
+    copies = []
+    low = lax.broadcasted_iota(jnp.int32, (SIG, LANES), 1) < LANES // 2
     for q in range(2):
         for e in range(n_row):
-            owned = [map_ref[me_row * n_col + row_at[d], col_at[e] * n_col + me_col] == 1 for d in range(n_col)]
-            for s2 in range(SIG):
-                b_at = col_at[e] * SIG + s2
-                for d in range(n_col):
-                    if d * rows % LANES == 0:
-                        tile = (q * n_row + e) * tiles + d * rows // LANES
-                        x = product[tile, pl.ds(s2, channels, stride=SIG), :].T
-                    start = d * rows % LANES
-                    kept = x[start : start + SIG]
-                    for i in range(1, BATCH):
-                        kept = jnp.where(inner_of == i, x[start + i * SIG : start + (i + 1) * SIG], kept)
-                    kept = jnp.where(owned[d], kept * (1.0 / times), 0.0)
-                    a_at = pl.ds(pl.multiple_of(row_at[d] * SIG, SIG), SIG)
-                    if before:
-                        kept = jnp.concatenate([earlier[q, b_at, a_at, :], kept], axis=1)
-                    out_ref[q, b_at, a_at, :] = kept
+            for d in range(n_col):
+                if d % (LANES // rows) == 0:
+                    x = chosen[(q * n_row + e) * tiles + d * rows // LANES].T
+                start = d * rows % LANES
+                v = [x[start + i * SIG : start + (i + 1) * SIG] for i in range(BATCH)]
+                if last:
+                    owned = map_ref[me_row * n_col + row_at[d], col_at[e] * n_col + me_col] == 1
+                    keep = jnp.where(owned, 1.0 / times, 0.0)
+                a_at = pl.ds(pl.multiple_of(row_at[d] * SIG, SIG), SIG)
+                mine = slice(d * SIG, (d + 1) * SIG)
+                if dense:
+                    for g, w in enumerate(regroup(v)):
+                        if last:
+                            before = earlier[q, e, g, mine, :]
+                            pair = [
+                                jnp.where(low, before, pltpu.roll(w, LANES // 2, axis=1)),
+                                jnp.where(low, pltpu.roll(before, LANES // 2, axis=1), w),
+                            ]
+                            for half in range(2):
+                                out_ref[q, col_at[e] * SIG + half * BATCH + g, a_at, :] = pair[half] * keep
+                        else:
+                            out_ref[q, e, g, mine, :] = w
+                else:
+                    for s2 in range(SIG):
+                        w = jnp.concatenate([each[:, s2 * steps : (s2 + 1) * steps] for each in v], axis=1)
+                        if part > 0:
+                            w = jnp.concatenate([earlier[q, e, s2, mine, :], w], axis=1)
+                        if last:
+                            out_ref[q, col_at[e] * SIG + s2, a_at, :] = w * keep
+                        else:
+                            out_ref[q, e, s2, mine, :] = w
             if last:
                 where = pl.ds(pl.multiple_of(col_at[e] * SIG, SIG), SIG)
                 copy = pltpu.make_async_copy(out_ref.at[q, where], out_hbm.at[q, where], sems.at[q * n_row + e])
@@ -340,18 +368,24 @@
 def correlate(tile_map, blocks, earlier, part, n_row, n_col):
     h = blocks[0].shape[1] // SIG
     times = blocks[0].shape[2] // 2
-    before = earlier.shape[3] if earlier is not None else 0
-    operands = list(blocks) + ([earlier] if before else [])
+    channels = 2 * h
+    dense = channels * 2 == LANES and PARTS == 2
+    operands = list(blocks) + ([earlier] if part else [])
     last = part == PARTS - 1
-    out_shape = (2, n_row * SIG, n_col * SIG, before + 2 * h)
+    if last:
+        out_shape = (2, n_row * SIG, n_col * SIG, (part + 1) * channels)
+    elif dense:
+        out_shape = (2, n_row, SIG // 2, n_col * SIG, LANES)
+    else:
+        out_shape = (2, n_row, SIG, n_col * SIG, (part + 1) * channels)
     in_last = [pltpu.VMEM(out_shape, jnp.float32), pltpu.SemaphoreType.DMA((2 * n_row,))]
+    kept = pltpu.VMEM((2 * n_row * n_col * BATCH * SIG // LANES, SIG * channels // BATCH, LANES), jnp.float32)
     return pl.pallas_call(
-        functools.partial(correlate_kernel, n_row, n_col, h, times, part, before),
+        functools.partial(correlate_kernel, n_row, n_col, h, times, part, dense),
         out_shape=jax.ShapeDtypeStruct(out_shape, jnp.float32),
         in_specs=[IN_SMEM] + [IN_VMEM] * len(operands),
         out_specs=IN_HBM if last else IN_VMEM,
-        scratch_shapes=[pltpu.VMEM((2 * n_row * n_col * BATCH * SIG // LANES, 2 * h * SIG, LANES), jnp.float32)]
-        + (in_last if last else []),
+        scratch_shapes=[kept] + (in_last if last else []),
         compiler_params=pltpu.CompilerParams(vmem_limit_bytes=VMEM_BYTES),
         cost_estimate=pl.CostEstimate(flops=0, bytes_accessed=1 << 10, transcendentals=0),
         name="correlate",

time: 35.1 us -> 33.8 us (0.963)
  Pallas kernels: 9.4 us -> 8.19 us
    pallas_call x2, Pallas kernels: 5.25 us -> 3.62 us  [correlate(): pl.pallas_call(functools.partial(correlate_kernel, n_row, n_col, h, times...]
    pallas_call x2, Pallas kernels: 0.9 us -> 1.32 us  [equalize(): pl.pallas_call(functools.partial(equalize_kernel, owners, frames, h, part...]
  transfers between devices with their start and end apart: 14 -> 14, of which waited for: 5 -> 6; matrix products, arithmetic and copies ran while one was open for 0% -> 0% of each run, Pallas kernels for 11% -> 10%
where the time goes in v7:
time: 33.8 us; the launch traced here: 33.6 us
  starting transfers between devices  17 us (50%)
  Pallas kernels  8.19 us (24%)
  waiting for transfers between devices  8.15 us (24%)
    ppermute x6, starting transfers between devices, to_owners(): lax.ppermute(pieces[d], 'chan', [(i, i ^ d) for i in range(owners)])  10.7 us
    ppermute x2, waiting for transfers between devices, shards(): lax.ppermute(own[part], 'bcol', across[d])  4.81 us
    pallas_call x2, Pallas kernels, correlate(): pl.pallas_call(functools.partial(correlate_kernel, n_row, n_col, h, times...  3.62 us
    ppermute x6, waiting for transfers between devices, to_owners(): lax.ppermute(pieces[d], 'chan', [(i, i ^ d) for i in range(owners)])  3.26 us
    ppermute x2, starting transfers between devices, shards(): lax.ppermute(own[part], 'bcol', across[d])  3.05 us
    ppermute x2, starting transfers between devices, shards(): lax.ppermute(own[part], 'brow', along[d])  2.65 us
    pallas_call x1, Pallas kernels, filtered_and_first(): pl.pallas_call(functools.partial(filter_kernel, frames, pieces, spectrum_...  2.62 us
    pallas_call x2, Pallas kernels, equalize(): pl.pallas_call(functools.partial(equalize_kernel, owners, frames, h, part...  1.32 us
  transfers between devices with their start and end apart: 14, of which 6 were waited for; matrix products, arithmetic and copies ran while one was open for 0% of the time, Pallas kernels for 10%

profile of v7, /device:TPU:0, one launch (start us, length us, event | category | flops | bytes accessed | tf_op | source)
XLA Modules:
  0.0 33.6 jit_solution(712469712455541151)
XLA Ops:
  0.0 2.6 %filter_and_transform.1 = (bf16[280,128]{1,0:T(8,128)(2,1)S(1)}, bf16[280,128]{1,0:T(8,128)(2,1)S(1)}, bf16[280,128]{1,0:T(8,128)(2,1)S(1)}, bf16[280,128]{1,0:T...) custom-call(s32[2,8,32768]{2,1,0:T(8,128)} %volt_hbm.1, ...), custom_call_target="tpu_custom_call" | custom-call | flops 536870912 | bytes 4194304 | tf_op jit(solution)/shard_map/filter_and_transform/pallas_call | solution.py:167
  2.6 0.0 copy-start.1
  2.6 5.1 %collective-permute-start = (bf16[280,128]{1,0:T(8,128)(2,1)S(1)}, bf16[280,128]{1,0:T(8,128)(2,1)S(1)}, u32[]{:S(2)}, u32[]{:S(2)}) collective-permute-start(bf16[280,128]{1,0:T(8,128)(2,1)S(1)} %get-tuple-element.23), channel_id=1, source_target_pairs={{0,24},{8,16},{16,8},{24,0},{1,25},{9,17},{17,9},{25,1},{2,26},{10... | collective-permute-start | bytes 215048 | tf_op jit(solution)/shard_map/ppermute | solution.py:399
  7.8 0.0 collective-permute-start.8
  7.8 0.6 %collective-permute-start.9 = (bf16[280,128]{1,0:T(8,128)(2,1)S(1)}, bf16[280,128]{1,0:T(8,128)(2,1)S(1)}, u32[]{:S(2)}, u32[]{:S(2)}) collective-permute-start(bf16[280,128]{1,0:T(8,128)(2,1)S(1)} %get-tuple-element.29), channel_id=1, source_target_pairs={{0,8},{8,0},{16,24},{24,16},{1,9},{9,1},{17,25},{25,17},{2,10},{10... | collective-permute-start | bytes 215048 | tf_op jit(solution)/shard_map/ppermute | solution.py:399
  8.4 0.6 %transform.1 = (bf16[280,128]{1,0:T(8,128)(2,1)S(1)}, bf16[280,128]{1,0:T(8,128)(2,1)S(1)}, bf16[280,128]{1,0:T(8,128)(2,1)S(1)}, bf16[280,128]{1,0:T(8,128)(2,1)S(1)}) custom-call(bf16[2,288,1024]{2,1,0:T(8,128)(2,1)S(1)} %get-tuple-element.18.filt, bf16[2048,256]{1,0:T(8,128)(2,1)S(1)} %get-tuple-element.19.later), custom_call_target="tpu_custom_call" | custom-call | flops 536870912 | bytes 2097152 | tf_op jit(solution)/shard_map/transform/pallas_call | solution.py:194
  9.0 0.0 copy-start
  9.0 1.5 %collective-permute-done.refs_3_.refs_0_ = bf16[280,128]{1,0:T(8,128)(2,1)S(1)} collective-permute-done((bf16[280,128]{1,0:T(8,128)(2,1)S(1)}, bf16[280,128]{1,0:T(8,128)(2,1)S(1)}, u32[]{:S(2)}, u32[]{:S(2)}) %collective-permute-start) | collective-permute-done | bytes 71712 | tf_op jit(solution)/shard_map/ppermute | solution.py:399
  10.5 4.3 %collective-permute-start.1 = (bf16[280,128]{1,0:T(8,128)(2,1)S(1)}, bf16[280,128]{1,0:T(8,128)(2,1)S(1)}, u32[]{:S(2)}, u32[]{:S(2)}) collective-permute-start(bf16[280,128]{1,0:T(8,128)(2,1)S(1)} %get-tuple-element.24), channel_id=1, source_target_pairs={{0,24},{8,16},{16,8},{24,0},{1,25},{9,17},{17,9},{25,1},{2,26},{10... | collective-permute-start | bytes 215048 | tf_op jit(solution)/shard_map/ppermute | solution.py:399
  14.7 0.3 collective-permute-start.2
  15.0 0.4 %collective-permute-start.3 = (bf16[280,128]{1,0:T(8,128)(2,1)S(1)}, bf16[280,128]{1,0:T(8,128)(2,1)S(1)}, u32[]{:S(2)}, u32[]{:S(2)}) collective-permute-start(bf16[280,128]{1,0:T(8,128)(2,1)S(1)} %get-tuple-element.26), channel_id=1, source_target_pairs={{0,8},{8,0},{16,24},{24,16},{1,9},{9,1},{17,25},{25,17},{2,10},{10... | collective-permute-start | bytes 215048 | tf_op jit(solution)/shard_map/ppermute | solution.py:399
  15.4 0.0 copy-done.1
  15.4 0.1 copy.6
  15.5 0.5 %collective-permute-done.8.refs_1_ = bf16[280,128]{1,0:T(8,128)(2,1)S(1)} collective-permute-done((bf16[280,128]{1,0:T(8,128)(2,1)S(1)}, bf16[280,128]{1,0:T(8,128)(2,1)S(1)}, u32[]{:S(2)}, u32[]{:S(2)}) %collective-permute-start.8) | collective-permute-done | bytes 71712 | tf_op jit(solution)/shard_map/ppermute | solution.py:399
  16.0 0.0 collective-permute-done.9.refs_2_
  16.0 0.7 %equalize.3.refs_0_ = bf16[2,256,256]{2,1,0:T(8,128)(2,1)S(1)} custom-call(bf16[280,128]{1,0:T(8,128)(2,1)S(1)} %collective-permute-done.refs_3_.refs_0_, bf16[280,128]{1,0:T(8,128)(2,1)S(1)} %collective-permute-done.8.refs_1_, bf16[280,128]{1,0:T(8,128)(2,1)S(1)} %collective-permute-done.9.refs_2_, bf16[280,128]{1,0:T(8,128)(2,1)S(1)} %get-tuple-element.30.refs_3_, ...), custom_call_target="tpu_custom_call" | custom-call | bytes 1024 | tf_op jit(solution)/shard_map/equalize/pallas_call | solution.py:251
  16.7 1.1 %collective-permute-start.11 = (bf16[2,256,256]{2,1,0:T(8,128)(2,1)S(1)}, bf16[2,256,256]{2,1,0:T(8,128)(2,1)S(1)}, u32[]{:S(2)}, u32[]{:S(2)}) collective-permute-start(bf16[2,256,256]{2,1,0:T(8,128)(2,1)S(1)} %equalize.3.refs_0_), channel_id=1, source_target_pairs={{0,4},{4,0},{1,5},{5,1},{2,6},{6,2},{3,7},{7,3},{8,12},{12,8},{9,1... | collective-permute-start | bytes 786440 | tf_op jit(solution)/shard_map/ppermute | solution.py:459
  17.8 1.5 %collective-permute-start.10 = (bf16[2,256,256]{2,1,0:T(8,128)(2,1)S(1)}, bf16[2,256,256]{2,1,0:T(8,128)(2,1)S(1)}, u32[]{:S(2)}, u32[]{:S(2)}) collective-permute-start(bf16[2,256,256]{2,1,0:T(8,128)(2,1)S(1)} %equalize.3.refs_0_), channel_id=1, source_target_pairs={{0,2},{1,3},{2,0},{3,1},{4,6},{5,7},{6,4},{7,5},{8,10},{9,11},{10,... | collective-permute-start | bytes 786440 | tf_op jit(solution)/shard_map/ppermute | solution.py:458
  19.3 0.0 collective-permute-done.1.refs_0_
  19.3 1.3 %collective-permute-done.2.refs_1_ = bf16[280,128]{1,0:T(8,128)(2,1)S(1)} collective-permute-done((bf16[280,128]{1,0:T(8,128)(2,1)S(1)}, bf16[280,128]{1,0:T(8,128)(2,1)S(1)}, u32[]{:S(2)}, u32[]{:S(2)}) %collective-permute-start.2) | collective-permute-done | bytes 71712 | tf_op jit(solution)/shard_map/ppermute | solution.py:399
  20.6 0.0 collective-permute-done.3.refs_2_
  20.6 0.7 %equalize.2.refs_1_.refs_0_ = bf16[2,256,256]{2,1,0:T(8,128)(2,1)S(1)} custom-call(bf16[280,128]{1,0:T(8,128)(2,1)S(1)} %collective-permute-done.1.refs_0_, bf16[280,128]{1,0:T(8,128)(2,1)S(1)} %collective-permute-done.2.refs_1_, bf16[280,128]{1,0:T(8,128)(2,1)S(1)} %collective-permute-done.3.refs_2_, bf16[280,128]{1,0:T(8,128)(2,1)S(1)} %get-tuple-element.27.refs_3_, ...), custom_call_target="tpu_custom_call" | custom-call | bytes 1024 | tf_op jit(solution)/shard_map/equalize/pallas_call | solution.py:251
  21.3 1.6 %collective-permute-start.4 = (bf16[2,256,256]{2,1,0:T(8,128)(2,1)S(1)}, bf16[2,256,256]{2,1,0:T(8,128)(2,1)S(1)}, u32[]{:S(2)}, u32[]{:S(2)}) collective-permute-start(bf16[2,256,256]{2,1,0:T(8,128)(2,1)S(1)} %equalize.2.refs_1_.refs_0_), channel_id=1, source_target_pairs={{0,2},{1,3},{2,0},{3,1},{4,6},{5,7},{6,4},{7,5},{8,10},{9,11},{10,... | collective-permute-start | bytes 786440 | tf_op jit(solution)/shard_map/ppermute | solution.py:458
  22.8 1.5 %collective-permute-start.5 = (bf16[2,256,256]{2,1,0:T(8,128)(2,1)S(1)}, bf16[2,256,256]{2,1,0:T(8,128)(2,1)S(1)}, u32[]{:S(2)}, u32[]{:S(2)}) collective-permute-start(bf16[2,256,256]{2,1,0:T(8,128)(2,1)S(1)} %equalize.2.refs_1_.refs_0_), channel_id=1, source_target_pairs={{0,4},{4,0},{1,5},{5,1},{2,6},{6,2},{3,7},{7,3},{8,12},{12,8},{9,1... | collective-permute-start | bytes 786440 | tf_op jit(solution)/shard_map/ppermute | solution.py:459
  24.3 0.0 collective-permute-start.12
  24.3 0.0 collective-permute-done.11.refs_2_.refs_4_
  24.3 0.5 %collective-permute-start.6 = (bf16[2,256,256]{2,1,0:T(8,128)(2,1)S(1)}, bf16[2,256,256]{2,1,0:T(8,128)(2,1)S(1)}, u32[]{:S(2)}, u32[]{:S(2)}) collective-permute-start(bf16[2,256,256]{2,1,0:T(8,128)(2,1)S(1)} %equalize.2.refs_1_.refs_0_), channel_id=1, source_target_pairs={{0,1},{1,0},{2,3},{3,2},{4,5},{5,4},{6,7},{7,6},{8,9},{9,8},{10,11... | collective-permute-start | bytes 786440 | tf_op jit(solution)/shard_map/ppermute | solution.py:461
  24.9 2.1 %collective-permute-done.10.refs_0_ = bf16[2,256,256]{2,1,0:T(8,128)(2,1)S(1)} collective-permute-done((bf16[2,256,256]{2,1,0:T(8,128)(2,1)S(1)}, bf16[2,256,256]{2,1,0:T(8,128)(2,1)S(1)}, u32[]{:S(2)}, u32[]{:S(2)}) %collective-permute-start.10) | collective-permute-done | bytes 262176 | tf_op jit(solution)/shard_map/ppermute | solution.py:458
  27.0 0.1 collective-permute-start.13
  27.1 2.7 %collective-permute-done.4.refs_0_ = bf16[2,256,256]{2,1,0:T(8,128)(2,1)S(1)} collective-permute-done((bf16[2,256,256]{2,1,0:T(8,128)(2,1)S(1)}, bf16[2,256,256]{2,1,0:T(8,128)(2,1)S(1)}, u32[]{:S(2)}, u32[]{:S(2)}) %collective-permute-start.4) | collective-permute-done | bytes 262176 | tf_op jit(solution)/shard_map/ppermute | solution.py:458
  29.8 0.0 collective-permute-done.5.refs_2_.refs_4_
  29.8 0.1 collective-permute-start.7
  29.9 0.0 collective-permute-done.12.refs_2_
  29.9 0.0 collective-permute-done.13.refs_3_
  29.9 0.0 copy-done
  29.9 1.4 %correlate.2.refs_5_ = f32[2,2,4,32,128]{4,3,2,1,0:T(8,128)S(1)} custom-call(s32[8,8]{1,0:T(8,128)S(1)} %copy-done, bf16[2,256,256]{2,1,0:T(8,128)(2,1)S(1)} %equalize.3.refs_0_, bf16[2,256,256]{2,1,0:T(8,128)(2,1)S(1)} %held_back.5.refs_1_, bf16[2,256,256]{2,1,0:T(8,128)(2,1)S(1)} %collective-permute-done.12.refs_2_, ...), custom_call_target="tpu_custom_call" | custom-call | bytes 1024 | tf_op jit(solution)/shard_map/correlate/pallas_call | solution.py:383
  31.3 0.0 collective-permute-done.6.refs_2_
  31.3 0.1 collective-permute-done.7.refs_3_
  31.4 2.2 %correlate.3 = f32[2,16,32,128]{3,2,1,0:T(8,128)} custom-call(s32[8,8]{1,0:T(8,128)S(1)} %copy-done, bf16[2,256,256]{2,1,0:T(8,128)(2,1)S(1)} %equalize.2.refs_1_.refs_0_, bf16[2,256,256]{2,1,0:T(8,128)(2,1)S(1)} %held_back.4.refs_1_, bf16[2,256,256]{2,1,0:T(8,128)(2,1)S(1)} %collective-permute-done.6.refs_2_, ...), custom_call_target="tpu_custom_call" | custom-call | bytes 1024 | tf_op jit(solution)/shard_map/correlate/pallas_call | solution.py:383
  (4 shorter events, 0.1 us)
Async XLA Ops:
  2.6 12.8 %copy-start.1 = (f32[8,2,128]{2,1,0:T(2,128)S(1)}, f32[8,2,128]{2,1,0:T(2,128)}, u32[]{:S(2)}) copy-start(f32[8,2,128]{2,1,0:T(2,128)} %param.5) | copy-start | bytes 24580
  2.6 7.8 %collective-permute-start = (bf16[280,128]{1,0:T(8,128)(2,1)S(1)}, bf16[280,128]{1,0:T(8,128)(2,1)S(1)}, u32[]{:S(2)}, u32[]{:S(2)}) collective-permute-start(bf16[280,128]{1,0:T(8,128)(2,1)S(1)} %get-tuple-element.23), channel_id=1, source_target_pairs={{0,24},{8,16},{16,8},{24,0},{1,25},{9,17},{17,9},{25,1},{2,26},{10... | collective-permute-start | bytes 215048 | tf_op jit(solution)/shard_map/ppermute | solution.py:399
  7.8 8.2 %collective-permute-start.8 = (bf16[280,128]{1,0:T(8,128)(2,1)S(1)}, bf16[280,128]{1,0:T(8,128)(2,1)S(1)}, u32[]{:S(2)}, u32[]{:S(2)}) collective-permute-start(bf16[280,128]{1,0:T(8,128)(2,1)S(1)} %get-tuple-element.28), channel_id=1, source_target_pairs={{0,16},{8,24},{16,0},{24,8},{1,17},{9,25},{17,1},{25,9},{2,18},{10... | collective-permute-start | bytes 215048 | tf_op jit(solution)/shard_map/ppermute | solution.py:399
  7.8 8.2 %collective-permute-start.9 = (bf16[280,128]{1,0:T(8,128)(2,1)S(1)}, bf16[280,128]{1,0:T(8,128)(2,1)S(1)}, u32[]{:S(2)}, u32[]{:S(2)}) collective-permute-start(bf16[280,128]{1,0:T(8,128)(2,1)S(1)} %get-tuple-element.29), channel_id=1, source_target_pairs={{0,8},{8,0},{16,24},{24,16},{1,9},{9,1},{17,25},{25,17},{2,10},{10... | collective-permute-start | bytes 215048 | tf_op jit(solution)/shard_map/ppermute | solution.py:399
  9.0 20.9 %copy-start = (s32[8,8]{1,0:T(8,128)S(1)}, s32[8,8]{1,0:T(8,128)}, u32[]{:S(2)}) copy-start(s32[8,8]{1,0:T(8,128)} %map_ref.3) | copy-start | bytes 772
  10.5 8.8 %collective-permute-start.1 = (bf16[280,128]{1,0:T(8,128)(2,1)S(1)}, bf16[280,128]{1,0:T(8,128)(2,1)S(1)}, u32[]{:S(2)}, u32[]{:S(2)}) collective-permute-start(bf16[280,128]{1,0:T(8,128)(2,1)S(1)} %get-tuple-element.24), channel_id=1, source_target_pairs={{0,24},{8,16},{16,8},{24,0},{1,25},{9,17},{17,9},{25,1},{2,26},{10... | collective-permute-start | bytes 215048 | tf_op jit(solution)/shard_map/ppermute | solution.py:399
  14.7 5.8 %collective-permute-start.2 = (bf16[280,128]{1,0:T(8,128)(2,1)S(1)}, bf16[280,128]{1,0:T(8,128)(2,1)S(1)}, u32[]{:S(2)}, u32[]{:S(2)}) collective-permute-start(bf16[280,128]{1,0:T(8,128)(2,1)S(1)} %get-tuple-element.25), channel_id=1, source_target_pairs={{0,16},{8,24},{16,0},{24,8},{1,17},{9,25},{17,1},{25,9},{2,18},{10... | collective-permute-start | bytes 215048 | tf_op jit(solution)/shard_map/ppermute | solution.py:399
  15.0 5.6 %collective-permute-start.3 = (bf16[280,128]{1,0:T(8,128)(2,1)S(1)}, bf16[280,128]{1,0:T(8,128)(2,1)S(1)}, u32[]{:S(2)}, u32[]{:S(2)}) collective-permute-start(bf16[280,128]{1,0:T(8,128)(2,1)S(1)} %get-tuple-element.26), channel_id=1, source_target_pairs={{0,8},{8,0},{16,24},{24,16},{1,9},{9,1},{17,25},{25,17},{2,10},{10... | collective-permute-start | bytes 215048 | tf_op jit(solution)/shard_map/ppermute | solution.py:399
  16.7 7.7 %collective-permute-start.11 = (bf16[2,256,256]{2,1,0:T(8,128)(2,1)S(1)}, bf16[2,256,256]{2,1,0:T(8,128)(2,1)S(1)}, u32[]{:S(2)}, u32[]{:S(2)}) collective-permute-start(bf16[2,256,256]{2,1,0:T(8,128)(2,1)S(1)} %equalize.3.refs_0_), channel_id=1, source_target_pairs={{0,4},{4,0},{1,5},{5,1},{2,6},{6,2},{3,7},{7,3},{8,12},{12,8},{9,1... | collective-permute-start | bytes 786440 | tf_op jit(solution)/shard_map/ppermute | solution.py:459
  17.8 9.2 %collective-permute-start.10 = (bf16[2,256,256]{2,1,0:T(8,128)(2,1)S(1)}, bf16[2,256,256]{2,1,0:T(8,128)(2,1)S(1)}, u32[]{:S(2)}, u32[]{:S(2)}) collective-permute-start(bf16[2,256,256]{2,1,0:T(8,128)(2,1)S(1)} %equalize.3.refs_0_), channel_id=1, source_target_pairs={{0,2},{1,3},{2,0},{3,1},{4,6},{5,7},{6,4},{7,5},{8,10},{9,11},{10,... | collective-permute-start | bytes 786440 | tf_op jit(solution)/shard_map/ppermute | solution.py:458
  21.3 8.5 %collective-permute-start.4 = (bf16[2,256,256]{2,1,0:T(8,128)(2,1)S(1)}, bf16[2,256,256]{2,1,0:T(8,128)(2,1)S(1)}, u32[]{:S(2)}, u32[]{:S(2)}) collective-permute-start(bf16[2,256,256]{2,1,0:T(8,128)(2,1)S(1)} %equalize.2.refs_1_.refs_0_), channel_id=1, source_target_pairs={{0,2},{1,3},{2,0},{3,1},{4,6},{5,7},{6,4},{7,5},{8,10},{9,11},{10,... | collective-permute-start | bytes 786440 | tf_op jit(solution)/shard_map/ppermute | solution.py:458
  22.8 6.9 %collective-permute-start.5 = (bf16[2,256,256]{2,1,0:T(8,128)(2,1)S(1)}, bf16[2,256,256]{2,1,0:T(8,128)(2,1)S(1)}, u32[]{:S(2)}, u32[]{:S(2)}) collective-permute-start(bf16[2,256,256]{2,1,0:T(8,128)(2,1)S(1)} %equalize.2.refs_1_.refs_0_), channel_id=1, source_target_pairs={{0,4},{4,0},{1,5},{5,1},{2,6},{6,2},{3,7},{7,3},{8,12},{12,8},{9,1... | collective-permute-start | bytes 786440 | tf_op jit(solution)/shard_map/ppermute | solution.py:459
  24.3 5.5 %collective-permute-start.12 = (bf16[2,256,256]{2,1,0:T(8,128)(2,1)S(1)}, bf16[2,256,256]{2,1,0:T(8,128)(2,1)S(1)}, u32[]{:S(2)}, u32[]{:S(2)}) collective-permute-start(bf16[2,256,256]{2,1,0:T(8,128)(2,1)S(1)} %equalize.3.refs_0_), channel_id=1, source_target_pairs={{0,1},{1,0},{2,3},{3,2},{4,5},{5,4},{6,7},{7,6},{8,9},{9,8},{10,11... | collective-permute-start | bytes 786440 | tf_op jit(solution)/shard_map/ppermute | solution.py:461
  24.3 7.0 %collective-permute-start.6 = (bf16[2,256,256]{2,1,0:T(8,128)(2,1)S(1)}, bf16[2,256,256]{2,1,0:T(8,128)(2,1)S(1)}, u32[]{:S(2)}, u32[]{:S(2)}) collective-permute-start(bf16[2,256,256]{2,1,0:T(8,128)(2,1)S(1)} %equalize.2.refs_1_.refs_0_), channel_id=1, source_target_pairs={{0,1},{1,0},{2,3},{3,2},{4,5},{5,4},{6,7},{7,6},{8,9},{9,8},{10,11... | collective-permute-start | bytes 786440 | tf_op jit(solution)/shard_map/ppermute | solution.py:461
  27.0 2.9 %collective-permute-start.13 = (bf16[2,256,256]{2,1,0:T(8,128)(2,1)S(1)}, bf16[2,256,256]{2,1,0:T(8,128)(2,1)S(1)}, u32[]{:S(2)}, u32[]{:S(2)}) collective-permute-start(bf16[2,256,256]{2,1,0:T(8,128)(2,1)S(1)} %held_back.5.refs_1_), channel_id=1, source_target_pairs={{0,1},{1,0},{2,3},{3,2},{4,5},{5,4},{6,7},{7,6},{8,9},{9,8},{10,11... | collective-permute-start | bytes 786440 | tf_op jit(solution)/shard_map/ppermute | solution.py:466
  29.8 1.6 %collective-permute-start.7 = (bf16[2,256,256]{2,1,0:T(8,128)(2,1)S(1)}, bf16[2,256,256]{2,1,0:T(8,128)(2,1)S(1)}, u32[]{:S(2)}, u32[]{:S(2)}) collective-permute-start(bf16[2,256,256]{2,1,0:T(8,128)(2,1)S(1)} %held_back.4.refs_1_), channel_id=1, source_target_pairs={{0,1},{1,0},{2,3},{3,2},{4,5},{5,4},{6,7},{7,6},{8,9},{9,8},{10,11... | collective-permute-start | bytes 786440 | tf_op jit(solution)/shard_map/ppermute | solution.py:466

commit v8 on v7

--- a/solution.py
+++ b/solution.py
@@ -37,14 +37,14 @@
 
 
 def dft_tables(owners):
-    n = np.arange(HALF, dtype=np.int64)[:, None, None, None, None]
-    k = FIRST + np.arange(CHANNELS, dtype=np.int64).reshape(owners, PARTS, -1, 2)
+    n = np.arange(HALF, dtype=np.int64).reshape(HALF, 1, 1, 1, 1, 1)
+    k = FIRST + np.arange(CHANNELS, dtype=np.int64).reshape(owners, PARTS, BATCH, -1, 2)
     angles = (n * k % NCHAN) * (2.0 * math.pi / NCHAN)
     cosine, sine = np.cos(angles), np.sin(angles)
     first = np.stack([cosine, -sine], axis=2)
     second = np.stack([sine, cosine], axis=2)
     tables = np.stack([first, second])
-    tables = np.transpose(tables, (4, 6, 0, 1, 2, 3, 5))
+    tables = np.transpose(tables, (4, 7, 0, 1, 2, 3, 6, 5))
     return tables.reshape(PARTS, 2 * NCHAN, -1).astype(np.float32).astype(ml_dtypes.bfloat16)
 
 
@@ -97,11 +97,9 @@
     coef_copy.start()
     for copy in copies:
         copy.start()
-    table_copy.start()
     later_copy = pltpu.make_async_copy(
         table_hbm.at[pl.ds(2 * NCHAN, (PARTS - 1) * 2 * NCHAN)], later, sems.at[pieces + 2]
     )
-    later_copy.start()
     tail = volt.shape[2] - (lead + frames) * NCHAN
     volt[:, :, : lead * NCHAN] = jnp.zeros((2, SIG, lead * NCHAN), jnp.int32)
     volt[:, :, (lead + frames) * NCHAN :] = jnp.zeros((2, SIG, tail), jnp.int32)
@@ -139,6 +137,10 @@
     groups = per // GROUP
     for piece in range(pieces):
         copies[piece].wait()
+        if piece == pieces // 4:
+            table_copy.start()
+        if piece == pieces // 2:
+            later_copy.start()
         lax.fori_loop(piece * groups, (piece + 1) * groups, filter_group, 0)
     lax.fori_loop(frames // GROUP, frames // GROUP + 1, filter_group, 0)
     table_copy.wait()
@@ -160,7 +162,7 @@
     frames = voltages.shape[2] // NCHAN
     rows = (frames + GROUP) * SIG
     sent = (frames + TAPS - 1) * SIG
-    pieces = 4
+    pieces = 8
     across = table.shape[1]
     terms = table.shape[0] - PARTS * 2 * NCHAN
     lanes = 2 * CHANNELS // owners // PARTS
@@ -225,7 +227,7 @@
             start = pl.multiple_of((source + 1) * own_rows, own_rows)
             by_time[pl.ds(start, over), :width] += pieces[d][own_rows:, :].astype(jnp.float32)
 
-    gains = [gains_ref[pl.ds(part * 2 * h + r, h, stride=2), :] for r in range(2)]
+    gains = [gains_ref[(2 * part + r) * h : (2 * part + r + 1) * h, :] for r in range(2)]
     for s in range(SIG):
         x = by_time[pl.ds(s, times, stride=SIG), :][:, :width].T
         for r in range(2):
@@ -234,11 +236,9 @@
             both = [real * gain_real - imag * gain_imag, real * gain_imag + imag * gain_real]
             for q in range(2):
                 for tile in range(tiles):
-                    for i in range(BATCH):
-                        where = pl.ds(i * SIG + s, h // BATCH, stride=BATCH * SIG)
-                        by_channel[(2 * r + q) * tiles + tile, where, :] = both[q][
-                            i * h // BATCH : (i + 1) * h // BATCH, tile * LANES : (tile + 1) * LANES
-                        ]
+                    by_channel[(2 * r + q) * tiles + tile, pl.ds(s, h, stride=SIG), :] = both[q][
+                        :, tile * LANES : (tile + 1) * LANES
+                    ]
     for r in range(2):
         for tile in range(2 * tiles):
             out_ref[r, :, tile * LANES : (tile + 1) * LANES] = by_channel[r * 2 * tiles + tile].astype(jnp.bfloat16)
@@ -357,7 +357,7 @@
                         else:
                             out_ref[q, e, s2, mine, :] = w
             if last:
-                where = pl.ds(pl.multiple_of(col_at[e] * SIG, SIG), SIG)
+                where = pl.ds(col_at[e] * SIG, SIG)
                 copy = pltpu.make_async_copy(out_ref.at[q, where], out_hbm.at[q, where], sems.at[q * n_row + e])
                 copy.start()
                 copies.append(copy)
@@ -439,7 +439,8 @@
     chips = n_col // 2
     frames = voltages.shape[2] // NCHAN
     table = jnp.asarray(constants(owners))
-    gains = jnp.transpose(antenna_gains, (2, 0, 1)).reshape(-1, 2 * SIG)
+    gains = antenna_gains.reshape(2 * SIG, PARTS, BATCH, -1, 2)
+    gains = jnp.transpose(gains, (1, 4, 3, 2, 0)).reshape(-1, 2 * SIG)
     pad = -gains.shape[1] % LANES
     gains = jnp.pad(gains, ((0, 0), (0, pad)))
     across = [[(i, (i // 2 + d) % chips * 2 + i % 2) for i in range(n_col)] for d in range(chips)]

time: 33.8 us -> 34.1 us (level)
  waiting for transfers between devices: 8.15 us -> 7.22 us
  local copies, waits for them, and re-layouts: 0.12 us -> 1.05 us
    ppermute x6, waiting for transfers between devices: 3.26 us -> 2.05 us  [to_owners(): lax.ppermute(pieces[d], 'chan', [(i, i ^ d) for i in range(owners)])]
    pallas_call x1, Pallas kernels: 2.62 us -> 3.16 us  [filtered_and_first(): pl.pallas_call(functools.partial(filter_kernel, frames, pieces, spectrum_...]
    transpose x0 -> x1, local copies, waits for them, and re-layouts: none -> 0.54 us  [shards(): gains = jnp.transpose(gains, (1, 4, 3, 2, 0)).reshape(-1, 2 * SIG)]
    ppermute x2, starting transfers between devices: 2.65 us -> 3.1 us  [shards(): lax.ppermute(own[part], 'brow', along[d])]
    pallas_call x2, Pallas kernels: 1.32 us -> 0.9 us  [equalize(): pl.pallas_call(functools.partial(equalize_kernel, owners, frames, h, part...]
    reshape x1, local copies, waits for them, and re-layouts: 0.1 us -> 0.49 us  [shards(): gains = antenna_gains.reshape(2 * SIG, PARTS, BATCH, -1, 2)]
  transfers between devices with their start and end apart: 14 -> 14, of which waited for: 6 -> 6; matrix products, arithmetic and copies ran while one was open for 0% -> 3% of each run, Pallas kernels for 10% -> 9%
where the time goes in v8:
time: 34.1 us; the launch traced here: 34 us
  starting transfers between devices  17.2 us (50%)
  Pallas kernels  8.3 us (24%)
  waiting for transfers between devices  7.22 us (21%)
  local copies, waits for them, and re-layouts  1.05 us (3%)
    ppermute x6, starting transfers between devices, to_owners(): lax.ppermute(pieces[d], 'chan', [(i, i ^ d) for i in range(owners)])  10.7 us
    ppermute x2, waiting for transfers between devices, shards(): lax.ppermute(own[part], 'bcol', across[d])  4.84 us
    pallas_call x2, Pallas kernels, correlate(): pl.pallas_call(functools.partial(correlate_kernel, n_row, n_col, h, times...  3.6 us
    pallas_call x1, Pallas kernels, filtered_and_first(): pl.pallas_call(functools.partial(filter_kernel, frames, pieces, spectrum_...  3.16 us
    ppermute x2, starting transfers between devices, shards(): lax.ppermute(own[part], 'brow', along[d])  3.1 us
    ppermute x2, starting transfers between devices, shards(): lax.ppermute(own[part], 'bcol', across[d])  3.05 us
    ppermute x6, waiting for transfers between devices, to_owners(): lax.ppermute(pieces[d], 'chan', [(i, i ^ d) for i in range(owners)])  2.05 us
    pallas_call x2, Pallas kernels, equalize(): pl.pallas_call(functools.partial(equalize_kernel, owners, frames, h, part...  0.9 us
  transfers between devices with their start and end apart: 14, of which 6 were waited for; matrix products, arithmetic and copies ran while one was open for 3% of the time, Pallas kernels for 9%

profile of v8, /device:TPU:0, one launch (start us, length us, event | category | flops | bytes accessed | tf_op | source)
XLA Modules:
  0.0 34.0 jit_solution(4694796073156797410)
XLA Ops:
  0.0 3.2 %filter_and_transform.1 = (bf16[280,128]{1,0:T(8,128)(2,1)S(1)}, bf16[280,128]{1,0:T(8,128)(2,1)S(1)}, bf16[280,128]{1,0:T(8,128)(2,1)S(1)}, bf16[280,128]{1,0:T...) custom-call(s32[2,8,32768]{2,1,0:T(8,128)} %volt_hbm.1, ...), custom_call_target="tpu_custom_call" | custom-call | flops 536870912 | bytes 4194304 | tf_op jit(solution)/shard_map/filter_and_transform/pallas_call | solution.py:169
  3.2 0.0 copy-start.1
  3.2 5.1 %collective-permute-start = (bf16[280,128]{1,0:T(8,128)(2,1)S(1)}, bf16[280,128]{1,0:T(8,128)(2,1)S(1)}, u32[]{:S(2)}, u32[]{:S(2)}) collective-permute-start(bf16[280,128]{1,0:T(8,128)(2,1)S(1)} %get-tuple-element.23), channel_id=1, source_target_pairs={{0,24},{8,16},{16,8},{24,0},{1,25},{9,17},{17,9},{25,1},{2,26},{10... | collective-permute-start | bytes 215048 | tf_op jit(solution)/shard_map/ppermute | solution.py:399
  8.3 0.0 collective-permute-start.8
  8.3 0.6 %collective-permute-start.9 = (bf16[280,128]{1,0:T(8,128)(2,1)S(1)}, bf16[280,128]{1,0:T(8,128)(2,1)S(1)}, u32[]{:S(2)}, u32[]{:S(2)}) collective-permute-start(bf16[280,128]{1,0:T(8,128)(2,1)S(1)} %get-tuple-element.29), channel_id=1, source_target_pairs={{0,8},{8,0},{16,24},{24,16},{1,9},{9,1},{17,25},{25,17},{2,10},{10... | collective-permute-start | bytes 215048 | tf_op jit(solution)/shard_map/ppermute | solution.py:399
  8.9 0.6 %transform.1 = (bf16[280,128]{1,0:T(8,128)(2,1)S(1)}, bf16[280,128]{1,0:T(8,128)(2,1)S(1)}, bf16[280,128]{1,0:T(8,128)(2,1)S(1)}, bf16[280,128]{1,0:T(8,128)(2,1)S(1)}) custom-call(bf16[2,288,1024]{2,1,0:T(8,128)(2,1)S(1)} %get-tuple-element.18.filt, bf16[2048,256]{1,0:T(8,128)(2,1)S(1)} %get-tuple-element.19.later), custom_call_target="tpu_custom_call" | custom-call | flops 536870912 | bytes 2097152 | tf_op jit(solution)/shard_map/transform/pallas_call | solution.py:196
  9.5 1.5 %collective-permute-done.refs_3_.refs_0_ = bf16[280,128]{1,0:T(8,128)(2,1)S(1)} collective-permute-done((bf16[280,128]{1,0:T(8,128)(2,1)S(1)}, bf16[280,128]{1,0:T(8,128)(2,1)S(1)}, u32[]{:S(2)}, u32[]{:S(2)}) %collective-permute-start) | collective-permute-done | bytes 71712 | tf_op jit(solution)/shard_map/ppermute | solution.py:399
  11.0 4.3 %collective-permute-start.1 = (bf16[280,128]{1,0:T(8,128)(2,1)S(1)}, bf16[280,128]{1,0:T(8,128)(2,1)S(1)}, u32[]{:S(2)}, u32[]{:S(2)}) collective-permute-start(bf16[280,128]{1,0:T(8,128)(2,1)S(1)} %get-tuple-element.24), channel_id=1, source_target_pairs={{0,24},{8,16},{16,8},{24,0},{1,25},{9,17},{17,9},{25,1},{2,26},{10... | collective-permute-start | bytes 215048 | tf_op jit(solution)/shard_map/ppermute | solution.py:399
  15.3 0.3 collective-permute-start.2
  15.6 0.4 %collective-permute-start.3 = (bf16[280,128]{1,0:T(8,128)(2,1)S(1)}, bf16[280,128]{1,0:T(8,128)(2,1)S(1)}, u32[]{:S(2)}, u32[]{:S(2)}) collective-permute-start(bf16[280,128]{1,0:T(8,128)(2,1)S(1)} %get-tuple-element.26), channel_id=1, source_target_pairs={{0,8},{8,0},{16,24},{24,16},{1,9},{9,1},{17,25},{25,17},{2,10},{10... | collective-permute-start | bytes 215048 | tf_op jit(solution)/shard_map/ppermute | solution.py:399
  15.9 0.0 copy-done.1
  15.9 0.5 %reshape.6 = f32[16,2,4,8,2]{4,3,2,1,0:T(8,128)S(1)} reshape(f32[8,2,128]{2,1,0:T(2,128)S(1)} %copy-done.1) | data formatting | bytes 16384 | tf_op jit(solution)/shard_map/reshape | solution.py:442
  16.4 0.0 copy-start
  16.4 0.5 %copy.6 = f32[2,2,8,4,16]{4,3,2,1,0:T(4,128)S(1)} copy(f32[2,2,8,4,16]{1,2,3,0,4:T(8,128)S(1)} %bitcast.5) | data formatting | bytes 16384 | tf_op jit(solution)/shard_map/transpose | solution.py:443
  17.0 0.0 collective-permute-done.8.refs_1_
  17.0 0.0 collective-permute-done.9.refs_2_
  17.0 0.5 %equalize.3.refs_0_ = bf16[2,256,256]{2,1,0:T(8,128)(2,1)S(1)} custom-call(bf16[280,128]{1,0:T(8,128)(2,1)S(1)} %collective-permute-done.refs_3_.refs_0_, bf16[280,128]{1,0:T(8,128)(2,1)S(1)} %collective-permute-done.8.refs_1_, bf16[280,128]{1,0:T(8,128)(2,1)S(1)} %collective-permute-done.9.refs_2_, bf16[280,128]{1,0:T(8,128)(2,1)S(1)} %get-tuple-element.30.refs_3_, ...), custom_call_target="tpu_custom_call" | custom-call | bytes 1024 | tf_op jit(solution)/shard_map/equalize/pallas_call | solution.py:251
  17.5 1.6 %collective-permute-start.11 = (bf16[2,256,256]{2,1,0:T(8,128)(2,1)S(1)}, bf16[2,256,256]{2,1,0:T(8,128)(2,1)S(1)}, u32[]{:S(2)}, u32[]{:S(2)}) collective-permute-start(bf16[2,256,256]{2,1,0:T(8,128)(2,1)S(1)} %equalize.3.refs_0_), channel_id=1, source_target_pairs={{0,4},{4,0},{1,5},{5,1},{2,6},{6,2},{3,7},{7,3},{8,12},{12,8},{9,1... | collective-permute-start | bytes 786440 | tf_op jit(solution)/shard_map/ppermute | solution.py:460
  19.1 1.5 %collective-permute-start.10 = (bf16[2,256,256]{2,1,0:T(8,128)(2,1)S(1)}, bf16[2,256,256]{2,1,0:T(8,128)(2,1)S(1)}, u32[]{:S(2)}, u32[]{:S(2)}) collective-permute-start(bf16[2,256,256]{2,1,0:T(8,128)(2,1)S(1)} %equalize.3.refs_0_), channel_id=1, source_target_pairs={{0,2},{1,3},{2,0},{3,1},{4,6},{5,7},{6,4},{7,5},{8,10},{9,11},{10,... | collective-permute-start | bytes 786440 | tf_op jit(solution)/shard_map/ppermute | solution.py:459
  20.6 0.0 collective-permute-done.1.refs_0_
  20.6 0.6 %collective-permute-done.2.refs_1_ = bf16[280,128]{1,0:T(8,128)(2,1)S(1)} collective-permute-done((bf16[280,128]{1,0:T(8,128)(2,1)S(1)}, bf16[280,128]{1,0:T(8,128)(2,1)S(1)}, u32[]{:S(2)}, u32[]{:S(2)}) %collective-permute-start.2) | collective-permute-done | bytes 71712 | tf_op jit(solution)/shard_map/ppermute | solution.py:399
  21.1 0.0 collective-permute-done.3.refs_2_
  21.1 0.4 %equalize.2.refs_1_.refs_0_ = bf16[2,256,256]{2,1,0:T(8,128)(2,1)S(1)} custom-call(bf16[280,128]{1,0:T(8,128)(2,1)S(1)} %collective-permute-done.1.refs_0_, bf16[280,128]{1,0:T(8,128)(2,1)S(1)} %collective-permute-done.2.refs_1_, bf16[280,128]{1,0:T(8,128)(2,1)S(1)} %collective-permute-done.3.refs_2_, bf16[280,128]{1,0:T(8,128)(2,1)S(1)} %get-tuple-element.27.refs_3_, ...), custom_call_target="tpu_custom_call" | custom-call | bytes 1024 | tf_op jit(solution)/shard_map/equalize/pallas_call | solution.py:251
  21.6 1.6 %collective-permute-start.4 = (bf16[2,256,256]{2,1,0:T(8,128)(2,1)S(1)}, bf16[2,256,256]{2,1,0:T(8,128)(2,1)S(1)}, u32[]{:S(2)}, u32[]{:S(2)}) collective-permute-start(bf16[2,256,256]{2,1,0:T(8,128)(2,1)S(1)} %equalize.2.refs_1_.refs_0_), channel_id=1, source_target_pairs={{0,2},{1,3},{2,0},{3,1},{4,6},{5,7},{6,4},{7,5},{8,10},{9,11},{10,... | collective-permute-start | bytes 786440 | tf_op jit(solution)/shard_map/ppermute | solution.py:459
  23.2 1.5 %collective-permute-start.5 = (bf16[2,256,256]{2,1,0:T(8,128)(2,1)S(1)}, bf16[2,256,256]{2,1,0:T(8,128)(2,1)S(1)}, u32[]{:S(2)}, u32[]{:S(2)}) collective-permute-start(bf16[2,256,256]{2,1,0:T(8,128)(2,1)S(1)} %equalize.2.refs_1_.refs_0_), channel_id=1, source_target_pairs={{0,4},{4,0},{1,5},{5,1},{2,6},{6,2},{3,7},{7,3},{8,12},{12,8},{9,1... | collective-permute-start | bytes 786440 | tf_op jit(solution)/shard_map/ppermute | solution.py:460
  24.7 0.0 collective-permute-start.12
  24.7 0.2 collective-permute-done.11.refs_2_.refs_4_
  24.9 0.3 collective-permute-start.6
  25.2 2.1 %collective-permute-done.10.refs_0_ = bf16[2,256,256]{2,1,0:T(8,128)(2,1)S(1)} collective-permute-done((bf16[2,256,256]{2,1,0:T(8,128)(2,1)S(1)}, bf16[2,256,256]{2,1,0:T(8,128)(2,1)S(1)}, u32[]{:S(2)}, u32[]{:S(2)}) %collective-permute-start.10) | collective-permute-done | bytes 262176 | tf_op jit(solution)/shard_map/ppermute | solution.py:459
  27.3 0.1 collective-permute-start.13
  27.4 2.7 %collective-permute-done.4.refs_0_ = bf16[2,256,256]{2,1,0:T(8,128)(2,1)S(1)} collective-permute-done((bf16[2,256,256]{2,1,0:T(8,128)(2,1)S(1)}, bf16[2,256,256]{2,1,0:T(8,128)(2,1)S(1)}, u32[]{:S(2)}, u32[]{:S(2)}) %collective-permute-start.4) | collective-permute-done | bytes 262176 | tf_op jit(solution)/shard_map/ppermute | solution.py:459
  30.1 0.0 collective-permute-done.5.refs_2_.refs_4_
  30.2 0.1 collective-permute-start.7
  30.2 0.0 collective-permute-done.12.refs_2_
  30.2 0.0 collective-permute-done.13.refs_3_
  30.3 0.0 copy-done
  30.3 1.4 %correlate.2.refs_5_ = f32[2,2,4,32,128]{4,3,2,1,0:T(8,128)S(1)} custom-call(s32[8,8]{1,0:T(8,128)S(1)} %copy-done, bf16[2,256,256]{2,1,0:T(8,128)(2,1)S(1)} %equalize.3.refs_0_, bf16[2,256,256]{2,1,0:T(8,128)(2,1)S(1)} %held_back.5.refs_1_, bf16[2,256,256]{2,1,0:T(8,128)(2,1)S(1)} %collective-permute-done.12.refs_2_, ...), custom_call_target="tpu_custom_call" | custom-call | bytes 1024 | tf_op jit(solution)/shard_map/correlate/pallas_call | solution.py:383
  31.7 0.0 collective-permute-done.6.refs_2_
  31.7 0.1 collective-permute-done.7.refs_3_
  31.8 2.2 %correlate.3 = f32[2,16,32,128]{3,2,1,0:T(8,128)} custom-call(s32[8,8]{1,0:T(8,128)S(1)} %copy-done, bf16[2,256,256]{2,1,0:T(8,128)(2,1)S(1)} %equalize.2.refs_1_.refs_0_, bf16[2,256,256]{2,1,0:T(8,128)(2,1)S(1)} %held_back.4.refs_1_, bf16[2,256,256]{2,1,0:T(8,128)(2,1)S(1)} %collective-permute-done.6.refs_2_, ...), custom_call_target="tpu_custom_call" | custom-call | bytes 1024 | tf_op jit(solution)/shard_map/correlate/pallas_call | solution.py:383
  (4 shorter events, 0.1 us)
Async XLA Ops:
  3.2 12.8 %copy-start.1 = (f32[8,2,128]{2,1,0:T(2,128)S(1)}, f32[8,2,128]{2,1,0:T(2,128)}, u32[]{:S(2)}) copy-start(f32[8,2,128]{2,1,0:T(2,128)} %param.5) | copy-start | bytes 24580
  3.2 7.8 %collective-permute-start = (bf16[280,128]{1,0:T(8,128)(2,1)S(1)}, bf16[280,128]{1,0:T(8,128)(2,1)S(1)}, u32[]{:S(2)}, u32[]{:S(2)}) collective-permute-start(bf16[280,128]{1,0:T(8,128)(2,1)S(1)} %get-tuple-element.23), channel_id=1, source_target_pairs={{0,24},{8,16},{16,8},{24,0},{1,25},{9,17},{17,9},{25,1},{2,26},{10... | collective-permute-start | bytes 215048 | tf_op jit(solution)/shard_map/ppermute | solution.py:399
  8.3 8.7 %collective-permute-start.8 = (bf16[280,128]{1,0:T(8,128)(2,1)S(1)}, bf16[280,128]{1,0:T(8,128)(2,1)S(1)}, u32[]{:S(2)}, u32[]{:S(2)}) collective-permute-start(bf16[280,128]{1,0:T(8,128)(2,1)S(1)} %get-tuple-element.28), channel_id=1, source_target_pairs={{0,16},{8,24},{16,0},{24,8},{1,17},{9,25},{17,1},{25,9},{2,18},{10... | collective-permute-start | bytes 215048 | tf_op jit(solution)/shard_map/ppermute | solution.py:399
  8.3 8.7 %collective-permute-start.9 = (bf16[280,128]{1,0:T(8,128)(2,1)S(1)}, bf16[280,128]{1,0:T(8,128)(2,1)S(1)}, u32[]{:S(2)}, u32[]{:S(2)}) collective-permute-start(bf16[280,128]{1,0:T(8,128)(2,1)S(1)} %get-tuple-element.29), channel_id=1, source_target_pairs={{0,8},{8,0},{16,24},{24,16},{1,9},{9,1},{17,25},{25,17},{2,10},{10... | collective-permute-start | bytes 215048 | tf_op jit(solution)/shard_map/ppermute | solution.py:399
  11.0 9.5 %collective-permute-start.1 = (bf16[280,128]{1,0:T(8,128)(2,1)S(1)}, bf16[280,128]{1,0:T(8,128)(2,1)S(1)}, u32[]{:S(2)}, u32[]{:S(2)}) collective-permute-start(bf16[280,128]{1,0:T(8,128)(2,1)S(1)} %get-tuple-element.24), channel_id=1, source_target_pairs={{0,24},{8,16},{16,8},{24,0},{1,25},{9,17},{17,9},{25,1},{2,26},{10... | collective-permute-start | bytes 215048 | tf_op jit(solution)/shard_map/ppermute | solution.py:399
  15.3 5.8 %collective-permute-start.2 = (bf16[280,128]{1,0:T(8,128)(2,1)S(1)}, bf16[280,128]{1,0:T(8,128)(2,1)S(1)}, u32[]{:S(2)}, u32[]{:S(2)}) collective-permute-start(bf16[280,128]{1,0:T(8,128)(2,1)S(1)} %get-tuple-element.25), channel_id=1, source_target_pairs={{0,16},{8,24},{16,0},{24,8},{1,17},{9,25},{17,1},{25,9},{2,18},{10... | collective-permute-start | bytes 215048 | tf_op jit(solution)/shard_map/ppermute | solution.py:399
  15.6 5.6 %collective-permute-start.3 = (bf16[280,128]{1,0:T(8,128)(2,1)S(1)}, bf16[280,128]{1,0:T(8,128)(2,1)S(1)}, u32[]{:S(2)}, u32[]{:S(2)}) collective-permute-start(bf16[280,128]{1,0:T(8,128)(2,1)S(1)} %get-tuple-element.26), channel_id=1, source_target_pairs={{0,8},{8,0},{16,24},{24,16},{1,9},{9,1},{17,25},{25,17},{2,10},{10... | collective-permute-start | bytes 215048 | tf_op jit(solution)/shard_map/ppermute | solution.py:399
  16.4 13.8 %copy-start = (s32[8,8]{1,0:T(8,128)S(1)}, s32[8,8]{1,0:T(8,128)}, u32[]{:S(2)}) copy-start(s32[8,8]{1,0:T(8,128)} %map_ref.3) | copy-start | bytes 772
  17.5 7.4 %collective-permute-start.11 = (bf16[2,256,256]{2,1,0:T(8,128)(2,1)S(1)}, bf16[2,256,256]{2,1,0:T(8,128)(2,1)S(1)}, u32[]{:S(2)}, u32[]{:S(2)}) collective-permute-start(bf16[2,256,256]{2,1,0:T(8,128)(2,1)S(1)} %equalize.3.refs_0_), channel_id=1, source_target_pairs={{0,4},{4,0},{1,5},{5,1},{2,6},{6,2},{3,7},{7,3},{8,12},{12,8},{9,1... | collective-permute-start | bytes 786440 | tf_op jit(solution)/shard_map/ppermute | solution.py:460
  19.1 8.2 %collective-permute-start.10 = (bf16[2,256,256]{2,1,0:T(8,128)(2,1)S(1)}, bf16[2,256,256]{2,1,0:T(8,128)(2,1)S(1)}, u32[]{:S(2)}, u32[]{:S(2)}) collective-permute-start(bf16[2,256,256]{2,1,0:T(8,128)(2,1)S(1)} %equalize.3.refs_0_), channel_id=1, source_target_pairs={{0,2},{1,3},{2,0},{3,1},{4,6},{5,7},{6,4},{7,5},{8,10},{9,11},{10,... | collective-permute-start | bytes 786440 | tf_op jit(solution)/shard_map/ppermute | solution.py:459
  21.6 8.5 %collective-permute-start.4 = (bf16[2,256,256]{2,1,0:T(8,128)(2,1)S(1)}, bf16[2,256,256]{2,1,0:T(8,128)(2,1)S(1)}, u32[]{:S(2)}, u32[]{:S(2)}) collective-permute-start(bf16[2,256,256]{2,1,0:T(8,128)(2,1)S(1)} %equalize.2.refs_1_.refs_0_), channel_id=1, source_target_pairs={{0,2},{1,3},{2,0},{3,1},{4,6},{5,7},{6,4},{7,5},{8,10},{9,11},{10,... | collective-permute-start | bytes 786440 | tf_op jit(solution)/shard_map/ppermute | solution.py:459
  23.2 7.0 %collective-permute-start.5 = (bf16[2,256,256]{2,1,0:T(8,128)(2,1)S(1)}, bf16[2,256,256]{2,1,0:T(8,128)(2,1)S(1)}, u32[]{:S(2)}, u32[]{:S(2)}) collective-permute-start(bf16[2,256,256]{2,1,0:T(8,128)(2,1)S(1)} %equalize.2.refs_1_.refs_0_), channel_id=1, source_target_pairs={{0,4},{4,0},{1,5},{5,1},{2,6},{6,2},{3,7},{7,3},{8,12},{12,8},{9,1... | collective-permute-start | bytes 786440 | tf_op jit(solution)/shard_map/ppermute | solution.py:460
  24.7 5.6 %collective-permute-start.12 = (bf16[2,256,256]{2,1,0:T(8,128)(2,1)S(1)}, bf16[2,256,256]{2,1,0:T(8,128)(2,1)S(1)}, u32[]{:S(2)}, u32[]{:S(2)}) collective-permute-start(bf16[2,256,256]{2,1,0:T(8,128)(2,1)S(1)} %equalize.3.refs_0_), channel_id=1, source_target_pairs={{0,1},{1,0},{2,3},{3,2},{4,5},{5,4},{6,7},{7,6},{8,9},{9,8},{10,11... | collective-permute-start | bytes 786440 | tf_op jit(solution)/shard_map/ppermute | solution.py:462
  24.9 6.8 %collective-permute-start.6 = (bf16[2,256,256]{2,1,0:T(8,128)(2,1)S(1)}, bf16[2,256,256]{2,1,0:T(8,128)(2,1)S(1)}, u32[]{:S(2)}, u32[]{:S(2)}) collective-permute-start(bf16[2,256,256]{2,1,0:T(8,128)(2,1)S(1)} %equalize.2.refs_1_.refs_0_), channel_id=1, source_target_pairs={{0,1},{1,0},{2,3},{3,2},{4,5},{5,4},{6,7},{7,6},{8,9},{9,8},{10,11... | collective-permute-start | bytes 786440 | tf_op jit(solution)/shard_map/ppermute | solution.py:462
  27.3 2.9 %collective-permute-start.13 = (bf16[2,256,256]{2,1,0:T(8,128)(2,1)S(1)}, bf16[2,256,256]{2,1,0:T(8,128)(2,1)S(1)}, u32[]{:S(2)}, u32[]{:S(2)}) collective-permute-start(bf16[2,256,256]{2,1,0:T(8,128)(2,1)S(1)} %held_back.5.refs_1_), channel_id=1, source_target_pairs={{0,1},{1,0},{2,3},{3,2},{4,5},{5,4},{6,7},{7,6},{8,9},{9,8},{10,11... | collective-permute-start | bytes 786440 | tf_op jit(solution)/shard_map/ppermute | solution.py:467
  30.2 1.6 %collective-permute-start.7 = (bf16[2,256,256]{2,1,0:T(8,128)(2,1)S(1)}, bf16[2,256,256]{2,1,0:T(8,128)(2,1)S(1)}, u32[]{:S(2)}, u32[]{:S(2)}) collective-permute-start(bf16[2,256,256]{2,1,0:T(8,128)(2,1)S(1)} %held_back.4.refs_1_), channel_id=1, source_target_pairs={{0,1},{1,0},{2,3},{3,2},{4,5},{5,4},{6,7},{7,6},{8,9},{9,8},{10,11... | collective-permute-start | bytes 786440 | tf_op jit(solution)/shard_map/ppermute | solution.py:467

commit v9 on v8

--- a/solution.py
+++ b/solution.py
@@ -100,6 +100,8 @@
     later_copy = pltpu.make_async_copy(
         table_hbm.at[pl.ds(2 * NCHAN, (PARTS - 1) * 2 * NCHAN)], later, sems.at[pieces + 2]
     )
+    table_copy.start()
+    later_copy.start()
     tail = volt.shape[2] - (lead + frames) * NCHAN
     volt[:, :, : lead * NCHAN] = jnp.zeros((2, SIG, lead * NCHAN), jnp.int32)
     volt[:, :, (lead + frames) * NCHAN :] = jnp.zeros((2, SIG, tail), jnp.int32)
@@ -137,10 +139,6 @@
     groups = per // GROUP
     for piece in range(pieces):
         copies[piece].wait()
-        if piece == pieces // 4:
-            table_copy.start()
-        if piece == pieces // 2:
-            later_copy.start()
         lax.fori_loop(piece * groups, (piece + 1) * groups, filter_group, 0)
     lax.fori_loop(frames // GROUP, frames // GROUP + 1, filter_group, 0)
     table_copy.wait()
@@ -148,9 +146,21 @@
     later_copy.wait()
 
 
-def transform_kernel(part, scale, filt, later, *refs):
+def transform_kernel(part, scale, filt, later, gains_ref, pick_ref, *refs):
     table = later.at[pl.ds((part - 1) * 2 * NCHAN, 2 * NCHAN)]
-    transform(filt, table, scale, refs[-1], refs[:-1])
+    if part == 1:
+        columns, stage = refs[-2:]
+        gains = jnp.concatenate([gains_ref[:, 0, :], gains_ref[:, 1, :]], axis=0)
+        columns[...] = lax.dot_general(
+            pick_ref[...],
+            gains,
+            (((1,), (1,)), ((), ())),
+            precision=lax.Precision.HIGHEST,
+            preferred_element_type=jnp.float32,
+        )
+        transform(filt, table, scale, stage, refs[:-2])
+    else:
+        transform(filt, table, scale, refs[-1], refs[:-1])
 
 
 IN_VMEM = pl.BlockSpec(memory_space=pltpu.VMEM)
@@ -162,7 +172,7 @@
     frames = voltages.shape[2] // NCHAN
     rows = (frames + GROUP) * SIG
     sent = (frames + TAPS - 1) * SIG
-    pieces = 8
+    pieces = 4
     across = table.shape[1]
     terms = table.shape[0] - PARTS * 2 * NCHAN
     lanes = 2 * CHANNELS // owners // PARTS
@@ -190,19 +200,28 @@
     return filt, later, first
 
 
-def next_part(part, filt, later, owners):
+def pick_rows(channels):
+    order = np.arange(channels).reshape(PARTS, BATCH, -1, 2)
+    return np.eye(channels, dtype=np.float32)[np.transpose(order, (0, 3, 2, 1)).reshape(-1)]
+
+
+def next_part(part, filt, later, gains, owners):
     rows = filt.shape[1] - (GROUP - TAPS + 1) * SIG
     lanes = 2 * CHANNELS // owners // PARTS
+    channels = gains.shape[2]
+    shapes = [jax.ShapeDtypeStruct((rows, lanes), jnp.bfloat16)] * owners
+    if part == 1:
+        shapes.append(jax.ShapeDtypeStruct((channels, 2 * SIG), jnp.float32))
     return pl.pallas_call(
         functools.partial(transform_kernel, part, spectrum_scale()),
-        out_shape=[jax.ShapeDtypeStruct((rows, lanes), jnp.bfloat16)] * owners,
-        in_specs=[IN_VMEM, IN_VMEM],
-        out_specs=[IN_VMEM] * owners,
+        out_shape=shapes,
+        in_specs=[IN_VMEM] * 4,
+        out_specs=[IN_VMEM] * len(shapes),
         scratch_shapes=[pltpu.VMEM((owners, rows, lanes), jnp.bfloat16)],
         compiler_params=pltpu.CompilerParams(vmem_limit_bytes=VMEM_BYTES),
         cost_estimate=pl.CostEstimate(flops=1 << 29, bytes_accessed=2 << 20, transcendentals=0),
         name="transform",
-    )(filt, later)
+    )(filt, later, gains, jnp.asarray(pick_rows(channels)))
 
 
 def equalize_kernel(owners, frames, h, part, *refs):
@@ -232,7 +251,7 @@
         x = by_time[pl.ds(s, times, stride=SIG), :][:, :width].T
         for r in range(2):
             real, imag = x[2 * r * h : (2 * r + 1) * h], x[(2 * r + 1) * h : (2 * r + 2) * h]
-            gain_real, gain_imag = gains[r][:, 2 * s : 2 * s + 1], gains[r][:, 2 * s + 1 : 2 * s + 2]
+            gain_real, gain_imag = gains[r][:, s : s + 1], gains[r][:, SIG + s : SIG + s + 1]
             both = [real * gain_real - imag * gain_imag, real * gain_imag + imag * gain_real]
             for q in range(2):
                 for tile in range(tiles):
@@ -439,10 +458,6 @@
     chips = n_col // 2
     frames = voltages.shape[2] // NCHAN
     table = jnp.asarray(constants(owners))
-    gains = antenna_gains.reshape(2 * SIG, PARTS, BATCH, -1, 2)
-    gains = jnp.transpose(gains, (1, 4, 3, 2, 0)).reshape(-1, 2 * SIG)
-    pad = -gains.shape[1] % LANES
-    gains = jnp.pad(gains, ((0, 0), (0, pad)))
     across = [[(i, (i // 2 + d) % chips * 2 + i % 2) for i in range(n_col)] for d in range(chips)]
     along = [[(i, (i + d) % n_row) for i in range(n_row)] for d in range(n_row)]
     other_core = [(i, i ^ 1) for i in range(n_col)]
@@ -453,7 +468,9 @@
     for part in range(PARTS):
         later = None
         if part < PARTS - 1:
-            pieces = next_part(part + 1, filt, tables, owners)
+            pieces = next_part(part + 1, filt, tables, antenna_gains, owners)
+            if part == 0:
+                *pieces, gains = pieces
             later = to_owners([pieces[0], *held_back(pieces[1:], arrived[-1:])])
         own.append(equalize(arrived, gains, part, frames))
         far.append([lax.ppermute(own[part], "bcol", across[d]) for d in range(1, chips)])

time: 34.1 us -> 33.4 us (0.979)
  waiting for transfers between devices: 7.22 us -> 8.97 us
  local copies, waits for them, and re-layouts: 1.05 us -> 0.01 us
  starting transfers between devices: 17.2 us -> 16.4 us
  Pallas kernels: 8.3 us -> 7.81 us
    ppermute x2, waiting for transfers between devices: 0.22 us -> 3.71 us  [shards(): lax.ppermute(own[part], 'brow', along[d])]
    ppermute x2, waiting for transfers between devices: 4.84 us -> 1.49 us  [shards(): lax.ppermute(own[part], 'bcol', across[d])]
    ppermute x6, waiting for transfers between devices: 2.05 us -> 3.68 us  [to_owners(): lax.ppermute(pieces[d], 'chan', [(i, i ^ d) for i in range(owners)])]
    transpose x1 -> x0, local copies, waits for them, and re-layouts: 0.54 us -> none  [shards(): gains = jnp.transpose(gains, (1, 4, 3, 2, 0)).reshape(-1, 2 * SIG)]
    ppermute x2, starting transfers between devices: 3.1 us -> 2.58 us  [shards(): lax.ppermute(own[part], 'brow', along[d])]
    pallas_call x1, Pallas kernels: 3.16 us -> 2.65 us  [filtered_and_first(): pl.pallas_call(functools.partial(filter_kernel, frames, pieces, spectrum_...]
    reshape x1 -> x0, local copies, waits for them, and re-layouts: 0.49 us -> none  [shards(): gains = antenna_gains.reshape(2 * SIG, PARTS, BATCH, -1, 2)]
  transfers between devices with their start and end apart: 14 -> 14, of which waited for: 6 -> 8; matrix products, arithmetic and copies ran while one was open for 3% -> 0% of each run, Pallas kernels for 9% -> 9%
where the time goes in v9:
time: 33.4 us; the launch traced here: 33.3 us
  starting transfers between devices  16.4 us (49%)
  waiting for transfers between devices  8.97 us (27%)
  Pallas kernels  7.81 us (23%)
    ppermute x6, starting transfers between devices, to_owners(): lax.ppermute(pieces[d], 'chan', [(i, i ^ d) for i in range(owners)])  10.7 us
    ppermute x2, waiting for transfers between devices, shards(): lax.ppermute(own[part], 'brow', along[d])  3.71 us
    ppermute x6, waiting for transfers between devices, to_owners(): lax.ppermute(pieces[d], 'chan', [(i, i ^ d) for i in range(owners)])  3.68 us
    pallas_call x2, Pallas kernels, correlate(): pl.pallas_call(functools.partial(correlate_kernel, n_row, n_col, h, times...  3.6 us
    ppermute x2, starting transfers between devices, shards(): lax.ppermute(own[part], 'bcol', across[d])  2.98 us
    pallas_call x1, Pallas kernels, filtered_and_first(): pl.pallas_call(functools.partial(filter_kernel, frames, pieces, spectrum_...  2.65 us
    ppermute x2, starting transfers between devices, shards(): lax.ppermute(own[part], 'brow', along[d])  2.58 us
    ppermute x2, waiting for transfers between devices, shards(): lax.ppermute(own[part], 'bcol', across[d])  1.49 us
  transfers between devices with their start and end apart: 14, of which 8 were waited for; matrix products, arithmetic and copies ran while one was open for 0% of the time, Pallas kernels for 9%

profile of v9, /device:TPU:0, one launch (start us, length us, event | category | flops | bytes accessed | tf_op | source)
XLA Modules:
  0.0 33.3 jit_solution(1393086111407963863)
XLA Ops:
  0.0 0.0 copy-start
  0.0 0.0 copy-start.2
  0.0 2.6 %filter_and_transform.1 = (bf16[280,128]{1,0:T(8,128)(2,1)S(1)}, bf16[280,128]{1,0:T(8,128)(2,1)S(1)}, bf16[280,128]{1,0:T(8,128)(2,1)S(1)}, bf16[280,128]{1,0:T...) custom-call(s32[2,8,32768]{2,1,0:T(8,128)} %volt_hbm.1, ...), custom_call_target="tpu_custom_call" | custom-call | flops 536870912 | bytes 4194304 | tf_op jit(solution)/shard_map/filter_and_transform/pallas_call | solution.py:179
  2.7 5.1 %collective-permute-start = (bf16[280,128]{1,0:T(8,128)(2,1)S(1)}, bf16[280,128]{1,0:T(8,128)(2,1)S(1)}, u32[]{:S(2)}, u32[]{:S(2)}) collective-permute-start(bf16[280,128]{1,0:T(8,128)(2,1)S(1)} %get-tuple-element.24), channel_id=1, source_target_pairs={{0,24},{8,16},{16,8},{24,0},{1,25},{9,17},{17,9},{25,1},{2,26},{10... | collective-permute-start | bytes 215048 | tf_op jit(solution)/shard_map/ppermute | solution.py:418
  7.8 0.0 collective-permute-start.8
  7.8 0.6 %collective-permute-start.9 = (bf16[280,128]{1,0:T(8,128)(2,1)S(1)}, bf16[280,128]{1,0:T(8,128)(2,1)S(1)}, u32[]{:S(2)}, u32[]{:S(2)}) collective-permute-start(bf16[280,128]{1,0:T(8,128)(2,1)S(1)} %get-tuple-element.31), channel_id=1, source_target_pairs={{0,8},{8,0},{16,24},{24,16},{1,9},{9,1},{17,25},{25,17},{2,10},{10... | collective-permute-start | bytes 215048 | tf_op jit(solution)/shard_map/ppermute | solution.py:418
  8.4 0.0 copy-done
  8.4 0.0 copy-done.2
  8.4 0.6 %transform.1 = (bf16[280,128]{1,0:T(8,128)(2,1)S(1)}, bf16[280,128]{1,0:T(8,128)(2,1)S(1)}, bf16[280,128]{1,0:T(8,128)(2,1)S(1)}, bf16[280,128]{1,0:T(8,128)(2,1)S(1)}, f32[128,16]{1,0:T(8,128)S(1)}) custom-call(bf16[2,288,1024]{2,1,0:T(8,128)(2,1)S(1)} %get-tuple-element.19.filt, bf16[2048,256]{1,0:T(8,128)(2,1)S(1)} %get-tuple-element.20.later, ...), custom_call_target="tpu_custom_call" | custom-call | flops 536870912 | bytes 2097152 | tf_op jit(solution)/shard_map/transform/pallas_call | solution.py:215
  9.1 0.0 copy-start.1
  9.1 1.4 %collective-permute-done.refs_3_.refs_0_ = bf16[280,128]{1,0:T(8,128)(2,1)S(1)} collective-permute-done((bf16[280,128]{1,0:T(8,128)(2,1)S(1)}, bf16[280,128]{1,0:T(8,128)(2,1)S(1)}, u32[]{:S(2)}, u32[]{:S(2)}) %collective-permute-start) | collective-permute-done | bytes 71712 | tf_op jit(solution)/shard_map/ppermute | solution.py:418
  10.5 4.3 %collective-permute-start.1 = (bf16[280,128]{1,0:T(8,128)(2,1)S(1)}, bf16[280,128]{1,0:T(8,128)(2,1)S(1)}, u32[]{:S(2)}, u32[]{:S(2)}) collective-permute-start(bf16[280,128]{1,0:T(8,128)(2,1)S(1)} %get-tuple-element.25), channel_id=1, source_target_pairs={{0,24},{8,16},{16,8},{24,0},{1,25},{9,17},{17,9},{25,1},{2,26},{10... | collective-permute-start | bytes 215048 | tf_op jit(solution)/shard_map/ppermute | solution.py:418
  14.8 0.3 collective-permute-start.2
  15.0 0.4 %collective-permute-start.3 = (bf16[280,128]{1,0:T(8,128)(2,1)S(1)}, bf16[280,128]{1,0:T(8,128)(2,1)S(1)}, u32[]{:S(2)}, u32[]{:S(2)}) collective-permute-start(bf16[280,128]{1,0:T(8,128)(2,1)S(1)} %get-tuple-element.27), channel_id=1, source_target_pairs={{0,8},{8,0},{16,24},{24,16},{1,9},{9,1},{17,25},{25,17},{2,10},{10... | collective-permute-start | bytes 215048 | tf_op jit(solution)/shard_map/ppermute | solution.py:418
  15.4 0.6 %collective-permute-done.8.refs_1_ = bf16[280,128]{1,0:T(8,128)(2,1)S(1)} collective-permute-done((bf16[280,128]{1,0:T(8,128)(2,1)S(1)}, bf16[280,128]{1,0:T(8,128)(2,1)S(1)}, u32[]{:S(2)}, u32[]{:S(2)}) %collective-permute-start.8) | collective-permute-done | bytes 71712 | tf_op jit(solution)/shard_map/ppermute | solution.py:418
  16.0 0.0 collective-permute-done.9.refs_2_
  16.0 0.4 %equalize.3.refs_0_ = bf16[2,256,256]{2,1,0:T(8,128)(2,1)S(1)} custom-call(bf16[280,128]{1,0:T(8,128)(2,1)S(1)} %collective-permute-done.refs_3_.refs_0_, bf16[280,128]{1,0:T(8,128)(2,1)S(1)} %collective-permute-done.8.refs_1_, bf16[280,128]{1,0:T(8,128)(2,1)S(1)} %collective-permute-done.9.refs_2_, bf16[280,128]{1,0:T(8,128)(2,1)S(1)} %get-tuple-element.32.refs_3_, ...), custom_call_target="tpu_custom_call" | custom-call | bytes 1024 | tf_op jit(solution)/shard_map/equalize/pallas_call | solution.py:270
  16.5 1.0 %collective-permute-start.11 = (bf16[2,256,256]{2,1,0:T(8,128)(2,1)S(1)}, bf16[2,256,256]{2,1,0:T(8,128)(2,1)S(1)}, u32[]{:S(2)}, u32[]{:S(2)}) collective-permute-start(bf16[2,256,256]{2,1,0:T(8,128)(2,1)S(1)} %equalize.3.refs_0_), channel_id=1, source_target_pairs={{0,4},{4,0},{1,5},{5,1},{2,6},{6,2},{3,7},{7,3},{8,12},{12,8},{9,1... | collective-permute-start | bytes 786440 | tf_op jit(solution)/shard_map/ppermute | solution.py:477
  17.5 1.5 %collective-permute-start.10 = (bf16[2,256,256]{2,1,0:T(8,128)(2,1)S(1)}, bf16[2,256,256]{2,1,0:T(8,128)(2,1)S(1)}, u32[]{:S(2)}, u32[]{:S(2)}) collective-permute-start(bf16[2,256,256]{2,1,0:T(8,128)(2,1)S(1)} %equalize.3.refs_0_), channel_id=1, source_target_pairs={{0,2},{1,3},{2,0},{3,1},{4,6},{5,7},{6,4},{7,5},{8,10},{9,11},{10,... | collective-permute-start | bytes 786440 | tf_op jit(solution)/shard_map/ppermute | solution.py:476
  19.0 0.0 collective-permute-done.1.refs_0_
  19.0 1.7 %collective-permute-done.2.refs_1_ = bf16[280,128]{1,0:T(8,128)(2,1)S(1)} collective-permute-done((bf16[280,128]{1,0:T(8,128)(2,1)S(1)}, bf16[280,128]{1,0:T(8,128)(2,1)S(1)}, u32[]{:S(2)}, u32[]{:S(2)}) %collective-permute-start.2) | collective-permute-done | bytes 71712 | tf_op jit(solution)/shard_map/ppermute | solution.py:418
  20.6 0.0 collective-permute-done.3.refs_2_
  20.6 0.4 %equalize.2.refs_1_.refs_0_ = bf16[2,256,256]{2,1,0:T(8,128)(2,1)S(1)} custom-call(bf16[280,128]{1,0:T(8,128)(2,1)S(1)} %collective-permute-done.1.refs_0_, bf16[280,128]{1,0:T(8,128)(2,1)S(1)} %collective-permute-done.2.refs_1_, bf16[280,128]{1,0:T(8,128)(2,1)S(1)} %collective-permute-done.3.refs_2_, bf16[280,128]{1,0:T(8,128)(2,1)S(1)} %get-tuple-element.28.refs_3_, ...), custom_call_target="tpu_custom_call" | custom-call | bytes 1024 | tf_op jit(solution)/shard_map/equalize/pallas_call | solution.py:270
  21.1 1.6 %collective-permute-start.5 = (bf16[2,256,256]{2,1,0:T(8,128)(2,1)S(1)}, bf16[2,256,256]{2,1,0:T(8,128)(2,1)S(1)}, u32[]{:S(2)}, u32[]{:S(2)}) collective-permute-start(bf16[2,256,256]{2,1,0:T(8,128)(2,1)S(1)} %equalize.2.refs_1_.refs_0_), channel_id=1, source_target_pairs={{0,4},{4,0},{1,5},{5,1},{2,6},{6,2},{3,7},{7,3},{8,12},{12,8},{9,1... | collective-permute-start | bytes 786440 | tf_op jit(solution)/shard_map/ppermute | solution.py:477
  22.7 1.5 %collective-permute-start.4 = (bf16[2,256,256]{2,1,0:T(8,128)(2,1)S(1)}, bf16[2,256,256]{2,1,0:T(8,128)(2,1)S(1)}, u32[]{:S(2)}, u32[]{:S(2)}) collective-permute-start(bf16[2,256,256]{2,1,0:T(8,128)(2,1)S(1)} %equalize.2.refs_1_.refs_0_), channel_id=1, source_target_pairs={{0,2},{1,3},{2,0},{3,1},{4,6},{5,7},{6,4},{7,5},{8,10},{9,11},{10,... | collective-permute-start | bytes 786440 | tf_op jit(solution)/shard_map/ppermute | solution.py:476
  24.2 0.0 collective-permute-start.12
  24.2 0.5 %collective-permute-done.11.refs_2_.refs_4_ = bf16[2,256,256]{2,1,0:T(8,128)(2,1)S(1)} collective-permute-done((bf16[2,256,256]{2,1,0:T(8,128)(2,1)S(1)}, bf16[2,256,256]{2,1,0:T(8,128)(2,1)S(1)}, u32[]{:S(2)}, u32[]{:S(2)}) %collective-permute-start.11) | collective-permute-done | bytes 262176 | tf_op jit(solution)/shard_map/ppermute | solution.py:477
  24.7 0.0 collective-permute-start.6
  24.7 0.6 %collective-permute-done.10.refs_0_ = bf16[2,256,256]{2,1,0:T(8,128)(2,1)S(1)} collective-permute-done((bf16[2,256,256]{2,1,0:T(8,128)(2,1)S(1)}, bf16[2,256,256]{2,1,0:T(8,128)(2,1)S(1)}, u32[]{:S(2)}, u32[]{:S(2)}) %collective-permute-start.10) | collective-permute-done | bytes 262176 | tf_op jit(solution)/shard_map/ppermute | solution.py:476
  25.2 0.1 collective-permute-start.13
  25.3 3.2 %collective-permute-done.5.refs_2_.refs_4_ = bf16[2,256,256]{2,1,0:T(8,128)(2,1)S(1)} collective-permute-done((bf16[2,256,256]{2,1,0:T(8,128)(2,1)S(1)}, bf16[2,256,256]{2,1,0:T(8,128)(2,1)S(1)}, u32[]{:S(2)}, u32[]{:S(2)}) %collective-permute-start.5) | collective-permute-done | bytes 262176 | tf_op jit(solution)/shard_map/ppermute | solution.py:477
  28.5 0.9 %collective-permute-done.4.refs_0_ = bf16[2,256,256]{2,1,0:T(8,128)(2,1)S(1)} collective-permute-done((bf16[2,256,256]{2,1,0:T(8,128)(2,1)S(1)}, bf16[2,256,256]{2,1,0:T(8,128)(2,1)S(1)}, u32[]{:S(2)}, u32[]{:S(2)}) %collective-permute-start.4) | collective-permute-done | bytes 262176 | tf_op jit(solution)/shard_map/ppermute | solution.py:476
  29.5 0.1 collective-permute-start.7
  29.6 0.0 collective-permute-done.12.refs_2_
  29.6 0.0 collective-permute-done.13.refs_3_
  29.6 0.0 copy-done.1
  29.6 1.4 %correlate.2.refs_5_ = f32[2,2,4,32,128]{4,3,2,1,0:T(8,128)S(1)} custom-call(s32[8,8]{1,0:T(8,128)S(1)} %copy-done.1, bf16[2,256,256]{2,1,0:T(8,128)(2,1)S(1)} %equalize.3.refs_0_, bf16[2,256,256]{2,1,0:T(8,128)(2,1)S(1)} %held_back.5.refs_1_, bf16[2,256,256]{2,1,0:T(8,128)(2,1)S(1)} %collective-permute-done.12.refs_2_, ...), custom_call_target="tpu_custom_call" | custom-call | bytes 1024 | tf_op jit(solution)/shard_map/correlate/pallas_call | solution.py:402
  31.0 0.0 collective-permute-done.6.refs_2_
  31.0 0.1 collective-permute-done.7.refs_3_
  31.1 2.2 %correlate.3 = f32[2,16,32,128]{3,2,1,0:T(8,128)} custom-call(s32[8,8]{1,0:T(8,128)S(1)} %copy-done.1, bf16[2,256,256]{2,1,0:T(8,128)(2,1)S(1)} %equalize.2.refs_1_.refs_0_, bf16[2,256,256]{2,1,0:T(8,128)(2,1)S(1)} %held_back.4.refs_1_, bf16[2,256,256]{2,1,0:T(8,128)(2,1)S(1)} %collective-permute-done.6.refs_2_, ...), custom_call_target="tpu_custom_call" | custom-call | bytes 1024 | tf_op jit(solution)/shard_map/correlate/pallas_call | solution.py:402
  (3 shorter events, 0.1 us)
Async XLA Ops:
  0.0 8.4 %copy-start = (f32[128,128]{1,0:T(8,128)S(1)}, f32[128,128]{1,0:T(8,128)}, u32[]{:S(2)}) copy-start(f32[128,128]{1,0:T(8,128)} %constant.5.clone.pick_ref) | copy-start | bytes 196612
  0.0 8.4 %copy-start.2 = (f32[8,2,128]{2,1,0:T(2,128)S(1)}, f32[8,2,128]{2,1,0:T(2,128)}, u32[]{:S(2)}) copy-start(f32[8,2,128]{2,1,0:T(2,128)} %gains_ref.1) | copy-start | bytes 24580
  2.7 7.8 %collective-permute-start = (bf16[280,128]{1,0:T(8,128)(2,1)S(1)}, bf16[280,128]{1,0:T(8,128)(2,1)S(1)}, u32[]{:S(2)}, u32[]{:S(2)}) collective-permute-start(bf16[280,128]{1,0:T(8,128)(2,1)S(1)} %get-tuple-element.24), channel_id=1, source_target_pairs={{0,24},{8,16},{16,8},{24,0},{1,25},{9,17},{17,9},{25,1},{2,26},{10... | collective-permute-start | bytes 215048 | tf_op jit(solution)/shard_map/ppermute | solution.py:418
  7.8 8.2 %collective-permute-start.8 = (bf16[280,128]{1,0:T(8,128)(2,1)S(1)}, bf16[280,128]{1,0:T(8,128)(2,1)S(1)}, u32[]{:S(2)}, u32[]{:S(2)}) collective-permute-start(bf16[280,128]{1,0:T(8,128)(2,1)S(1)} %get-tuple-element.30), channel_id=1, source_target_pairs={{0,16},{8,24},{16,0},{24,8},{1,17},{9,25},{17,1},{25,9},{2,18},{10... | collective-permute-start | bytes 215048 | tf_op jit(solution)/shard_map/ppermute | solution.py:418
  7.8 8.2 %collective-permute-start.9 = (bf16[280,128]{1,0:T(8,128)(2,1)S(1)}, bf16[280,128]{1,0:T(8,128)(2,1)S(1)}, u32[]{:S(2)}, u32[]{:S(2)}) collective-permute-start(bf16[280,128]{1,0:T(8,128)(2,1)S(1)} %get-tuple-element.31), channel_id=1, source_target_pairs={{0,8},{8,0},{16,24},{24,16},{1,9},{9,1},{17,25},{25,17},{2,10},{10... | collective-permute-start | bytes 215048 | tf_op jit(solution)/shard_map/ppermute | solution.py:418
  9.1 20.5 %copy-start.1 = (s32[8,8]{1,0:T(8,128)S(1)}, s32[8,8]{1,0:T(8,128)}, u32[]{:S(2)}) copy-start(s32[8,8]{1,0:T(8,128)} %map_ref.3) | copy-start | bytes 772
  10.5 8.5 %collective-permute-start.1 = (bf16[280,128]{1,0:T(8,128)(2,1)S(1)}, bf16[280,128]{1,0:T(8,128)(2,1)S(1)}, u32[]{:S(2)}, u32[]{:S(2)}) collective-permute-start(bf16[280,128]{1,0:T(8,128)(2,1)S(1)} %get-tuple-element.25), channel_id=1, source_target_pairs={{0,24},{8,16},{16,8},{24,0},{1,25},{9,17},{17,9},{25,1},{2,26},{10... | collective-permute-start | bytes 215048 | tf_op jit(solution)/shard_map/ppermute | solution.py:418
  14.8 5.8 %collective-permute-start.2 = (bf16[280,128]{1,0:T(8,128)(2,1)S(1)}, bf16[280,128]{1,0:T(8,128)(2,1)S(1)}, u32[]{:S(2)}, u32[]{:S(2)}) collective-permute-start(bf16[280,128]{1,0:T(8,128)(2,1)S(1)} %get-tuple-element.26), channel_id=1, source_target_pairs={{0,16},{8,24},{16,0},{24,8},{1,17},{9,25},{17,1},{25,9},{2,18},{10... | collective-permute-start | bytes 215048 | tf_op jit(solution)/shard_map/ppermute | solution.py:418
  15.0 5.6 %collective-permute-start.3 = (bf16[280,128]{1,0:T(8,128)(2,1)S(1)}, bf16[280,128]{1,0:T(8,128)(2,1)S(1)}, u32[]{:S(2)}, u32[]{:S(2)}) collective-permute-start(bf16[280,128]{1,0:T(8,128)(2,1)S(1)} %get-tuple-element.27), channel_id=1, source_target_pairs={{0,8},{8,0},{16,24},{24,16},{1,9},{9,1},{17,25},{25,17},{2,10},{10... | collective-permute-start | bytes 215048 | tf_op jit(solution)/shard_map/ppermute | solution.py:418
  16.5 8.2 %collective-permute-start.11 = (bf16[2,256,256]{2,1,0:T(8,128)(2,1)S(1)}, bf16[2,256,256]{2,1,0:T(8,128)(2,1)S(1)}, u32[]{:S(2)}, u32[]{:S(2)}) collective-permute-start(bf16[2,256,256]{2,1,0:T(8,128)(2,1)S(1)} %equalize.3.refs_0_), channel_id=1, source_target_pairs={{0,4},{4,0},{1,5},{5,1},{2,6},{6,2},{3,7},{7,3},{8,12},{12,8},{9,1... | collective-permute-start | bytes 786440 | tf_op jit(solution)/shard_map/ppermute | solution.py:477
  17.5 7.8 %collective-permute-start.10 = (bf16[2,256,256]{2,1,0:T(8,128)(2,1)S(1)}, bf16[2,256,256]{2,1,0:T(8,128)(2,1)S(1)}, u32[]{:S(2)}, u32[]{:S(2)}) collective-permute-start(bf16[2,256,256]{2,1,0:T(8,128)(2,1)S(1)} %equalize.3.refs_0_), channel_id=1, source_target_pairs={{0,2},{1,3},{2,0},{3,1},{4,6},{5,7},{6,4},{7,5},{8,10},{9,11},{10,... | collective-permute-start | bytes 786440 | tf_op jit(solution)/shard_map/ppermute | solution.py:476
  21.1 7.5 %collective-permute-start.5 = (bf16[2,256,256]{2,1,0:T(8,128)(2,1)S(1)}, bf16[2,256,256]{2,1,0:T(8,128)(2,1)S(1)}, u32[]{:S(2)}, u32[]{:S(2)}) collective-permute-start(bf16[2,256,256]{2,1,0:T(8,128)(2,1)S(1)} %equalize.2.refs_1_.refs_0_), channel_id=1, source_target_pairs={{0,4},{4,0},{1,5},{5,1},{2,6},{6,2},{3,7},{7,3},{8,12},{12,8},{9,1... | collective-permute-start | bytes 786440 | tf_op jit(solution)/shard_map/ppermute | solution.py:477
  22.7 6.8 %collective-permute-start.4 = (bf16[2,256,256]{2,1,0:T(8,128)(2,1)S(1)}, bf16[2,256,256]{2,1,0:T(8,128)(2,1)S(1)}, u32[]{:S(2)}, u32[]{:S(2)}) collective-permute-start(bf16[2,256,256]{2,1,0:T(8,128)(2,1)S(1)} %equalize.2.refs_1_.refs_0_), channel_id=1, source_target_pairs={{0,2},{1,3},{2,0},{3,1},{4,6},{5,7},{6,4},{7,5},{8,10},{9,11},{10,... | collective-permute-start | bytes 786440 | tf_op jit(solution)/shard_map/ppermute | solution.py:476
  24.2 5.4 %collective-permute-start.12 = (bf16[2,256,256]{2,1,0:T(8,128)(2,1)S(1)}, bf16[2,256,256]{2,1,0:T(8,128)(2,1)S(1)}, u32[]{:S(2)}, u32[]{:S(2)}) collective-permute-start(bf16[2,256,256]{2,1,0:T(8,128)(2,1)S(1)} %equalize.3.refs_0_), channel_id=1, source_target_pairs={{0,1},{1,0},{2,3},{3,2},{4,5},{5,4},{6,7},{7,6},{8,9},{9,8},{10,11... | collective-permute-start | bytes 786440 | tf_op jit(solution)/shard_map/ppermute | solution.py:479
  24.7 6.3 %collective-permute-start.6 = (bf16[2,256,256]{2,1,0:T(8,128)(2,1)S(1)}, bf16[2,256,256]{2,1,0:T(8,128)(2,1)S(1)}, u32[]{:S(2)}, u32[]{:S(2)}) collective-permute-start(bf16[2,256,256]{2,1,0:T(8,128)(2,1)S(1)} %equalize.2.refs_1_.refs_0_), channel_id=1, source_target_pairs={{0,1},{1,0},{2,3},{3,2},{4,5},{5,4},{6,7},{7,6},{8,9},{9,8},{10,11... | collective-permute-start | bytes 786440 | tf_op jit(solution)/shard_map/ppermute | solution.py:479
  25.2 4.3 %collective-permute-start.13 = (bf16[2,256,256]{2,1,0:T(8,128)(2,1)S(1)}, bf16[2,256,256]{2,1,0:T(8,128)(2,1)S(1)}, u32[]{:S(2)}, u32[]{:S(2)}) collective-permute-start(bf16[2,256,256]{2,1,0:T(8,128)(2,1)S(1)} %held_back.5.refs_1_), channel_id=1, source_target_pairs={{0,1},{1,0},{2,3},{3,2},{4,5},{5,4},{6,7},{7,6},{8,9},{9,8},{10,11... | collective-permute-start | bytes 786440 | tf_op jit(solution)/shard_map/ppermute | solution.py:484
  29.5 1.6 %collective-permute-start.7 = (bf16[2,256,256]{2,1,0:T(8,128)(2,1)S(1)}, bf16[2,256,256]{2,1,0:T(8,128)(2,1)S(1)}, u32[]{:S(2)}, u32[]{:S(2)}) collective-permute-start(bf16[2,256,256]{2,1,0:T(8,128)(2,1)S(1)} %held_back.4.refs_1_), channel_id=1, source_target_pairs={{0,1},{1,0},{2,3},{3,2},{4,5},{5,4},{6,7},{7,6},{8,9},{9,8},{10,11... | collective-permute-start | bytes 786440 | tf_op jit(solution)/shard_map/ppermute | solution.py:484

commit v10 on v9

--- a/solution.py
+++ b/solution.py
@@ -165,7 +165,6 @@
 
 IN_VMEM = pl.BlockSpec(memory_space=pltpu.VMEM)
 IN_HBM = pl.BlockSpec(memory_space=pl.ANY)
-IN_SMEM = pl.BlockSpec(memory_space=pltpu.SMEM)
 
 
 def filtered_and_first(voltages, owners, table):
@@ -307,20 +306,32 @@
     return v
 
 
-def correlate_kernel(n_row, n_col, h, times, part, dense, map_ref, *refs):
+def correlate_kernel(n_row, n_col, h, times, part, dense, *refs):
     row_blocks = refs[:n_col]
     col_blocks = (refs[0],) + refs[n_col : n_col + n_row - 1]
     last = part == PARTS - 1
+    given = refs[n_col + n_row - 1 :]
+    if part > 0:
+        earlier, keeps = given[:2]
     if last:
         out_hbm, chosen, out_ref, sems = refs[-4:]
     else:
-        out_ref, chosen = refs[-2:]
-    earlier = refs[n_col + n_row - 1]
+        out_ref, keeps_out, chosen = refs[-3:]
     me_row, me_col = lax.axis_index("brow"), lax.axis_index("bcol")
     row_at, col_at = row_places(me_col, n_col), column_places(me_row, n_row)
     rows = BATCH * SIG
     tiles = n_col * rows // LANES
     steps = 2 * h // BATCH
+    if part == 0:
+        owned = given[0][...]
+        first, second = (lax.broadcasted_iota(jnp.int32, owned.shape, axis) for axis in range(2))
+        for e in range(n_row):
+            for d in range(n_col):
+                here = (first == me_row * n_col + row_at[d]) & (second == col_at[e] * n_col + me_col)
+                found = jnp.max(jnp.where(here, (owned == 1).astype(jnp.float32), 0.0), axis=(0, 1), keepdims=True)
+                keeps_out[e, d] = jnp.broadcast_to(found * (1.0 / times), (SIG, LANES))
+    elif not last:
+        keeps_out[...] = keeps[...]
     index_in_batch = (lax.broadcasted_iota(jnp.int32, (SIG, LANES), 1) // SIG) % BATCH
 
     for step in range(steps):
@@ -350,8 +361,7 @@
                 start = d * rows % LANES
                 v = [x[start + i * SIG : start + (i + 1) * SIG] for i in range(BATCH)]
                 if last:
-                    owned = map_ref[me_row * n_col + row_at[d], col_at[e] * n_col + me_col] == 1
-                    keep = jnp.where(owned, 1.0 / times, 0.0)
+                    keep = keeps[e, d]
                 a_at = pl.ds(pl.multiple_of(row_at[d] * SIG, SIG), SIG)
                 mine = slice(d * SIG, (d + 1) * SIG)
                 if dense:
@@ -372,7 +382,7 @@
                         if part > 0:
                             w = jnp.concatenate([earlier[q, e, s2, mine, :], w], axis=1)
                         if last:
-                            out_ref[q, col_at[e] * SIG + s2, a_at, :] = w * keep
+                            out_ref[q, col_at[e] * SIG + s2, a_at, :] = w * keep[:, : w.shape[1]]
                         else:
                             out_ref[q, e, s2, mine, :] = w
             if last:
@@ -384,12 +394,12 @@
         copy.wait()
 
 
-def correlate(tile_map, blocks, earlier, part, n_row, n_col):
+def correlate(blocks, given, part, n_row, n_col):
     h = blocks[0].shape[1] // SIG
     times = blocks[0].shape[2] // 2
     channels = 2 * h
     dense = channels * 2 == LANES and PARTS == 2
-    operands = list(blocks) + ([earlier] if part else [])
+    operands = list(blocks) + list(given)
     last = part == PARTS - 1
     if last:
         out_shape = (2, n_row * SIG, n_col * SIG, (part + 1) * channels)
@@ -397,18 +407,19 @@
         out_shape = (2, n_row, SIG // 2, n_col * SIG, LANES)
     else:
         out_shape = (2, n_row, SIG, n_col * SIG, (part + 1) * channels)
+    shapes = [out_shape] if last else [out_shape, (n_row, n_col, SIG, LANES)]
     in_last = [pltpu.VMEM(out_shape, jnp.float32), pltpu.SemaphoreType.DMA((2 * n_row,))]
     kept = pltpu.VMEM((2 * n_row * n_col * BATCH * SIG // LANES, SIG * channels // BATCH, LANES), jnp.float32)
     return pl.pallas_call(
         functools.partial(correlate_kernel, n_row, n_col, h, times, part, dense),
-        out_shape=jax.ShapeDtypeStruct(out_shape, jnp.float32),
-        in_specs=[IN_SMEM] + [IN_VMEM] * len(operands),
-        out_specs=IN_HBM if last else IN_VMEM,
+        out_shape=[jax.ShapeDtypeStruct(shape, jnp.float32) for shape in shapes],
+        in_specs=[IN_VMEM] * len(operands),
+        out_specs=[IN_HBM] if last else [IN_VMEM] * len(shapes),
         scratch_shapes=[kept] + (in_last if last else []),
         compiler_params=pltpu.CompilerParams(vmem_limit_bytes=VMEM_BYTES),
         cost_estimate=pl.CostEstimate(flops=0, bytes_accessed=1 << 10, transcendentals=0),
         name="correlate",
-    )(tile_map, *operands)
+    )(*operands)
 
 
 def to_owners(pieces):
@@ -477,14 +488,14 @@
         column.append([lax.ppermute(own[part], "brow", along[d]) for d in range(1, n_row)])
         arrived = later
     beside = [lax.ppermute(block, "bcol", other_core) for block in own]
-    result = None
+    result = [tile_map]
     for part in range(PARTS):
         after = own[-1:] + column[part]
         far[part] = list(held_back(far[part], after))
         near = [lax.ppermute(block, "bcol", other_core) for block in far[part]]
         blocks = [own[part]] + far[part] + [beside[part]] + near + column[part]
-        result = correlate(tile_map, blocks, result, part, n_row, n_col)
-    return jnp.transpose(result, (3, 0, 1, 2))[None, None]
+        result = correlate(blocks, result, part, n_row, n_col)
+    return jnp.transpose(result[0], (3, 0, 1, 2))[None, None]
 
 
 def solution(mesh):

time: 33.4 us -> 32.8 us (0.982)
  Pallas kernels: 7.81 us -> 6.58 us
  waiting for transfers between devices: 8.97 us -> 9.61 us
    pallas_call x2, Pallas kernels: 3.6 us -> 2.36 us  [correlate(): pl.pallas_call(functools.partial(correlate_kernel, n_row, n_col, h, times...]
    ppermute x2, waiting for transfers between devices: 0.1 us -> 0.74 us  [shards(): near = [lax.ppermute(block, 'bcol', other_core) for block in far[part]]]
  transfers between devices with their start and end apart: 14 -> 14, of which waited for: 8 -> 8; matrix products, arithmetic and copies ran while one was open for 0% -> 0% of each run, Pallas kernels for 9% -> 7%
where the time goes in v10:
time: 32.8 us; the launch traced here: 32.7 us
  starting transfers between devices  16.4 us (50%)
  waiting for transfers between devices  9.61 us (29%)
  Pallas kernels  6.58 us (20%)
    ppermute x6, starting transfers between devices, to_owners(): lax.ppermute(pieces[d], 'chan', [(i, i ^ d) for i in range(owners)])  10.7 us
    ppermute x2, waiting for transfers between devices, shards(): lax.ppermute(own[part], 'brow', along[d])  3.71 us
    ppermute x6, waiting for transfers between devices, to_owners(): lax.ppermute(pieces[d], 'chan', [(i, i ^ d) for i in range(owners)])  3.68 us
    ppermute x2, starting transfers between devices, shards(): lax.ppermute(own[part], 'bcol', across[d])  2.98 us
    pallas_call x1, Pallas kernels, filtered_and_first(): pl.pallas_call(functools.partial(filter_kernel, frames, pieces, spectrum_...  2.65 us
    ppermute x2, starting transfers between devices, shards(): lax.ppermute(own[part], 'brow', along[d])  2.58 us
    pallas_call x2, Pallas kernels, correlate(): pl.pallas_call(functools.partial(correlate_kernel, n_row, n_col, h, times...  2.36 us
    ppermute x2, waiting for transfers between devices, shards(): lax.ppermute(own[part], 'bcol', across[d])  1.49 us
  transfers between devices with their start and end apart: 14, of which 8 were waited for; matrix products, arithmetic and copies ran while one was open for 0% of the time, Pallas kernels for 7%

profile of v10, /device:TPU:0, one launch (start us, length us, event | category | flops | bytes accessed | tf_op | source)
XLA Modules:
  0.0 32.7 jit_solution(17661388975856649063)
XLA Ops:
  0.0 0.0 copy-start
  0.0 0.0 copy-start.1
  0.0 2.6 %filter_and_transform.1 = (bf16[280,128]{1,0:T(8,128)(2,1)S(1)}, bf16[280,128]{1,0:T(8,128)(2,1)S(1)}, bf16[280,128]{1,0:T(8,128)(2,1)S(1)}, bf16[280,128]{1,0:T...) custom-call(s32[2,8,32768]{2,1,0:T(8,128)} %volt_hbm.1, ...), custom_call_target="tpu_custom_call" | custom-call | flops 536870912 | bytes 4194304 | tf_op jit(solution)/shard_map/filter_and_transform/pallas_call | solution.py:178
  2.7 5.1 %collective-permute-start = (bf16[280,128]{1,0:T(8,128)(2,1)S(1)}, bf16[280,128]{1,0:T(8,128)(2,1)S(1)}, u32[]{:S(2)}, u32[]{:S(2)}) collective-permute-start(bf16[280,128]{1,0:T(8,128)(2,1)S(1)} %get-tuple-element.26), channel_id=1, source_target_pairs={{0,24},{8,16},{16,8},{24,0},{1,25},{9,17},{17,9},{25,1},{2,26},{10... | collective-permute-start | bytes 215048 | tf_op jit(solution)/shard_map/ppermute | solution.py:429
  7.8 0.0 collective-permute-start.8
  7.8 0.6 %collective-permute-start.9 = (bf16[280,128]{1,0:T(8,128)(2,1)S(1)}, bf16[280,128]{1,0:T(8,128)(2,1)S(1)}, u32[]{:S(2)}, u32[]{:S(2)}) collective-permute-start(bf16[280,128]{1,0:T(8,128)(2,1)S(1)} %get-tuple-element.33), channel_id=1, source_target_pairs={{0,8},{8,0},{16,24},{24,16},{1,9},{9,1},{17,25},{25,17},{2,10},{10... | collective-permute-start | bytes 215048 | tf_op jit(solution)/shard_map/ppermute | solution.py:429
  8.4 0.0 copy-done
  8.4 0.0 copy-done.1
  8.4 0.6 %transform.1 = (bf16[280,128]{1,0:T(8,128)(2,1)S(1)}, bf16[280,128]{1,0:T(8,128)(2,1)S(1)}, bf16[280,128]{1,0:T(8,128)(2,1)S(1)}, bf16[280,128]{1,0:T(8,128)(2,1)S(1)}, f32[128,16]{1,0:T(8,128)S(1)}) custom-call(bf16[2,288,1024]{2,1,0:T(8,128)(2,1)S(1)} %get-tuple-element.21.filt, bf16[2048,256]{1,0:T(8,128)(2,1)S(1)} %get-tuple-element.22.later, ...), custom_call_target="tpu_custom_call" | custom-call | flops 536870912 | bytes 2097152 | tf_op jit(solution)/shard_map/transform/pallas_call | solution.py:214
  9.1 0.0 copy-start.2
  9.1 1.4 %collective-permute-done.refs_3_.refs_0_ = bf16[280,128]{1,0:T(8,128)(2,1)S(1)} collective-permute-done((bf16[280,128]{1,0:T(8,128)(2,1)S(1)}, bf16[280,128]{1,0:T(8,128)(2,1)S(1)}, u32[]{:S(2)}, u32[]{:S(2)}) %collective-permute-start) | collective-permute-done | bytes 71712 | tf_op jit(solution)/shard_map/ppermute | solution.py:429
  10.5 4.3 %collective-permute-start.1 = (bf16[280,128]{1,0:T(8,128)(2,1)S(1)}, bf16[280,128]{1,0:T(8,128)(2,1)S(1)}, u32[]{:S(2)}, u32[]{:S(2)}) collective-permute-start(bf16[280,128]{1,0:T(8,128)(2,1)S(1)} %get-tuple-element.27), channel_id=1, source_target_pairs={{0,24},{8,16},{16,8},{24,0},{1,25},{9,17},{17,9},{25,1},{2,26},{10... | collective-permute-start | bytes 215048 | tf_op jit(solution)/shard_map/ppermute | solution.py:429
  14.8 0.3 collective-permute-start.2
  15.0 0.4 %collective-permute-start.3 = (bf16[280,128]{1,0:T(8,128)(2,1)S(1)}, bf16[280,128]{1,0:T(8,128)(2,1)S(1)}, u32[]{:S(2)}, u32[]{:S(2)}) collective-permute-start(bf16[280,128]{1,0:T(8,128)(2,1)S(1)} %get-tuple-element.29), channel_id=1, source_target_pairs={{0,8},{8,0},{16,24},{24,16},{1,9},{9,1},{17,25},{25,17},{2,10},{10... | collective-permute-start | bytes 215048 | tf_op jit(solution)/shard_map/ppermute | solution.py:429
  15.4 0.6 %collective-permute-done.8.refs_1_ = bf16[280,128]{1,0:T(8,128)(2,1)S(1)} collective-permute-done((bf16[280,128]{1,0:T(8,128)(2,1)S(1)}, bf16[280,128]{1,0:T(8,128)(2,1)S(1)}, u32[]{:S(2)}, u32[]{:S(2)}) %collective-permute-start.8) | collective-permute-done | bytes 71712 | tf_op jit(solution)/shard_map/ppermute | solution.py:429
  16.0 0.0 collective-permute-done.9.refs_2_
  16.0 0.4 %equalize.3.refs_0_ = bf16[2,256,256]{2,1,0:T(8,128)(2,1)S(1)} custom-call(bf16[280,128]{1,0:T(8,128)(2,1)S(1)} %collective-permute-done.refs_3_.refs_0_, bf16[280,128]{1,0:T(8,128)(2,1)S(1)} %collective-permute-done.8.refs_1_, bf16[280,128]{1,0:T(8,128)(2,1)S(1)} %collective-permute-done.9.refs_2_, bf16[280,128]{1,0:T(8,128)(2,1)S(1)} %get-tuple-element.34.refs_3_, ...), custom_call_target="tpu_custom_call" | custom-call | bytes 1024 | tf_op jit(solution)/shard_map/equalize/pallas_call | solution.py:269
  16.5 1.0 %collective-permute-start.11 = (bf16[2,256,256]{2,1,0:T(8,128)(2,1)S(1)}, bf16[2,256,256]{2,1,0:T(8,128)(2,1)S(1)}, u32[]{:S(2)}, u32[]{:S(2)}) collective-permute-start(bf16[2,256,256]{2,1,0:T(8,128)(2,1)S(1)} %equalize.3.refs_0_), channel_id=1, source_target_pairs={{0,4},{4,0},{1,5},{5,1},{2,6},{6,2},{3,7},{7,3},{8,12},{12,8},{9,1... | collective-permute-start | bytes 786440 | tf_op jit(solution)/shard_map/ppermute | solution.py:488
  17.5 1.5 %collective-permute-start.10 = (bf16[2,256,256]{2,1,0:T(8,128)(2,1)S(1)}, bf16[2,256,256]{2,1,0:T(8,128)(2,1)S(1)}, u32[]{:S(2)}, u32[]{:S(2)}) collective-permute-start(bf16[2,256,256]{2,1,0:T(8,128)(2,1)S(1)} %equalize.3.refs_0_), channel_id=1, source_target_pairs={{0,2},{1,3},{2,0},{3,1},{4,6},{5,7},{6,4},{7,5},{8,10},{9,11},{10,... | collective-permute-start | bytes 786440 | tf_op jit(solution)/shard_map/ppermute | solution.py:487
  19.0 0.0 collective-permute-done.1.refs_0_
  19.0 1.7 %collective-permute-done.2.refs_1_ = bf16[280,128]{1,0:T(8,128)(2,1)S(1)} collective-permute-done((bf16[280,128]{1,0:T(8,128)(2,1)S(1)}, bf16[280,128]{1,0:T(8,128)(2,1)S(1)}, u32[]{:S(2)}, u32[]{:S(2)}) %collective-permute-start.2) | collective-permute-done | bytes 71712 | tf_op jit(solution)/shard_map/ppermute | solution.py:429
  20.6 0.0 collective-permute-done.3.refs_2_
  20.6 0.4 %equalize.2.refs_1_.refs_0_ = bf16[2,256,256]{2,1,0:T(8,128)(2,1)S(1)} custom-call(bf16[280,128]{1,0:T(8,128)(2,1)S(1)} %collective-permute-done.1.refs_0_, bf16[280,128]{1,0:T(8,128)(2,1)S(1)} %collective-permute-done.2.refs_1_, bf16[280,128]{1,0:T(8,128)(2,1)S(1)} %collective-permute-done.3.refs_2_, bf16[280,128]{1,0:T(8,128)(2,1)S(1)} %get-tuple-element.30.refs_3_, ...), custom_call_target="tpu_custom_call" | custom-call | bytes 1024 | tf_op jit(solution)/shard_map/equalize/pallas_call | solution.py:269
  21.1 1.6 %collective-permute-start.5 = (bf16[2,256,256]{2,1,0:T(8,128)(2,1)S(1)}, bf16[2,256,256]{2,1,0:T(8,128)(2,1)S(1)}, u32[]{:S(2)}, u32[]{:S(2)}) collective-permute-start(bf16[2,256,256]{2,1,0:T(8,128)(2,1)S(1)} %equalize.2.refs_1_.refs_0_), channel_id=1, source_target_pairs={{0,4},{4,0},{1,5},{5,1},{2,6},{6,2},{3,7},{7,3},{8,12},{12,8},{9,1... | collective-permute-start | bytes 786440 | tf_op jit(solution)/shard_map/ppermute | solution.py:488
  22.7 1.5 %collective-permute-start.4 = (bf16[2,256,256]{2,1,0:T(8,128)(2,1)S(1)}, bf16[2,256,256]{2,1,0:T(8,128)(2,1)S(1)}, u32[]{:S(2)}, u32[]{:S(2)}) collective-permute-start(bf16[2,256,256]{2,1,0:T(8,128)(2,1)S(1)} %equalize.2.refs_1_.refs_0_), channel_id=1, source_target_pairs={{0,2},{1,3},{2,0},{3,1},{4,6},{5,7},{6,4},{7,5},{8,10},{9,11},{10,... | collective-permute-start | bytes 786440 | tf_op jit(solution)/shard_map/ppermute | solution.py:487
  24.2 0.0 collective-permute-start.12
  24.2 0.5 %collective-permute-done.11.refs_2_.refs_4_ = bf16[2,256,256]{2,1,0:T(8,128)(2,1)S(1)} collective-permute-done((bf16[2,256,256]{2,1,0:T(8,128)(2,1)S(1)}, bf16[2,256,256]{2,1,0:T(8,128)(2,1)S(1)}, u32[]{:S(2)}, u32[]{:S(2)}) %collective-permute-start.11) | collective-permute-done | bytes 262176 | tf_op jit(solution)/shard_map/ppermute | solution.py:488
  24.7 0.0 collective-permute-start.6
  24.7 0.6 %collective-permute-done.10.refs_0_ = bf16[2,256,256]{2,1,0:T(8,128)(2,1)S(1)} collective-permute-done((bf16[2,256,256]{2,1,0:T(8,128)(2,1)S(1)}, bf16[2,256,256]{2,1,0:T(8,128)(2,1)S(1)}, u32[]{:S(2)}, u32[]{:S(2)}) %collective-permute-start.10) | collective-permute-done | bytes 262176 | tf_op jit(solution)/shard_map/ppermute | solution.py:487
  25.2 0.1 collective-permute-start.13
  25.3 3.2 %collective-permute-done.5.refs_2_.refs_4_ = bf16[2,256,256]{2,1,0:T(8,128)(2,1)S(1)} collective-permute-done((bf16[2,256,256]{2,1,0:T(8,128)(2,1)S(1)}, bf16[2,256,256]{2,1,0:T(8,128)(2,1)S(1)}, u32[]{:S(2)}, u32[]{:S(2)}) %collective-permute-start.5) | collective-permute-done | bytes 262176 | tf_op jit(solution)/shard_map/ppermute | solution.py:488
  28.5 0.9 %collective-permute-done.4.refs_0_ = bf16[2,256,256]{2,1,0:T(8,128)(2,1)S(1)} collective-permute-done((bf16[2,256,256]{2,1,0:T(8,128)(2,1)S(1)}, bf16[2,256,256]{2,1,0:T(8,128)(2,1)S(1)}, u32[]{:S(2)}, u32[]{:S(2)}) %collective-permute-start.4) | collective-permute-done | bytes 262176 | tf_op jit(solution)/shard_map/ppermute | solution.py:487
  29.5 0.1 collective-permute-start.7
  29.6 0.0 collective-permute-done.12.refs_2_
  29.6 0.0 collective-permute-done.13.refs_3_
  29.6 0.0 copy-done.2
  29.6 0.7 %correlate.2 = (f32[2,2,4,32,128]{4,3,2,1,0:T(8,128)S(1)}, f32[2,4,8,128]{3,2,1,0:T(8,128)S(1)}) custom-call(bf16[2,256,256]{2,1,0:T(8,128)(2,1)S(1)} %equalize.3.refs_0_, bf16[2,256,256]{2,1,0:T(8,128)(2,1)S(1)} %held_back.5.refs_1_, bf16[2,256,256]{2,1,0:T(8,128)(2,1)S(1)} %collective-permute-done.12.refs_2_, ...), custom_call_target="tpu_custom_call" | custom-call | bytes 1024 | tf_op jit(solution)/shard_map/correlate/pallas_call | solution.py:413
  30.3 0.0 collective-permute-done.6.refs_2_
  30.3 0.7 %collective-permute-done.7.refs_3_ = bf16[2,256,256]{2,1,0:T(8,128)(2,1)S(1)} collective-permute-done((bf16[2,256,256]{2,1,0:T(8,128)(2,1)S(1)}, bf16[2,256,256]{2,1,0:T(8,128)(2,1)S(1)}, u32[]{:S(2)}, u32[]{:S(2)}) %collective-permute-start.7) | collective-permute-done | bytes 262176 | tf_op jit(solution)/shard_map/ppermute | solution.py:495
  31.1 1.6 %correlate.3 = f32[2,16,32,128]{3,2,1,0:T(8,128)} custom-call(bf16[2,256,256]{2,1,0:T(8,128)(2,1)S(1)} %equalize.2.refs_1_.refs_0_, bf16[2,256,256]{2,1,0:T(8,128)(2,1)S(1)} %held_back.4.refs_1_, bf16[2,256,256]{2,1,0:T(8,128)(2,1)S(1)} %collective-permute-done.6.refs_2_, bf16[2,256,256]{2,1,0:T(8,128)(2,1)S(1)} %collective-permute-done.7.refs_3_, ...), custom_call_target="tpu_custom_call" | custom-call | bytes 1024 | tf_op jit(solution)/shard_map/correlate/pallas_call | solution.py:413
  (3 shorter events, 0.1 us)
Async XLA Ops:
  0.0 8.4 %copy-start = (f32[128,128]{1,0:T(8,128)S(1)}, f32[128,128]{1,0:T(8,128)}, u32[]{:S(2)}) copy-start(f32[128,128]{1,0:T(8,128)} %constant.5.clone.pick_ref) | copy-start | bytes 196612
  0.0 8.4 %copy-start.1 = (f32[8,2,128]{2,1,0:T(2,128)S(1)}, f32[8,2,128]{2,1,0:T(2,128)}, u32[]{:S(2)}) copy-start(f32[8,2,128]{2,1,0:T(2,128)} %gains_ref.1) | copy-start | bytes 24580
  2.7 7.8 %collective-permute-start = (bf16[280,128]{1,0:T(8,128)(2,1)S(1)}, bf16[280,128]{1,0:T(8,128)(2,1)S(1)}, u32[]{:S(2)}, u32[]{:S(2)}) collective-permute-start(bf16[280,128]{1,0:T(8,128)(2,1)S(1)} %get-tuple-element.26), channel_id=1, source_target_pairs={{0,24},{8,16},{16,8},{24,0},{1,25},{9,17},{17,9},{25,1},{2,26},{10... | collective-permute-start | bytes 215048 | tf_op jit(solution)/shard_map/ppermute | solution.py:429
  7.8 8.2 %collective-permute-start.8 = (bf16[280,128]{1,0:T(8,128)(2,1)S(1)}, bf16[280,128]{1,0:T(8,128)(2,1)S(1)}, u32[]{:S(2)}, u32[]{:S(2)}) collective-permute-start(bf16[280,128]{1,0:T(8,128)(2,1)S(1)} %get-tuple-element.32), channel_id=1, source_target_pairs={{0,16},{8,24},{16,0},{24,8},{1,17},{9,25},{17,1},{25,9},{2,18},{10... | collective-permute-start | bytes 215048 | tf_op jit(solution)/shard_map/ppermute | solution.py:429
  7.8 8.2 %collective-permute-start.9 = (bf16[280,128]{1,0:T(8,128)(2,1)S(1)}, bf16[280,128]{1,0:T(8,128)(2,1)S(1)}, u32[]{:S(2)}, u32[]{:S(2)}) collective-permute-start(bf16[280,128]{1,0:T(8,128)(2,1)S(1)} %get-tuple-element.33), channel_id=1, source_target_pairs={{0,8},{8,0},{16,24},{24,16},{1,9},{9,1},{17,25},{25,17},{2,10},{10... | collective-permute-start | bytes 215048 | tf_op jit(solution)/shard_map/ppermute | solution.py:429
  9.1 20.5 %copy-start.2 = (s32[8,8]{1,0:T(8,128)S(1)}, s32[8,8]{1,0:T(8,128)}, u32[]{:S(2)}) copy-start(s32[8,8]{1,0:T(8,128)} %refs_5_.1) | copy-start | bytes 772
  10.5 8.5 %collective-permute-start.1 = (bf16[280,128]{1,0:T(8,128)(2,1)S(1)}, bf16[280,128]{1,0:T(8,128)(2,1)S(1)}, u32[]{:S(2)}, u32[]{:S(2)}) collective-permute-start(bf16[280,128]{1,0:T(8,128)(2,1)S(1)} %get-tuple-element.27), channel_id=1, source_target_pairs={{0,24},{8,16},{16,8},{24,0},{1,25},{9,17},{17,9},{25,1},{2,26},{10... | collective-permute-start | bytes 215048 | tf_op jit(solution)/shard_map/ppermute | solution.py:429
  14.8 5.8 %collective-permute-start.2 = (bf16[280,128]{1,0:T(8,128)(2,1)S(1)}, bf16[280,128]{1,0:T(8,128)(2,1)S(1)}, u32[]{:S(2)}, u32[]{:S(2)}) collective-permute-start(bf16[280,128]{1,0:T(8,128)(2,1)S(1)} %get-tuple-element.28), channel_id=1, source_target_pairs={{0,16},{8,24},{16,0},{24,8},{1,17},{9,25},{17,1},{25,9},{2,18},{10... | collective-permute-start | bytes 215048 | tf_op jit(solution)/shard_map/ppermute | solution.py:429
  15.0 5.6 %collective-permute-start.3 = (bf16[280,128]{1,0:T(8,128)(2,1)S(1)}, bf16[280,128]{1,0:T(8,128)(2,1)S(1)}, u32[]{:S(2)}, u32[]{:S(2)}) collective-permute-start(bf16[280,128]{1,0:T(8,128)(2,1)S(1)} %get-tuple-element.29), channel_id=1, source_target_pairs={{0,8},{8,0},{16,24},{24,16},{1,9},{9,1},{17,25},{25,17},{2,10},{10... | collective-permute-start | bytes 215048 | tf_op jit(solution)/shard_map/ppermute | solution.py:429
  16.5 8.2 %collective-permute-start.11 = (bf16[2,256,256]{2,1,0:T(8,128)(2,1)S(1)}, bf16[2,256,256]{2,1,0:T(8,128)(2,1)S(1)}, u32[]{:S(2)}, u32[]{:S(2)}) collective-permute-start(bf16[2,256,256]{2,1,0:T(8,128)(2,1)S(1)} %equalize.3.refs_0_), channel_id=1, source_target_pairs={{0,4},{4,0},{1,5},{5,1},{2,6},{6,2},{3,7},{7,3},{8,12},{12,8},{9,1... | collective-permute-start | bytes 786440 | tf_op jit(solution)/shard_map/ppermute | solution.py:488
  17.5 7.8 %collective-permute-start.10 = (bf16[2,256,256]{2,1,0:T(8,128)(2,1)S(1)}, bf16[2,256,256]{2,1,0:T(8,128)(2,1)S(1)}, u32[]{:S(2)}, u32[]{:S(2)}) collective-permute-start(bf16[2,256,256]{2,1,0:T(8,128)(2,1)S(1)} %equalize.3.refs_0_), channel_id=1, source_target_pairs={{0,2},{1,3},{2,0},{3,1},{4,6},{5,7},{6,4},{7,5},{8,10},{9,11},{10,... | collective-permute-start | bytes 786440 | tf_op jit(solution)/shard_map/ppermute | solution.py:487
  21.1 7.5 %collective-permute-start.5 = (bf16[2,256,256]{2,1,0:T(8,128)(2,1)S(1)}, bf16[2,256,256]{2,1,0:T(8,128)(2,1)S(1)}, u32[]{:S(2)}, u32[]{:S(2)}) collective-permute-start(bf16[2,256,256]{2,1,0:T(8,128)(2,1)S(1)} %equalize.2.refs_1_.refs_0_), channel_id=1, source_target_pairs={{0,4},{4,0},{1,5},{5,1},{2,6},{6,2},{3,7},{7,3},{8,12},{12,8},{9,1... | collective-permute-start | bytes 786440 | tf_op jit(solution)/shard_map/ppermute | solution.py:488
  22.7 6.8 %collective-permute-start.4 = (bf16[2,256,256]{2,1,0:T(8,128)(2,1)S(1)}, bf16[2,256,256]{2,1,0:T(8,128)(2,1)S(1)}, u32[]{:S(2)}, u32[]{:S(2)}) collective-permute-start(bf16[2,256,256]{2,1,0:T(8,128)(2,1)S(1)} %equalize.2.refs_1_.refs_0_), channel_id=1, source_target_pairs={{0,2},{1,3},{2,0},{3,1},{4,6},{5,7},{6,4},{7,5},{8,10},{9,11},{10,... | collective-permute-start | bytes 786440 | tf_op jit(solution)/shard_map/ppermute | solution.py:487
  24.2 5.4 %collective-permute-start.12 = (bf16[2,256,256]{2,1,0:T(8,128)(2,1)S(1)}, bf16[2,256,256]{2,1,0:T(8,128)(2,1)S(1)}, u32[]{:S(2)}, u32[]{:S(2)}) collective-permute-start(bf16[2,256,256]{2,1,0:T(8,128)(2,1)S(1)} %equalize.3.refs_0_), channel_id=1, source_target_pairs={{0,1},{1,0},{2,3},{3,2},{4,5},{5,4},{6,7},{7,6},{8,9},{9,8},{10,11... | collective-permute-start | bytes 786440 | tf_op jit(solution)/shard_map/ppermute | solution.py:490
  24.7 5.7 %collective-permute-start.6 = (bf16[2,256,256]{2,1,0:T(8,128)(2,1)S(1)}, bf16[2,256,256]{2,1,0:T(8,128)(2,1)S(1)}, u32[]{:S(2)}, u32[]{:S(2)}) collective-permute-start(bf16[2,256,256]{2,1,0:T(8,128)(2,1)S(1)} %equalize.2.refs_1_.refs_0_), channel_id=1, source_target_pairs={{0,1},{1,0},{2,3},{3,2},{4,5},{5,4},{6,7},{7,6},{8,9},{9,8},{10,11... | collective-permute-start | bytes 786440 | tf_op jit(solution)/shard_map/ppermute | solution.py:490
  25.2 4.3 %collective-permute-start.13 = (bf16[2,256,256]{2,1,0:T(8,128)(2,1)S(1)}, bf16[2,256,256]{2,1,0:T(8,128)(2,1)S(1)}, u32[]{:S(2)}, u32[]{:S(2)}) collective-permute-start(bf16[2,256,256]{2,1,0:T(8,128)(2,1)S(1)} %held_back.5.refs_1_), channel_id=1, source_target_pairs={{0,1},{1,0},{2,3},{3,2},{4,5},{5,4},{6,7},{7,6},{8,9},{9,8},{10,11... | collective-permute-start | bytes 786440 | tf_op jit(solution)/shard_map/ppermute | solution.py:495
  29.5 1.6 %collective-permute-start.7 = (bf16[2,256,256]{2,1,0:T(8,128)(2,1)S(1)}, bf16[2,256,256]{2,1,0:T(8,128)(2,1)S(1)}, u32[]{:S(2)}, u32[]{:S(2)}) collective-permute-start(bf16[2,256,256]{2,1,0:T(8,128)(2,1)S(1)} %held_back.4.refs_1_), channel_id=1, source_target_pairs={{0,1},{1,0},{2,3},{3,2},{4,5},{5,4},{6,7},{7,6},{8,9},{9,8},{10,11... | collective-permute-start | bytes 786440 | tf_op jit(solution)/shard_map/ppermute | solution.py:495

commit v11 on v10

--- a/solution.py
+++ b/solution.py
@@ -430,51 +430,79 @@
     return arrived
 
 
+def copied(kernel, out_like, operands, name):
+    return pl.pallas_call(
+        kernel,
+        out_shape=[jax.ShapeDtypeStruct(block.shape, block.dtype) for block in out_like],
+        in_specs=[IN_VMEM] * len(operands),
+        out_specs=[IN_VMEM] * len(out_like),
+        compiler_params=pltpu.CompilerParams(vmem_limit_bytes=VMEM_BYTES),
+        cost_estimate=pl.CostEstimate(flops=0, bytes_accessed=1 << 10, transcendentals=0),
+        name=name,
+    )(*operands)
+
+
 def held_back(blocks, after):
     def kernel(*refs):
         for i in range(len(blocks)):
             refs[len(blocks) + len(after) + i][...] = refs[i][...]
 
-    return pl.pallas_call(
-        kernel,
-        out_shape=[jax.ShapeDtypeStruct(block.shape, block.dtype) for block in blocks],
-        in_specs=[IN_VMEM] * (len(blocks) + len(after)),
-        out_specs=[IN_VMEM] * len(blocks),
-        compiler_params=pltpu.CompilerParams(vmem_limit_bytes=VMEM_BYTES),
-        cost_estimate=pl.CostEstimate(flops=0, bytes_accessed=1 << 10, transcendentals=0),
-        name="held_back",
-    )(*blocks, *after)
-
-
-def together(blocks):
+    return copied(kernel, blocks, list(blocks) + list(after), "held_back")
+
+
+def sorted_by_core(first, second, after):
+    count = len(first)
+
     def kernel(*refs):
-        for i in range(len(blocks)):
-            refs[-1][i] = refs[i][...]
-
-    return pl.pallas_call(
-        kernel,
-        out_shape=jax.ShapeDtypeStruct((len(blocks),) + blocks[0].shape, blocks[0].dtype),
-        in_specs=[IN_VMEM] * len(blocks),
-        out_specs=IN_VMEM,
-        compiler_params=pltpu.CompilerParams(vmem_limit_bytes=VMEM_BYTES),
-        cost_estimate=pl.CostEstimate(flops=0, bytes_accessed=1 << 10, transcendentals=0),
-        name="together",
-    )(*blocks)
+        core = lax.rem(lax.axis_index("bcol"), 2)
+        outs = refs[2 * count + len(after) :]
+        for flip in range(2):
+
+            @pl.when(core == flip)
+            def _():
+                for i in range(count):
+                    outs[i][...] = refs[i + flip * count][...]
+                    outs[count + i][...] = refs[i + (1 - flip) * count][...]
+
+    both = copied(kernel, list(first) + list(second), list(first) + list(second) + list(after), "sorted_by_core")
+    return list(both[:count]), list(both[count:])
+
+
+def panel_permutes(block, n_row, n_col):
+    chips = n_col // 2
+
+    def x_step(row, col, d):
+        return row * n_col + (col // 2 + d) % chips * 2 + col % 2
+
+    def y_step(row, col, d):
+        return (row + d) % n_row * n_col + col
+
+    devices = [(row, col) for row in range(n_row) for col in range(n_col)]
+    axes = ("brow", "bcol")
+    first, second, far, column = [], [], [], []
+    for d in range(1, max(chips, n_row)):
+        if d < min(chips, n_row):
+            for turn, results in ((0, first), (1, second)):
+                route = [
+                    (row * n_col + col, (x_step if col % 2 == turn else y_step)(row, col, d)) for row, col in devices
+                ]
+                results.append(lax.ppermute(block, axes, route))
+        else:
+            step, results = (x_step, far) if d < chips else (y_step, column)
+            results.append(lax.ppermute(block, axes, [(row * n_col + col, step(row, col, d)) for row, col in devices]))
+    return first, second, far, column
 
 
 def shards(voltages, antenna_gains, tile_map):
     owners = lax.axis_size("chan")
     n_row = lax.axis_size("brow")
     n_col = lax.axis_size("bcol")
-    chips = n_col // 2
     frames = voltages.shape[2] // NCHAN
     table = jnp.asarray(constants(owners))
-    across = [[(i, (i // 2 + d) % chips * 2 + i % 2) for i in range(n_col)] for d in range(chips)]
-    along = [[(i, (i + d) % n_row) for i in range(n_row)] for d in range(n_row)]
     other_core = [(i, i ^ 1) for i in range(n_col)]
 
     filt, tables, pieces = filtered_and_first(voltages, owners, table)
-    own, far, column = [], [], []
+    own, panels = [], []
     arrived = to_owners(pieces)
     for part in range(PARTS):
         later = None
@@ -484,16 +512,16 @@
                 *pieces, gains = pieces
             later = to_owners([pieces[0], *held_back(pieces[1:], arrived[-1:])])
         own.append(equalize(arrived, gains, part, frames))
-        far.append([lax.ppermute(own[part], "bcol", across[d]) for d in range(1, chips)])
-        column.append([lax.ppermute(own[part], "brow", along[d]) for d in range(1, n_row)])
+        panels.append(panel_permutes(own[part], n_row, n_col))
         arrived = later
     beside = [lax.ppermute(block, "bcol", other_core) for block in own]
     result = [tile_map]
     for part in range(PARTS):
-        after = own[-1:] + column[part]
-        far[part] = list(held_back(far[part], after))
-        near = [lax.ppermute(block, "bcol", other_core) for block in far[part]]
-        blocks = [own[part]] + far[part] + [beside[part]] + near + column[part]
+        first, second, far, column = panels[part]
+        near_far, near_column = sorted_by_core(first, second, own[-1:] + far + column)
+        far, column = near_far + far, near_column + column
+        relayed = [lax.ppermute(block, "bcol", other_core) for block in far]
+        blocks = [own[part]] + far + [beside[part]] + relayed + column
         result = correlate(blocks, result, part, n_row, n_col)
     return jnp.transpose(result[0], (3, 0, 1, 2))[None, None]
 

time: 32.8 us -> 32.9 us (level)
  no operation moved by 1% of the time
where the time goes in v11:
time: 32.9 us; the launch traced here: 32.7 us
  starting transfers between devices  16.4 us (50%)
  waiting for transfers between devices  9.59 us (29%)
  Pallas kernels  6.61 us (20%)
    ppermute x6, starting transfers between devices, to_owners(): lax.ppermute(pieces[d], 'chan', [(i, i ^ d) for i in range(owners)])  10.7 us
    ppermute x4, starting transfers between devices, panel_permutes(): results.append(lax.ppermute(block, axes, route))  5.56 us
    ppermute x4, waiting for transfers between devices, panel_permutes(): results.append(lax.ppermute(block, axes, route))  5.16 us
    ppermute x6, waiting for transfers between devices, to_owners(): lax.ppermute(pieces[d], 'chan', [(i, i ^ d) for i in range(owners)])  3.68 us
    pallas_call x1, Pallas kernels, filtered_and_first(): pl.pallas_call(functools.partial(filter_kernel, frames, pieces, spectrum_...  2.65 us
    pallas_call x2, Pallas kernels, correlate(): pl.pallas_call(functools.partial(correlate_kernel, n_row, n_col, h, times...  2.35 us
    pallas_call x2, Pallas kernels, equalize(): pl.pallas_call(functools.partial(equalize_kernel, owners, frames, h, part...  0.9 us
    ppermute x2, waiting for transfers between devices, shards(): relayed = [lax.ppermute(block, 'bcol', other_core) for block in far]  0.75 us
  transfers between devices with their start and end apart: 14, of which 8 were waited for; matrix products, arithmetic and copies ran while one was open for 0% of the time, Pallas kernels for 7%

profile of v11, /device:TPU:0, one launch (start us, length us, event | category | flops | bytes accessed | tf_op | source)
XLA Modules:
  0.0 32.7 jit_solution(9857435571781140799)
XLA Ops:
  0.0 0.0 copy-start
  0.0 0.0 copy-start.1
  0.0 2.6 %filter_and_transform.1 = (bf16[280,128]{1,0:T(8,128)(2,1)S(1)}, bf16[280,128]{1,0:T(8,128)(2,1)S(1)}, bf16[280,128]{1,0:T(8,128)(2,1)S(1)}, bf16[280,128]{1,0:T...) custom-call(s32[2,8,32768]{2,1,0:T(8,128)} %volt_hbm.1, ...), custom_call_target="tpu_custom_call" | custom-call | flops 536870912 | bytes 4194304 | tf_op jit(solution)/shard_map/filter_and_transform/pallas_call | solution.py:178
  2.7 5.1 %collective-permute-start = (bf16[280,128]{1,0:T(8,128)(2,1)S(1)}, bf16[280,128]{1,0:T(8,128)(2,1)S(1)}, u32[]{:S(2)}, u32[]{:S(2)}) collective-permute-start(bf16[280,128]{1,0:T(8,128)(2,1)S(1)} %get-tuple-element.30), channel_id=1, source_target_pairs={{0,24},{8,16},{16,8},{24,0},{1,25},{9,17},{17,9},{25,1},{2,26},{10... | collective-permute-start | bytes 215048 | tf_op jit(solution)/shard_map/ppermute | solution.py:429
  7.8 0.0 collective-permute-start.8
  7.8 0.6 %collective-permute-start.9 = (bf16[280,128]{1,0:T(8,128)(2,1)S(1)}, bf16[280,128]{1,0:T(8,128)(2,1)S(1)}, u32[]{:S(2)}, u32[]{:S(2)}) collective-permute-start(bf16[280,128]{1,0:T(8,128)(2,1)S(1)} %get-tuple-element.39), channel_id=1, source_target_pairs={{0,8},{8,0},{16,24},{24,16},{1,9},{9,1},{17,25},{25,17},{2,10},{10... | collective-permute-start | bytes 215048 | tf_op jit(solution)/shard_map/ppermute | solution.py:429
  8.4 0.0 copy-done
  8.4 0.0 copy-done.1
  8.4 0.6 %transform.1 = (bf16[280,128]{1,0:T(8,128)(2,1)S(1)}, bf16[280,128]{1,0:T(8,128)(2,1)S(1)}, bf16[280,128]{1,0:T(8,128)(2,1)S(1)}, bf16[280,128]{1,0:T(8,128)(2,1)S(1)}, f32[128,16]{1,0:T(8,128)S(1)}) custom-call(bf16[2,288,1024]{2,1,0:T(8,128)(2,1)S(1)} %get-tuple-element.25.filt, bf16[2048,256]{1,0:T(8,128)(2,1)S(1)} %get-tuple-element.26.later, ...), custom_call_target="tpu_custom_call" | custom-call | flops 536870912 | bytes 2097152 | tf_op jit(solution)/shard_map/transform/pallas_call | solution.py:214
  9.1 0.0 copy-start.2
  9.1 1.4 %collective-permute-done.refs_3_.refs_0_ = bf16[280,128]{1,0:T(8,128)(2,1)S(1)} collective-permute-done((bf16[280,128]{1,0:T(8,128)(2,1)S(1)}, bf16[280,128]{1,0:T(8,128)(2,1)S(1)}, u32[]{:S(2)}, u32[]{:S(2)}) %collective-permute-start) | collective-permute-done | bytes 71712 | tf_op jit(solution)/shard_map/ppermute | solution.py:429
  10.5 4.3 %collective-permute-start.1 = (bf16[280,128]{1,0:T(8,128)(2,1)S(1)}, bf16[280,128]{1,0:T(8,128)(2,1)S(1)}, u32[]{:S(2)}, u32[]{:S(2)}) collective-permute-start(bf16[280,128]{1,0:T(8,128)(2,1)S(1)} %get-tuple-element.31), channel_id=1, source_target_pairs={{0,24},{8,16},{16,8},{24,0},{1,25},{9,17},{17,9},{25,1},{2,26},{10... | collective-permute-start | bytes 215048 | tf_op jit(solution)/shard_map/ppermute | solution.py:429
  14.8 0.3 collective-permute-start.2
  15.0 0.4 %collective-permute-start.3 = (bf16[280,128]{1,0:T(8,128)(2,1)S(1)}, bf16[280,128]{1,0:T(8,128)(2,1)S(1)}, u32[]{:S(2)}, u32[]{:S(2)}) collective-permute-start(bf16[280,128]{1,0:T(8,128)(2,1)S(1)} %get-tuple-element.33), channel_id=1, source_target_pairs={{0,8},{8,0},{16,24},{24,16},{1,9},{9,1},{17,25},{25,17},{2,10},{10... | collective-permute-start | bytes 215048 | tf_op jit(solution)/shard_map/ppermute | solution.py:429
  15.4 0.6 %collective-permute-done.8.refs_1_ = bf16[280,128]{1,0:T(8,128)(2,1)S(1)} collective-permute-done((bf16[280,128]{1,0:T(8,128)(2,1)S(1)}, bf16[280,128]{1,0:T(8,128)(2,1)S(1)}, u32[]{:S(2)}, u32[]{:S(2)}) %collective-permute-start.8) | collective-permute-done | bytes 71712 | tf_op jit(solution)/shard_map/ppermute | solution.py:429
  16.0 0.0 collective-permute-done.9.refs_2_
  16.0 0.4 %equalize.3.refs_0_ = bf16[2,256,256]{2,1,0:T(8,128)(2,1)S(1)} custom-call(bf16[280,128]{1,0:T(8,128)(2,1)S(1)} %collective-permute-done.refs_3_.refs_0_, bf16[280,128]{1,0:T(8,128)(2,1)S(1)} %collective-permute-done.8.refs_1_, bf16[280,128]{1,0:T(8,128)(2,1)S(1)} %collective-permute-done.9.refs_2_, bf16[280,128]{1,0:T(8,128)(2,1)S(1)} %get-tuple-element.40.refs_3_, ...), custom_call_target="tpu_custom_call" | custom-call | bytes 1024 | tf_op jit(solution)/shard_map/equalize/pallas_call | solution.py:269
  16.5 1.0 %collective-permute-start.11 = (bf16[2,256,256]{2,1,0:T(8,128)(2,1)S(1)}, bf16[2,256,256]{2,1,0:T(8,128)(2,1)S(1)}, u32[]{:S(2)}, u32[]{:S(2)}) collective-permute-start(bf16[2,256,256]{2,1,0:T(8,128)(2,1)S(1)} %equalize.3.refs_0_), channel_id=1, source_target_pairs={{0,4},{1,3},{2,6},{3,1},{4,0},{5,7},{6,2},{7,5},{8,12},{9,11},{10,... | collective-permute-start | bytes 786440 | tf_op jit(solution)/shard_map/ppermute | solution.py:489
  17.5 1.5 %collective-permute-start.10 = (bf16[2,256,256]{2,1,0:T(8,128)(2,1)S(1)}, bf16[2,256,256]{2,1,0:T(8,128)(2,1)S(1)}, u32[]{:S(2)}, u32[]{:S(2)}) collective-permute-start(bf16[2,256,256]{2,1,0:T(8,128)(2,1)S(1)} %equalize.3.refs_0_), channel_id=1, source_target_pairs={{0,2},{1,5},{2,0},{3,7},{4,6},{5,1},{6,4},{7,3},{8,10},{9,13},{10,... | collective-permute-start | bytes 786440 | tf_op jit(solution)/shard_map/ppermute | solution.py:489
  19.0 0.0 collective-permute-done.1.refs_0_
  19.0 1.7 %collective-permute-done.2.refs_1_ = bf16[280,128]{1,0:T(8,128)(2,1)S(1)} collective-permute-done((bf16[280,128]{1,0:T(8,128)(2,1)S(1)}, bf16[280,128]{1,0:T(8,128)(2,1)S(1)}, u32[]{:S(2)}, u32[]{:S(2)}) %collective-permute-start.2) | collective-permute-done | bytes 71712 | tf_op jit(solution)/shard_map/ppermute | solution.py:429
  20.6 0.0 collective-permute-done.3.refs_2_
  20.6 0.4 %equalize.2.refs_2_.refs_0_ = bf16[2,256,256]{2,1,0:T(8,128)(2,1)S(1)} custom-call(bf16[280,128]{1,0:T(8,128)(2,1)S(1)} %collective-permute-done.1.refs_0_, bf16[280,128]{1,0:T(8,128)(2,1)S(1)} %collective-permute-done.2.refs_1_, bf16[280,128]{1,0:T(8,128)(2,1)S(1)} %collective-permute-done.3.refs_2_, bf16[280,128]{1,0:T(8,128)(2,1)S(1)} %get-tuple-element.34.refs_3_, ...), custom_call_target="tpu_custom_call" | custom-call | bytes 1024 | tf_op jit(solution)/shard_map/equalize/pallas_call | solution.py:269
  21.1 1.6 %collective-permute-start.5 = (bf16[2,256,256]{2,1,0:T(8,128)(2,1)S(1)}, bf16[2,256,256]{2,1,0:T(8,128)(2,1)S(1)}, u32[]{:S(2)}, u32[]{:S(2)}) collective-permute-start(bf16[2,256,256]{2,1,0:T(8,128)(2,1)S(1)} %equalize.2.refs_2_.refs_0_), channel_id=1, source_target_pairs={{0,4},{1,3},{2,6},{3,1},{4,0},{5,7},{6,2},{7,5},{8,12},{9,11},{10,... | collective-permute-start | bytes 786440 | tf_op jit(solution)/shard_map/ppermute | solution.py:489
  22.7 1.5 %collective-permute-start.4 = (bf16[2,256,256]{2,1,0:T(8,128)(2,1)S(1)}, bf16[2,256,256]{2,1,0:T(8,128)(2,1)S(1)}, u32[]{:S(2)}, u32[]{:S(2)}) collective-permute-start(bf16[2,256,256]{2,1,0:T(8,128)(2,1)S(1)} %equalize.2.refs_2_.refs_0_), channel_id=1, source_target_pairs={{0,2},{1,5},{2,0},{3,7},{4,6},{5,1},{6,4},{7,3},{8,10},{9,13},{10,... | collective-permute-start | bytes 786440 | tf_op jit(solution)/shard_map/ppermute | solution.py:489
  24.2 0.0 collective-permute-start.12
  24.2 0.5 %collective-permute-done.11.refs_1_ = bf16[2,256,256]{2,1,0:T(8,128)(2,1)S(1)} collective-permute-done((bf16[2,256,256]{2,1,0:T(8,128)(2,1)S(1)}, bf16[2,256,256]{2,1,0:T(8,128)(2,1)S(1)}, u32[]{:S(2)}, u32[]{:S(2)}) %collective-permute-start.11) | collective-permute-done | bytes 262176 | tf_op jit(solution)/shard_map/ppermute | solution.py:489
  24.7 0.0 collective-permute-start.6
  24.7 1.9 %collective-permute-done.10.refs_0_ = bf16[2,256,256]{2,1,0:T(8,128)(2,1)S(1)} collective-permute-done((bf16[2,256,256]{2,1,0:T(8,128)(2,1)S(1)}, bf16[2,256,256]{2,1,0:T(8,128)(2,1)S(1)}, u32[]{:S(2)}, u32[]{:S(2)}) %collective-permute-start.10) | collective-permute-done | bytes 262176 | tf_op jit(solution)/shard_map/ppermute | solution.py:489
  26.6 0.1 collective-permute-start.13
  26.6 2.5 %collective-permute-done.5.refs_1_ = bf16[2,256,256]{2,1,0:T(8,128)(2,1)S(1)} collective-permute-done((bf16[2,256,256]{2,1,0:T(8,128)(2,1)S(1)}, bf16[2,256,256]{2,1,0:T(8,128)(2,1)S(1)}, u32[]{:S(2)}, u32[]{:S(2)}) %collective-permute-start.5) | collective-permute-done | bytes 262176 | tf_op jit(solution)/shard_map/ppermute | solution.py:489
  29.2 0.3 collective-permute-done.4.refs_0_
  29.5 0.1 collective-permute-start.7
  29.6 0.0 collective-permute-done.12.refs_2_
  29.6 0.0 collective-permute-done.13.refs_3_
  29.6 0.0 copy-done.2
  29.6 0.7 %correlate.2 = (f32[2,2,4,32,128]{4,3,2,1,0:T(8,128)S(1)}, f32[2,4,8,128]{3,2,1,0:T(8,128)S(1)}) custom-call(bf16[2,256,256]{2,1,0:T(8,128)(2,1)S(1)} %equalize.3.refs_0_, bf16[2,256,256]{2,1,0:T(8,128)(2,1)S(1)} %get-tuple-element.41.refs_1_, bf16[2,256,256]{2,1,0:T(8,128)(2,1)S(1)} %collective-permute-done.12.refs_2_, ...), custom_call_target="tpu_custom_call" | custom-call | bytes 1024 | tf_op jit(solution)/shard_map/correlate/pallas_call | solution.py:413
  30.3 0.0 collective-permute-done.6.refs_2_
  30.4 0.7 %collective-permute-done.7.refs_3_ = bf16[2,256,256]{2,1,0:T(8,128)(2,1)S(1)} collective-permute-done((bf16[2,256,256]{2,1,0:T(8,128)(2,1)S(1)}, bf16[2,256,256]{2,1,0:T(8,128)(2,1)S(1)}, u32[]{:S(2)}, u32[]{:S(2)}) %collective-permute-start.7) | collective-permute-done | bytes 262176 | tf_op jit(solution)/shard_map/ppermute | solution.py:523
  31.1 1.6 %correlate.3 = f32[2,16,32,128]{3,2,1,0:T(8,128)} custom-call(bf16[2,256,256]{2,1,0:T(8,128)(2,1)S(1)} %equalize.2.refs_2_.refs_0_, bf16[2,256,256]{2,1,0:T(8,128)(2,1)S(1)} %get-tuple-element.36.refs_1_, bf16[2,256,256]{2,1,0:T(8,128)(2,1)S(1)} %collective-permute-done.6.refs_2_, bf16[2,256,256]{2,1,0:T(8,128)(2,1)S(1)} %collective-permute-done.7.refs_3_, ...), custom_call_target="tpu_custom_call" | custom-call | bytes 1024 | tf_op jit(solution)/shard_map/correlate/pallas_call | solution.py:413
  (3 shorter events, 0.1 us)
Async XLA Ops:
  0.0 8.4 %copy-start = (f32[128,128]{1,0:T(8,128)S(1)}, f32[128,128]{1,0:T(8,128)}, u32[]{:S(2)}) copy-start(f32[128,128]{1,0:T(8,128)} %constant.5.clone.pick_ref) | copy-start | bytes 196612
  0.0 8.4 %copy-start.1 = (f32[8,2,128]{2,1,0:T(2,128)S(1)}, f32[8,2,128]{2,1,0:T(2,128)}, u32[]{:S(2)}) copy-start(f32[8,2,128]{2,1,0:T(2,128)} %gains_ref.1) | copy-start | bytes 24580
  2.7 7.8 %collective-permute-start = (bf16[280,128]{1,0:T(8,128)(2,1)S(1)}, bf16[280,128]{1,0:T(8,128)(2,1)S(1)}, u32[]{:S(2)}, u32[]{:S(2)}) collective-permute-start(bf16[280,128]{1,0:T(8,128)(2,1)S(1)} %get-tuple-element.30), channel_id=1, source_target_pairs={{0,24},{8,16},{16,8},{24,0},{1,25},{9,17},{17,9},{25,1},{2,26},{10... | collective-permute-start | bytes 215048 | tf_op jit(solution)/shard_map/ppermute | solution.py:429
  7.8 8.2 %collective-permute-start.8 = (bf16[280,128]{1,0:T(8,128)(2,1)S(1)}, bf16[280,128]{1,0:T(8,128)(2,1)S(1)}, u32[]{:S(2)}, u32[]{:S(2)}) collective-permute-start(bf16[280,128]{1,0:T(8,128)(2,1)S(1)} %get-tuple-element.38), channel_id=1, source_target_pairs={{0,16},{8,24},{16,0},{24,8},{1,17},{9,25},{17,1},{25,9},{2,18},{10... | collective-permute-start | bytes 215048 | tf_op jit(solution)/shard_map/ppermute | solution.py:429
  7.8 8.2 %collective-permute-start.9 = (bf16[280,128]{1,0:T(8,128)(2,1)S(1)}, bf16[280,128]{1,0:T(8,128)(2,1)S(1)}, u32[]{:S(2)}, u32[]{:S(2)}) collective-permute-start(bf16[280,128]{1,0:T(8,128)(2,1)S(1)} %get-tuple-element.39), channel_id=1, source_target_pairs={{0,8},{8,0},{16,24},{24,16},{1,9},{9,1},{17,25},{25,17},{2,10},{10... | collective-permute-start | bytes 215048 | tf_op jit(solution)/shard_map/ppermute | solution.py:429
  9.1 20.5 %copy-start.2 = (s32[8,8]{1,0:T(8,128)S(1)}, s32[8,8]{1,0:T(8,128)}, u32[]{:S(2)}) copy-start(s32[8,8]{1,0:T(8,128)} %refs_5_.1) | copy-start | bytes 772
  10.5 8.5 %collective-permute-start.1 = (bf16[280,128]{1,0:T(8,128)(2,1)S(1)}, bf16[280,128]{1,0:T(8,128)(2,1)S(1)}, u32[]{:S(2)}, u32[]{:S(2)}) collective-permute-start(bf16[280,128]{1,0:T(8,128)(2,1)S(1)} %get-tuple-element.31), channel_id=1, source_target_pairs={{0,24},{8,16},{16,8},{24,0},{1,25},{9,17},{17,9},{25,1},{2,26},{10... | collective-permute-start | bytes 215048 | tf_op jit(solution)/shard_map/ppermute | solution.py:429
  14.8 5.8 %collective-permute-start.2 = (bf16[280,128]{1,0:T(8,128)(2,1)S(1)}, bf16[280,128]{1,0:T(8,128)(2,1)S(1)}, u32[]{:S(2)}, u32[]{:S(2)}) collective-permute-start(bf16[280,128]{1,0:T(8,128)(2,1)S(1)} %get-tuple-element.32), channel_id=1, source_target_pairs={{0,16},{8,24},{16,0},{24,8},{1,17},{9,25},{17,1},{25,9},{2,18},{10... | collective-permute-start | bytes 215048 | tf_op jit(solution)/shard_map/ppermute | solution.py:429
  15.0 5.6 %collective-permute-start.3 = (bf16[280,128]{1,0:T(8,128)(2,1)S(1)}, bf16[280,128]{1,0:T(8,128)(2,1)S(1)}, u32[]{:S(2)}, u32[]{:S(2)}) collective-permute-start(bf16[280,128]{1,0:T(8,128)(2,1)S(1)} %get-tuple-element.33), channel_id=1, source_target_pairs={{0,8},{8,0},{16,24},{24,16},{1,9},{9,1},{17,25},{25,17},{2,10},{10... | collective-permute-start | bytes 215048 | tf_op jit(solution)/shard_map/ppermute | solution.py:429
  16.5 8.2 %collective-permute-start.11 = (bf16[2,256,256]{2,1,0:T(8,128)(2,1)S(1)}, bf16[2,256,256]{2,1,0:T(8,128)(2,1)S(1)}, u32[]{:S(2)}, u32[]{:S(2)}) collective-permute-start(bf16[2,256,256]{2,1,0:T(8,128)(2,1)S(1)} %equalize.3.refs_0_), channel_id=1, source_target_pairs={{0,4},{1,3},{2,6},{3,1},{4,0},{5,7},{6,2},{7,5},{8,12},{9,11},{10,... | collective-permute-start | bytes 786440 | tf_op jit(solution)/shard_map/ppermute | solution.py:489
  17.5 9.1 %collective-permute-start.10 = (bf16[2,256,256]{2,1,0:T(8,128)(2,1)S(1)}, bf16[2,256,256]{2,1,0:T(8,128)(2,1)S(1)}, u32[]{:S(2)}, u32[]{:S(2)}) collective-permute-start(bf16[2,256,256]{2,1,0:T(8,128)(2,1)S(1)} %equalize.3.refs_0_), channel_id=1, source_target_pairs={{0,2},{1,5},{2,0},{3,7},{4,6},{5,1},{6,4},{7,3},{8,10},{9,13},{10,... | collective-permute-start | bytes 786440 | tf_op jit(solution)/shard_map/ppermute | solution.py:489
  21.1 8.1 %collective-permute-start.5 = (bf16[2,256,256]{2,1,0:T(8,128)(2,1)S(1)}, bf16[2,256,256]{2,1,0:T(8,128)(2,1)S(1)}, u32[]{:S(2)}, u32[]{:S(2)}) collective-permute-start(bf16[2,256,256]{2,1,0:T(8,128)(2,1)S(1)} %equalize.2.refs_2_.refs_0_), channel_id=1, source_target_pairs={{0,4},{1,3},{2,6},{3,1},{4,0},{5,7},{6,2},{7,5},{8,12},{9,11},{10,... | collective-permute-start | bytes 786440 | tf_op jit(solution)/shard_map/ppermute | solution.py:489
  22.7 6.8 %collective-permute-start.4 = (bf16[2,256,256]{2,1,0:T(8,128)(2,1)S(1)}, bf16[2,256,256]{2,1,0:T(8,128)(2,1)S(1)}, u32[]{:S(2)}, u32[]{:S(2)}) collective-permute-start(bf16[2,256,256]{2,1,0:T(8,128)(2,1)S(1)} %equalize.2.refs_2_.refs_0_), channel_id=1, source_target_pairs={{0,2},{1,5},{2,0},{3,7},{4,6},{5,1},{6,4},{7,3},{8,10},{9,13},{10,... | collective-permute-start | bytes 786440 | tf_op jit(solution)/shard_map/ppermute | solution.py:489
  24.2 5.4 %collective-permute-start.12 = (bf16[2,256,256]{2,1,0:T(8,128)(2,1)S(1)}, bf16[2,256,256]{2,1,0:T(8,128)(2,1)S(1)}, u32[]{:S(2)}, u32[]{:S(2)}) collective-permute-start(bf16[2,256,256]{2,1,0:T(8,128)(2,1)S(1)} %equalize.3.refs_0_), channel_id=1, source_target_pairs={{0,1},{1,0},{2,3},{3,2},{4,5},{5,4},{6,7},{7,6},{8,9},{9,8},{10,11... | collective-permute-start | bytes 786440 | tf_op jit(solution)/shard_map/ppermute | solution.py:517
  24.7 5.7 %collective-permute-start.6 = (bf16[2,256,256]{2,1,0:T(8,128)(2,1)S(1)}, bf16[2,256,256]{2,1,0:T(8,128)(2,1)S(1)}, u32[]{:S(2)}, u32[]{:S(2)}) collective-permute-start(bf16[2,256,256]{2,1,0:T(8,128)(2,1)S(1)} %equalize.2.refs_2_.refs_0_), channel_id=1, source_target_pairs={{0,1},{1,0},{2,3},{3,2},{4,5},{5,4},{6,7},{7,6},{8,9},{9,8},{10,11... | collective-permute-start | bytes 786440 | tf_op jit(solution)/shard_map/ppermute | solution.py:517
  26.6 3.0 %collective-permute-start.13 = (bf16[2,256,256]{2,1,0:T(8,128)(2,1)S(1)}, bf16[2,256,256]{2,1,0:T(8,128)(2,1)S(1)}, u32[]{:S(2)}, u32[]{:S(2)}) collective-permute-start(bf16[2,256,256]{2,1,0:T(8,128)(2,1)S(1)} %get-tuple-element.41.refs_1_), channel_id=1, source_target_pairs={{0,1},{1,0},{2,3},{3,2},{4,5},{5,4},{6,7},{7,6},{8,9},{9,8},{10,11... | collective-permute-start | bytes 786440 | tf_op jit(solution)/shard_map/ppermute | solution.py:523
  29.5 1.6 %collective-permute-start.7 = (bf16[2,256,256]{2,1,0:T(8,128)(2,1)S(1)}, bf16[2,256,256]{2,1,0:T(8,128)(2,1)S(1)}, u32[]{:S(2)}, u32[]{:S(2)}) collective-permute-start(bf16[2,256,256]{2,1,0:T(8,128)(2,1)S(1)} %get-tuple-element.36.refs_1_), channel_id=1, source_target_pairs={{0,1},{1,0},{2,3},{3,2},{4,5},{5,4},{6,7},{7,6},{8,9},{9,8},{10,11... | collective-permute-start | bytes 786440 | tf_op jit(solution)/shard_map/ppermute | solution.py:523

commit v12 on v11

--- a/solution.py
+++ b/solution.py
@@ -442,14 +442,6 @@
     )(*operands)
 
 
-def held_back(blocks, after):
-    def kernel(*refs):
-        for i in range(len(blocks)):
-            refs[len(blocks) + len(after) + i][...] = refs[i][...]
-
-    return copied(kernel, blocks, list(blocks) + list(after), "held_back")
-
-
 def sorted_by_core(first, second, after):
     count = len(first)
 
@@ -510,7 +502,7 @@
             pieces = next_part(part + 1, filt, tables, antenna_gains, owners)
             if part == 0:
                 *pieces, gains = pieces
-            later = to_owners([pieces[0], *held_back(pieces[1:], arrived[-1:])])
+            later = to_owners(pieces)
         own.append(equalize(arrived, gains, part, frames))
         panels.append(panel_permutes(own[part], n_row, n_col))
         arrived = later

time: 32.9 us -> 34.5 us (1.049)
  waiting for transfers between devices: 9.59 us -> 11.4 us
    ppermute x4, waiting for transfers between devices: 5.16 us -> 7.39 us  [panel_permutes(): results.append(lax.ppermute(block, axes, route))]
    ppermute x4, starting transfers between devices: 5.56 us -> 5.04 us  [panel_permutes(): results.append(lax.ppermute(block, axes, route))]
    ppermute x6, waiting for transfers between devices: 3.68 us -> 3.29 us  [to_owners(): lax.ppermute(pieces[d], 'chan', [(i, i ^ d) for i in range(owners)])]
  transfers between devices with their start and end apart: 14 -> 14, of which waited for: 8 -> 6; matrix products, arithmetic and copies ran while one was open for 0% -> 0% of each run, Pallas kernels for 7% -> 7%
where the time goes in v12:
time: 34.5 us; the launch traced here: 34.3 us
  starting transfers between devices  16.2 us (47%)
  waiting for transfers between devices  11.4 us (33%)
  Pallas kernels  6.61 us (19%)
    ppermute x6, starting transfers between devices, to_owners(): lax.ppermute(pieces[d], 'chan', [(i, i ^ d) for i in range(owners)])  11 us
    ppermute x4, waiting for transfers between devices, panel_permutes(): results.append(lax.ppermute(block, axes, route))  7.39 us
    ppermute x4, starting transfers between devices, panel_permutes(): results.append(lax.ppermute(block, axes, route))  5.04 us
    ppermute x6, waiting for transfers between devices, to_owners(): lax.ppermute(pieces[d], 'chan', [(i, i ^ d) for i in range(owners)])  3.29 us
    pallas_call x1, Pallas kernels, filtered_and_first(): pl.pallas_call(functools.partial(filter_kernel, frames, pieces, spectrum_...  2.65 us
    pallas_call x2, Pallas kernels, correlate(): pl.pallas_call(functools.partial(correlate_kernel, n_row, n_col, h, times...  2.36 us
    pallas_call x2, Pallas kernels, equalize(): pl.pallas_call(functools.partial(equalize_kernel, owners, frames, h, part...  0.9 us
    ppermute x2, waiting for transfers between devices, shards(): relayed = [lax.ppermute(block, 'bcol', other_core) for block in far]  0.74 us
  transfers between devices with their start and end apart: 14, of which 6 were waited for; matrix products, arithmetic and copies ran while one was open for 0% of the time, Pallas kernels for 7%

profile of v12, /device:TPU:0, one launch (start us, length us, event | category | flops | bytes accessed | tf_op | source)
XLA Modules:
  0.0 34.3 jit_solution(14168468681842186976)
XLA Ops:
  0.0 0.0 copy-start
  0.0 0.0 copy-start.1
  0.0 2.6 %filter_and_transform.1 = (bf16[280,128]{1,0:T(8,128)(2,1)S(1)}, bf16[280,128]{1,0:T(8,128)(2,1)S(1)}, bf16[280,128]{1,0:T(8,128)(2,1)S(1)}, bf16[280,128]{1,0:T...) custom-call(s32[2,8,32768]{2,1,0:T(8,128)} %volt_hbm.1, ...), custom_call_target="tpu_custom_call" | custom-call | flops 536870912 | bytes 4194304 | tf_op jit(solution)/shard_map/filter_and_transform/pallas_call | solution.py:178
  2.7 5.1 %collective-permute-start.7 = (bf16[280,128]{1,0:T(8,128)(2,1)S(1)}, bf16[280,128]{1,0:T(8,128)(2,1)S(1)}, u32[]{:S(2)}, u32[]{:S(2)}) collective-permute-start(bf16[280,128]{1,0:T(8,128)(2,1)S(1)} %get-tuple-element.31), channel_id=1, source_target_pairs={{0,24},{8,16},{16,8},{24,0},{1,25},{9,17},{17,9},{25,1},{2,26},{10... | collective-permute-start | bytes 215048 | tf_op jit(solution)/shard_map/ppermute | solution.py:429
  7.8 0.0 collective-permute-start.8
  7.8 0.6 %collective-permute-start.9 = (bf16[280,128]{1,0:T(8,128)(2,1)S(1)}, bf16[280,128]{1,0:T(8,128)(2,1)S(1)}, u32[]{:S(2)}, u32[]{:S(2)}) collective-permute-start(bf16[280,128]{1,0:T(8,128)(2,1)S(1)} %get-tuple-element.33), channel_id=1, source_target_pairs={{0,8},{8,0},{16,24},{24,16},{1,9},{9,1},{17,25},{25,17},{2,10},{10... | collective-permute-start | bytes 215048 | tf_op jit(solution)/shard_map/ppermute | solution.py:429
  8.4 0.0 copy-done
  8.4 0.0 copy-done.1
  8.4 0.0 copy-start.2
  8.4 0.6 %transform.1 = (bf16[280,128]{1,0:T(8,128)(2,1)S(1)}, bf16[280,128]{1,0:T(8,128)(2,1)S(1)}, bf16[280,128]{1,0:T(8,128)(2,1)S(1)}, bf16[280,128]{1,0:T(8,128)(2,1)S(1)}, f32[128,16]{1,0:T(8,128)S(1)}) custom-call(bf16[2,288,1024]{2,1,0:T(8,128)(2,1)S(1)} %get-tuple-element.22.filt, bf16[2048,256]{1,0:T(8,128)(2,1)S(1)} %get-tuple-element.23.later, ...), custom_call_target="tpu_custom_call" | custom-call | flops 536870912 | bytes 2097152 | tf_op jit(solution)/shard_map/transform/pallas_call | solution.py:214
  9.1 3.8 %collective-permute-start = (bf16[280,128]{1,0:T(8,128)(2,1)S(1)}, bf16[280,128]{1,0:T(8,128)(2,1)S(1)}, u32[]{:S(2)}, u32[]{:S(2)}) collective-permute-start(bf16[280,128]{1,0:T(8,128)(2,1)S(1)} %get-tuple-element.24), channel_id=1, source_target_pairs={{0,24},{8,16},{16,8},{24,0},{1,25},{9,17},{17,9},{25,1},{2,26},{10... | collective-permute-start | bytes 215048 | tf_op jit(solution)/shard_map/ppermute | solution.py:429
  12.9 0.0 collective-permute-start.1
  12.9 0.0 collective-permute-done.7.refs_0_
  12.9 1.4 %collective-permute-start.2 = (bf16[280,128]{1,0:T(8,128)(2,1)S(1)}, bf16[280,128]{1,0:T(8,128)(2,1)S(1)}, u32[]{:S(2)}, u32[]{:S(2)}) collective-permute-start(bf16[280,128]{1,0:T(8,128)(2,1)S(1)} %get-tuple-element.26), channel_id=1, source_target_pairs={{0,8},{8,0},{16,24},{24,16},{1,9},{9,1},{17,25},{25,17},{2,10},{10... | collective-permute-start | bytes 215048 | tf_op jit(solution)/shard_map/ppermute | solution.py:429
  14.3 3.3 %collective-permute-done.8.refs_1_ = bf16[280,128]{1,0:T(8,128)(2,1)S(1)} collective-permute-done((bf16[280,128]{1,0:T(8,128)(2,1)S(1)}, bf16[280,128]{1,0:T(8,128)(2,1)S(1)}, u32[]{:S(2)}, u32[]{:S(2)}) %collective-permute-start.8) | collective-permute-done | bytes 71712 | tf_op jit(solution)/shard_map/ppermute | solution.py:429
  17.5 0.0 collective-permute-done.9.refs_2_
  17.6 0.4 %equalize.3.refs_0_ = bf16[2,256,256]{2,1,0:T(8,128)(2,1)S(1)} custom-call(bf16[280,128]{1,0:T(8,128)(2,1)S(1)} %collective-permute-done.7.refs_0_, bf16[280,128]{1,0:T(8,128)(2,1)S(1)} %collective-permute-done.8.refs_1_, bf16[280,128]{1,0:T(8,128)(2,1)S(1)} %collective-permute-done.9.refs_2_, bf16[280,128]{1,0:T(8,128)(2,1)S(1)} %get-tuple-element.34.refs_3_, ...), custom_call_target="tpu_custom_call" | custom-call | bytes 1024 | tf_op jit(solution)/shard_map/equalize/pallas_call | solution.py:269
  18.0 1.3 %collective-permute-start.11 = (bf16[2,256,256]{2,1,0:T(8,128)(2,1)S(1)}, bf16[2,256,256]{2,1,0:T(8,128)(2,1)S(1)}, u32[]{:S(2)}, u32[]{:S(2)}) collective-permute-start(bf16[2,256,256]{2,1,0:T(8,128)(2,1)S(1)} %equalize.3.refs_0_), channel_id=1, source_target_pairs={{0,4},{1,3},{2,6},{3,1},{4,0},{5,7},{6,2},{7,5},{8,12},{9,11},{10,... | collective-permute-start | bytes 786440 | tf_op jit(solution)/shard_map/ppermute | solution.py:481
  19.3 1.5 %collective-permute-start.10 = (bf16[2,256,256]{2,1,0:T(8,128)(2,1)S(1)}, bf16[2,256,256]{2,1,0:T(8,128)(2,1)S(1)}, u32[]{:S(2)}, u32[]{:S(2)}) collective-permute-start(bf16[2,256,256]{2,1,0:T(8,128)(2,1)S(1)} %equalize.3.refs_0_), channel_id=1, source_target_pairs={{0,2},{1,5},{2,0},{3,7},{4,6},{5,1},{6,4},{7,3},{8,10},{9,13},{10,... | collective-permute-start | bytes 786440 | tf_op jit(solution)/shard_map/ppermute | solution.py:481
  20.8 0.0 collective-permute-done.refs_0_
  20.8 0.0 collective-permute-done.1.refs_1_
  20.8 0.0 collective-permute-done.2.refs_2_
  20.8 0.5 %equalize.2.refs_2_.refs_0_ = bf16[2,256,256]{2,1,0:T(8,128)(2,1)S(1)} custom-call(bf16[280,128]{1,0:T(8,128)(2,1)S(1)} %collective-permute-done.refs_0_, bf16[280,128]{1,0:T(8,128)(2,1)S(1)} %collective-permute-done.1.refs_1_, bf16[280,128]{1,0:T(8,128)(2,1)S(1)} %collective-permute-done.2.refs_2_, bf16[280,128]{1,0:T(8,128)(2,1)S(1)} %get-tuple-element.27.refs_3_, ...), custom_call_target="tpu_custom_call" | custom-call | bytes 1024 | tf_op jit(solution)/shard_map/equalize/pallas_call | solution.py:269
  21.3 0.8 %collective-permute-start.4 = (bf16[2,256,256]{2,1,0:T(8,128)(2,1)S(1)}, bf16[2,256,256]{2,1,0:T(8,128)(2,1)S(1)}, u32[]{:S(2)}, u32[]{:S(2)}) collective-permute-start(bf16[2,256,256]{2,1,0:T(8,128)(2,1)S(1)} %equalize.2.refs_2_.refs_0_), channel_id=1, source_target_pairs={{0,4},{1,3},{2,6},{3,1},{4,0},{5,7},{6,2},{7,5},{8,12},{9,11},{10,... | collective-permute-start | bytes 786440 | tf_op jit(solution)/shard_map/ppermute | solution.py:481
  22.0 1.5 %collective-permute-start.3 = (bf16[2,256,256]{2,1,0:T(8,128)(2,1)S(1)}, bf16[2,256,256]{2,1,0:T(8,128)(2,1)S(1)}, u32[]{:S(2)}, u32[]{:S(2)}) collective-permute-start(bf16[2,256,256]{2,1,0:T(8,128)(2,1)S(1)} %equalize.2.refs_2_.refs_0_), channel_id=1, source_target_pairs={{0,2},{1,5},{2,0},{3,7},{4,6},{5,1},{6,4},{7,3},{8,10},{9,13},{10,... | collective-permute-start | bytes 786440 | tf_op jit(solution)/shard_map/ppermute | solution.py:481
  23.5 0.0 collective-permute-start.12
  23.5 1.6 %collective-permute-done.11.refs_1_ = bf16[2,256,256]{2,1,0:T(8,128)(2,1)S(1)} collective-permute-done((bf16[2,256,256]{2,1,0:T(8,128)(2,1)S(1)}, bf16[2,256,256]{2,1,0:T(8,128)(2,1)S(1)}, u32[]{:S(2)}, u32[]{:S(2)}) %collective-permute-start.11) | collective-permute-done | bytes 262176 | tf_op jit(solution)/shard_map/ppermute | solution.py:481
  25.2 0.0 collective-permute-start.5
  25.2 3.1 %collective-permute-done.10.refs_0_ = bf16[2,256,256]{2,1,0:T(8,128)(2,1)S(1)} collective-permute-done((bf16[2,256,256]{2,1,0:T(8,128)(2,1)S(1)}, bf16[2,256,256]{2,1,0:T(8,128)(2,1)S(1)}, u32[]{:S(2)}, u32[]{:S(2)}) %collective-permute-start.10) | collective-permute-done | bytes 262176 | tf_op jit(solution)/shard_map/ppermute | solution.py:481
  28.3 0.1 collective-permute-start.13
  28.4 1.9 %collective-permute-done.4.refs_1_ = bf16[2,256,256]{2,1,0:T(8,128)(2,1)S(1)} collective-permute-done((bf16[2,256,256]{2,1,0:T(8,128)(2,1)S(1)}, bf16[2,256,256]{2,1,0:T(8,128)(2,1)S(1)}, u32[]{:S(2)}, u32[]{:S(2)}) %collective-permute-start.4) | collective-permute-done | bytes 262176 | tf_op jit(solution)/shard_map/ppermute | solution.py:481
  30.3 0.8 %collective-permute-done.3.refs_0_ = bf16[2,256,256]{2,1,0:T(8,128)(2,1)S(1)} collective-permute-done((bf16[2,256,256]{2,1,0:T(8,128)(2,1)S(1)}, bf16[2,256,256]{2,1,0:T(8,128)(2,1)S(1)}, u32[]{:S(2)}, u32[]{:S(2)}) %collective-permute-start.3) | collective-permute-done | bytes 262176 | tf_op jit(solution)/shard_map/ppermute | solution.py:481
  31.1 0.1 collective-permute-start.6
  31.2 0.0 collective-permute-done.12.refs_2_
  31.2 0.0 collective-permute-done.13.refs_3_
  31.2 0.0 copy-done.2
  31.2 0.7 %correlate.2 = (f32[2,2,4,32,128]{4,3,2,1,0:T(8,128)S(1)}, f32[2,4,8,128]{3,2,1,0:T(8,128)S(1)}) custom-call(bf16[2,256,256]{2,1,0:T(8,128)(2,1)S(1)} %equalize.3.refs_0_, bf16[2,256,256]{2,1,0:T(8,128)(2,1)S(1)} %get-tuple-element.35.refs_1_, bf16[2,256,256]{2,1,0:T(8,128)(2,1)S(1)} %collective-permute-done.12.refs_2_, ...), custom_call_target="tpu_custom_call" | custom-call | bytes 1024 | tf_op jit(solution)/shard_map/correlate/pallas_call | solution.py:413
  31.9 0.0 collective-permute-done.5.refs_2_
  31.9 0.7 %collective-permute-done.6.refs_3_ = bf16[2,256,256]{2,1,0:T(8,128)(2,1)S(1)} collective-permute-done((bf16[2,256,256]{2,1,0:T(8,128)(2,1)S(1)}, bf16[2,256,256]{2,1,0:T(8,128)(2,1)S(1)}, u32[]{:S(2)}, u32[]{:S(2)}) %collective-permute-start.6) | collective-permute-done | bytes 262176 | tf_op jit(solution)/shard_map/ppermute | solution.py:515
  32.7 1.6 %correlate.3 = f32[2,16,32,128]{3,2,1,0:T(8,128)} custom-call(bf16[2,256,256]{2,1,0:T(8,128)(2,1)S(1)} %equalize.2.refs_2_.refs_0_, bf16[2,256,256]{2,1,0:T(8,128)(2,1)S(1)} %get-tuple-element.29.refs_1_, bf16[2,256,256]{2,1,0:T(8,128)(2,1)S(1)} %collective-permute-done.5.refs_2_, bf16[2,256,256]{2,1,0:T(8,128)(2,1)S(1)} %collective-permute-done.6.refs_3_, ...), custom_call_target="tpu_custom_call" | custom-call | bytes 1024 | tf_op jit(solution)/shard_map/correlate/pallas_call | solution.py:413
  (2 shorter events, 0.1 us)
Async XLA Ops:
  0.0 8.4 %copy-start = (f32[128,128]{1,0:T(8,128)S(1)}, f32[128,128]{1,0:T(8,128)}, u32[]{:S(2)}) copy-start(f32[128,128]{1,0:T(8,128)} %constant.5.clone.pick_ref) | copy-start | bytes 196612
  0.0 8.4 %copy-start.1 = (f32[8,2,128]{2,1,0:T(2,128)S(1)}, f32[8,2,128]{2,1,0:T(2,128)}, u32[]{:S(2)}) copy-start(f32[8,2,128]{2,1,0:T(2,128)} %gains_ref.1) | copy-start | bytes 24580
  2.7 10.2 %collective-permute-start.7 = (bf16[280,128]{1,0:T(8,128)(2,1)S(1)}, bf16[280,128]{1,0:T(8,128)(2,1)S(1)}, u32[]{:S(2)}, u32[]{:S(2)}) collective-permute-start(bf16[280,128]{1,0:T(8,128)(2,1)S(1)} %get-tuple-element.31), channel_id=1, source_target_pairs={{0,24},{8,16},{16,8},{24,0},{1,25},{9,17},{17,9},{25,1},{2,26},{10... | collective-permute-start | bytes 215048 | tf_op jit(solution)/shard_map/ppermute | solution.py:429
  7.8 9.8 %collective-permute-start.8 = (bf16[280,128]{1,0:T(8,128)(2,1)S(1)}, bf16[280,128]{1,0:T(8,128)(2,1)S(1)}, u32[]{:S(2)}, u32[]{:S(2)}) collective-permute-start(bf16[280,128]{1,0:T(8,128)(2,1)S(1)} %get-tuple-element.32), channel_id=1, source_target_pairs={{0,16},{8,24},{16,0},{24,8},{1,17},{9,25},{17,1},{25,9},{2,18},{10... | collective-permute-start | bytes 215048 | tf_op jit(solution)/shard_map/ppermute | solution.py:429
  7.8 9.8 %collective-permute-start.9 = (bf16[280,128]{1,0:T(8,128)(2,1)S(1)}, bf16[280,128]{1,0:T(8,128)(2,1)S(1)}, u32[]{:S(2)}, u32[]{:S(2)}) collective-permute-start(bf16[280,128]{1,0:T(8,128)(2,1)S(1)} %get-tuple-element.33), channel_id=1, source_target_pairs={{0,8},{8,0},{16,24},{24,16},{1,9},{9,1},{17,25},{25,17},{2,10},{10... | collective-permute-start | bytes 215048 | tf_op jit(solution)/shard_map/ppermute | solution.py:429
  8.4 22.8 %copy-start.2 = (s32[8,8]{1,0:T(8,128)S(1)}, s32[8,8]{1,0:T(8,128)}, u32[]{:S(2)}) copy-start(s32[8,8]{1,0:T(8,128)} %refs_5_.1) | copy-start | bytes 772
  9.1 11.7 %collective-permute-start = (bf16[280,128]{1,0:T(8,128)(2,1)S(1)}, bf16[280,128]{1,0:T(8,128)(2,1)S(1)}, u32[]{:S(2)}, u32[]{:S(2)}) collective-permute-start(bf16[280,128]{1,0:T(8,128)(2,1)S(1)} %get-tuple-element.24), channel_id=1, source_target_pairs={{0,24},{8,16},{16,8},{24,0},{1,25},{9,17},{17,9},{25,1},{2,26},{10... | collective-permute-start | bytes 215048 | tf_op jit(solution)/shard_map/ppermute | solution.py:429
  12.9 7.9 %collective-permute-start.1 = (bf16[280,128]{1,0:T(8,128)(2,1)S(1)}, bf16[280,128]{1,0:T(8,128)(2,1)S(1)}, u32[]{:S(2)}, u32[]{:S(2)}) collective-permute-start(bf16[280,128]{1,0:T(8,128)(2,1)S(1)} %get-tuple-element.25), channel_id=1, source_target_pairs={{0,16},{8,24},{16,0},{24,8},{1,17},{9,25},{17,1},{25,9},{2,18},{10... | collective-permute-start | bytes 215048 | tf_op jit(solution)/shard_map/ppermute | solution.py:429
  12.9 7.9 %collective-permute-start.2 = (bf16[280,128]{1,0:T(8,128)(2,1)S(1)}, bf16[280,128]{1,0:T(8,128)(2,1)S(1)}, u32[]{:S(2)}, u32[]{:S(2)}) collective-permute-start(bf16[280,128]{1,0:T(8,128)(2,1)S(1)} %get-tuple-element.26), channel_id=1, source_target_pairs={{0,8},{8,0},{16,24},{24,16},{1,9},{9,1},{17,25},{25,17},{2,10},{10... | collective-permute-start | bytes 215048 | tf_op jit(solution)/shard_map/ppermute | solution.py:429
  18.0 7.2 %collective-permute-start.11 = (bf16[2,256,256]{2,1,0:T(8,128)(2,1)S(1)}, bf16[2,256,256]{2,1,0:T(8,128)(2,1)S(1)}, u32[]{:S(2)}, u32[]{:S(2)}) collective-permute-start(bf16[2,256,256]{2,1,0:T(8,128)(2,1)S(1)} %equalize.3.refs_0_), channel_id=1, source_target_pairs={{0,4},{1,3},{2,6},{3,1},{4,0},{5,7},{6,2},{7,5},{8,12},{9,11},{10,... | collective-permute-start | bytes 786440 | tf_op jit(solution)/shard_map/ppermute | solution.py:481
  19.3 8.9 %collective-permute-start.10 = (bf16[2,256,256]{2,1,0:T(8,128)(2,1)S(1)}, bf16[2,256,256]{2,1,0:T(8,128)(2,1)S(1)}, u32[]{:S(2)}, u32[]{:S(2)}) collective-permute-start(bf16[2,256,256]{2,1,0:T(8,128)(2,1)S(1)} %equalize.3.refs_0_), channel_id=1, source_target_pairs={{0,2},{1,5},{2,0},{3,7},{4,6},{5,1},{6,4},{7,3},{8,10},{9,13},{10,... | collective-permute-start | bytes 786440 | tf_op jit(solution)/shard_map/ppermute | solution.py:481
  21.3 9.0 %collective-permute-start.4 = (bf16[2,256,256]{2,1,0:T(8,128)(2,1)S(1)}, bf16[2,256,256]{2,1,0:T(8,128)(2,1)S(1)}, u32[]{:S(2)}, u32[]{:S(2)}) collective-permute-start(bf16[2,256,256]{2,1,0:T(8,128)(2,1)S(1)} %equalize.2.refs_2_.refs_0_), channel_id=1, source_target_pairs={{0,4},{1,3},{2,6},{3,1},{4,0},{5,7},{6,2},{7,5},{8,12},{9,11},{10,... | collective-permute-start | bytes 786440 | tf_op jit(solution)/shard_map/ppermute | solution.py:481
  22.0 9.0 %collective-permute-start.3 = (bf16[2,256,256]{2,1,0:T(8,128)(2,1)S(1)}, bf16[2,256,256]{2,1,0:T(8,128)(2,1)S(1)}, u32[]{:S(2)}, u32[]{:S(2)}) collective-permute-start(bf16[2,256,256]{2,1,0:T(8,128)(2,1)S(1)} %equalize.2.refs_2_.refs_0_), channel_id=1, source_target_pairs={{0,2},{1,5},{2,0},{3,7},{4,6},{5,1},{6,4},{7,3},{8,10},{9,13},{10,... | collective-permute-start | bytes 786440 | tf_op jit(solution)/shard_map/ppermute | solution.py:481
  23.5 7.6 %collective-permute-start.12 = (bf16[2,256,256]{2,1,0:T(8,128)(2,1)S(1)}, bf16[2,256,256]{2,1,0:T(8,128)(2,1)S(1)}, u32[]{:S(2)}, u32[]{:S(2)}) collective-permute-start(bf16[2,256,256]{2,1,0:T(8,128)(2,1)S(1)} %equalize.3.refs_0_), channel_id=1, source_target_pairs={{0,1},{1,0},{2,3},{3,2},{4,5},{5,4},{6,7},{7,6},{8,9},{9,8},{10,11... | collective-permute-start | bytes 786440 | tf_op jit(solution)/shard_map/ppermute | solution.py:509
  25.2 6.8 %collective-permute-start.5 = (bf16[2,256,256]{2,1,0:T(8,128)(2,1)S(1)}, bf16[2,256,256]{2,1,0:T(8,128)(2,1)S(1)}, u32[]{:S(2)}, u32[]{:S(2)}) collective-permute-start(bf16[2,256,256]{2,1,0:T(8,128)(2,1)S(1)} %equalize.2.refs_2_.refs_0_), channel_id=1, source_target_pairs={{0,1},{1,0},{2,3},{3,2},{4,5},{5,4},{6,7},{7,6},{8,9},{9,8},{10,11... | collective-permute-start | bytes 786440 | tf_op jit(solution)/shard_map/ppermute | solution.py:509
  28.3 2.9 %collective-permute-start.13 = (bf16[2,256,256]{2,1,0:T(8,128)(2,1)S(1)}, bf16[2,256,256]{2,1,0:T(8,128)(2,1)S(1)}, u32[]{:S(2)}, u32[]{:S(2)}) collective-permute-start(bf16[2,256,256]{2,1,0:T(8,128)(2,1)S(1)} %get-tuple-element.35.refs_1_), channel_id=1, source_target_pairs={{0,1},{1,0},{2,3},{3,2},{4,5},{5,4},{6,7},{7,6},{8,9},{9,8},{10,11... | collective-permute-start | bytes 786440 | tf_op jit(solution)/shard_map/ppermute | solution.py:515
  31.1 1.6 %collective-permute-start.6 = (bf16[2,256,256]{2,1,0:T(8,128)(2,1)S(1)}, bf16[2,256,256]{2,1,0:T(8,128)(2,1)S(1)}, u32[]{:S(2)}, u32[]{:S(2)}) collective-permute-start(bf16[2,256,256]{2,1,0:T(8,128)(2,1)S(1)} %get-tuple-element.29.refs_1_), channel_id=1, source_target_pairs={{0,1},{1,0},{2,3},{3,2},{4,5},{5,4},{6,7},{7,6},{8,9},{9,8},{10,11... | collective-permute-start | bytes 786440 | tf_op jit(solution)/shard_map/ppermute | solution.py:515

commit v13 on v11

--- a/solution.py
+++ b/solution.py
@@ -226,7 +226,7 @@
 def equalize_kernel(owners, frames, h, part, *refs):
     pieces = refs[owners - 1 :: -1]
     gains_ref, by_time, by_channel = refs[owners], refs[-2], refs[-1]
-    out_ref = refs[owners + 1]
+    out_ref = refs[-3]
     width = 4 * h
     own_rows = frames * SIG
     over = (TAPS - 1) * SIG
@@ -262,14 +262,14 @@
             out_ref[r, :, tile * LANES : (tile + 1) * LANES] = by_channel[r * 2 * tiles + tile].astype(jnp.bfloat16)
 
 
-def equalize(pieces, gains, part, frames):
+def equalize(pieces, gains, part, frames, after):
     owners = len(pieces)
     h = gains.shape[0] // PARTS // 2
     times = owners * frames
     return pl.pallas_call(
         functools.partial(equalize_kernel, owners, frames, h, part),
         out_shape=jax.ShapeDtypeStruct((2, h * SIG, 2 * times), jnp.bfloat16),
-        in_specs=[IN_VMEM] * (owners + 1),
+        in_specs=[IN_VMEM] * (owners + 1 + len(after)),
         out_specs=IN_VMEM,
         scratch_shapes=[
             pltpu.VMEM((times * SIG, LANES), jnp.float32),
@@ -278,7 +278,7 @@
         compiler_params=pltpu.CompilerParams(vmem_limit_bytes=VMEM_BYTES),
         cost_estimate=pl.CostEstimate(flops=0, bytes_accessed=1 << 10, transcendentals=0),
         name="equalize",
-    )(*pieces[::-1], gains)
+    )(*pieces[::-1], gains, *after)
 
 
 def row_places(col, n_col):
@@ -505,21 +505,22 @@
     own, panels = [], []
     arrived = to_owners(pieces)
     for part in range(PARTS):
-        later = None
         if part < PARTS - 1:
             pieces = next_part(part + 1, filt, tables, antenna_gains, owners)
             if part == 0:
                 *pieces, gains = pieces
-            later = to_owners([pieces[0], *held_back(pieces[1:], arrived[-1:])])
-        own.append(equalize(arrived, gains, part, frames))
-        panels.append(panel_permutes(own[part], n_row, n_col))
-        arrived = later
+        own.append(equalize(arrived, gains, part, frames, panels[-1][0] if part else []))
+        first, second, far, column = panel_permutes(own[part], n_row, n_col)
+        near_far, near_column = sorted_by_core(first, second, far + column)
+        panels.append((near_far + far, near_column + column))
+        if part < PARTS - 1:
+            arrived = to_owners([pieces[0], *held_back(pieces[1:], own[part:])])
     beside = [lax.ppermute(block, "bcol", other_core) for block in own]
     result = [tile_map]
     for part in range(PARTS):
-        first, second, far, column = panels[part]
-        near_far, near_column = sorted_by_core(first, second, own[-1:] + far + column)
-        far, column = near_far + far, near_column + column
+        far, column = panels[part]
+        if part < PARTS - 1:
+            far = list(held_back(far, own[-1:]))
         relayed = [lax.ppermute(block, "bcol", other_core) for block in far]
         blocks = [own[part]] + far + [beside[part]] + relayed + column
         result = correlate(blocks, result, part, n_row, n_col)

time: 32.9 us -> 37.9 us (1.15)
  waiting for transfers between devices: 9.59 us -> 16 us
  starting transfers between devices: 16.4 us -> 14.9 us
    ppermute x6, waiting for transfers between devices: 3.68 us -> 7.62 us  [to_owners(): lax.ppermute(pieces[d], 'chan', [(i, i ^ d) for i in range(owners)])]
    ppermute x4, waiting for transfers between devices: 5.16 us -> 7.66 us  [panel_permutes(): results.append(lax.ppermute(block, axes, route))]
    ppermute x4, starting transfers between devices: 5.56 us -> 4 us  [panel_permutes(): results.append(lax.ppermute(block, axes, route))]
    ppermute x2, starting transfers between devices: 0.02 us -> 0.57 us  [shards(): beside = [lax.ppermute(block, 'bcol', other_core) for block in own]]
    ppermute x6, starting transfers between devices: 10.7 us -> 10.2 us  [to_owners(): lax.ppermute(pieces[d], 'chan', [(i, i ^ d) for i in range(owners)])]
  transfers between devices with their start and end apart: 14 -> 14, of which waited for: 8 -> 7; matrix products, arithmetic and copies ran while one was open for 0% -> 0% of each run, Pallas kernels for 7% -> 4%
where the time goes in v13:
time: 37.9 us; the launch traced here: 37.7 us
  waiting for transfers between devices  16 us (42%)
  starting transfers between devices  14.9 us (39%)
  Pallas kernels  6.63 us (17%)
    ppermute x6, starting transfers between devices, to_owners(): lax.ppermute(pieces[d], 'chan', [(i, i ^ d) for i in range(owners)])  10.2 us
    ppermute x4, waiting for transfers between devices, panel_permutes(): results.append(lax.ppermute(block, axes, route))  7.66 us
    ppermute x6, waiting for transfers between devices, to_owners(): lax.ppermute(pieces[d], 'chan', [(i, i ^ d) for i in range(owners)])  7.62 us
    ppermute x4, starting transfers between devices, panel_permutes(): results.append(lax.ppermute(block, axes, route))  4 us
    pallas_call x1, Pallas kernels, filtered_and_first(): pl.pallas_call(functools.partial(filter_kernel, frames, pieces, spectrum_...  2.65 us
    pallas_call x2, Pallas kernels, correlate(): pl.pallas_call(functools.partial(correlate_kernel, n_row, n_col, h, times...  2.36 us
    pallas_call x2, Pallas kernels, equalize(): pl.pallas_call(functools.partial(equalize_kernel, owners, frames, h, part...  0.9 us
  transfers between devices with their start and end apart: 14, of which 7 were waited for; matrix products, arithmetic and copies ran while one was open for 0% of the time, Pallas kernels for 4%

profile of v13, /device:TPU:0, one launch (start us, length us, event | category | flops | bytes accessed | tf_op | source)
XLA Modules:
  0.0 37.7 jit_solution(14868216112123910606)
XLA Ops:
  0.0 0.0 copy-start
  0.0 0.0 copy-start.1
  0.0 2.6 %filter_and_transform.1 = (bf16[280,128]{1,0:T(8,128)(2,1)S(1)}, bf16[280,128]{1,0:T(8,128)(2,1)S(1)}, bf16[280,128]{1,0:T(8,128)(2,1)S(1)}, bf16[280,128]{1,0:T...) custom-call(s32[2,8,32768]{2,1,0:T(8,128)} %volt_hbm.1, ...), custom_call_target="tpu_custom_call" | custom-call | flops 536870912 | bytes 4194304 | tf_op jit(solution)/shard_map/filter_and_transform/pallas_call | solution.py:178
  2.7 5.1 %collective-permute-start = (bf16[280,128]{1,0:T(8,128)(2,1)S(1)}, bf16[280,128]{1,0:T(8,128)(2,1)S(1)}, u32[]{:S(2)}, u32[]{:S(2)}) collective-permute-start(bf16[280,128]{1,0:T(8,128)(2,1)S(1)} %get-tuple-element.30), channel_id=1, source_target_pairs={{0,24},{8,16},{16,8},{24,0},{1,25},{9,17},{17,9},{25,1},{2,26},{10... | collective-permute-start | bytes 215048 | tf_op jit(solution)/shard_map/ppermute | solution.py:429
  7.8 0.0 collective-permute-start.1
  7.8 0.6 %collective-permute-start.2 = (bf16[280,128]{1,0:T(8,128)(2,1)S(1)}, bf16[280,128]{1,0:T(8,128)(2,1)S(1)}, u32[]{:S(2)}, u32[]{:S(2)}) collective-permute-start(bf16[280,128]{1,0:T(8,128)(2,1)S(1)} %get-tuple-element.32), channel_id=1, source_target_pairs={{0,8},{8,0},{16,24},{24,16},{1,9},{9,1},{17,25},{25,17},{2,10},{10... | collective-permute-start | bytes 215048 | tf_op jit(solution)/shard_map/ppermute | solution.py:429
  8.4 0.0 copy-done
  8.4 0.0 copy-done.1
  8.4 0.6 %transform.1 = (bf16[280,128]{1,0:T(8,128)(2,1)S(1)}, bf16[280,128]{1,0:T(8,128)(2,1)S(1)}, bf16[280,128]{1,0:T(8,128)(2,1)S(1)}, bf16[280,128]{1,0:T(8,128)(2,1)S(1)}, f32[128,16]{1,0:T(8,128)S(1)}) custom-call(bf16[2,288,1024]{2,1,0:T(8,128)(2,1)S(1)} %get-tuple-element.25.filt, bf16[2048,256]{1,0:T(8,128)(2,1)S(1)} %get-tuple-element.26.later, ...), custom_call_target="tpu_custom_call" | custom-call | flops 536870912 | bytes 2097152 | tf_op jit(solution)/shard_map/transform/pallas_call | solution.py:214
  9.1 0.0 copy-start.2
  9.1 1.4 %collective-permute-done.refs_0_ = bf16[280,128]{1,0:T(8,128)(2,1)S(1)} collective-permute-done((bf16[280,128]{1,0:T(8,128)(2,1)S(1)}, bf16[280,128]{1,0:T(8,128)(2,1)S(1)}, u32[]{:S(2)}, u32[]{:S(2)}) %collective-permute-start) | collective-permute-done | bytes 71712 | tf_op jit(solution)/shard_map/ppermute | solution.py:429
  10.5 3.4 %collective-permute-done.1.refs_1_ = bf16[280,128]{1,0:T(8,128)(2,1)S(1)} collective-permute-done((bf16[280,128]{1,0:T(8,128)(2,1)S(1)}, bf16[280,128]{1,0:T(8,128)(2,1)S(1)}, u32[]{:S(2)}, u32[]{:S(2)}) %collective-permute-start.1) | collective-permute-done | bytes 71712 | tf_op jit(solution)/shard_map/ppermute | solution.py:429
  13.8 0.0 collective-permute-done.2.refs_2_
  13.8 0.4 %equalize.2.refs_3_.refs_0_ = bf16[2,256,256]{2,1,0:T(8,128)(2,1)S(1)} custom-call(bf16[280,128]{1,0:T(8,128)(2,1)S(1)} %collective-permute-done.refs_0_, bf16[280,128]{1,0:T(8,128)(2,1)S(1)} %collective-permute-done.1.refs_1_, bf16[280,128]{1,0:T(8,128)(2,1)S(1)} %collective-permute-done.2.refs_2_, bf16[280,128]{1,0:T(8,128)(2,1)S(1)} %get-tuple-element.33.refs_3_, ...), custom_call_target="tpu_custom_call" | custom-call | bytes 1024 | tf_op jit(solution)/shard_map/equalize/pallas_call | solution.py:269
  14.3 1.6 %collective-permute-start.7 = (bf16[2,256,256]{2,1,0:T(8,128)(2,1)S(1)}, bf16[2,256,256]{2,1,0:T(8,128)(2,1)S(1)}, u32[]{:S(2)}, u32[]{:S(2)}) collective-permute-start(bf16[2,256,256]{2,1,0:T(8,128)(2,1)S(1)} %equalize.2.refs_3_.refs_0_), channel_id=1, source_target_pairs={{0,4},{1,3},{2,6},{3,1},{4,0},{5,7},{6,2},{7,5},{8,12},{9,11},{10,... | collective-permute-start | bytes 786440 | tf_op jit(solution)/shard_map/ppermute | solution.py:489
  15.9 1.5 %collective-permute-start.6 = (bf16[2,256,256]{2,1,0:T(8,128)(2,1)S(1)}, bf16[2,256,256]{2,1,0:T(8,128)(2,1)S(1)}, u32[]{:S(2)}, u32[]{:S(2)}) collective-permute-start(bf16[2,256,256]{2,1,0:T(8,128)(2,1)S(1)} %equalize.2.refs_3_.refs_0_), channel_id=1, source_target_pairs={{0,2},{1,5},{2,0},{3,7},{4,6},{5,1},{6,4},{7,3},{8,10},{9,13},{10,... | collective-permute-start | bytes 786440 | tf_op jit(solution)/shard_map/ppermute | solution.py:489
  17.4 2.8 %collective-permute-start.3 = (bf16[280,128]{1,0:T(8,128)(2,1)S(1)}, bf16[280,128]{1,0:T(8,128)(2,1)S(1)}, u32[]{:S(2)}, u32[]{:S(2)}) collective-permute-start(bf16[280,128]{1,0:T(8,128)(2,1)S(1)} %get-tuple-element.35), channel_id=1, source_target_pairs={{0,24},{8,16},{16,8},{24,0},{1,25},{9,17},{17,9},{25,1},{2,26},{10... | collective-permute-start | bytes 215048 | tf_op jit(solution)/shard_map/ppermute | solution.py:429
  20.2 0.0 collective-permute-start.4
  20.2 1.7 %collective-permute-start.5 = (bf16[280,128]{1,0:T(8,128)(2,1)S(1)}, bf16[280,128]{1,0:T(8,128)(2,1)S(1)}, u32[]{:S(2)}, u32[]{:S(2)}) collective-permute-start(bf16[280,128]{1,0:T(8,128)(2,1)S(1)} %get-tuple-element.37), channel_id=1, source_target_pairs={{0,8},{8,0},{16,24},{24,16},{1,9},{9,1},{17,25},{25,17},{2,10},{10... | collective-permute-start | bytes 215048 | tf_op jit(solution)/shard_map/ppermute | solution.py:429
  21.9 1.7 %collective-permute-done.7.refs_1_ = bf16[2,256,256]{2,1,0:T(8,128)(2,1)S(1)} collective-permute-done((bf16[2,256,256]{2,1,0:T(8,128)(2,1)S(1)}, bf16[2,256,256]{2,1,0:T(8,128)(2,1)S(1)}, u32[]{:S(2)}, u32[]{:S(2)}) %collective-permute-start.7) | collective-permute-done | bytes 262176 | tf_op jit(solution)/shard_map/ppermute | solution.py:489
  23.5 0.0 collective-permute-done.6.refs_0_
  23.6 0.6 %collective-permute-done.3.refs_0_ = bf16[280,128]{1,0:T(8,128)(2,1)S(1)} collective-permute-done((bf16[280,128]{1,0:T(8,128)(2,1)S(1)}, bf16[280,128]{1,0:T(8,128)(2,1)S(1)}, u32[]{:S(2)}, u32[]{:S(2)}) %collective-permute-start.3) | collective-permute-done | bytes 71712 | tf_op jit(solution)/shard_map/ppermute | solution.py:429
  24.2 2.3 %collective-permute-done.4.refs_1_ = bf16[280,128]{1,0:T(8,128)(2,1)S(1)} collective-permute-done((bf16[280,128]{1,0:T(8,128)(2,1)S(1)}, bf16[280,128]{1,0:T(8,128)(2,1)S(1)}, u32[]{:S(2)}, u32[]{:S(2)}) %collective-permute-start.4) | collective-permute-done | bytes 71712 | tf_op jit(solution)/shard_map/ppermute | solution.py:429
  26.4 0.0 collective-permute-done.5.refs_2_
  26.4 0.4 %equalize.3.refs_1_.refs_0_ = bf16[2,256,256]{2,1,0:T(8,128)(2,1)S(1)} custom-call(bf16[280,128]{1,0:T(8,128)(2,1)S(1)} %collective-permute-done.3.refs_0_, bf16[280,128]{1,0:T(8,128)(2,1)S(1)} %collective-permute-done.4.refs_1_, bf16[280,128]{1,0:T(8,128)(2,1)S(1)} %collective-permute-done.5.refs_2_, bf16[280,128]{1,0:T(8,128)(2,1)S(1)} %get-tuple-element.38.refs_3_, ...), custom_call_target="tpu_custom_call" | custom-call | bytes 1024 | tf_op jit(solution)/shard_map/equalize/pallas_call | solution.py:269
  26.9 0.6 %collective-permute-start.9 = (bf16[2,256,256]{2,1,0:T(8,128)(2,1)S(1)}, bf16[2,256,256]{2,1,0:T(8,128)(2,1)S(1)}, u32[]{:S(2)}, u32[]{:S(2)}) collective-permute-start(bf16[2,256,256]{2,1,0:T(8,128)(2,1)S(1)} %equalize.3.refs_1_.refs_0_), channel_id=1, source_target_pairs={{0,4},{1,3},{2,6},{3,1},{4,0},{5,7},{6,2},{7,5},{8,12},{9,11},{10,... | collective-permute-start | bytes 786440 | tf_op jit(solution)/shard_map/ppermute | solution.py:489
  27.5 0.4 collective-permute-start.8
  27.8 0.0 collective-permute-start.12
  27.8 0.6 %collective-permute-start.10 = (bf16[2,256,256]{2,1,0:T(8,128)(2,1)S(1)}, bf16[2,256,256]{2,1,0:T(8,128)(2,1)S(1)}, u32[]{:S(2)}, u32[]{:S(2)}) collective-permute-start(bf16[2,256,256]{2,1,0:T(8,128)(2,1)S(1)} %equalize.3.refs_1_.refs_0_), channel_id=1, source_target_pairs={{0,1},{1,0},{2,3},{3,2},{4,5},{5,4},{6,7},{7,6},{8,9},{9,8},{10,11... | collective-permute-start | bytes 786440 | tf_op jit(solution)/shard_map/ppermute | solution.py:518
  28.4 0.1 collective-permute-start.13
  28.5 6.0 %collective-permute-done.9.refs_1_ = bf16[2,256,256]{2,1,0:T(8,128)(2,1)S(1)} collective-permute-done((bf16[2,256,256]{2,1,0:T(8,128)(2,1)S(1)}, bf16[2,256,256]{2,1,0:T(8,128)(2,1)S(1)}, u32[]{:S(2)}, u32[]{:S(2)}) %collective-permute-start.9) | collective-permute-done | bytes 262176 | tf_op jit(solution)/shard_map/ppermute | solution.py:489
  34.5 0.0 collective-permute-done.8.refs_0_
  34.5 0.1 collective-permute-start.11
  34.6 0.0 collective-permute-done.12.refs_2_
  34.6 0.0 collective-permute-done.13.refs_3_
  34.6 0.0 copy-done.2
  34.6 0.7 %correlate.2 = (f32[2,2,4,32,128]{4,3,2,1,0:T(8,128)S(1)}, f32[2,4,8,128]{3,2,1,0:T(8,128)S(1)}) custom-call(bf16[2,256,256]{2,1,0:T(8,128)(2,1)S(1)} %equalize.2.refs_3_.refs_0_, bf16[2,256,256]{2,1,0:T(8,128)(2,1)S(1)} %held_back.3.refs_1_, bf16[2,256,256]{2,1,0:T(8,128)(2,1)S(1)} %collective-permute-done.12.refs_2_, ...), custom_call_target="tpu_custom_call" | custom-call | bytes 1024 | tf_op jit(solution)/shard_map/correlate/pallas_call | solution.py:413
  35.4 0.0 collective-permute-done.10.refs_2_
  35.4 0.7 %collective-permute-done.11.refs_3_ = bf16[2,256,256]{2,1,0:T(8,128)(2,1)S(1)} collective-permute-done((bf16[2,256,256]{2,1,0:T(8,128)(2,1)S(1)}, bf16[2,256,256]{2,1,0:T(8,128)(2,1)S(1)}, u32[]{:S(2)}, u32[]{:S(2)}) %collective-permute-start.11) | collective-permute-done | bytes 262176 | tf_op jit(solution)/shard_map/ppermute | solution.py:524
  36.1 1.6 %correlate.3 = f32[2,16,32,128]{3,2,1,0:T(8,128)} custom-call(bf16[2,256,256]{2,1,0:T(8,128)(2,1)S(1)} %equalize.3.refs_1_.refs_0_, bf16[2,256,256]{2,1,0:T(8,128)(2,1)S(1)} %get-tuple-element.40.refs_1_, bf16[2,256,256]{2,1,0:T(8,128)(2,1)S(1)} %collective-permute-done.10.refs_2_, bf16[2,256,256]{2,1,0:T(8,128)(2,1)S(1)} %collective-permute-done.11.refs_3_, ...), custom_call_target="tpu_custom_call" | custom-call | bytes 1024 | tf_op jit(solution)/shard_map/correlate/pallas_call | solution.py:413
  (4 shorter events, 0.1 us)
Async XLA Ops:
  0.0 8.4 %copy-start = (f32[128,128]{1,0:T(8,128)S(1)}, f32[128,128]{1,0:T(8,128)}, u32[]{:S(2)}) copy-start(f32[128,128]{1,0:T(8,128)} %constant.5.clone.pick_ref) | copy-start | bytes 196612
  0.0 8.4 %copy-start.1 = (f32[8,2,128]{2,1,0:T(2,128)S(1)}, f32[8,2,128]{2,1,0:T(2,128)}, u32[]{:S(2)}) copy-start(f32[8,2,128]{2,1,0:T(2,128)} %gains_ref.1) | copy-start | bytes 24580
  2.7 7.8 %collective-permute-start = (bf16[280,128]{1,0:T(8,128)(2,1)S(1)}, bf16[280,128]{1,0:T(8,128)(2,1)S(1)}, u32[]{:S(2)}, u32[]{:S(2)}) collective-permute-start(bf16[280,128]{1,0:T(8,128)(2,1)S(1)} %get-tuple-element.30), channel_id=1, source_target_pairs={{0,24},{8,16},{16,8},{24,0},{1,25},{9,17},{17,9},{25,1},{2,26},{10... | collective-permute-start | bytes 215048 | tf_op jit(solution)/shard_map/ppermute | solution.py:429
  7.8 6.1 %collective-permute-start.1 = (bf16[280,128]{1,0:T(8,128)(2,1)S(1)}, bf16[280,128]{1,0:T(8,128)(2,1)S(1)}, u32[]{:S(2)}, u32[]{:S(2)}) collective-permute-start(bf16[280,128]{1,0:T(8,128)(2,1)S(1)} %get-tuple-element.31), channel_id=1, source_target_pairs={{0,16},{8,24},{16,0},{24,8},{1,17},{9,25},{17,1},{25,9},{2,18},{10... | collective-permute-start | bytes 215048 | tf_op jit(solution)/shard_map/ppermute | solution.py:429
  7.8 6.1 %collective-permute-start.2 = (bf16[280,128]{1,0:T(8,128)(2,1)S(1)}, bf16[280,128]{1,0:T(8,128)(2,1)S(1)}, u32[]{:S(2)}, u32[]{:S(2)}) collective-permute-start(bf16[280,128]{1,0:T(8,128)(2,1)S(1)} %get-tuple-element.32), channel_id=1, source_target_pairs={{0,8},{8,0},{16,24},{24,16},{1,9},{9,1},{17,25},{25,17},{2,10},{10... | collective-permute-start | bytes 215048 | tf_op jit(solution)/shard_map/ppermute | solution.py:429
  9.1 25.6 %copy-start.2 = (s32[8,8]{1,0:T(8,128)S(1)}, s32[8,8]{1,0:T(8,128)}, u32[]{:S(2)}) copy-start(s32[8,8]{1,0:T(8,128)} %refs_5_.1) | copy-start | bytes 772
  14.3 9.2 %collective-permute-start.7 = (bf16[2,256,256]{2,1,0:T(8,128)(2,1)S(1)}, bf16[2,256,256]{2,1,0:T(8,128)(2,1)S(1)}, u32[]{:S(2)}, u32[]{:S(2)}) collective-permute-start(bf16[2,256,256]{2,1,0:T(8,128)(2,1)S(1)} %equalize.2.refs_3_.refs_0_), channel_id=1, source_target_pairs={{0,4},{1,3},{2,6},{3,1},{4,0},{5,7},{6,2},{7,5},{8,12},{9,11},{10,... | collective-permute-start | bytes 786440 | tf_op jit(solution)/shard_map/ppermute | solution.py:489
  15.9 7.7 %collective-permute-start.6 = (bf16[2,256,256]{2,1,0:T(8,128)(2,1)S(1)}, bf16[2,256,256]{2,1,0:T(8,128)(2,1)S(1)}, u32[]{:S(2)}, u32[]{:S(2)}) collective-permute-start(bf16[2,256,256]{2,1,0:T(8,128)(2,1)S(1)} %equalize.2.refs_3_.refs_0_), channel_id=1, source_target_pairs={{0,2},{1,5},{2,0},{3,7},{4,6},{5,1},{6,4},{7,3},{8,10},{9,13},{10,... | collective-permute-start | bytes 786440 | tf_op jit(solution)/shard_map/ppermute | solution.py:489
  17.4 6.8 %collective-permute-start.3 = (bf16[280,128]{1,0:T(8,128)(2,1)S(1)}, bf16[280,128]{1,0:T(8,128)(2,1)S(1)}, u32[]{:S(2)}, u32[]{:S(2)}) collective-permute-start(bf16[280,128]{1,0:T(8,128)(2,1)S(1)} %get-tuple-element.35), channel_id=1, source_target_pairs={{0,24},{8,16},{16,8},{24,0},{1,25},{9,17},{17,9},{25,1},{2,26},{10... | collective-permute-start | bytes 215048 | tf_op jit(solution)/shard_map/ppermute | solution.py:429
  20.2 6.3 %collective-permute-start.4 = (bf16[280,128]{1,0:T(8,128)(2,1)S(1)}, bf16[280,128]{1,0:T(8,128)(2,1)S(1)}, u32[]{:S(2)}, u32[]{:S(2)}) collective-permute-start(bf16[280,128]{1,0:T(8,128)(2,1)S(1)} %get-tuple-element.36), channel_id=1, source_target_pairs={{0,16},{8,24},{16,0},{24,8},{1,17},{9,25},{17,1},{25,9},{2,18},{10... | collective-permute-start | bytes 215048 | tf_op jit(solution)/shard_map/ppermute | solution.py:429
  20.2 6.3 %collective-permute-start.5 = (bf16[280,128]{1,0:T(8,128)(2,1)S(1)}, bf16[280,128]{1,0:T(8,128)(2,1)S(1)}, u32[]{:S(2)}, u32[]{:S(2)}) collective-permute-start(bf16[280,128]{1,0:T(8,128)(2,1)S(1)} %get-tuple-element.37), channel_id=1, source_target_pairs={{0,8},{8,0},{16,24},{24,16},{1,9},{9,1},{17,25},{25,17},{2,10},{10... | collective-permute-start | bytes 215048 | tf_op jit(solution)/shard_map/ppermute | solution.py:429
  26.9 7.6 %collective-permute-start.9 = (bf16[2,256,256]{2,1,0:T(8,128)(2,1)S(1)}, bf16[2,256,256]{2,1,0:T(8,128)(2,1)S(1)}, u32[]{:S(2)}, u32[]{:S(2)}) collective-permute-start(bf16[2,256,256]{2,1,0:T(8,128)(2,1)S(1)} %equalize.3.refs_1_.refs_0_), channel_id=1, source_target_pairs={{0,4},{1,3},{2,6},{3,1},{4,0},{5,7},{6,2},{7,5},{8,12},{9,11},{10,... | collective-permute-start | bytes 786440 | tf_op jit(solution)/shard_map/ppermute | solution.py:489
  27.5 7.0 %collective-permute-start.8 = (bf16[2,256,256]{2,1,0:T(8,128)(2,1)S(1)}, bf16[2,256,256]{2,1,0:T(8,128)(2,1)S(1)}, u32[]{:S(2)}, u32[]{:S(2)}) collective-permute-start(bf16[2,256,256]{2,1,0:T(8,128)(2,1)S(1)} %equalize.3.refs_1_.refs_0_), channel_id=1, source_target_pairs={{0,2},{1,5},{2,0},{3,7},{4,6},{5,1},{6,4},{7,3},{8,10},{9,13},{10,... | collective-permute-start | bytes 786440 | tf_op jit(solution)/shard_map/ppermute | solution.py:489
  27.8 6.8 %collective-permute-start.12 = (bf16[2,256,256]{2,1,0:T(8,128)(2,1)S(1)}, bf16[2,256,256]{2,1,0:T(8,128)(2,1)S(1)}, u32[]{:S(2)}, u32[]{:S(2)}) collective-permute-start(bf16[2,256,256]{2,1,0:T(8,128)(2,1)S(1)} %equalize.2.refs_3_.refs_0_), channel_id=1, source_target_pairs={{0,1},{1,0},{2,3},{3,2},{4,5},{5,4},{6,7},{7,6},{8,9},{9,8},{10,11... | collective-permute-start | bytes 786440 | tf_op jit(solution)/shard_map/ppermute | solution.py:518
  27.8 7.5 %collective-permute-start.10 = (bf16[2,256,256]{2,1,0:T(8,128)(2,1)S(1)}, bf16[2,256,256]{2,1,0:T(8,128)(2,1)S(1)}, u32[]{:S(2)}, u32[]{:S(2)}) collective-permute-start(bf16[2,256,256]{2,1,0:T(8,128)(2,1)S(1)} %equalize.3.refs_1_.refs_0_), channel_id=1, source_target_pairs={{0,1},{1,0},{2,3},{3,2},{4,5},{5,4},{6,7},{7,6},{8,9},{9,8},{10,11... | collective-permute-start | bytes 786440 | tf_op jit(solution)/shard_map/ppermute | solution.py:518
  28.4 6.2 %collective-permute-start.13 = (bf16[2,256,256]{2,1,0:T(8,128)(2,1)S(1)}, bf16[2,256,256]{2,1,0:T(8,128)(2,1)S(1)}, u32[]{:S(2)}, u32[]{:S(2)}) collective-permute-start(bf16[2,256,256]{2,1,0:T(8,128)(2,1)S(1)} %held_back.3.refs_1_), channel_id=1, source_target_pairs={{0,1},{1,0},{2,3},{3,2},{4,5},{5,4},{6,7},{7,6},{8,9},{9,8},{10,11... | collective-permute-start | bytes 786440 | tf_op jit(solution)/shard_map/ppermute | solution.py:524
  34.5 1.6 %collective-permute-start.11 = (bf16[2,256,256]{2,1,0:T(8,128)(2,1)S(1)}, bf16[2,256,256]{2,1,0:T(8,128)(2,1)S(1)}, u32[]{:S(2)}, u32[]{:S(2)}) collective-permute-start(bf16[2,256,256]{2,1,0:T(8,128)(2,1)S(1)} %get-tuple-element.40.refs_1_), channel_id=1, source_target_pairs={{0,1},{1,0},{2,3},{3,2},{4,5},{5,4},{6,7},{7,6},{8,9},{9,8},{10,11... | collective-permute-start | bytes 786440 | tf_op jit(solution)/shard_map/ppermute | solution.py:524

commit v14 on v11

--- a/solution.py
+++ b/solution.py
@@ -306,32 +306,35 @@
     return v
 
 
-def correlate_kernel(n_row, n_col, h, times, part, dense, *refs):
-    row_blocks = refs[:n_col]
-    col_blocks = (refs[0],) + refs[n_col : n_col + n_row - 1]
-    last = part == PARTS - 1
-    given = refs[n_col + n_row - 1 :]
-    if part > 0:
-        earlier, keeps = given[:2]
-    if last:
-        out_hbm, chosen, out_ref, sems = refs[-4:]
+def correlate_kernel(stage, slots, n_row, n_col, h, times, dense, *refs):
+    row_blocks, col_blocks, refs = refs[: len(slots)], refs[len(slots) : len(slots) + n_row], refs[len(slots) + n_row :]
+    if stage == "first":
+        tile_map, out_ref, keeps, chosen = refs
+    elif stage == "middle":
+        earlier, keeps, out_ref, chosen = refs
     else:
-        out_ref, keeps_out, chosen = refs[-3:]
+        earlier, keeps, others, out_hbm, chosen, out_ref, sems = refs
     me_row, me_col = lax.axis_index("brow"), lax.axis_index("bcol")
     row_at, col_at = row_places(me_col, n_col), column_places(me_row, n_row)
     rows = BATCH * SIG
-    tiles = n_col * rows // LANES
+    width = len(slots) * rows
+    tiles = -(-width // LANES)
     steps = 2 * h // BATCH
-    if part == 0:
-        owned = given[0][...]
+    copies = []
+    if stage == "last":
+        for d in range(n_col):
+            if d not in slots:
+                where = pl.ds(pl.multiple_of(row_at[d] * SIG, SIG), SIG)
+                copies.append(pltpu.make_async_copy(others.at[:, :, where], out_hbm.at[:, :, where], sems.at[d]))
+                copies[-1].start()
+    if stage == "first":
+        owned = tile_map[...]
         first, second = (lax.broadcasted_iota(jnp.int32, owned.shape, axis) for axis in range(2))
         for e in range(n_row):
             for d in range(n_col):
                 here = (first == me_row * n_col + row_at[d]) & (second == col_at[e] * n_col + me_col)
                 found = jnp.max(jnp.where(here, (owned == 1).astype(jnp.float32), 0.0), axis=(0, 1), keepdims=True)
-                keeps_out[e, d] = jnp.broadcast_to(found * (1.0 / times), (SIG, LANES))
-    elif not last:
-        keeps_out[...] = keeps[...]
+                keeps[e, d] = jnp.broadcast_to(found * (1.0 / times), (SIG, LANES))
     index_in_batch = (lax.broadcasted_iota(jnp.int32, (SIG, LANES), 1) // SIG) % BATCH
 
     for step in range(steps):
@@ -344,81 +347,86 @@
         result = lax.dot_general(both, a, (((1,), (1,)), ((), ())), preferred_element_type=jnp.float32)
         for k in range(2 * n_row):
             for tile in range(tiles):
-                lanes = slice(tile * LANES, (tile + 1) * LANES)
+                lanes = slice(tile * LANES, min((tile + 1) * LANES, width))
+                count = lanes.stop - lanes.start
                 own = [result[k * rows + i * SIG : k * rows + (i + 1) * SIG, lanes] for i in range(BATCH)]
                 kept = own[0]
                 for i in range(1, BATCH):
-                    kept = jnp.where(index_in_batch == i, own[i], kept)
-                chosen[k * tiles + tile, pl.ds(step, SIG, stride=steps), :] = kept
-
-    copies = []
+                    kept = jnp.where(index_in_batch[:, :count] == i, own[i], kept)
+                chosen[k * tiles + tile, pl.ds(step, SIG, stride=steps), :count] = kept
+
     low = lax.broadcasted_iota(jnp.int32, (SIG, LANES), 1) < LANES // 2
     for q in range(2):
         for e in range(n_row):
-            for d in range(n_col):
-                if d % (LANES // rows) == 0:
-                    x = chosen[(q * n_row + e) * tiles + d * rows // LANES].T
-                start = d * rows % LANES
+            for slot, d in enumerate(slots):
+                if slot % (LANES // rows) == 0:
+                    x = chosen[(q * n_row + e) * tiles + slot * rows // LANES].T
+                start = slot * rows % LANES
                 v = [x[start + i * SIG : start + (i + 1) * SIG] for i in range(BATCH)]
-                if last:
-                    keep = keeps[e, d]
-                a_at = pl.ds(pl.multiple_of(row_at[d] * SIG, SIG), SIG)
                 mine = slice(d * SIG, (d + 1) * SIG)
+                if stage == "middle":
+                    a_at = pl.ds(pl.multiple_of(row_at[d] * SIG, SIG), SIG)
+                else:
+                    a_at = slice(slot * SIG, (slot + 1) * SIG)
                 if dense:
                     for g, w in enumerate(regroup(v)):
-                        if last:
+                        if stage == "first":
+                            out_ref[q, e, g, mine, :] = w
+                        else:
                             before = earlier[q, e, g, mine, :]
                             pair = [
                                 jnp.where(low, before, pltpu.roll(w, LANES // 2, axis=1)),
                                 jnp.where(low, pltpu.roll(before, LANES // 2, axis=1), w),
                             ]
                             for half in range(2):
-                                out_ref[q, col_at[e] * SIG + half * BATCH + g, a_at, :] = pair[half] * keep
-                        else:
-                            out_ref[q, e, g, mine, :] = w
+                                out_ref[q, col_at[e] * SIG + half * BATCH + g, a_at, :] = pair[half] * keeps[e, d]
                 else:
                     for s2 in range(SIG):
                         w = jnp.concatenate([each[:, s2 * steps : (s2 + 1) * steps] for each in v], axis=1)
-                        if part > 0:
+                        if stage == "first":
+                            out_ref[q, e, s2, mine, :] = w
+                        else:
                             w = jnp.concatenate([earlier[q, e, s2, mine, :], w], axis=1)
-                        if last:
-                            out_ref[q, col_at[e] * SIG + s2, a_at, :] = w * keep[:, : w.shape[1]]
-                        else:
-                            out_ref[q, e, s2, mine, :] = w
-            if last:
-                where = pl.ds(col_at[e] * SIG, SIG)
-                copy = pltpu.make_async_copy(out_ref.at[q, where], out_hbm.at[q, where], sems.at[q * n_row + e])
-                copy.start()
-                copies.append(copy)
+                            out_ref[q, col_at[e] * SIG + s2, a_at, :] = w * keeps[e, d][:, : w.shape[1]]
+            if stage == "last":
+                there = pl.ds(col_at[e] * SIG, SIG)
+                for slot, d in enumerate(slots):
+                    copy = pltpu.make_async_copy(
+                        out_ref.at[q, there, slice(slot * SIG, (slot + 1) * SIG)],
+                        out_hbm.at[q, there, pl.ds(pl.multiple_of(row_at[d] * SIG, SIG), SIG)],
+                        sems.at[n_col + (q * n_row + e) * len(slots) + slot],
+                    )
+                    copy.start()
+                    copies.append(copy)
     for copy in copies:
         copy.wait()
 
 
-def correlate(blocks, given, part, n_row, n_col):
-    h = blocks[0].shape[1] // SIG
-    times = blocks[0].shape[2] // 2
+def correlate(stage, slots, row_blocks, col_blocks, given, n_col):
+    n_row = len(col_blocks)
+    h = row_blocks[0].shape[1] // SIG
+    times = row_blocks[0].shape[2] // 2
     channels = 2 * h
-    dense = channels * 2 == LANES and PARTS == 2
-    operands = list(blocks) + list(given)
-    last = part == PARTS - 1
-    if last:
-        out_shape = (2, n_row * SIG, n_col * SIG, (part + 1) * channels)
-    elif dense:
-        out_shape = (2, n_row, SIG // 2, n_col * SIG, LANES)
-    else:
-        out_shape = (2, n_row, SIG, n_col * SIG, (part + 1) * channels)
-    shapes = [out_shape] if last else [out_shape, (n_row, n_col, SIG, LANES)]
-    in_last = [pltpu.VMEM(out_shape, jnp.float32), pltpu.SemaphoreType.DMA((2 * n_row,))]
-    kept = pltpu.VMEM((2 * n_row * n_col * BATCH * SIG // LANES, SIG * channels // BATCH, LANES), jnp.float32)
+    dense = channels * 2 == LANES
+    operands = [row_blocks[d] for d in slots] + list(col_blocks) + list(given)
+    shapes = [(2, n_row * SIG, n_col * SIG, 2 * channels)]
+    tiles = -(-len(slots) * BATCH * SIG // LANES)
+    scratch = [pltpu.VMEM((2 * n_row * tiles, SIG * channels // BATCH, LANES), jnp.float32)]
+    if stage == "first":
+        shapes = [(2, n_row, SIG // 2, n_col * SIG, LANES) if dense else (2, n_row, SIG, n_col * SIG, channels)]
+        shapes.append((n_row, n_col, SIG, LANES))
+    if stage == "last":
+        scratch.append(pltpu.VMEM((2, n_row * SIG, len(slots) * SIG, 2 * channels), jnp.float32))
+        scratch.append(pltpu.SemaphoreType.DMA((n_col + 2 * n_row * len(slots),)))
     return pl.pallas_call(
-        functools.partial(correlate_kernel, n_row, n_col, h, times, part, dense),
+        functools.partial(correlate_kernel, stage, slots, n_row, n_col, h, times, dense),
         out_shape=[jax.ShapeDtypeStruct(shape, jnp.float32) for shape in shapes],
         in_specs=[IN_VMEM] * len(operands),
-        out_specs=[IN_HBM] if last else [IN_VMEM] * len(shapes),
-        scratch_shapes=[kept] + (in_last if last else []),
+        out_specs=[IN_HBM] if stage == "last" else [IN_VMEM] * len(shapes),
+        scratch_shapes=scratch,
         compiler_params=pltpu.CompilerParams(vmem_limit_bytes=VMEM_BYTES),
         cost_estimate=pl.CostEstimate(flops=0, bytes_accessed=1 << 10, transcendentals=0),
-        name="correlate",
+        name="correlate_" + stage,
     )(*operands)
 
 
@@ -515,14 +523,20 @@
         panels.append(panel_permutes(own[part], n_row, n_col))
         arrived = later
     beside = [lax.ppermute(block, "bcol", other_core) for block in own]
-    result = [tile_map]
+    all_slots = tuple(range(n_col))
+    at_hand = tuple(range(n_col // 2 + 1))
+    given = [tile_map]
     for part in range(PARTS):
         first, second, far, column = panels[part]
         near_far, near_column = sorted_by_core(first, second, own[-1:] + far + column)
-        far, column = near_far + far, near_column + column
+        far, column = near_far + far, [own[part]] + near_column + column
         relayed = [lax.ppermute(block, "bcol", other_core) for block in far]
-        blocks = [own[part]] + far + [beside[part]] + relayed + column
-        result = correlate(blocks, result, part, n_row, n_col)
+        rows = [own[part]] + far + [beside[part]] + relayed
+        if part == 0:
+            given = correlate("first", all_slots, rows, column, given, n_col)
+        else:
+            middle = correlate("middle", at_hand, rows, column, given, n_col)
+            result = correlate("last", all_slots[len(at_hand) :], rows, column, list(given) + list(middle), n_col)
     return jnp.transpose(result[0], (3, 0, 1, 2))[None, None]
 
 

time: 32.9 us -> 32.8 us (level)
  waiting for transfers between devices: 9.59 us -> 8.37 us
  Pallas kernels: 6.61 us -> 7.25 us
  starting transfers between devices: 16.4 us -> 16.9 us
    ppermute x2, waiting for transfers between devices: 0.75 us -> 0.01 us  [shards(): relayed = [lax.ppermute(block, 'bcol', other_core) for block in far]]
    pallas_call x2 -> x3, Pallas kernels: 2.35 us -> 2.99 us  [correlate(): pl.pallas_call(functools.partial(correlate_kernel, stage, slots, n_row, n...]
    ppermute x4, waiting for transfers between devices: 5.16 us -> 4.68 us  [panel_permutes(): results.append(lax.ppermute(block, axes, route))]
    ppermute x2, starting transfers between devices: 0.02 us -> 0.5 us  [shards(): beside = [lax.ppermute(block, 'bcol', other_core) for block in own]]
  transfers between devices with their start and end apart: 14 -> 14, of which waited for: 8 -> 7; matrix products, arithmetic and copies ran while one was open for 0% -> 0% of each run, Pallas kernels for 7% -> 10%
where the time goes in v14:
time: 32.8 us; the launch traced here: 32.6 us
  starting transfers between devices  16.9 us (52%)
  waiting for transfers between devices  8.37 us (26%)
  Pallas kernels  7.25 us (22%)
    ppermute x6, starting transfers between devices, to_owners(): lax.ppermute(pieces[d], 'chan', [(i, i ^ d) for i in range(owners)])  10.7 us
    ppermute x4, starting transfers between devices, panel_permutes(): results.append(lax.ppermute(block, axes, route))  5.56 us
    ppermute x4, waiting for transfers between devices, panel_permutes(): results.append(lax.ppermute(block, axes, route))  4.68 us
    ppermute x6, waiting for transfers between devices, to_owners(): lax.ppermute(pieces[d], 'chan', [(i, i ^ d) for i in range(owners)])  3.68 us
    pallas_call x3, Pallas kernels, correlate(): pl.pallas_call(functools.partial(correlate_kernel, stage, slots, n_row, n...  2.99 us
    pallas_call x1, Pallas kernels, filtered_and_first(): pl.pallas_call(functools.partial(filter_kernel, frames, pieces, spectrum_...  2.65 us
    pallas_call x2, Pallas kernels, equalize(): pl.pallas_call(functools.partial(equalize_kernel, owners, frames, h, part...  0.9 us
  transfers between devices with their start and end apart: 14, of which 7 were waited for; matrix products, arithmetic and copies ran while one was open for 0% of the time, Pallas kernels for 10%

profile of v14, /device:TPU:0, one launch (start us, length us, event | category | flops | bytes accessed | tf_op | source)
XLA Modules:
  0.0 32.6 jit_solution(17587928074333083980)
XLA Ops:
  0.0 0.0 copy-start
  0.0 0.0 copy-start.1
  0.0 2.6 %filter_and_transform.1 = (bf16[280,128]{1,0:T(8,128)(2,1)S(1)}, bf16[280,128]{1,0:T(8,128)(2,1)S(1)}, bf16[280,128]{1,0:T(8,128)(2,1)S(1)}, bf16[280,128]{1,0:T...) custom-call(s32[2,8,32768]{2,1,0:T(8,128)} %volt_hbm.1, ...), custom_call_target="tpu_custom_call" | custom-call | flops 536870912 | bytes 4194304 | tf_op jit(solution)/shard_map/filter_and_transform/pallas_call | solution.py:178
  2.7 5.1 %collective-permute-start = (bf16[280,128]{1,0:T(8,128)(2,1)S(1)}, bf16[280,128]{1,0:T(8,128)(2,1)S(1)}, u32[]{:S(2)}, u32[]{:S(2)}) collective-permute-start(bf16[280,128]{1,0:T(8,128)(2,1)S(1)} %get-tuple-element.30), channel_id=1, source_target_pairs={{0,24},{8,16},{16,8},{24,0},{1,25},{9,17},{17,9},{25,1},{2,26},{10... | collective-permute-start | bytes 215048 | tf_op jit(solution)/shard_map/ppermute | solution.py:437
  7.8 0.0 collective-permute-start.7
  7.8 0.6 %collective-permute-start.8 = (bf16[280,128]{1,0:T(8,128)(2,1)S(1)}, bf16[280,128]{1,0:T(8,128)(2,1)S(1)}, u32[]{:S(2)}, u32[]{:S(2)}) collective-permute-start(bf16[280,128]{1,0:T(8,128)(2,1)S(1)} %get-tuple-element.39), channel_id=1, source_target_pairs={{0,8},{8,0},{16,24},{24,16},{1,9},{9,1},{17,25},{25,17},{2,10},{10... | collective-permute-start | bytes 215048 | tf_op jit(solution)/shard_map/ppermute | solution.py:437
  8.4 0.0 copy-done
  8.4 0.0 copy-done.1
  8.4 0.6 %transform.1 = (bf16[280,128]{1,0:T(8,128)(2,1)S(1)}, bf16[280,128]{1,0:T(8,128)(2,1)S(1)}, bf16[280,128]{1,0:T(8,128)(2,1)S(1)}, bf16[280,128]{1,0:T(8,128)(2,1)S(1)}, f32[128,16]{1,0:T(8,128)S(1)}) custom-call(bf16[2,288,1024]{2,1,0:T(8,128)(2,1)S(1)} %get-tuple-element.25.filt, bf16[2048,256]{1,0:T(8,128)(2,1)S(1)} %get-tuple-element.26.later, ...), custom_call_target="tpu_custom_call" | custom-call | flops 536870912 | bytes 2097152 | tf_op jit(solution)/shard_map/transform/pallas_call | solution.py:214
  9.1 0.0 copy-start.2
  9.1 1.4 %collective-permute-done.refs_3_.refs_0_ = bf16[280,128]{1,0:T(8,128)(2,1)S(1)} collective-permute-done((bf16[280,128]{1,0:T(8,128)(2,1)S(1)}, bf16[280,128]{1,0:T(8,128)(2,1)S(1)}, u32[]{:S(2)}, u32[]{:S(2)}) %collective-permute-start) | collective-permute-done | bytes 71712 | tf_op jit(solution)/shard_map/ppermute | solution.py:437
  10.5 4.3 %collective-permute-start.1 = (bf16[280,128]{1,0:T(8,128)(2,1)S(1)}, bf16[280,128]{1,0:T(8,128)(2,1)S(1)}, u32[]{:S(2)}, u32[]{:S(2)}) collective-permute-start(bf16[280,128]{1,0:T(8,128)(2,1)S(1)} %get-tuple-element.31), channel_id=1, source_target_pairs={{0,24},{8,16},{16,8},{24,0},{1,25},{9,17},{17,9},{25,1},{2,26},{10... | collective-permute-start | bytes 215048 | tf_op jit(solution)/shard_map/ppermute | solution.py:437
  14.8 0.3 collective-permute-start.2
  15.0 0.4 %collective-permute-start.3 = (bf16[280,128]{1,0:T(8,128)(2,1)S(1)}, bf16[280,128]{1,0:T(8,128)(2,1)S(1)}, u32[]{:S(2)}, u32[]{:S(2)}) collective-permute-start(bf16[280,128]{1,0:T(8,128)(2,1)S(1)} %get-tuple-element.33), channel_id=1, source_target_pairs={{0,8},{8,0},{16,24},{24,16},{1,9},{9,1},{17,25},{25,17},{2,10},{10... | collective-permute-start | bytes 215048 | tf_op jit(solution)/shard_map/ppermute | solution.py:437
  15.4 0.6 %collective-permute-done.7.refs_1_ = bf16[280,128]{1,0:T(8,128)(2,1)S(1)} collective-permute-done((bf16[280,128]{1,0:T(8,128)(2,1)S(1)}, bf16[280,128]{1,0:T(8,128)(2,1)S(1)}, u32[]{:S(2)}, u32[]{:S(2)}) %collective-permute-start.7) | collective-permute-done | bytes 71712 | tf_op jit(solution)/shard_map/ppermute | solution.py:437
  16.0 0.0 collective-permute-done.8.refs_2_
  16.0 0.4 %equalize.3.refs_0_.refs_4_ = bf16[2,256,256]{2,1,0:T(8,128)(2,1)S(1)} custom-call(bf16[280,128]{1,0:T(8,128)(2,1)S(1)} %collective-permute-done.refs_3_.refs_0_, bf16[280,128]{1,0:T(8,128)(2,1)S(1)} %collective-permute-done.7.refs_1_, bf16[280,128]{1,0:T(8,128)(2,1)S(1)} %collective-permute-done.8.refs_2_, bf16[280,128]{1,0:T(8,128)(2,1)S(1)} %get-tuple-element.40.refs_3_, ...), custom_call_target="tpu_custom_call" | custom-call | bytes 1024 | tf_op jit(solution)/shard_map/equalize/pallas_call | solution.py:269
  16.5 1.0 %collective-permute-start.10 = (bf16[2,256,256]{2,1,0:T(8,128)(2,1)S(1)}, bf16[2,256,256]{2,1,0:T(8,128)(2,1)S(1)}, u32[]{:S(2)}, u32[]{:S(2)}) collective-permute-start(bf16[2,256,256]{2,1,0:T(8,128)(2,1)S(1)} %equalize.3.refs_0_.refs_4_), channel_id=1, source_target_pairs={{0,4},{1,3},{2,6},{3,1},{4,0},{5,7},{6,2},{7,5},{8,12},{9,11},{10,... | collective-permute-start | bytes 786440 | tf_op jit(solution)/shard_map/ppermute | solution.py:497
  17.5 1.5 %collective-permute-start.9 = (bf16[2,256,256]{2,1,0:T(8,128)(2,1)S(1)}, bf16[2,256,256]{2,1,0:T(8,128)(2,1)S(1)}, u32[]{:S(2)}, u32[]{:S(2)}) collective-permute-start(bf16[2,256,256]{2,1,0:T(8,128)(2,1)S(1)} %equalize.3.refs_0_.refs_4_), channel_id=1, source_target_pairs={{0,2},{1,5},{2,0},{3,7},{4,6},{5,1},{6,4},{7,3},{8,10},{9,13},{10,... | collective-permute-start | bytes 786440 | tf_op jit(solution)/shard_map/ppermute | solution.py:497
  19.0 0.0 collective-permute-done.1.refs_0_
  19.0 1.7 %collective-permute-done.2.refs_1_ = bf16[280,128]{1,0:T(8,128)(2,1)S(1)} collective-permute-done((bf16[280,128]{1,0:T(8,128)(2,1)S(1)}, bf16[280,128]{1,0:T(8,128)(2,1)S(1)}, u32[]{:S(2)}, u32[]{:S(2)}) %collective-permute-start.2) | collective-permute-done | bytes 71712 | tf_op jit(solution)/shard_map/ppermute | solution.py:437
  20.6 0.0 collective-permute-done.3.refs_2_
  20.6 0.4 %equalize.2.refs_2_.refs_0_.refs_3_.refs_1_ = bf16[2,256,256]{2,1,0:T(8,128)(2,1)S(1)} custom-call(bf16[280,128]{1,0:T(8,128)(2,1)S(1)} %collective-permute-done.1.refs_0_, bf16[280,128]{1,0:T(8,128)(2,1)S(1)} %collective-permute-done.2.refs_1_, bf16[280,128]{1,0:T(8,128)(2,1)S(1)} %collective-permute-done.3.refs_2_, ...), custom_call_target="tpu_custom_call" | custom-call | bytes 1024 | tf_op jit(solution)/shard_map/equalize/pallas_call | solution.py:269
  21.1 1.6 %collective-permute-start.5 = (bf16[2,256,256]{2,1,0:T(8,128)(2,1)S(1)}, bf16[2,256,256]{2,1,0:T(8,128)(2,1)S(1)}, u32[]{:S(2)}, u32[]{:S(2)}) collective-permute-start(bf16[2,256,256]{2,1,0:T(8,128)(2,1)S(1)} %equalize.2.refs_2_.refs_0_.refs_3_.refs_1_), channel_id=1, source_target_pairs={{0,4},{1,3},{2,6},{3,1},{4,0},{5,7},{6,2},{7,5},{8,12},{9,11},{10,... | collective-permute-start | bytes 786440 | tf_op jit(solution)/shard_map/ppermute | solution.py:497
  22.7 1.5 %collective-permute-start.4 = (bf16[2,256,256]{2,1,0:T(8,128)(2,1)S(1)}, bf16[2,256,256]{2,1,0:T(8,128)(2,1)S(1)}, u32[]{:S(2)}, u32[]{:S(2)}) collective-permute-start(bf16[2,256,256]{2,1,0:T(8,128)(2,1)S(1)} %equalize.2.refs_2_.refs_0_.refs_3_.refs_1_), channel_id=1, source_target_pairs={{0,2},{1,5},{2,0},{3,7},{4,6},{5,1},{6,4},{7,3},{8,10},{9,13},{10,... | collective-permute-start | bytes 786440 | tf_op jit(solution)/shard_map/ppermute | solution.py:497
  24.2 0.0 collective-permute-start.11
  24.2 0.5 %collective-permute-done.10.refs_1_ = bf16[2,256,256]{2,1,0:T(8,128)(2,1)S(1)} collective-permute-done((bf16[2,256,256]{2,1,0:T(8,128)(2,1)S(1)}, bf16[2,256,256]{2,1,0:T(8,128)(2,1)S(1)}, u32[]{:S(2)}, u32[]{:S(2)}) %collective-permute-start.10) | collective-permute-done | bytes 262176 | tf_op jit(solution)/shard_map/ppermute | solution.py:497
  24.7 1.9 %collective-permute-done.9.refs_0_ = bf16[2,256,256]{2,1,0:T(8,128)(2,1)S(1)} collective-permute-done((bf16[2,256,256]{2,1,0:T(8,128)(2,1)S(1)}, bf16[2,256,256]{2,1,0:T(8,128)(2,1)S(1)}, u32[]{:S(2)}, u32[]{:S(2)}) %collective-permute-start.9) | collective-permute-done | bytes 262176 | tf_op jit(solution)/shard_map/ppermute | solution.py:497
  26.6 0.1 collective-permute-start.12
  26.6 0.5 %collective-permute-start.13 = (bf16[2,256,256]{2,1,0:T(8,128)(2,1)S(1)}, bf16[2,256,256]{2,1,0:T(8,128)(2,1)S(1)}, u32[]{:S(2)}, u32[]{:S(2)}) collective-permute-start(bf16[2,256,256]{2,1,0:T(8,128)(2,1)S(1)} %equalize.2.refs_2_.refs_0_.refs_3_.refs_1_), channel_id=1, source_target_pairs={{0,1},{1,0},{2,3},{3,2},{4,5},{5,4},{6,7},{7,6},{8,9},{9,8},{10,11... | collective-permute-start | bytes 786440 | tf_op jit(solution)/shard_map/ppermute | solution.py:525
  27.1 2.0 %collective-permute-done.5.refs_1_ = bf16[2,256,256]{2,1,0:T(8,128)(2,1)S(1)} collective-permute-done((bf16[2,256,256]{2,1,0:T(8,128)(2,1)S(1)}, bf16[2,256,256]{2,1,0:T(8,128)(2,1)S(1)}, u32[]{:S(2)}, u32[]{:S(2)}) %collective-permute-start.5) | collective-permute-done | bytes 262176 | tf_op jit(solution)/shard_map/ppermute | solution.py:497
  29.2 0.3 collective-permute-done.4.refs_0_
  29.5 0.1 collective-permute-start.6
  29.6 0.0 collective-permute-done.11.refs_2_
  29.6 0.0 collective-permute-done.12.refs_3_
  29.6 0.0 copy-done.2
  29.6 0.7 %correlate_first.1 = (f32[2,2,4,32,128]{4,3,2,1,0:T(8,128)S(1)}, f32[2,4,8,128]{3,2,1,0:T(8,128)S(1)}) custom-call(bf16[2,256,256]{2,1,0:T(8,128)(2,1)S(1)} %equalize.3.refs_0_.refs_4_, bf16[2,256,256]{2,1,0:T(8,128)(2,1)S(1)} %get-tuple-element.41.refs_1_, bf16[2,256,256]{2,1,0:T(8,128)(2,1)S(1)} %collective-permute-done.11.refs_2_, ...), custom_call_target="tpu_custom_call" | custom-call | bytes 1024 | tf_op jit(solution)/shard_map/correlate_first/pallas_call | solution.py:421
  30.3 0.0 collective-permute-done.13.refs_2_
  30.4 0.8 %correlate_middle.1.refs_5_ = f32[2,16,32,128]{3,2,1,0:T(8,128)S(1)} custom-call(bf16[2,256,256]{2,1,0:T(8,128)(2,1)S(1)} %equalize.2.refs_2_.refs_0_.refs_3_.refs_1_, bf16[2,256,256]{2,1,0:T(8,128)(2,1)S(1)} %get-tuple-element.36.refs_1_, bf16[2,256,256]{2,1,0:T(8,128)(2,1)S(1)} %collective-permute-done.13.refs_2_, ...), custom_call_target="tpu_custom_call" | custom-call | bytes 1024 | tf_op jit(solution)/shard_map/correlate_middle/pallas_call | solution.py:421
  31.2 0.0 collective-permute-done.6.refs_0_
  31.2 1.5 %correlate_last.1 = f32[2,16,32,128]{3,2,1,0:T(8,128)} custom-call(bf16[2,256,256]{2,1,0:T(8,128)(2,1)S(1)} %collective-permute-done.6.refs_0_, bf16[2,256,256]{2,1,0:T(8,128)(2,1)S(1)} %equalize.2.refs_2_.refs_0_.refs_3_.refs_1_, bf16[2,256,256]{2,1,0:T(8,128)(2,1)S(1)} %get-tuple-element.37.refs_4_.refs_2_, ...), custom_call_target="tpu_custom_call" | custom-call | bytes 1024 | tf_op jit(solution)/shard_map/correlate_last/pallas_call | solution.py:421
  (3 shorter events, 0.1 us)
Async XLA Ops:
  0.0 8.4 %copy-start = (f32[128,128]{1,0:T(8,128)S(1)}, f32[128,128]{1,0:T(8,128)}, u32[]{:S(2)}) copy-start(f32[128,128]{1,0:T(8,128)} %constant.5.clone.pick_ref) | copy-start | bytes 196612
  0.0 8.4 %copy-start.1 = (f32[8,2,128]{2,1,0:T(2,128)S(1)}, f32[8,2,128]{2,1,0:T(2,128)}, u32[]{:S(2)}) copy-start(f32[8,2,128]{2,1,0:T(2,128)} %gains_ref.1) | copy-start | bytes 24580
  2.7 7.8 %collective-permute-start = (bf16[280,128]{1,0:T(8,128)(2,1)S(1)}, bf16[280,128]{1,0:T(8,128)(2,1)S(1)}, u32[]{:S(2)}, u32[]{:S(2)}) collective-permute-start(bf16[280,128]{1,0:T(8,128)(2,1)S(1)} %get-tuple-element.30), channel_id=1, source_target_pairs={{0,24},{8,16},{16,8},{24,0},{1,25},{9,17},{17,9},{25,1},{2,26},{10... | collective-permute-start | bytes 215048 | tf_op jit(solution)/shard_map/ppermute | solution.py:437
  7.8 8.2 %collective-permute-start.7 = (bf16[280,128]{1,0:T(8,128)(2,1)S(1)}, bf16[280,128]{1,0:T(8,128)(2,1)S(1)}, u32[]{:S(2)}, u32[]{:S(2)}) collective-permute-start(bf16[280,128]{1,0:T(8,128)(2,1)S(1)} %get-tuple-element.38), channel_id=1, source_target_pairs={{0,16},{8,24},{16,0},{24,8},{1,17},{9,25},{17,1},{25,9},{2,18},{10... | collective-permute-start | bytes 215048 | tf_op jit(solution)/shard_map/ppermute | solution.py:437
  7.8 8.2 %collective-permute-start.8 = (bf16[280,128]{1,0:T(8,128)(2,1)S(1)}, bf16[280,128]{1,0:T(8,128)(2,1)S(1)}, u32[]{:S(2)}, u32[]{:S(2)}) collective-permute-start(bf16[280,128]{1,0:T(8,128)(2,1)S(1)} %get-tuple-element.39), channel_id=1, source_target_pairs={{0,8},{8,0},{16,24},{24,16},{1,9},{9,1},{17,25},{25,17},{2,10},{10... | collective-permute-start | bytes 215048 | tf_op jit(solution)/shard_map/ppermute | solution.py:437
  9.1 20.5 %copy-start.2 = (s32[8,8]{1,0:T(8,128)S(1)}, s32[8,8]{1,0:T(8,128)}, u32[]{:S(2)}) copy-start(s32[8,8]{1,0:T(8,128)} %refs_6_.1) | copy-start | bytes 772
  10.5 8.5 %collective-permute-start.1 = (bf16[280,128]{1,0:T(8,128)(2,1)S(1)}, bf16[280,128]{1,0:T(8,128)(2,1)S(1)}, u32[]{:S(2)}, u32[]{:S(2)}) collective-permute-start(bf16[280,128]{1,0:T(8,128)(2,1)S(1)} %get-tuple-element.31), channel_id=1, source_target_pairs={{0,24},{8,16},{16,8},{24,0},{1,25},{9,17},{17,9},{25,1},{2,26},{10... | collective-permute-start | bytes 215048 | tf_op jit(solution)/shard_map/ppermute | solution.py:437
  14.8 5.8 %collective-permute-start.2 = (bf16[280,128]{1,0:T(8,128)(2,1)S(1)}, bf16[280,128]{1,0:T(8,128)(2,1)S(1)}, u32[]{:S(2)}, u32[]{:S(2)}) collective-permute-start(bf16[280,128]{1,0:T(8,128)(2,1)S(1)} %get-tuple-element.32), channel_id=1, source_target_pairs={{0,16},{8,24},{16,0},{24,8},{1,17},{9,25},{17,1},{25,9},{2,18},{10... | collective-permute-start | bytes 215048 | tf_op jit(solution)/shard_map/ppermute | solution.py:437
  15.0 5.6 %collective-permute-start.3 = (bf16[280,128]{1,0:T(8,128)(2,1)S(1)}, bf16[280,128]{1,0:T(8,128)(2,1)S(1)}, u32[]{:S(2)}, u32[]{:S(2)}) collective-permute-start(bf16[280,128]{1,0:T(8,128)(2,1)S(1)} %get-tuple-element.33), channel_id=1, source_target_pairs={{0,8},{8,0},{16,24},{24,16},{1,9},{9,1},{17,25},{25,17},{2,10},{10... | collective-permute-start | bytes 215048 | tf_op jit(solution)/shard_map/ppermute | solution.py:437
  16.5 8.2 %collective-permute-start.10 = (bf16[2,256,256]{2,1,0:T(8,128)(2,1)S(1)}, bf16[2,256,256]{2,1,0:T(8,128)(2,1)S(1)}, u32[]{:S(2)}, u32[]{:S(2)}) collective-permute-start(bf16[2,256,256]{2,1,0:T(8,128)(2,1)S(1)} %equalize.3.refs_0_.refs_4_), channel_id=1, source_target_pairs={{0,4},{1,3},{2,6},{3,1},{4,0},{5,7},{6,2},{7,5},{8,12},{9,11},{10,... | collective-permute-start | bytes 786440 | tf_op jit(solution)/shard_map/ppermute | solution.py:497
  17.5 9.1 %collective-permute-start.9 = (bf16[2,256,256]{2,1,0:T(8,128)(2,1)S(1)}, bf16[2,256,256]{2,1,0:T(8,128)(2,1)S(1)}, u32[]{:S(2)}, u32[]{:S(2)}) collective-permute-start(bf16[2,256,256]{2,1,0:T(8,128)(2,1)S(1)} %equalize.3.refs_0_.refs_4_), channel_id=1, source_target_pairs={{0,2},{1,5},{2,0},{3,7},{4,6},{5,1},{6,4},{7,3},{8,10},{9,13},{10,... | collective-permute-start | bytes 786440 | tf_op jit(solution)/shard_map/ppermute | solution.py:497
  21.1 8.1 %collective-permute-start.5 = (bf16[2,256,256]{2,1,0:T(8,128)(2,1)S(1)}, bf16[2,256,256]{2,1,0:T(8,128)(2,1)S(1)}, u32[]{:S(2)}, u32[]{:S(2)}) collective-permute-start(bf16[2,256,256]{2,1,0:T(8,128)(2,1)S(1)} %equalize.2.refs_2_.refs_0_.refs_3_.refs_1_), channel_id=1, source_target_pairs={{0,4},{1,3},{2,6},{3,1},{4,0},{5,7},{6,2},{7,5},{8,12},{9,11},{10,... | collective-permute-start | bytes 786440 | tf_op jit(solution)/shard_map/ppermute | solution.py:497
  22.7 6.8 %collective-permute-start.4 = (bf16[2,256,256]{2,1,0:T(8,128)(2,1)S(1)}, bf16[2,256,256]{2,1,0:T(8,128)(2,1)S(1)}, u32[]{:S(2)}, u32[]{:S(2)}) collective-permute-start(bf16[2,256,256]{2,1,0:T(8,128)(2,1)S(1)} %equalize.2.refs_2_.refs_0_.refs_3_.refs_1_), channel_id=1, source_target_pairs={{0,2},{1,5},{2,0},{3,7},{4,6},{5,1},{6,4},{7,3},{8,10},{9,13},{10,... | collective-permute-start | bytes 786440 | tf_op jit(solution)/shard_map/ppermute | solution.py:497
  24.2 5.4 %collective-permute-start.11 = (bf16[2,256,256]{2,1,0:T(8,128)(2,1)S(1)}, bf16[2,256,256]{2,1,0:T(8,128)(2,1)S(1)}, u32[]{:S(2)}, u32[]{:S(2)}) collective-permute-start(bf16[2,256,256]{2,1,0:T(8,128)(2,1)S(1)} %equalize.3.refs_0_.refs_4_), channel_id=1, source_target_pairs={{0,1},{1,0},{2,3},{3,2},{4,5},{5,4},{6,7},{7,6},{8,9},{9,8},{10,11... | collective-permute-start | bytes 786440 | tf_op jit(solution)/shard_map/ppermute | solution.py:525
  26.6 3.0 %collective-permute-start.12 = (bf16[2,256,256]{2,1,0:T(8,128)(2,1)S(1)}, bf16[2,256,256]{2,1,0:T(8,128)(2,1)S(1)}, u32[]{:S(2)}, u32[]{:S(2)}) collective-permute-start(bf16[2,256,256]{2,1,0:T(8,128)(2,1)S(1)} %get-tuple-element.41.refs_1_), channel_id=1, source_target_pairs={{0,1},{1,0},{2,3},{3,2},{4,5},{5,4},{6,7},{7,6},{8,9},{9,8},{10,11... | collective-permute-start | bytes 786440 | tf_op jit(solution)/shard_map/ppermute | solution.py:533
  26.6 3.7 %collective-permute-start.13 = (bf16[2,256,256]{2,1,0:T(8,128)(2,1)S(1)}, bf16[2,256,256]{2,1,0:T(8,128)(2,1)S(1)}, u32[]{:S(2)}, u32[]{:S(2)}) collective-permute-start(bf16[2,256,256]{2,1,0:T(8,128)(2,1)S(1)} %equalize.2.refs_2_.refs_0_.refs_3_.refs_1_), channel_id=1, source_target_pairs={{0,1},{1,0},{2,3},{3,2},{4,5},{5,4},{6,7},{7,6},{8,9},{9,8},{10,11... | collective-permute-start | bytes 786440 | tf_op jit(solution)/shard_map/ppermute | solution.py:525
  29.5 1.7 %collective-permute-start.6 = (bf16[2,256,256]{2,1,0:T(8,128)(2,1)S(1)}, bf16[2,256,256]{2,1,0:T(8,128)(2,1)S(1)}, u32[]{:S(2)}, u32[]{:S(2)}) collective-permute-start(bf16[2,256,256]{2,1,0:T(8,128)(2,1)S(1)} %get-tuple-element.36.refs_1_), channel_id=1, source_target_pairs={{0,1},{1,0},{2,3},{3,2},{4,5},{5,4},{6,7},{7,6},{8,9},{9,8},{10,11... | collective-permute-start | bytes 786440 | tf_op jit(solution)/shard_map/ppermute | solution.py:533

commit v15 on v11

--- a/solution.py
+++ b/solution.py
@@ -468,7 +468,7 @@
     return list(both[:count]), list(both[count:])
 
 
-def panel_permutes(block, n_row, n_col):
+def panel_permutes(block, n_row, n_col, crossed):
     chips = n_col // 2
 
     def x_step(row, col, d):
@@ -481,15 +481,17 @@
     axes = ("brow", "bcol")
     first, second, far, column = [], [], [], []
     for d in range(1, max(chips, n_row)):
-        if d < min(chips, n_row):
+        if crossed and d < min(chips, n_row):
             for turn, results in ((0, first), (1, second)):
                 route = [
                     (row * n_col + col, (x_step if col % 2 == turn else y_step)(row, col, d)) for row, col in devices
                 ]
                 results.append(lax.ppermute(block, axes, route))
         else:
-            step, results = (x_step, far) if d < chips else (y_step, column)
-            results.append(lax.ppermute(block, axes, [(row * n_col + col, step(row, col, d)) for row, col in devices]))
+            for step, results, steps in ((x_step, far, chips), (y_step, column, n_row)):
+                if d < steps:
+                    route = [(row * n_col + col, step(row, col, d)) for row, col in devices]
+                    results.append(lax.ppermute(block, axes, route))
     return first, second, far, column
 
 
@@ -512,17 +514,20 @@
                 *pieces, gains = pieces
             later = to_owners([pieces[0], *held_back(pieces[1:], arrived[-1:])])
         own.append(equalize(arrived, gains, part, frames))
-        panels.append(panel_permutes(own[part], n_row, n_col))
+        panels.append(panel_permutes(own[part], n_row, n_col, part < PARTS - 1))
         arrived = later
-    beside = [lax.ppermute(block, "bcol", other_core) for block in own]
     result = [tile_map]
     for part in range(PARTS):
         first, second, far, column = panels[part]
-        near_far, near_column = sorted_by_core(first, second, own[-1:] + far + column)
-        far, column = near_far + far, near_column + column
+        if first:
+            near_far, near_column = sorted_by_core(first, second, own[-1:] + far + column)
+            far, column = near_far + far, near_column + column
+        mine = held_back(own[part : part + 1], far[:1])[0] if first else own[part]
+        beside = lax.ppermute(mine, "bcol", other_core)
         relayed = [lax.ppermute(block, "bcol", other_core) for block in far]
-        blocks = [own[part]] + far + [beside[part]] + relayed + column
-        result = correlate(blocks, result, part, n_row, n_col)
+        blocks = [own[part]] + far + [beside] + relayed + column
+        after = panels[-1][3] if part == 0 else []
+        result = correlate(blocks, list(result) + after, part, n_row, n_col)
     return jnp.transpose(result[0], (3, 0, 1, 2))[None, None]
 
 

time: 32.9 us -> 32.8 us (level)
  waiting for transfers between devices: 9.59 us -> 9.02 us
  starting transfers between devices: 16.4 us -> 16.9 us
    ppermute x4, waiting for transfers between devices: 5.16 us -> 4.58 us  [panel_permutes(): results.append(lax.ppermute(block, axes, route))]
    ppermute x2, starting transfers between devices: 0.14 us -> 0.5 us  [shards(): relayed = [lax.ppermute(block, 'bcol', other_core) for block in far]]
  transfers between devices with their start and end apart: 14 -> 14, of which waited for: 8 -> 7; matrix products, arithmetic and copies ran while one was open for 0% -> 0% of each run, Pallas kernels for 7% -> 7%
where the time goes in v15:
time: 32.8 us; the launch traced here: 32.6 us
  starting transfers between devices  16.9 us (52%)
  waiting for transfers between devices  9.02 us (28%)
  Pallas kernels  6.61 us (20%)
    ppermute x6, starting transfers between devices, to_owners(): lax.ppermute(pieces[d], 'chan', [(i, i ^ d) for i in range(owners)])  10.7 us
    ppermute x4, starting transfers between devices, panel_permutes(): results.append(lax.ppermute(block, axes, route))  5.56 us
    ppermute x4, waiting for transfers between devices, panel_permutes(): results.append(lax.ppermute(block, axes, route))  4.58 us
    ppermute x6, waiting for transfers between devices, to_owners(): lax.ppermute(pieces[d], 'chan', [(i, i ^ d) for i in range(owners)])  3.68 us
    pallas_call x1, Pallas kernels, filtered_and_first(): pl.pallas_call(functools.partial(filter_kernel, frames, pieces, spectrum_...  2.65 us
    pallas_call x2, Pallas kernels, correlate(): pl.pallas_call(functools.partial(correlate_kernel, n_row, n_col, h, times...  2.37 us
    pallas_call x2, Pallas kernels, equalize(): pl.pallas_call(functools.partial(equalize_kernel, owners, frames, h, part...  0.9 us
    ppermute x2, waiting for transfers between devices, shards(): relayed = [lax.ppermute(block, 'bcol', other_core) for block in far]  0.76 us
  transfers between devices with their start and end apart: 14, of which 7 were waited for; matrix products, arithmetic and copies ran while one was open for 0% of the time, Pallas kernels for 7%

profile of v15, /device:TPU:0, one launch (start us, length us, event | category | flops | bytes accessed | tf_op | source)
XLA Modules:
  0.0 32.6 jit_solution(15936860733217413542)
XLA Ops:
  0.0 0.0 copy-start
  0.0 0.0 copy-start.1
  0.0 2.6 %filter_and_transform.1 = (bf16[280,128]{1,0:T(8,128)(2,1)S(1)}, bf16[280,128]{1,0:T(8,128)(2,1)S(1)}, bf16[280,128]{1,0:T(8,128)(2,1)S(1)}, bf16[280,128]{1,0:T...) custom-call(s32[2,8,32768]{2,1,0:T(8,128)} %volt_hbm.1, ...), custom_call_target="tpu_custom_call" | custom-call | flops 536870912 | bytes 4194304 | tf_op jit(solution)/shard_map/filter_and_transform/pallas_call | solution.py:178
  2.7 5.1 %collective-permute-start = (bf16[280,128]{1,0:T(8,128)(2,1)S(1)}, bf16[280,128]{1,0:T(8,128)(2,1)S(1)}, u32[]{:S(2)}, u32[]{:S(2)}) collective-permute-start(bf16[280,128]{1,0:T(8,128)(2,1)S(1)} %get-tuple-element.28), channel_id=1, source_target_pairs={{0,24},{8,16},{16,8},{24,0},{1,25},{9,17},{17,9},{25,1},{2,26},{10... | collective-permute-start | bytes 215048 | tf_op jit(solution)/shard_map/ppermute | solution.py:429
  7.8 0.0 collective-permute-start.8
  7.8 0.6 %collective-permute-start.9 = (bf16[280,128]{1,0:T(8,128)(2,1)S(1)}, bf16[280,128]{1,0:T(8,128)(2,1)S(1)}, u32[]{:S(2)}, u32[]{:S(2)}) collective-permute-start(bf16[280,128]{1,0:T(8,128)(2,1)S(1)} %get-tuple-element.35), channel_id=1, source_target_pairs={{0,8},{8,0},{16,24},{24,16},{1,9},{9,1},{17,25},{25,17},{2,10},{10... | collective-permute-start | bytes 215048 | tf_op jit(solution)/shard_map/ppermute | solution.py:429
  8.4 0.0 copy-done
  8.4 0.0 copy-done.1
  8.4 0.6 %transform.1 = (bf16[280,128]{1,0:T(8,128)(2,1)S(1)}, bf16[280,128]{1,0:T(8,128)(2,1)S(1)}, bf16[280,128]{1,0:T(8,128)(2,1)S(1)}, bf16[280,128]{1,0:T(8,128)(2,1)S(1)}, f32[128,16]{1,0:T(8,128)S(1)}) custom-call(bf16[2,288,1024]{2,1,0:T(8,128)(2,1)S(1)} %get-tuple-element.23.filt, bf16[2048,256]{1,0:T(8,128)(2,1)S(1)} %get-tuple-element.24.later, ...), custom_call_target="tpu_custom_call" | custom-call | flops 536870912 | bytes 2097152 | tf_op jit(solution)/shard_map/transform/pallas_call | solution.py:214
  9.1 0.0 copy-start.2
  9.1 1.4 %collective-permute-done.refs_3_.refs_0_ = bf16[280,128]{1,0:T(8,128)(2,1)S(1)} collective-permute-done((bf16[280,128]{1,0:T(8,128)(2,1)S(1)}, bf16[280,128]{1,0:T(8,128)(2,1)S(1)}, u32[]{:S(2)}, u32[]{:S(2)}) %collective-permute-start) | collective-permute-done | bytes 71712 | tf_op jit(solution)/shard_map/ppermute | solution.py:429
  10.5 4.3 %collective-permute-start.1 = (bf16[280,128]{1,0:T(8,128)(2,1)S(1)}, bf16[280,128]{1,0:T(8,128)(2,1)S(1)}, u32[]{:S(2)}, u32[]{:S(2)}) collective-permute-start(bf16[280,128]{1,0:T(8,128)(2,1)S(1)} %get-tuple-element.29), channel_id=1, source_target_pairs={{0,24},{8,16},{16,8},{24,0},{1,25},{9,17},{17,9},{25,1},{2,26},{10... | collective-permute-start | bytes 215048 | tf_op jit(solution)/shard_map/ppermute | solution.py:429
  14.8 0.3 collective-permute-start.2
  15.0 0.4 %collective-permute-start.3 = (bf16[280,128]{1,0:T(8,128)(2,1)S(1)}, bf16[280,128]{1,0:T(8,128)(2,1)S(1)}, u32[]{:S(2)}, u32[]{:S(2)}) collective-permute-start(bf16[280,128]{1,0:T(8,128)(2,1)S(1)} %get-tuple-element.31), channel_id=1, source_target_pairs={{0,8},{8,0},{16,24},{24,16},{1,9},{9,1},{17,25},{25,17},{2,10},{10... | collective-permute-start | bytes 215048 | tf_op jit(solution)/shard_map/ppermute | solution.py:429
  15.4 0.6 %collective-permute-done.8.refs_1_ = bf16[280,128]{1,0:T(8,128)(2,1)S(1)} collective-permute-done((bf16[280,128]{1,0:T(8,128)(2,1)S(1)}, bf16[280,128]{1,0:T(8,128)(2,1)S(1)}, u32[]{:S(2)}, u32[]{:S(2)}) %collective-permute-start.8) | collective-permute-done | bytes 71712 | tf_op jit(solution)/shard_map/ppermute | solution.py:429
  16.0 0.0 collective-permute-done.9.refs_2_
  16.0 0.4 %equalize.3.refs_0_ = bf16[2,256,256]{2,1,0:T(8,128)(2,1)S(1)} custom-call(bf16[280,128]{1,0:T(8,128)(2,1)S(1)} %collective-permute-done.refs_3_.refs_0_, bf16[280,128]{1,0:T(8,128)(2,1)S(1)} %collective-permute-done.8.refs_1_, bf16[280,128]{1,0:T(8,128)(2,1)S(1)} %collective-permute-done.9.refs_2_, bf16[280,128]{1,0:T(8,128)(2,1)S(1)} %get-tuple-element.36.refs_3_, ...), custom_call_target="tpu_custom_call" | custom-call | bytes 1024 | tf_op jit(solution)/shard_map/equalize/pallas_call | solution.py:269
  16.5 1.0 %collective-permute-start.11 = (bf16[2,256,256]{2,1,0:T(8,128)(2,1)S(1)}, bf16[2,256,256]{2,1,0:T(8,128)(2,1)S(1)}, u32[]{:S(2)}, u32[]{:S(2)}) collective-permute-start(bf16[2,256,256]{2,1,0:T(8,128)(2,1)S(1)} %equalize.3.refs_0_), channel_id=1, source_target_pairs={{0,4},{1,3},{2,6},{3,1},{4,0},{5,7},{6,2},{7,5},{8,12},{9,11},{10,... | collective-permute-start | bytes 786440 | tf_op jit(solution)/shard_map/ppermute | solution.py:489
  17.5 1.5 %collective-permute-start.10 = (bf16[2,256,256]{2,1,0:T(8,128)(2,1)S(1)}, bf16[2,256,256]{2,1,0:T(8,128)(2,1)S(1)}, u32[]{:S(2)}, u32[]{:S(2)}) collective-permute-start(bf16[2,256,256]{2,1,0:T(8,128)(2,1)S(1)} %equalize.3.refs_0_), channel_id=1, source_target_pairs={{0,2},{1,5},{2,0},{3,7},{4,6},{5,1},{6,4},{7,3},{8,10},{9,13},{10,... | collective-permute-start | bytes 786440 | tf_op jit(solution)/shard_map/ppermute | solution.py:489
  19.0 0.0 collective-permute-done.1.refs_0_
  19.0 1.7 %collective-permute-done.2.refs_1_ = bf16[280,128]{1,0:T(8,128)(2,1)S(1)} collective-permute-done((bf16[280,128]{1,0:T(8,128)(2,1)S(1)}, bf16[280,128]{1,0:T(8,128)(2,1)S(1)}, u32[]{:S(2)}, u32[]{:S(2)}) %collective-permute-start.2) | collective-permute-done | bytes 71712 | tf_op jit(solution)/shard_map/ppermute | solution.py:429
  20.6 0.0 collective-permute-done.3.refs_2_
  20.6 0.4 %equalize.2.refs_2_.refs_0_ = bf16[2,256,256]{2,1,0:T(8,128)(2,1)S(1)} custom-call(bf16[280,128]{1,0:T(8,128)(2,1)S(1)} %collective-permute-done.1.refs_0_, bf16[280,128]{1,0:T(8,128)(2,1)S(1)} %collective-permute-done.2.refs_1_, bf16[280,128]{1,0:T(8,128)(2,1)S(1)} %collective-permute-done.3.refs_2_, bf16[280,128]{1,0:T(8,128)(2,1)S(1)} %get-tuple-element.32.refs_3_, ...), custom_call_target="tpu_custom_call" | custom-call | bytes 1024 | tf_op jit(solution)/shard_map/equalize/pallas_call | solution.py:269
  21.1 1.6 %collective-permute-start.4 = (bf16[2,256,256]{2,1,0:T(8,128)(2,1)S(1)}, bf16[2,256,256]{2,1,0:T(8,128)(2,1)S(1)}, u32[]{:S(2)}, u32[]{:S(2)}) collective-permute-start(bf16[2,256,256]{2,1,0:T(8,128)(2,1)S(1)} %equalize.2.refs_2_.refs_0_), channel_id=1, source_target_pairs={{0,2},{1,3},{2,0},{3,1},{4,6},{5,7},{6,4},{7,5},{8,10},{9,11},{10,... | collective-permute-start | bytes 786440 | tf_op jit(solution)/shard_map/ppermute | solution.py:494
  22.6 1.5 %collective-permute-start.7 = (bf16[2,256,256]{2,1,0:T(8,128)(2,1)S(1)}, bf16[2,256,256]{2,1,0:T(8,128)(2,1)S(1)}, u32[]{:S(2)}, u32[]{:S(2)}) collective-permute-start(bf16[2,256,256]{2,1,0:T(8,128)(2,1)S(1)} %equalize.2.refs_2_.refs_0_), channel_id=1, source_target_pairs={{0,4},{1,5},{2,6},{3,7},{4,0},{5,1},{6,2},{7,3},{8,12},{9,13},{10,... | collective-permute-start | bytes 786440 | tf_op jit(solution)/shard_map/ppermute | solution.py:494
  24.2 0.5 %collective-permute-done.11.refs_1_ = bf16[2,256,256]{2,1,0:T(8,128)(2,1)S(1)} collective-permute-done((bf16[2,256,256]{2,1,0:T(8,128)(2,1)S(1)}, bf16[2,256,256]{2,1,0:T(8,128)(2,1)S(1)}, u32[]{:S(2)}, u32[]{:S(2)}) %collective-permute-start.11) | collective-permute-done | bytes 262176 | tf_op jit(solution)/shard_map/ppermute | solution.py:489
  24.7 1.9 %collective-permute-done.10.refs_0_ = bf16[2,256,256]{2,1,0:T(8,128)(2,1)S(1)} collective-permute-done((bf16[2,256,256]{2,1,0:T(8,128)(2,1)S(1)}, bf16[2,256,256]{2,1,0:T(8,128)(2,1)S(1)}, u32[]{:S(2)}, u32[]{:S(2)}) %collective-permute-start.10) | collective-permute-done | bytes 262176 | tf_op jit(solution)/shard_map/ppermute | solution.py:489
  26.6 0.1 collective-permute-start.12
  26.7 0.5 %collective-permute-start.13 = (bf16[2,256,256]{2,1,0:T(8,128)(2,1)S(1)}, bf16[2,256,256]{2,1,0:T(8,128)(2,1)S(1)}, u32[]{:S(2)}, u32[]{:S(2)}) collective-permute-start(bf16[2,256,256]{2,1,0:T(8,128)(2,1)S(1)} %get-tuple-element.37.refs_1_), channel_id=1, source_target_pairs={{0,1},{1,0},{2,3},{3,2},{4,5},{5,4},{6,7},{7,6},{8,9},{9,8},{10,11... | collective-permute-start | bytes 786440 | tf_op jit(solution)/shard_map/ppermute | solution.py:527
  27.2 0.1 collective-permute-start.5
  27.3 2.2 %collective-permute-done.4.refs_1_ = bf16[2,256,256]{2,1,0:T(8,128)(2,1)S(1)} collective-permute-done((bf16[2,256,256]{2,1,0:T(8,128)(2,1)S(1)}, bf16[2,256,256]{2,1,0:T(8,128)(2,1)S(1)}, u32[]{:S(2)}, u32[]{:S(2)}) %collective-permute-start.4) | collective-permute-done | bytes 262176 | tf_op jit(solution)/shard_map/ppermute | solution.py:494
  29.5 0.0 collective-permute-start.6
  29.5 0.0 collective-permute-done.7.refs_6_.refs_4_
  29.5 0.0 collective-permute-done.12.refs_2_
  29.5 0.0 collective-permute-done.13.refs_3_
  29.5 0.0 copy-done.2
  29.5 0.7 %correlate.2 = (f32[2,2,4,32,128]{4,3,2,1,0:T(8,128)S(1)}, f32[2,4,8,128]{3,2,1,0:T(8,128)S(1)}) custom-call(bf16[2,256,256]{2,1,0:T(8,128)(2,1)S(1)} %equalize.3.refs_0_, bf16[2,256,256]{2,1,0:T(8,128)(2,1)S(1)} %get-tuple-element.37.refs_1_, bf16[2,256,256]{2,1,0:T(8,128)(2,1)S(1)} %collective-permute-done.12.refs_2_, ...), custom_call_target="tpu_custom_call" | custom-call | bytes 1024 | tf_op jit(solution)/shard_map/correlate/pallas_call | solution.py:413
  30.2 0.0 collective-permute-done.5.refs_2_
  30.2 0.8 %collective-permute-done.6.refs_3_ = bf16[2,256,256]{2,1,0:T(8,128)(2,1)S(1)} collective-permute-done((bf16[2,256,256]{2,1,0:T(8,128)(2,1)S(1)}, bf16[2,256,256]{2,1,0:T(8,128)(2,1)S(1)}, u32[]{:S(2)}, u32[]{:S(2)}) %collective-permute-start.6) | collective-permute-done | bytes 262176 | tf_op jit(solution)/shard_map/ppermute | solution.py:527
  31.0 1.6 %correlate.3 = f32[2,16,32,128]{3,2,1,0:T(8,128)} custom-call(bf16[2,256,256]{2,1,0:T(8,128)(2,1)S(1)} %equalize.2.refs_2_.refs_0_, bf16[2,256,256]{2,1,0:T(8,128)(2,1)S(1)} %collective-permute-done.4.refs_1_, bf16[2,256,256]{2,1,0:T(8,128)(2,1)S(1)} %collective-permute-done.5.refs_2_, bf16[2,256,256]{2,1,0:T(8,128)(2,1)S(1)} %collective-permute-done.6.refs_3_, ...), custom_call_target="tpu_custom_call" | custom-call | bytes 1024 | tf_op jit(solution)/shard_map/correlate/pallas_call | solution.py:413
  (3 shorter events, 0.1 us)
Async XLA Ops:
  0.0 8.4 %copy-start = (f32[128,128]{1,0:T(8,128)S(1)}, f32[128,128]{1,0:T(8,128)}, u32[]{:S(2)}) copy-start(f32[128,128]{1,0:T(8,128)} %constant.5.clone.pick_ref) | copy-start | bytes 196612
  0.0 8.4 %copy-start.1 = (f32[8,2,128]{2,1,0:T(2,128)S(1)}, f32[8,2,128]{2,1,0:T(2,128)}, u32[]{:S(2)}) copy-start(f32[8,2,128]{2,1,0:T(2,128)} %gains_ref.1) | copy-start | bytes 24580
  2.7 7.8 %collective-permute-start = (bf16[280,128]{1,0:T(8,128)(2,1)S(1)}, bf16[280,128]{1,0:T(8,128)(2,1)S(1)}, u32[]{:S(2)}, u32[]{:S(2)}) collective-permute-start(bf16[280,128]{1,0:T(8,128)(2,1)S(1)} %get-tuple-element.28), channel_id=1, source_target_pairs={{0,24},{8,16},{16,8},{24,0},{1,25},{9,17},{17,9},{25,1},{2,26},{10... | collective-permute-start | bytes 215048 | tf_op jit(solution)/shard_map/ppermute | solution.py:429
  7.8 8.2 %collective-permute-start.8 = (bf16[280,128]{1,0:T(8,128)(2,1)S(1)}, bf16[280,128]{1,0:T(8,128)(2,1)S(1)}, u32[]{:S(2)}, u32[]{:S(2)}) collective-permute-start(bf16[280,128]{1,0:T(8,128)(2,1)S(1)} %get-tuple-element.34), channel_id=1, source_target_pairs={{0,16},{8,24},{16,0},{24,8},{1,17},{9,25},{17,1},{25,9},{2,18},{10... | collective-permute-start | bytes 215048 | tf_op jit(solution)/shard_map/ppermute | solution.py:429
  7.8 8.2 %collective-permute-start.9 = (bf16[280,128]{1,0:T(8,128)(2,1)S(1)}, bf16[280,128]{1,0:T(8,128)(2,1)S(1)}, u32[]{:S(2)}, u32[]{:S(2)}) collective-permute-start(bf16[280,128]{1,0:T(8,128)(2,1)S(1)} %get-tuple-element.35), channel_id=1, source_target_pairs={{0,8},{8,0},{16,24},{24,16},{1,9},{9,1},{17,25},{25,17},{2,10},{10... | collective-permute-start | bytes 215048 | tf_op jit(solution)/shard_map/ppermute | solution.py:429
  9.1 20.4 %copy-start.2 = (s32[8,8]{1,0:T(8,128)S(1)}, s32[8,8]{1,0:T(8,128)}, u32[]{:S(2)}) copy-start(s32[8,8]{1,0:T(8,128)} %refs_5_.1) | copy-start | bytes 772
  10.5 8.5 %collective-permute-start.1 = (bf16[280,128]{1,0:T(8,128)(2,1)S(1)}, bf16[280,128]{1,0:T(8,128)(2,1)S(1)}, u32[]{:S(2)}, u32[]{:S(2)}) collective-permute-start(bf16[280,128]{1,0:T(8,128)(2,1)S(1)} %get-tuple-element.29), channel_id=1, source_target_pairs={{0,24},{8,16},{16,8},{24,0},{1,25},{9,17},{17,9},{25,1},{2,26},{10... | collective-permute-start | bytes 215048 | tf_op jit(solution)/shard_map/ppermute | solution.py:429
  14.8 5.8 %collective-permute-start.2 = (bf16[280,128]{1,0:T(8,128)(2,1)S(1)}, bf16[280,128]{1,0:T(8,128)(2,1)S(1)}, u32[]{:S(2)}, u32[]{:S(2)}) collective-permute-start(bf16[280,128]{1,0:T(8,128)(2,1)S(1)} %get-tuple-element.30), channel_id=1, source_target_pairs={{0,16},{8,24},{16,0},{24,8},{1,17},{9,25},{17,1},{25,9},{2,18},{10... | collective-permute-start | bytes 215048 | tf_op jit(solution)/shard_map/ppermute | solution.py:429
  15.0 5.6 %collective-permute-start.3 = (bf16[280,128]{1,0:T(8,128)(2,1)S(1)}, bf16[280,128]{1,0:T(8,128)(2,1)S(1)}, u32[]{:S(2)}, u32[]{:S(2)}) collective-permute-start(bf16[280,128]{1,0:T(8,128)(2,1)S(1)} %get-tuple-element.31), channel_id=1, source_target_pairs={{0,8},{8,0},{16,24},{24,16},{1,9},{9,1},{17,25},{25,17},{2,10},{10... | collective-permute-start | bytes 215048 | tf_op jit(solution)/shard_map/ppermute | solution.py:429
  16.5 8.2 %collective-permute-start.11 = (bf16[2,256,256]{2,1,0:T(8,128)(2,1)S(1)}, bf16[2,256,256]{2,1,0:T(8,128)(2,1)S(1)}, u32[]{:S(2)}, u32[]{:S(2)}) collective-permute-start(bf16[2,256,256]{2,1,0:T(8,128)(2,1)S(1)} %equalize.3.refs_0_), channel_id=1, source_target_pairs={{0,4},{1,3},{2,6},{3,1},{4,0},{5,7},{6,2},{7,5},{8,12},{9,11},{10,... | collective-permute-start | bytes 786440 | tf_op jit(solution)/shard_map/ppermute | solution.py:489
  17.5 9.1 %collective-permute-start.10 = (bf16[2,256,256]{2,1,0:T(8,128)(2,1)S(1)}, bf16[2,256,256]{2,1,0:T(8,128)(2,1)S(1)}, u32[]{:S(2)}, u32[]{:S(2)}) collective-permute-start(bf16[2,256,256]{2,1,0:T(8,128)(2,1)S(1)} %equalize.3.refs_0_), channel_id=1, source_target_pairs={{0,2},{1,5},{2,0},{3,7},{4,6},{5,1},{6,4},{7,3},{8,10},{9,13},{10,... | collective-permute-start | bytes 786440 | tf_op jit(solution)/shard_map/ppermute | solution.py:489
  21.1 8.4 %collective-permute-start.4 = (bf16[2,256,256]{2,1,0:T(8,128)(2,1)S(1)}, bf16[2,256,256]{2,1,0:T(8,128)(2,1)S(1)}, u32[]{:S(2)}, u32[]{:S(2)}) collective-permute-start(bf16[2,256,256]{2,1,0:T(8,128)(2,1)S(1)} %equalize.2.refs_2_.refs_0_), channel_id=1, source_target_pairs={{0,2},{1,3},{2,0},{3,1},{4,6},{5,7},{6,4},{7,5},{8,10},{9,11},{10,... | collective-permute-start | bytes 786440 | tf_op jit(solution)/shard_map/ppermute | solution.py:494
  22.6 6.8 %collective-permute-start.7 = (bf16[2,256,256]{2,1,0:T(8,128)(2,1)S(1)}, bf16[2,256,256]{2,1,0:T(8,128)(2,1)S(1)}, u32[]{:S(2)}, u32[]{:S(2)}) collective-permute-start(bf16[2,256,256]{2,1,0:T(8,128)(2,1)S(1)} %equalize.2.refs_2_.refs_0_), channel_id=1, source_target_pairs={{0,4},{1,5},{2,6},{3,7},{4,0},{5,1},{6,2},{7,3},{8,12},{9,13},{10,... | collective-permute-start | bytes 786440 | tf_op jit(solution)/shard_map/ppermute | solution.py:494
  26.6 2.9 %collective-permute-start.12 = (bf16[2,256,256]{2,1,0:T(8,128)(2,1)S(1)}, bf16[2,256,256]{2,1,0:T(8,128)(2,1)S(1)}, u32[]{:S(2)}, u32[]{:S(2)}) collective-permute-start(bf16[2,256,256]{2,1,0:T(8,128)(2,1)S(1)} %held_back.3), channel_id=1, source_target_pairs={{0,1},{1,0},{2,3},{3,2},{4,5},{5,4},{6,7},{7,6},{8,9},{9,8},{10,11... | collective-permute-start | bytes 786440 | tf_op jit(solution)/shard_map/ppermute | solution.py:526
  26.7 2.8 %collective-permute-start.13 = (bf16[2,256,256]{2,1,0:T(8,128)(2,1)S(1)}, bf16[2,256,256]{2,1,0:T(8,128)(2,1)S(1)}, u32[]{:S(2)}, u32[]{:S(2)}) collective-permute-start(bf16[2,256,256]{2,1,0:T(8,128)(2,1)S(1)} %get-tuple-element.37.refs_1_), channel_id=1, source_target_pairs={{0,1},{1,0},{2,3},{3,2},{4,5},{5,4},{6,7},{7,6},{8,9},{9,8},{10,11... | collective-permute-start | bytes 786440 | tf_op jit(solution)/shard_map/ppermute | solution.py:527
  27.2 3.1 %collective-permute-start.5 = (bf16[2,256,256]{2,1,0:T(8,128)(2,1)S(1)}, bf16[2,256,256]{2,1,0:T(8,128)(2,1)S(1)}, u32[]{:S(2)}, u32[]{:S(2)}) collective-permute-start(bf16[2,256,256]{2,1,0:T(8,128)(2,1)S(1)} %equalize.2.refs_2_.refs_0_), channel_id=1, source_target_pairs={{0,1},{1,0},{2,3},{3,2},{4,5},{5,4},{6,7},{7,6},{8,9},{9,8},{10,11... | collective-permute-start | bytes 786440 | tf_op jit(solution)/shard_map/ppermute | solution.py:526
  29.5 1.5 %collective-permute-start.6 = (bf16[2,256,256]{2,1,0:T(8,128)(2,1)S(1)}, bf16[2,256,256]{2,1,0:T(8,128)(2,1)S(1)}, u32[]{:S(2)}, u32[]{:S(2)}) collective-permute-start(bf16[2,256,256]{2,1,0:T(8,128)(2,1)S(1)} %collective-permute-done.4.refs_1_), channel_id=1, source_target_pairs={{0,1},{1,0},{2,3},{3,2},{4,5},{5,4},{6,7},{7,6},{8,9},{9,8},{10,11... | collective-permute-start | bytes 786440 | tf_op jit(solution)/shard_map/ppermute | solution.py:527

commit v16 on v10

--- a/solution.py
+++ b/solution.py
@@ -446,35 +446,19 @@
     )(*blocks, *after)
 
 
-def together(blocks):
-    def kernel(*refs):
-        for i in range(len(blocks)):
-            refs[-1][i] = refs[i][...]
-
-    return pl.pallas_call(
-        kernel,
-        out_shape=jax.ShapeDtypeStruct((len(blocks),) + blocks[0].shape, blocks[0].dtype),
-        in_specs=[IN_VMEM] * len(blocks),
-        out_specs=IN_VMEM,
-        compiler_params=pltpu.CompilerParams(vmem_limit_bytes=VMEM_BYTES),
-        cost_estimate=pl.CostEstimate(flops=0, bytes_accessed=1 << 10, transcendentals=0),
-        name="together",
-    )(*blocks)
-
-
 def shards(voltages, antenna_gains, tile_map):
     owners = lax.axis_size("chan")
     n_row = lax.axis_size("brow")
     n_col = lax.axis_size("bcol")
     chips = n_col // 2
     frames = voltages.shape[2] // NCHAN
-    table = jnp.asarray(constants(owners))
     across = [[(i, (i // 2 + d) % chips * 2 + i % 2) for i in range(n_col)] for d in range(chips)]
     along = [[(i, (i + d) % n_row) for i in range(n_row)] for d in range(n_row)]
+    table = jnp.asarray(constants(owners))
     other_core = [(i, i ^ 1) for i in range(n_col)]
 
     filt, tables, pieces = filtered_and_first(voltages, owners, table)
-    own, far, column = [], [], []
+    own, panels = [], []
     arrived = to_owners(pieces)
     for part in range(PARTS):
         later = None
@@ -484,17 +468,21 @@
                 *pieces, gains = pieces
             later = to_owners([pieces[0], *held_back(pieces[1:], arrived[-1:])])
         own.append(equalize(arrived, gains, part, frames))
-        far.append([lax.ppermute(own[part], "bcol", across[d]) for d in range(1, chips)])
-        column.append([lax.ppermute(own[part], "brow", along[d]) for d in range(1, n_row)])
+        far = [lax.ppermute(own[part], "bcol", across[d]) for d in range(1, chips)]
+        column = [lax.ppermute(own[part], "brow", along[d]) for d in range(1, n_row)]
+        panels.append((far, column))
         arrived = later
-    beside = [lax.ppermute(block, "bcol", other_core) for block in own]
     result = [tile_map]
     for part in range(PARTS):
-        after = own[-1:] + column[part]
-        far[part] = list(held_back(far[part], after))
-        near = [lax.ppermute(block, "bcol", other_core) for block in far[part]]
-        blocks = [own[part]] + far[part] + [beside[part]] + near + column[part]
-        result = correlate(blocks, result, part, n_row, n_col)
+        far, column = panels[part]
+        mine = own[part]
+        if part < PARTS - 1:
+            mine, *far = held_back([mine] + far, own[-1:])
+        beside = lax.ppermute(mine, "bcol", other_core)
+        relayed = [lax.ppermute(block, "bcol", other_core) for block in far]
+        blocks = [own[part]] + far + [beside] + relayed + column
+        after = panels[-1][1] if part == 0 else []
+        result = correlate(blocks, list(result) + after, part, n_row, n_col)
     return jnp.transpose(result[0], (3, 0, 1, 2))[None, None]
 
 

time: 32.8 us -> 32 us (0.976)
  waiting for transfers between devices: 9.61 us -> 8.27 us
  starting transfers between devices: 16.4 us -> 16.9 us
    ppermute x2, waiting for transfers between devices: 3.71 us -> 0.9 us  [shards(): lax.ppermute(own[part], 'brow', along[d])]
    ppermute x6, waiting for transfers between devices: 2.23 us -> 3.69 us  [the longest x2 3.68 us: shards(): far = [lax.ppermute(own[part], 'bcol', across[d]) for d in range(1, chips)]]
    ppermute x2, starting transfers between devices: 2.58 us -> 3.04 us  [shards(): lax.ppermute(own[part], 'brow', along[d])]
  transfers between devices with their start and end apart: 14 -> 14, of which waited for: 8 -> 6; matrix products, arithmetic and copies ran while one was open for 0% -> 0% of each run, Pallas kernels for 7% -> 7%
where the time goes in v16:
time: 32 us; the launch traced here: 31.8 us
  starting transfers between devices  16.9 us (53%)
  waiting for transfers between devices  8.27 us (26%)
  Pallas kernels  6.59 us (21%)
    ppermute x6, starting transfers between devices, to_owners(): lax.ppermute(pieces[d], 'chan', [(i, i ^ d) for i in range(owners)])  10.7 us
    ppermute x6, waiting for transfers between devices, to_owners(): lax.ppermute(pieces[d], 'chan', [(i, i ^ d) for i in range(owners)])  3.68 us
    ppermute x2, waiting for transfers between devices, shards(): far = [lax.ppermute(own[part], 'bcol', across[d]) for d in range(1, chips)]  3.68 us
    ppermute x2, starting transfers between devices, shards(): lax.ppermute(own[part], 'brow', along[d])  3.04 us
    pallas_call x1, Pallas kernels, filtered_and_first(): pl.pallas_call(functools.partial(filter_kernel, frames, pieces, spectrum_...  2.65 us
    ppermute x2, starting transfers between devices, shards(): far = [lax.ppermute(own[part], 'bcol', across[d]) for d in range(1, chips)]  2.52 us
    pallas_call x2, Pallas kernels, correlate(): pl.pallas_call(functools.partial(correlate_kernel, n_row, n_col, h, times...  2.37 us
    ppermute x2, waiting for transfers between devices, shards(): lax.ppermute(own[part], 'brow', along[d])  0.9 us
  transfers between devices with their start and end apart: 14, of which 6 were waited for; matrix products, arithmetic and copies ran while one was open for 0% of the time, Pallas kernels for 7%

profile of v16, /device:TPU:0, one launch (start us, length us, event | category | flops | bytes accessed | tf_op | source)
XLA Modules:
  0.0 31.8 jit_solution(952272777420063280)
XLA Ops:
  0.0 0.0 copy-start
  0.0 0.0 copy-start.1
  0.0 2.6 %filter_and_transform.1 = (bf16[280,128]{1,0:T(8,128)(2,1)S(1)}, bf16[280,128]{1,0:T(8,128)(2,1)S(1)}, bf16[280,128]{1,0:T(8,128)(2,1)S(1)}, bf16[280,128]{1,0:T...) custom-call(s32[2,8,32768]{2,1,0:T(8,128)} %volt_hbm.1, ...), custom_call_target="tpu_custom_call" | custom-call | flops 536870912 | bytes 4194304 | tf_op jit(solution)/shard_map/filter_and_transform/pallas_call | solution.py:178
  2.7 5.1 %collective-permute-start = (bf16[280,128]{1,0:T(8,128)(2,1)S(1)}, bf16[280,128]{1,0:T(8,128)(2,1)S(1)}, u32[]{:S(2)}, u32[]{:S(2)}) collective-permute-start(bf16[280,128]{1,0:T(8,128)(2,1)S(1)} %get-tuple-element.28), channel_id=1, source_target_pairs={{0,24},{8,16},{16,8},{24,0},{1,25},{9,17},{17,9},{25,1},{2,26},{10... | collective-permute-start | bytes 215048 | tf_op jit(solution)/shard_map/ppermute | solution.py:429
  7.8 0.0 collective-permute-start.8
  7.8 0.6 %collective-permute-start.9 = (bf16[280,128]{1,0:T(8,128)(2,1)S(1)}, bf16[280,128]{1,0:T(8,128)(2,1)S(1)}, u32[]{:S(2)}, u32[]{:S(2)}) collective-permute-start(bf16[280,128]{1,0:T(8,128)(2,1)S(1)} %get-tuple-element.35), channel_id=1, source_target_pairs={{0,8},{8,0},{16,24},{24,16},{1,9},{9,1},{17,25},{25,17},{2,10},{10... | collective-permute-start | bytes 215048 | tf_op jit(solution)/shard_map/ppermute | solution.py:429
  8.4 0.0 copy-done
  8.4 0.0 copy-done.1
  8.4 0.0 copy-start.2
  8.4 0.6 %transform.1 = (bf16[280,128]{1,0:T(8,128)(2,1)S(1)}, bf16[280,128]{1,0:T(8,128)(2,1)S(1)}, bf16[280,128]{1,0:T(8,128)(2,1)S(1)}, bf16[280,128]{1,0:T(8,128)(2,1)S(1)}, f32[128,16]{1,0:T(8,128)S(1)}) custom-call(bf16[2,288,1024]{2,1,0:T(8,128)(2,1)S(1)} %get-tuple-element.23.filt, bf16[2048,256]{1,0:T(8,128)(2,1)S(1)} %get-tuple-element.24.later, ...), custom_call_target="tpu_custom_call" | custom-call | flops 536870912 | bytes 2097152 | tf_op jit(solution)/shard_map/transform/pallas_call | solution.py:214
  9.1 1.4 %collective-permute-done.refs_3_.refs_0_ = bf16[280,128]{1,0:T(8,128)(2,1)S(1)} collective-permute-done((bf16[280,128]{1,0:T(8,128)(2,1)S(1)}, bf16[280,128]{1,0:T(8,128)(2,1)S(1)}, u32[]{:S(2)}, u32[]{:S(2)}) %collective-permute-start) | collective-permute-done | bytes 71712 | tf_op jit(solution)/shard_map/ppermute | solution.py:429
  10.5 4.3 %collective-permute-start.1 = (bf16[280,128]{1,0:T(8,128)(2,1)S(1)}, bf16[280,128]{1,0:T(8,128)(2,1)S(1)}, u32[]{:S(2)}, u32[]{:S(2)}) collective-permute-start(bf16[280,128]{1,0:T(8,128)(2,1)S(1)} %get-tuple-element.29), channel_id=1, source_target_pairs={{0,24},{8,16},{16,8},{24,0},{1,25},{9,17},{17,9},{25,1},{2,26},{10... | collective-permute-start | bytes 215048 | tf_op jit(solution)/shard_map/ppermute | solution.py:429
  14.8 0.3 collective-permute-start.2
  15.0 0.4 %collective-permute-start.3 = (bf16[280,128]{1,0:T(8,128)(2,1)S(1)}, bf16[280,128]{1,0:T(8,128)(2,1)S(1)}, u32[]{:S(2)}, u32[]{:S(2)}) collective-permute-start(bf16[280,128]{1,0:T(8,128)(2,1)S(1)} %get-tuple-element.31), channel_id=1, source_target_pairs={{0,8},{8,0},{16,24},{24,16},{1,9},{9,1},{17,25},{25,17},{2,10},{10... | collective-permute-start | bytes 215048 | tf_op jit(solution)/shard_map/ppermute | solution.py:429
  15.4 0.6 %collective-permute-done.8.refs_1_ = bf16[280,128]{1,0:T(8,128)(2,1)S(1)} collective-permute-done((bf16[280,128]{1,0:T(8,128)(2,1)S(1)}, bf16[280,128]{1,0:T(8,128)(2,1)S(1)}, u32[]{:S(2)}, u32[]{:S(2)}) %collective-permute-start.8) | collective-permute-done | bytes 71712 | tf_op jit(solution)/shard_map/ppermute | solution.py:429
  16.0 0.0 collective-permute-done.9.refs_2_
  16.0 0.4 %equalize.3.refs_0_ = bf16[2,256,256]{2,1,0:T(8,128)(2,1)S(1)} custom-call(bf16[280,128]{1,0:T(8,128)(2,1)S(1)} %collective-permute-done.refs_3_.refs_0_, bf16[280,128]{1,0:T(8,128)(2,1)S(1)} %collective-permute-done.8.refs_1_, bf16[280,128]{1,0:T(8,128)(2,1)S(1)} %collective-permute-done.9.refs_2_, bf16[280,128]{1,0:T(8,128)(2,1)S(1)} %get-tuple-element.36.refs_3_, ...), custom_call_target="tpu_custom_call" | custom-call | bytes 1024 | tf_op jit(solution)/shard_map/equalize/pallas_call | solution.py:269
  16.5 1.0 %collective-permute-start.10 = (bf16[2,256,256]{2,1,0:T(8,128)(2,1)S(1)}, bf16[2,256,256]{2,1,0:T(8,128)(2,1)S(1)}, u32[]{:S(2)}, u32[]{:S(2)}) collective-permute-start(bf16[2,256,256]{2,1,0:T(8,128)(2,1)S(1)} %equalize.3.refs_0_), channel_id=1, source_target_pairs={{0,2},{1,3},{2,0},{3,1},{4,6},{5,7},{6,4},{7,5},{8,10},{9,11},{10,... | collective-permute-start | bytes 786440 | tf_op jit(solution)/shard_map/ppermute | solution.py:471
  17.4 1.5 %collective-permute-start.13 = (bf16[2,256,256]{2,1,0:T(8,128)(2,1)S(1)}, bf16[2,256,256]{2,1,0:T(8,128)(2,1)S(1)}, u32[]{:S(2)}, u32[]{:S(2)}) collective-permute-start(bf16[2,256,256]{2,1,0:T(8,128)(2,1)S(1)} %equalize.3.refs_0_), channel_id=1, source_target_pairs={{0,4},{4,0},{1,5},{5,1},{2,6},{6,2},{3,7},{7,3},{8,12},{12,8},{9,1... | collective-permute-start | bytes 786440 | tf_op jit(solution)/shard_map/ppermute | solution.py:472
  19.0 0.0 collective-permute-done.1.refs_0_
  19.0 1.7 %collective-permute-done.2.refs_1_ = bf16[280,128]{1,0:T(8,128)(2,1)S(1)} collective-permute-done((bf16[280,128]{1,0:T(8,128)(2,1)S(1)}, bf16[280,128]{1,0:T(8,128)(2,1)S(1)}, u32[]{:S(2)}, u32[]{:S(2)}) %collective-permute-start.2) | collective-permute-done | bytes 71712 | tf_op jit(solution)/shard_map/ppermute | solution.py:429
  20.6 0.0 collective-permute-done.3.refs_2_
  20.6 0.4 %equalize.2.refs_2_.refs_0_ = bf16[2,256,256]{2,1,0:T(8,128)(2,1)S(1)} custom-call(bf16[280,128]{1,0:T(8,128)(2,1)S(1)} %collective-permute-done.1.refs_0_, bf16[280,128]{1,0:T(8,128)(2,1)S(1)} %collective-permute-done.2.refs_1_, bf16[280,128]{1,0:T(8,128)(2,1)S(1)} %collective-permute-done.3.refs_2_, bf16[280,128]{1,0:T(8,128)(2,1)S(1)} %get-tuple-element.32.refs_3_, ...), custom_call_target="tpu_custom_call" | custom-call | bytes 1024 | tf_op jit(solution)/shard_map/equalize/pallas_call | solution.py:269
  21.1 1.6 %collective-permute-start.4 = (bf16[2,256,256]{2,1,0:T(8,128)(2,1)S(1)}, bf16[2,256,256]{2,1,0:T(8,128)(2,1)S(1)}, u32[]{:S(2)}, u32[]{:S(2)}) collective-permute-start(bf16[2,256,256]{2,1,0:T(8,128)(2,1)S(1)} %equalize.2.refs_2_.refs_0_), channel_id=1, source_target_pairs={{0,2},{1,3},{2,0},{3,1},{4,6},{5,7},{6,4},{7,5},{8,10},{9,11},{10,... | collective-permute-start | bytes 786440 | tf_op jit(solution)/shard_map/ppermute | solution.py:471
  22.6 1.5 %collective-permute-start.7 = (bf16[2,256,256]{2,1,0:T(8,128)(2,1)S(1)}, bf16[2,256,256]{2,1,0:T(8,128)(2,1)S(1)}, u32[]{:S(2)}, u32[]{:S(2)}) collective-permute-start(bf16[2,256,256]{2,1,0:T(8,128)(2,1)S(1)} %equalize.2.refs_2_.refs_0_), channel_id=1, source_target_pairs={{0,4},{4,0},{1,5},{5,1},{2,6},{6,2},{3,7},{7,3},{8,12},{12,8},{9,1... | collective-permute-start | bytes 786440 | tf_op jit(solution)/shard_map/ppermute | solution.py:472
  24.2 0.5 %collective-permute-done.10.refs_1_ = bf16[2,256,256]{2,1,0:T(8,128)(2,1)S(1)} collective-permute-done((bf16[2,256,256]{2,1,0:T(8,128)(2,1)S(1)}, bf16[2,256,256]{2,1,0:T(8,128)(2,1)S(1)}, u32[]{:S(2)}, u32[]{:S(2)}) %collective-permute-start.10) | collective-permute-done | bytes 262176 | tf_op jit(solution)/shard_map/ppermute | solution.py:471
  24.7 0.1 collective-permute-start.11
  24.8 0.5 %collective-permute-start.12 = (bf16[2,256,256]{2,1,0:T(8,128)(2,1)S(1)}, bf16[2,256,256]{2,1,0:T(8,128)(2,1)S(1)}, u32[]{:S(2)}, u32[]{:S(2)}) collective-permute-start(bf16[2,256,256]{2,1,0:T(8,128)(2,1)S(1)} %get-tuple-element.37.refs_1_), channel_id=1, source_target_pairs={{0,1},{1,0},{2,3},{3,2},{4,5},{5,4},{6,7},{7,6},{8,9},{9,8},{10,11... | collective-permute-start | bytes 786440 | tf_op jit(solution)/shard_map/ppermute | solution.py:482
  25.3 0.0 collective-permute-done.13.refs_4_
  25.3 0.1 collective-permute-start.5
  25.4 3.2 %collective-permute-done.4.refs_1_ = bf16[2,256,256]{2,1,0:T(8,128)(2,1)S(1)} collective-permute-done((bf16[2,256,256]{2,1,0:T(8,128)(2,1)S(1)}, bf16[2,256,256]{2,1,0:T(8,128)(2,1)S(1)}, u32[]{:S(2)}, u32[]{:S(2)}) %collective-permute-start.4) | collective-permute-done | bytes 262176 | tf_op jit(solution)/shard_map/ppermute | solution.py:471
  28.5 0.0 collective-permute-start.6
  28.5 0.9 %collective-permute-done.7.refs_6_.refs_4_ = bf16[2,256,256]{2,1,0:T(8,128)(2,1)S(1)} collective-permute-done((bf16[2,256,256]{2,1,0:T(8,128)(2,1)S(1)}, bf16[2,256,256]{2,1,0:T(8,128)(2,1)S(1)}, u32[]{:S(2)}, u32[]{:S(2)}) %collective-permute-start.7) | collective-permute-done | bytes 262176 | tf_op jit(solution)/shard_map/ppermute | solution.py:472
  29.4 0.0 collective-permute-done.11.refs_2_
  29.4 0.0 collective-permute-done.12.refs_3_
  29.4 0.0 copy-done.2
  29.4 0.7 %correlate.2 = (f32[2,2,4,32,128]{4,3,2,1,0:T(8,128)S(1)}, f32[2,4,8,128]{3,2,1,0:T(8,128)S(1)}) custom-call(bf16[2,256,256]{2,1,0:T(8,128)(2,1)S(1)} %equalize.3.refs_0_, bf16[2,256,256]{2,1,0:T(8,128)(2,1)S(1)} %get-tuple-element.37.refs_1_, bf16[2,256,256]{2,1,0:T(8,128)(2,1)S(1)} %collective-permute-done.11.refs_2_, ...), custom_call_target="tpu_custom_call" | custom-call | bytes 1024 | tf_op jit(solution)/shard_map/correlate/pallas_call | solution.py:413
  30.2 0.0 collective-permute-done.5.refs_2_
  30.2 0.0 collective-permute-done.6.refs_3_
  30.2 1.6 %correlate.3 = f32[2,16,32,128]{3,2,1,0:T(8,128)} custom-call(bf16[2,256,256]{2,1,0:T(8,128)(2,1)S(1)} %equalize.2.refs_2_.refs_0_, bf16[2,256,256]{2,1,0:T(8,128)(2,1)S(1)} %collective-permute-done.4.refs_1_, bf16[2,256,256]{2,1,0:T(8,128)(2,1)S(1)} %collective-permute-done.5.refs_2_, bf16[2,256,256]{2,1,0:T(8,128)(2,1)S(1)} %collective-permute-done.6.refs_3_, ...), custom_call_target="tpu_custom_call" | custom-call | bytes 1024 | tf_op jit(solution)/shard_map/correlate/pallas_call | solution.py:413
  (2 shorter events, 0.1 us)
Async XLA Ops:
  0.0 8.4 %copy-start = (f32[128,128]{1,0:T(8,128)S(1)}, f32[128,128]{1,0:T(8,128)}, u32[]{:S(2)}) copy-start(f32[128,128]{1,0:T(8,128)} %constant.5.clone.pick_ref) | copy-start | bytes 196612
  0.0 8.4 %copy-start.1 = (f32[8,2,128]{2,1,0:T(2,128)S(1)}, f32[8,2,128]{2,1,0:T(2,128)}, u32[]{:S(2)}) copy-start(f32[8,2,128]{2,1,0:T(2,128)} %gains_ref.1) | copy-start | bytes 24580
  2.7 7.8 %collective-permute-start = (bf16[280,128]{1,0:T(8,128)(2,1)S(1)}, bf16[280,128]{1,0:T(8,128)(2,1)S(1)}, u32[]{:S(2)}, u32[]{:S(2)}) collective-permute-start(bf16[280,128]{1,0:T(8,128)(2,1)S(1)} %get-tuple-element.28), channel_id=1, source_target_pairs={{0,24},{8,16},{16,8},{24,0},{1,25},{9,17},{17,9},{25,1},{2,26},{10... | collective-permute-start | bytes 215048 | tf_op jit(solution)/shard_map/ppermute | solution.py:429
  7.8 8.2 %collective-permute-start.8 = (bf16[280,128]{1,0:T(8,128)(2,1)S(1)}, bf16[280,128]{1,0:T(8,128)(2,1)S(1)}, u32[]{:S(2)}, u32[]{:S(2)}) collective-permute-start(bf16[280,128]{1,0:T(8,128)(2,1)S(1)} %get-tuple-element.34), channel_id=1, source_target_pairs={{0,16},{8,24},{16,0},{24,8},{1,17},{9,25},{17,1},{25,9},{2,18},{10... | collective-permute-start | bytes 215048 | tf_op jit(solution)/shard_map/ppermute | solution.py:429
  7.8 8.2 %collective-permute-start.9 = (bf16[280,128]{1,0:T(8,128)(2,1)S(1)}, bf16[280,128]{1,0:T(8,128)(2,1)S(1)}, u32[]{:S(2)}, u32[]{:S(2)}) collective-permute-start(bf16[280,128]{1,0:T(8,128)(2,1)S(1)} %get-tuple-element.35), channel_id=1, source_target_pairs={{0,8},{8,0},{16,24},{24,16},{1,9},{9,1},{17,25},{25,17},{2,10},{10... | collective-permute-start | bytes 215048 | tf_op jit(solution)/shard_map/ppermute | solution.py:429
  8.4 21.0 %copy-start.2 = (s32[8,8]{1,0:T(8,128)S(1)}, s32[8,8]{1,0:T(8,128)}, u32[]{:S(2)}) copy-start(s32[8,8]{1,0:T(8,128)} %refs_5_.1) | copy-start | bytes 772
  10.5 8.5 %collective-permute-start.1 = (bf16[280,128]{1,0:T(8,128)(2,1)S(1)}, bf16[280,128]{1,0:T(8,128)(2,1)S(1)}, u32[]{:S(2)}, u32[]{:S(2)}) collective-permute-start(bf16[280,128]{1,0:T(8,128)(2,1)S(1)} %get-tuple-element.29), channel_id=1, source_target_pairs={{0,24},{8,16},{16,8},{24,0},{1,25},{9,17},{17,9},{25,1},{2,26},{10... | collective-permute-start | bytes 215048 | tf_op jit(solution)/shard_map/ppermute | solution.py:429
  14.8 5.8 %collective-permute-start.2 = (bf16[280,128]{1,0:T(8,128)(2,1)S(1)}, bf16[280,128]{1,0:T(8,128)(2,1)S(1)}, u32[]{:S(2)}, u32[]{:S(2)}) collective-permute-start(bf16[280,128]{1,0:T(8,128)(2,1)S(1)} %get-tuple-element.30), channel_id=1, source_target_pairs={{0,16},{8,24},{16,0},{24,8},{1,17},{9,25},{17,1},{25,9},{2,18},{10... | collective-permute-start | bytes 215048 | tf_op jit(solution)/shard_map/ppermute | solution.py:429
  15.0 5.6 %collective-permute-start.3 = (bf16[280,128]{1,0:T(8,128)(2,1)S(1)}, bf16[280,128]{1,0:T(8,128)(2,1)S(1)}, u32[]{:S(2)}, u32[]{:S(2)}) collective-permute-start(bf16[280,128]{1,0:T(8,128)(2,1)S(1)} %get-tuple-element.31), channel_id=1, source_target_pairs={{0,8},{8,0},{16,24},{24,16},{1,9},{9,1},{17,25},{25,17},{2,10},{10... | collective-permute-start | bytes 215048 | tf_op jit(solution)/shard_map/ppermute | solution.py:429
  16.5 8.2 %collective-permute-start.10 = (bf16[2,256,256]{2,1,0:T(8,128)(2,1)S(1)}, bf16[2,256,256]{2,1,0:T(8,128)(2,1)S(1)}, u32[]{:S(2)}, u32[]{:S(2)}) collective-permute-start(bf16[2,256,256]{2,1,0:T(8,128)(2,1)S(1)} %equalize.3.refs_0_), channel_id=1, source_target_pairs={{0,2},{1,3},{2,0},{3,1},{4,6},{5,7},{6,4},{7,5},{8,10},{9,11},{10,... | collective-permute-start | bytes 786440 | tf_op jit(solution)/shard_map/ppermute | solution.py:471
  17.4 7.8 %collective-permute-start.13 = (bf16[2,256,256]{2,1,0:T(8,128)(2,1)S(1)}, bf16[2,256,256]{2,1,0:T(8,128)(2,1)S(1)}, u32[]{:S(2)}, u32[]{:S(2)}) collective-permute-start(bf16[2,256,256]{2,1,0:T(8,128)(2,1)S(1)} %equalize.3.refs_0_), channel_id=1, source_target_pairs={{0,4},{4,0},{1,5},{5,1},{2,6},{6,2},{3,7},{7,3},{8,12},{12,8},{9,1... | collective-permute-start | bytes 786440 | tf_op jit(solution)/shard_map/ppermute | solution.py:472
  21.1 7.5 %collective-permute-start.4 = (bf16[2,256,256]{2,1,0:T(8,128)(2,1)S(1)}, bf16[2,256,256]{2,1,0:T(8,128)(2,1)S(1)}, u32[]{:S(2)}, u32[]{:S(2)}) collective-permute-start(bf16[2,256,256]{2,1,0:T(8,128)(2,1)S(1)} %equalize.2.refs_2_.refs_0_), channel_id=1, source_target_pairs={{0,2},{1,3},{2,0},{3,1},{4,6},{5,7},{6,4},{7,5},{8,10},{9,11},{10,... | collective-permute-start | bytes 786440 | tf_op jit(solution)/shard_map/ppermute | solution.py:471
  22.6 6.8 %collective-permute-start.7 = (bf16[2,256,256]{2,1,0:T(8,128)(2,1)S(1)}, bf16[2,256,256]{2,1,0:T(8,128)(2,1)S(1)}, u32[]{:S(2)}, u32[]{:S(2)}) collective-permute-start(bf16[2,256,256]{2,1,0:T(8,128)(2,1)S(1)} %equalize.2.refs_2_.refs_0_), channel_id=1, source_target_pairs={{0,4},{4,0},{1,5},{5,1},{2,6},{6,2},{3,7},{7,3},{8,12},{12,8},{9,1... | collective-permute-start | bytes 786440 | tf_op jit(solution)/shard_map/ppermute | solution.py:472
  24.7 4.7 %collective-permute-start.11 = (bf16[2,256,256]{2,1,0:T(8,128)(2,1)S(1)}, bf16[2,256,256]{2,1,0:T(8,128)(2,1)S(1)}, u32[]{:S(2)}, u32[]{:S(2)}) collective-permute-start(bf16[2,256,256]{2,1,0:T(8,128)(2,1)S(1)} %get-tuple-element.38), channel_id=1, source_target_pairs={{0,1},{1,0},{2,3},{3,2},{4,5},{5,4},{6,7},{7,6},{8,9},{9,8},{10,11... | collective-permute-start | bytes 786440 | tf_op jit(solution)/shard_map/ppermute | solution.py:481
  24.8 4.7 %collective-permute-start.12 = (bf16[2,256,256]{2,1,0:T(8,128)(2,1)S(1)}, bf16[2,256,256]{2,1,0:T(8,128)(2,1)S(1)}, u32[]{:S(2)}, u32[]{:S(2)}) collective-permute-start(bf16[2,256,256]{2,1,0:T(8,128)(2,1)S(1)} %get-tuple-element.37.refs_1_), channel_id=1, source_target_pairs={{0,1},{1,0},{2,3},{3,2},{4,5},{5,4},{6,7},{7,6},{8,9},{9,8},{10,11... | collective-permute-start | bytes 786440 | tf_op jit(solution)/shard_map/ppermute | solution.py:482
  25.3 4.9 %collective-permute-start.5 = (bf16[2,256,256]{2,1,0:T(8,128)(2,1)S(1)}, bf16[2,256,256]{2,1,0:T(8,128)(2,1)S(1)}, u32[]{:S(2)}, u32[]{:S(2)}) collective-permute-start(bf16[2,256,256]{2,1,0:T(8,128)(2,1)S(1)} %equalize.2.refs_2_.refs_0_), channel_id=1, source_target_pairs={{0,1},{1,0},{2,3},{3,2},{4,5},{5,4},{6,7},{7,6},{8,9},{9,8},{10,11... | collective-permute-start | bytes 786440 | tf_op jit(solution)/shard_map/ppermute | solution.py:481
  28.5 1.7 %collective-permute-start.6 = (bf16[2,256,256]{2,1,0:T(8,128)(2,1)S(1)}, bf16[2,256,256]{2,1,0:T(8,128)(2,1)S(1)}, u32[]{:S(2)}, u32[]{:S(2)}) collective-permute-start(bf16[2,256,256]{2,1,0:T(8,128)(2,1)S(1)} %collective-permute-done.4.refs_1_), channel_id=1, source_target_pairs={{0,1},{1,0},{2,3},{3,2},{4,5},{5,4},{6,7},{7,6},{8,9},{9,8},{10,11... | collective-permute-start | bytes 786440 | tf_op jit(solution)/shard_map/ppermute | solution.py:482

commit v17 on v16

--- a/solution.py
+++ b/solution.py
@@ -21,6 +21,7 @@
 BATCH = 4
 PARTS = 2
 VMEM_BYTES = 16 * 1024 * 1024
+EXTRA_ROWS = 16
 FILTER_VMEM_BYTES = 101 * 512 * 1024
 COEF_ROWS = 64
 
@@ -226,7 +227,9 @@
 def equalize_kernel(owners, frames, h, part, *refs):
     pieces = refs[owners - 1 :: -1]
     gains_ref, by_time, by_channel = refs[owners], refs[-2], refs[-1]
-    out_ref = refs[owners + 1]
+    out_refs = refs[owners + 1 : -2]
+    for out_ref in out_refs[1:]:
+        out_ref[:, h * SIG :, :] = jnp.zeros((2, EXTRA_ROWS, out_ref.shape[2]), jnp.bfloat16)
     width = 4 * h
     own_rows = frames * SIG
     over = (TAPS - 1) * SIG
@@ -259,18 +262,21 @@
                     ]
     for r in range(2):
         for tile in range(2 * tiles):
-            out_ref[r, :, tile * LANES : (tile + 1) * LANES] = by_channel[r * 2 * tiles + tile].astype(jnp.bfloat16)
+            for out_ref in out_refs:
+                ready = by_channel[r * 2 * tiles + tile].astype(jnp.bfloat16)
+                out_ref[r, : h * SIG, tile * LANES : (tile + 1) * LANES] = ready
 
 
 def equalize(pieces, gains, part, frames):
     owners = len(pieces)
     h = gains.shape[0] // PARTS // 2
     times = owners * frames
+    lengths = [h * SIG] + ([h * SIG + EXTRA_ROWS] if part == PARTS - 1 else [])
     return pl.pallas_call(
         functools.partial(equalize_kernel, owners, frames, h, part),
-        out_shape=jax.ShapeDtypeStruct((2, h * SIG, 2 * times), jnp.bfloat16),
+        out_shape=[jax.ShapeDtypeStruct((2, rows, 2 * times), jnp.bfloat16) for rows in lengths],
         in_specs=[IN_VMEM] * (owners + 1),
-        out_specs=IN_VMEM,
+        out_specs=[IN_VMEM] * len(lengths),
         scratch_shapes=[
             pltpu.VMEM((times * SIG, LANES), jnp.float32),
             pltpu.VMEM((4 * times // LANES, h * SIG, LANES), jnp.float32),
@@ -467,9 +473,10 @@
             if part == 0:
                 *pieces, gains = pieces
             later = to_owners([pieces[0], *held_back(pieces[1:], arrived[-1:])])
-        own.append(equalize(arrived, gains, part, frames))
+        block, *longer = equalize(arrived, gains, part, frames)
+        own.append(block)
         far = [lax.ppermute(own[part], "bcol", across[d]) for d in range(1, chips)]
-        column = [lax.ppermute(own[part], "brow", along[d]) for d in range(1, n_row)]
+        column = [lax.ppermute((longer or own)[-1], "brow", along[d]) for d in range(1, n_row)]
         panels.append((far, column))
         arrived = later
     result = [tile_map]
@@ -480,9 +487,10 @@
             mine, *far = held_back([mine] + far, own[-1:])
         beside = lax.ppermute(mine, "bcol", other_core)
         relayed = [lax.ppermute(block, "bcol", other_core) for block in far]
+        if part > 0:
+            column = list(held_back(column, result[1:]))
         blocks = [own[part]] + far + [beside] + relayed + column
-        after = panels[-1][1] if part == 0 else []
-        result = correlate(blocks, list(result) + after, part, n_row, n_col)
+        result = correlate(blocks, result, part, n_row, n_col)
     return jnp.transpose(result[0], (3, 0, 1, 2))[None, None]
 
 

time: 32 us -> 31.8 us (level)
    ppermute x2, waiting for transfers between devices: 0.9 us -> 0.49 us  [shards(): lax.ppermute((longer or own)[-1], 'brow', along[d])]
  transfers between devices with their start and end apart: 14 -> 14, of which waited for: 6 -> 7; matrix products, arithmetic and copies ran while one was open for 0% -> 0% of each run, Pallas kernels for 7% -> 7%
where the time goes in v17:
time: 31.8 us; the launch traced here: 31.7 us
  starting transfers between devices  16.9 us (53%)
  waiting for transfers between devices  8.07 us (25%)
  Pallas kernels  6.64 us (21%)
    ppermute x6, starting transfers between devices, to_owners(): lax.ppermute(pieces[d], 'chan', [(i, i ^ d) for i in range(owners)])  10.7 us
    ppermute x6, waiting for transfers between devices, to_owners(): lax.ppermute(pieces[d], 'chan', [(i, i ^ d) for i in range(owners)])  3.68 us
    ppermute x2, waiting for transfers between devices, shards(): far = [lax.ppermute(own[part], 'bcol', across[d]) for d in range(1, chips)]  3.64 us
    ppermute x2, starting transfers between devices, shards(): lax.ppermute((longer or own)[-1], 'brow', along[d])  3.04 us
    pallas_call x1, Pallas kernels, filtered_and_first(): pl.pallas_call(functools.partial(filter_kernel, frames, pieces, spectrum_...  2.65 us
    ppermute x2, starting transfers between devices, shards(): far = [lax.ppermute(own[part], 'bcol', across[d]) for d in range(1, chips)]  2.52 us
    pallas_call x2, Pallas kernels, correlate(): pl.pallas_call(functools.partial(correlate_kernel, n_row, n_col, h, times...  2.36 us
    pallas_call x2, Pallas kernels, equalize(): pl.pallas_call(functools.partial(equalize_kernel, owners, frames, h, part...  0.93 us
  transfers between devices with their start and end apart: 14, of which 7 were waited for; matrix products, arithmetic and copies ran while one was open for 0% of the time, Pallas kernels for 7%

profile of v17, /device:TPU:0, one launch (start us, length us, event | category | flops | bytes accessed | tf_op | source)
XLA Modules:
  0.0 31.7 jit_solution(8392662358739023832)
XLA Ops:
  0.0 0.0 copy-start
  0.0 0.0 copy-start.1
  0.0 2.6 %filter_and_transform.1 = (bf16[280,128]{1,0:T(8,128)(2,1)S(1)}, bf16[280,128]{1,0:T(8,128)(2,1)S(1)}, bf16[280,128]{1,0:T(8,128)(2,1)S(1)}, bf16[280,128]{1,0:T...) custom-call(s32[2,8,32768]{2,1,0:T(8,128)} %volt_hbm.1, ...), custom_call_target="tpu_custom_call" | custom-call | flops 536870912 | bytes 4194304 | tf_op jit(solution)/shard_map/filter_and_transform/pallas_call | solution.py:179
  2.7 5.1 %collective-permute-start = (bf16[280,128]{1,0:T(8,128)(2,1)S(1)}, bf16[280,128]{1,0:T(8,128)(2,1)S(1)}, u32[]{:S(2)}, u32[]{:S(2)}) collective-permute-start(bf16[280,128]{1,0:T(8,128)(2,1)S(1)} %get-tuple-element.30), channel_id=1, source_target_pairs={{0,24},{8,16},{16,8},{24,0},{1,25},{9,17},{17,9},{25,1},{2,26},{10... | collective-permute-start | bytes 215048 | tf_op jit(solution)/shard_map/ppermute | solution.py:435
  7.8 0.0 collective-permute-start.8
  7.8 0.6 %collective-permute-start.9 = (bf16[280,128]{1,0:T(8,128)(2,1)S(1)}, bf16[280,128]{1,0:T(8,128)(2,1)S(1)}, u32[]{:S(2)}, u32[]{:S(2)}) collective-permute-start(bf16[280,128]{1,0:T(8,128)(2,1)S(1)} %get-tuple-element.39), channel_id=1, source_target_pairs={{0,8},{8,0},{16,24},{24,16},{1,9},{9,1},{17,25},{25,17},{2,10},{10... | collective-permute-start | bytes 215048 | tf_op jit(solution)/shard_map/ppermute | solution.py:435
  8.4 0.0 copy-done
  8.4 0.0 copy-done.1
  8.4 0.0 copy-start.2
  8.4 0.6 %transform.1 = (bf16[280,128]{1,0:T(8,128)(2,1)S(1)}, bf16[280,128]{1,0:T(8,128)(2,1)S(1)}, bf16[280,128]{1,0:T(8,128)(2,1)S(1)}, bf16[280,128]{1,0:T(8,128)(2,1)S(1)}, f32[128,16]{1,0:T(8,128)S(1)}) custom-call(bf16[2,288,1024]{2,1,0:T(8,128)(2,1)S(1)} %get-tuple-element.25.filt, bf16[2048,256]{1,0:T(8,128)(2,1)S(1)} %get-tuple-element.26.later, ...), custom_call_target="tpu_custom_call" | custom-call | flops 536870912 | bytes 2097152 | tf_op jit(solution)/shard_map/transform/pallas_call | solution.py:215
  9.1 1.4 %collective-permute-done.refs_3_.refs_0_ = bf16[280,128]{1,0:T(8,128)(2,1)S(1)} collective-permute-done((bf16[280,128]{1,0:T(8,128)(2,1)S(1)}, bf16[280,128]{1,0:T(8,128)(2,1)S(1)}, u32[]{:S(2)}, u32[]{:S(2)}) %collective-permute-start) | collective-permute-done | bytes 71712 | tf_op jit(solution)/shard_map/ppermute | solution.py:435
  10.5 4.3 %collective-permute-start.1 = (bf16[280,128]{1,0:T(8,128)(2,1)S(1)}, bf16[280,128]{1,0:T(8,128)(2,1)S(1)}, u32[]{:S(2)}, u32[]{:S(2)}) collective-permute-start(bf16[280,128]{1,0:T(8,128)(2,1)S(1)} %get-tuple-element.31), channel_id=1, source_target_pairs={{0,24},{8,16},{16,8},{24,0},{1,25},{9,17},{17,9},{25,1},{2,26},{10... | collective-permute-start | bytes 215048 | tf_op jit(solution)/shard_map/ppermute | solution.py:435
  14.8 0.3 collective-permute-start.2
  15.0 0.4 %collective-permute-start.3 = (bf16[280,128]{1,0:T(8,128)(2,1)S(1)}, bf16[280,128]{1,0:T(8,128)(2,1)S(1)}, u32[]{:S(2)}, u32[]{:S(2)}) collective-permute-start(bf16[280,128]{1,0:T(8,128)(2,1)S(1)} %get-tuple-element.33), channel_id=1, source_target_pairs={{0,8},{8,0},{16,24},{24,16},{1,9},{9,1},{17,25},{25,17},{2,10},{10... | collective-permute-start | bytes 215048 | tf_op jit(solution)/shard_map/ppermute | solution.py:435
  15.4 0.6 %collective-permute-done.8.refs_1_ = bf16[280,128]{1,0:T(8,128)(2,1)S(1)} collective-permute-done((bf16[280,128]{1,0:T(8,128)(2,1)S(1)}, bf16[280,128]{1,0:T(8,128)(2,1)S(1)}, u32[]{:S(2)}, u32[]{:S(2)}) %collective-permute-start.8) | collective-permute-done | bytes 71712 | tf_op jit(solution)/shard_map/ppermute | solution.py:435
  16.0 0.0 collective-permute-done.9.refs_2_
  16.0 0.4 %equalize.3.refs_0_ = bf16[2,256,256]{2,1,0:T(8,128)(2,1)S(1)} custom-call(bf16[280,128]{1,0:T(8,128)(2,1)S(1)} %collective-permute-done.refs_3_.refs_0_, bf16[280,128]{1,0:T(8,128)(2,1)S(1)} %collective-permute-done.8.refs_1_, bf16[280,128]{1,0:T(8,128)(2,1)S(1)} %collective-permute-done.9.refs_2_, bf16[280,128]{1,0:T(8,128)(2,1)S(1)} %get-tuple-element.40.refs_3_, ...), custom_call_target="tpu_custom_call" | custom-call | bytes 1024 | tf_op jit(solution)/shard_map/equalize/pallas_call | solution.py:275
  16.5 1.0 %collective-permute-start.10 = (bf16[2,256,256]{2,1,0:T(8,128)(2,1)S(1)}, bf16[2,256,256]{2,1,0:T(8,128)(2,1)S(1)}, u32[]{:S(2)}, u32[]{:S(2)}) collective-permute-start(bf16[2,256,256]{2,1,0:T(8,128)(2,1)S(1)} %equalize.3.refs_0_), channel_id=1, source_target_pairs={{0,2},{1,3},{2,0},{3,1},{4,6},{5,7},{6,4},{7,5},{8,10},{9,11},{10,... | collective-permute-start | bytes 786440 | tf_op jit(solution)/shard_map/ppermute | solution.py:478
  17.4 1.5 %collective-permute-start.13 = (bf16[2,256,256]{2,1,0:T(8,128)(2,1)S(1)}, bf16[2,256,256]{2,1,0:T(8,128)(2,1)S(1)}, u32[]{:S(2)}, u32[]{:S(2)}) collective-permute-start(bf16[2,256,256]{2,1,0:T(8,128)(2,1)S(1)} %equalize.3.refs_0_), channel_id=1, source_target_pairs={{0,4},{4,0},{1,5},{5,1},{2,6},{6,2},{3,7},{7,3},{8,12},{12,8},{9,1... | collective-permute-start | bytes 786440 | tf_op jit(solution)/shard_map/ppermute | solution.py:479
  19.0 0.0 collective-permute-done.1.refs_0_
  19.0 1.7 %collective-permute-done.2.refs_1_ = bf16[280,128]{1,0:T(8,128)(2,1)S(1)} collective-permute-done((bf16[280,128]{1,0:T(8,128)(2,1)S(1)}, bf16[280,128]{1,0:T(8,128)(2,1)S(1)}, u32[]{:S(2)}, u32[]{:S(2)}) %collective-permute-start.2) | collective-permute-done | bytes 71712 | tf_op jit(solution)/shard_map/ppermute | solution.py:435
  20.6 0.0 collective-permute-done.3.refs_2_
  20.6 0.5 %equalize.2 = (bf16[2,256,256]{2,1,0:T(8,128)(2,1)S(1)}, bf16[2,272,256]{2,1,0:T(8,128)(2,1)S(1)}) custom-call(bf16[280,128]{1,0:T(8,128)(2,1)S(1)} %collective-permute-done.1.refs_0_, bf16[280,128]{1,0:T(8,128)(2,1)S(1)} %collective-permute-done.2.refs_1_, bf16[280,128]{1,0:T(8,128)(2,1)S(1)} %collective-permute-done.3.refs_2_, ...), custom_call_target="tpu_custom_call" | custom-call | bytes 1024 | tf_op jit(solution)/shard_map/equalize/pallas_call | solution.py:275
  21.1 1.6 %collective-permute-start.4 = (bf16[2,256,256]{2,1,0:T(8,128)(2,1)S(1)}, bf16[2,256,256]{2,1,0:T(8,128)(2,1)S(1)}, u32[]{:S(2)}, u32[]{:S(2)}) collective-permute-start(bf16[2,256,256]{2,1,0:T(8,128)(2,1)S(1)} %get-tuple-element.36.refs_2_.refs_0_), channel_id=1, source_target_pairs={{0,2},{1,3},{2,0},{3,1},{4,6},{5,7},{6,4},{7,5},{8,10},{9,11},{10,... | collective-permute-start | bytes 786440 | tf_op jit(solution)/shard_map/ppermute | solution.py:478
  22.7 1.5 %collective-permute-start.7 = (bf16[2,272,256]{2,1,0:T(8,128)(2,1)S(1)}, bf16[2,272,256]{2,1,0:T(8,128)(2,1)S(1)}, u32[]{:S(2)}, u32[]{:S(2)}) collective-permute-start(bf16[2,272,256]{2,1,0:T(8,128)(2,1)S(1)} %get-tuple-element.37), channel_id=1, source_target_pairs={{0,4},{4,0},{1,5},{5,1},{2,6},{6,2},{3,7},{7,3},{8,12},{12,8},{9,1... | collective-permute-start | bytes 835592 | tf_op jit(solution)/shard_map/ppermute | solution.py:479
  24.2 0.4 %collective-permute-done.10.refs_1_ = bf16[2,256,256]{2,1,0:T(8,128)(2,1)S(1)} collective-permute-done((bf16[2,256,256]{2,1,0:T(8,128)(2,1)S(1)}, bf16[2,256,256]{2,1,0:T(8,128)(2,1)S(1)}, u32[]{:S(2)}, u32[]{:S(2)}) %collective-permute-start.10) | collective-permute-done | bytes 262176 | tf_op jit(solution)/shard_map/ppermute | solution.py:478
  24.7 0.1 collective-permute-start.11
  24.7 0.5 %collective-permute-start.12 = (bf16[2,256,256]{2,1,0:T(8,128)(2,1)S(1)}, bf16[2,256,256]{2,1,0:T(8,128)(2,1)S(1)}, u32[]{:S(2)}, u32[]{:S(2)}) collective-permute-start(bf16[2,256,256]{2,1,0:T(8,128)(2,1)S(1)} %get-tuple-element.41.refs_1_), channel_id=1, source_target_pairs={{0,1},{1,0},{2,3},{3,2},{4,5},{5,4},{6,7},{7,6},{8,9},{9,8},{10,11... | collective-permute-start | bytes 786440 | tf_op jit(solution)/shard_map/ppermute | solution.py:489
  25.2 0.0 collective-permute-done.13.refs_4_
  25.2 0.1 collective-permute-start.5
  25.3 3.2 %collective-permute-done.4.refs_1_ = bf16[2,256,256]{2,1,0:T(8,128)(2,1)S(1)} collective-permute-done((bf16[2,256,256]{2,1,0:T(8,128)(2,1)S(1)}, bf16[2,256,256]{2,1,0:T(8,128)(2,1)S(1)}, u32[]{:S(2)}, u32[]{:S(2)}) %collective-permute-start.4) | collective-permute-done | bytes 262176 | tf_op jit(solution)/shard_map/ppermute | solution.py:478
  28.5 0.0 collective-permute-start.6
  28.5 0.0 collective-permute-done.11.refs_2_
  28.5 0.0 collective-permute-done.12.refs_3_
  28.5 0.0 copy-done.2
  28.5 0.7 %correlate.2 = (f32[2,2,4,32,128]{4,3,2,1,0:T(8,128)S(1)}, f32[2,4,8,128]{3,2,1,0:T(8,128)S(1)}) custom-call(bf16[2,256,256]{2,1,0:T(8,128)(2,1)S(1)} %equalize.3.refs_0_, bf16[2,256,256]{2,1,0:T(8,128)(2,1)S(1)} %get-tuple-element.41.refs_1_, bf16[2,256,256]{2,1,0:T(8,128)(2,1)S(1)} %collective-permute-done.11.refs_2_, ...), custom_call_target="tpu_custom_call" | custom-call | bytes 1024 | tf_op jit(solution)/shard_map/correlate/pallas_call | solution.py:419
  29.3 0.5 %collective-permute-done.7.refs_0_ = bf16[2,272,256]{2,1,0:T(8,128)(2,1)S(1)} collective-permute-done((bf16[2,272,256]{2,1,0:T(8,128)(2,1)S(1)}, bf16[2,272,256]{2,1,0:T(8,128)(2,1)S(1)}, u32[]{:S(2)}, u32[]{:S(2)}) %collective-permute-start.7) | collective-permute-done | bytes 278560 | tf_op jit(solution)/shard_map/ppermute | solution.py:479
  29.8 0.0 collective-permute-done.5.refs_2_
  29.8 0.2 collective-permute-done.6.refs_3_
  30.1 1.6 %correlate.3 = f32[2,16,32,128]{3,2,1,0:T(8,128)} custom-call(bf16[2,256,256]{2,1,0:T(8,128)(2,1)S(1)} %get-tuple-element.36.refs_2_.refs_0_, bf16[2,256,256]{2,1,0:T(8,128)(2,1)S(1)} %collective-permute-done.4.refs_1_, bf16[2,256,256]{2,1,0:T(8,128)(2,1)S(1)} %collective-permute-done.5.refs_2_, bf16[2,256,256]{2,1,0:T(8,128)(2,1)S(1)} %collective-permute-done.6.refs_3_, ...), custom_call_target="tpu_custom_call" | custom-call | bytes 1024 | tf_op jit(solution)/shard_map/correlate/pallas_call | solution.py:419
  (3 shorter events, 0.1 us)
Async XLA Ops:
  0.0 8.4 %copy-start = (f32[128,128]{1,0:T(8,128)S(1)}, f32[128,128]{1,0:T(8,128)}, u32[]{:S(2)}) copy-start(f32[128,128]{1,0:T(8,128)} %constant.5.clone.pick_ref) | copy-start | bytes 196612
  0.0 8.4 %copy-start.1 = (f32[8,2,128]{2,1,0:T(2,128)S(1)}, f32[8,2,128]{2,1,0:T(2,128)}, u32[]{:S(2)}) copy-start(f32[8,2,128]{2,1,0:T(2,128)} %gains_ref.1) | copy-start | bytes 24580
  2.7 7.8 %collective-permute-start = (bf16[280,128]{1,0:T(8,128)(2,1)S(1)}, bf16[280,128]{1,0:T(8,128)(2,1)S(1)}, u32[]{:S(2)}, u32[]{:S(2)}) collective-permute-start(bf16[280,128]{1,0:T(8,128)(2,1)S(1)} %get-tuple-element.30), channel_id=1, source_target_pairs={{0,24},{8,16},{16,8},{24,0},{1,25},{9,17},{17,9},{25,1},{2,26},{10... | collective-permute-start | bytes 215048 | tf_op jit(solution)/shard_map/ppermute | solution.py:435
  7.8 8.2 %collective-permute-start.8 = (bf16[280,128]{1,0:T(8,128)(2,1)S(1)}, bf16[280,128]{1,0:T(8,128)(2,1)S(1)}, u32[]{:S(2)}, u32[]{:S(2)}) collective-permute-start(bf16[280,128]{1,0:T(8,128)(2,1)S(1)} %get-tuple-element.38), channel_id=1, source_target_pairs={{0,16},{8,24},{16,0},{24,8},{1,17},{9,25},{17,1},{25,9},{2,18},{10... | collective-permute-start | bytes 215048 | tf_op jit(solution)/shard_map/ppermute | solution.py:435
  7.8 8.2 %collective-permute-start.9 = (bf16[280,128]{1,0:T(8,128)(2,1)S(1)}, bf16[280,128]{1,0:T(8,128)(2,1)S(1)}, u32[]{:S(2)}, u32[]{:S(2)}) collective-permute-start(bf16[280,128]{1,0:T(8,128)(2,1)S(1)} %get-tuple-element.39), channel_id=1, source_target_pairs={{0,8},{8,0},{16,24},{24,16},{1,9},{9,1},{17,25},{25,17},{2,10},{10... | collective-permute-start | bytes 215048 | tf_op jit(solution)/shard_map/ppermute | solution.py:435
  8.4 20.1 %copy-start.2 = (s32[8,8]{1,0:T(8,128)S(1)}, s32[8,8]{1,0:T(8,128)}, u32[]{:S(2)}) copy-start(s32[8,8]{1,0:T(8,128)} %refs_5_.1) | copy-start | bytes 772
  10.5 8.5 %collective-permute-start.1 = (bf16[280,128]{1,0:T(8,128)(2,1)S(1)}, bf16[280,128]{1,0:T(8,128)(2,1)S(1)}, u32[]{:S(2)}, u32[]{:S(2)}) collective-permute-start(bf16[280,128]{1,0:T(8,128)(2,1)S(1)} %get-tuple-element.31), channel_id=1, source_target_pairs={{0,24},{8,16},{16,8},{24,0},{1,25},{9,17},{17,9},{25,1},{2,26},{10... | collective-permute-start | bytes 215048 | tf_op jit(solution)/shard_map/ppermute | solution.py:435
  14.8 5.8 %collective-permute-start.2 = (bf16[280,128]{1,0:T(8,128)(2,1)S(1)}, bf16[280,128]{1,0:T(8,128)(2,1)S(1)}, u32[]{:S(2)}, u32[]{:S(2)}) collective-permute-start(bf16[280,128]{1,0:T(8,128)(2,1)S(1)} %get-tuple-element.32), channel_id=1, source_target_pairs={{0,16},{8,24},{16,0},{24,8},{1,17},{9,25},{17,1},{25,9},{2,18},{10... | collective-permute-start | bytes 215048 | tf_op jit(solution)/shard_map/ppermute | solution.py:435
  15.0 5.6 %collective-permute-start.3 = (bf16[280,128]{1,0:T(8,128)(2,1)S(1)}, bf16[280,128]{1,0:T(8,128)(2,1)S(1)}, u32[]{:S(2)}, u32[]{:S(2)}) collective-permute-start(bf16[280,128]{1,0:T(8,128)(2,1)S(1)} %get-tuple-element.33), channel_id=1, source_target_pairs={{0,8},{8,0},{16,24},{24,16},{1,9},{9,1},{17,25},{25,17},{2,10},{10... | collective-permute-start | bytes 215048 | tf_op jit(solution)/shard_map/ppermute | solution.py:435
  16.5 8.1 %collective-permute-start.10 = (bf16[2,256,256]{2,1,0:T(8,128)(2,1)S(1)}, bf16[2,256,256]{2,1,0:T(8,128)(2,1)S(1)}, u32[]{:S(2)}, u32[]{:S(2)}) collective-permute-start(bf16[2,256,256]{2,1,0:T(8,128)(2,1)S(1)} %equalize.3.refs_0_), channel_id=1, source_target_pairs={{0,2},{1,3},{2,0},{3,1},{4,6},{5,7},{6,4},{7,5},{8,10},{9,11},{10,... | collective-permute-start | bytes 786440 | tf_op jit(solution)/shard_map/ppermute | solution.py:478
  17.4 7.8 %collective-permute-start.13 = (bf16[2,256,256]{2,1,0:T(8,128)(2,1)S(1)}, bf16[2,256,256]{2,1,0:T(8,128)(2,1)S(1)}, u32[]{:S(2)}, u32[]{:S(2)}) collective-permute-start(bf16[2,256,256]{2,1,0:T(8,128)(2,1)S(1)} %equalize.3.refs_0_), channel_id=1, source_target_pairs={{0,4},{4,0},{1,5},{5,1},{2,6},{6,2},{3,7},{7,3},{8,12},{12,8},{9,1... | collective-permute-start | bytes 786440 | tf_op jit(solution)/shard_map/ppermute | solution.py:479
  21.1 7.4 %collective-permute-start.4 = (bf16[2,256,256]{2,1,0:T(8,128)(2,1)S(1)}, bf16[2,256,256]{2,1,0:T(8,128)(2,1)S(1)}, u32[]{:S(2)}, u32[]{:S(2)}) collective-permute-start(bf16[2,256,256]{2,1,0:T(8,128)(2,1)S(1)} %get-tuple-element.36.refs_2_.refs_0_), channel_id=1, source_target_pairs={{0,2},{1,3},{2,0},{3,1},{4,6},{5,7},{6,4},{7,5},{8,10},{9,11},{10,... | collective-permute-start | bytes 786440 | tf_op jit(solution)/shard_map/ppermute | solution.py:478
  22.7 7.1 %collective-permute-start.7 = (bf16[2,272,256]{2,1,0:T(8,128)(2,1)S(1)}, bf16[2,272,256]{2,1,0:T(8,128)(2,1)S(1)}, u32[]{:S(2)}, u32[]{:S(2)}) collective-permute-start(bf16[2,272,256]{2,1,0:T(8,128)(2,1)S(1)} %get-tuple-element.37), channel_id=1, source_target_pairs={{0,4},{4,0},{1,5},{5,1},{2,6},{6,2},{3,7},{7,3},{8,12},{12,8},{9,1... | collective-permute-start | bytes 835592 | tf_op jit(solution)/shard_map/ppermute | solution.py:479
  24.7 3.9 %collective-permute-start.11 = (bf16[2,256,256]{2,1,0:T(8,128)(2,1)S(1)}, bf16[2,256,256]{2,1,0:T(8,128)(2,1)S(1)}, u32[]{:S(2)}, u32[]{:S(2)}) collective-permute-start(bf16[2,256,256]{2,1,0:T(8,128)(2,1)S(1)} %get-tuple-element.42), channel_id=1, source_target_pairs={{0,1},{1,0},{2,3},{3,2},{4,5},{5,4},{6,7},{7,6},{8,9},{9,8},{10,11... | collective-permute-start | bytes 786440 | tf_op jit(solution)/shard_map/ppermute | solution.py:488
  24.7 3.8 %collective-permute-start.12 = (bf16[2,256,256]{2,1,0:T(8,128)(2,1)S(1)}, bf16[2,256,256]{2,1,0:T(8,128)(2,1)S(1)}, u32[]{:S(2)}, u32[]{:S(2)}) collective-permute-start(bf16[2,256,256]{2,1,0:T(8,128)(2,1)S(1)} %get-tuple-element.41.refs_1_), channel_id=1, source_target_pairs={{0,1},{1,0},{2,3},{3,2},{4,5},{5,4},{6,7},{7,6},{8,9},{9,8},{10,11... | collective-permute-start | bytes 786440 | tf_op jit(solution)/shard_map/ppermute | solution.py:489
  25.2 4.6 %collective-permute-start.5 = (bf16[2,256,256]{2,1,0:T(8,128)(2,1)S(1)}, bf16[2,256,256]{2,1,0:T(8,128)(2,1)S(1)}, u32[]{:S(2)}, u32[]{:S(2)}) collective-permute-start(bf16[2,256,256]{2,1,0:T(8,128)(2,1)S(1)} %get-tuple-element.36.refs_2_.refs_0_), channel_id=1, source_target_pairs={{0,1},{1,0},{2,3},{3,2},{4,5},{5,4},{6,7},{7,6},{8,9},{9,8},{10,11... | collective-permute-start | bytes 786440 | tf_op jit(solution)/shard_map/ppermute | solution.py:488
  28.5 1.5 %collective-permute-start.6 = (bf16[2,256,256]{2,1,0:T(8,128)(2,1)S(1)}, bf16[2,256,256]{2,1,0:T(8,128)(2,1)S(1)}, u32[]{:S(2)}, u32[]{:S(2)}) collective-permute-start(bf16[2,256,256]{2,1,0:T(8,128)(2,1)S(1)} %collective-permute-done.4.refs_1_), channel_id=1, source_target_pairs={{0,1},{1,0},{2,3},{3,2},{4,5},{5,4},{6,7},{7,6},{8,9},{9,8},{10,11... | collective-permute-start | bytes 786440 | tf_op jit(solution)/shard_map/ppermute | solution.py:489

commit v18 on v17

--- a/solution.py
+++ b/solution.py
@@ -111,9 +111,9 @@
     per_term = TAPS * NCHAN // across
     coef[...] = sum(terms[t * per_term : (t + 1) * per_term, :].astype(jnp.float32) for t in range(3))
 
-    def filter_group(group, _):
-        base = pl.multiple_of(group * (GROUP * NCHAN), GROUP * NCHAN)
-        rows = pl.ds(pl.multiple_of(group * (GROUP * SIG), GROUP * SIG), GROUP * SIG)
+    def filter_group(start, count):
+        base = start * NCHAN
+        rows = slice(start * SIG, (start + count) * SIG)
         for column in range(HALF // LANES):
             for part in range(2):
                 halves = []
@@ -123,10 +123,10 @@
                     taps = [coef[i : i + 1, lane % across : lane % across + LANES] for i in at]
                     near = [
                         volt[part, :, pl.ds(base + f * NCHAN + lane, LANES)].astype(jnp.float32)
-                        for f in range(GROUP + TAPS - 1)
+                        for f in range(count + TAPS - 1)
                     ]
                     sums = []
-                    for m in range(GROUP):
+                    for m in range(count):
                         total = taps[0] * near[m]
                         for k in range(1, TAPS):
                             total = total + taps[k] * near[m + k]
@@ -135,13 +135,11 @@
                 where = pl.ds(part * HALF + column * LANES, LANES)
                 filt[0, rows, where] = (halves[0] + halves[1]).astype(jnp.bfloat16)
                 filt[1, rows, where] = (halves[0] - halves[1]).astype(jnp.bfloat16)
-        return 0
-
-    groups = per // GROUP
+
     for piece in range(pieces):
         copies[piece].wait()
-        lax.fori_loop(piece * groups, (piece + 1) * groups, filter_group, 0)
-    lax.fori_loop(frames // GROUP, frames // GROUP + 1, filter_group, 0)
+        filter_group(piece * per, per)
+    filter_group(frames, GROUP)
     table_copy.wait()
     transform(filt, table, scale, stage, out_refs)
     later_copy.wait()

time: 31.8 us -> 31.8 us (level)
  no operation moved by 1% of the time
where the time goes in v18:
time: 31.8 us; the launch traced here: 31.6 us
  starting transfers between devices  16.9 us (53%)
  waiting for transfers between devices  8.07 us (25%)
  Pallas kernels  6.56 us (21%)
    ppermute x6, starting transfers between devices, to_owners(): lax.ppermute(pieces[d], 'chan', [(i, i ^ d) for i in range(owners)])  10.7 us
    ppermute x6, waiting for transfers between devices, to_owners(): lax.ppermute(pieces[d], 'chan', [(i, i ^ d) for i in range(owners)])  3.68 us
    ppermute x2, waiting for transfers between devices, shards(): far = [lax.ppermute(own[part], 'bcol', across[d]) for d in range(1, chips)]  3.64 us
    ppermute x2, starting transfers between devices, shards(): lax.ppermute((longer or own)[-1], 'brow', along[d])  3.04 us
    pallas_call x1, Pallas kernels, filtered_and_first(): pl.pallas_call(functools.partial(filter_kernel, frames, pieces, spectrum_...  2.57 us
    ppermute x2, starting transfers between devices, shards(): far = [lax.ppermute(own[part], 'bcol', across[d]) for d in range(1, chips)]  2.52 us
    pallas_call x2, Pallas kernels, correlate(): pl.pallas_call(functools.partial(correlate_kernel, n_row, n_col, h, times...  2.37 us
    pallas_call x2, Pallas kernels, equalize(): pl.pallas_call(functools.partial(equalize_kernel, owners, frames, h, part...  0.93 us
  transfers between devices with their start and end apart: 14, of which 7 were waited for; matrix products, arithmetic and copies ran while one was open for 0% of the time, Pallas kernels for 7%

profile of v18, /device:TPU:0, one launch (start us, length us, event | category | flops | bytes accessed | tf_op | source)
XLA Modules:
  0.0 31.6 jit_solution(18373275163542081096)
XLA Ops:
  0.0 0.0 copy-start
  0.0 0.0 copy-start.1
  0.0 2.6 %filter_and_transform.1 = (bf16[280,128]{1,0:T(8,128)(2,1)S(1)}, bf16[280,128]{1,0:T(8,128)(2,1)S(1)}, bf16[280,128]{1,0:T(8,128)(2,1)S(1)}, bf16[280,128]{1,0:T...) custom-call(s32[2,8,32768]{2,1,0:T(8,128)} %volt_hbm.1, ...), custom_call_target="tpu_custom_call" | custom-call | flops 536870912 | bytes 4194304 | tf_op jit(solution)/shard_map/filter_and_transform/pallas_call | solution.py:177
  2.6 5.1 %collective-permute-start = (bf16[280,128]{1,0:T(8,128)(2,1)S(1)}, bf16[280,128]{1,0:T(8,128)(2,1)S(1)}, u32[]{:S(2)}, u32[]{:S(2)}) collective-permute-start(bf16[280,128]{1,0:T(8,128)(2,1)S(1)} %get-tuple-element.30), channel_id=1, source_target_pairs={{0,24},{8,16},{16,8},{24,0},{1,25},{9,17},{17,9},{25,1},{2,26},{10... | collective-permute-start | bytes 215048 | tf_op jit(solution)/shard_map/ppermute | solution.py:433
  7.7 0.0 collective-permute-start.8
  7.7 0.6 %collective-permute-start.9 = (bf16[280,128]{1,0:T(8,128)(2,1)S(1)}, bf16[280,128]{1,0:T(8,128)(2,1)S(1)}, u32[]{:S(2)}, u32[]{:S(2)}) collective-permute-start(bf16[280,128]{1,0:T(8,128)(2,1)S(1)} %get-tuple-element.39), channel_id=1, source_target_pairs={{0,8},{8,0},{16,24},{24,16},{1,9},{9,1},{17,25},{25,17},{2,10},{10... | collective-permute-start | bytes 215048 | tf_op jit(solution)/shard_map/ppermute | solution.py:433
  8.3 0.0 copy-done
  8.3 0.0 copy-done.1
  8.3 0.0 copy-start.2
  8.3 0.6 %transform.1 = (bf16[280,128]{1,0:T(8,128)(2,1)S(1)}, bf16[280,128]{1,0:T(8,128)(2,1)S(1)}, bf16[280,128]{1,0:T(8,128)(2,1)S(1)}, bf16[280,128]{1,0:T(8,128)(2,1)S(1)}, f32[128,16]{1,0:T(8,128)S(1)}) custom-call(bf16[2,288,1024]{2,1,0:T(8,128)(2,1)S(1)} %get-tuple-element.25.filt, bf16[2048,256]{1,0:T(8,128)(2,1)S(1)} %get-tuple-element.26.later, ...), custom_call_target="tpu_custom_call" | custom-call | flops 536870912 | bytes 2097152 | tf_op jit(solution)/shard_map/transform/pallas_call | solution.py:213
  9.0 1.4 %collective-permute-done.refs_3_.refs_0_ = bf16[280,128]{1,0:T(8,128)(2,1)S(1)} collective-permute-done((bf16[280,128]{1,0:T(8,128)(2,1)S(1)}, bf16[280,128]{1,0:T(8,128)(2,1)S(1)}, u32[]{:S(2)}, u32[]{:S(2)}) %collective-permute-start) | collective-permute-done | bytes 71712 | tf_op jit(solution)/shard_map/ppermute | solution.py:433
  10.4 4.3 %collective-permute-start.1 = (bf16[280,128]{1,0:T(8,128)(2,1)S(1)}, bf16[280,128]{1,0:T(8,128)(2,1)S(1)}, u32[]{:S(2)}, u32[]{:S(2)}) collective-permute-start(bf16[280,128]{1,0:T(8,128)(2,1)S(1)} %get-tuple-element.31), channel_id=1, source_target_pairs={{0,24},{8,16},{16,8},{24,0},{1,25},{9,17},{17,9},{25,1},{2,26},{10... | collective-permute-start | bytes 215048 | tf_op jit(solution)/shard_map/ppermute | solution.py:433
  14.7 0.3 collective-permute-start.2
  15.0 0.4 %collective-permute-start.3 = (bf16[280,128]{1,0:T(8,128)(2,1)S(1)}, bf16[280,128]{1,0:T(8,128)(2,1)S(1)}, u32[]{:S(2)}, u32[]{:S(2)}) collective-permute-start(bf16[280,128]{1,0:T(8,128)(2,1)S(1)} %get-tuple-element.33), channel_id=1, source_target_pairs={{0,8},{8,0},{16,24},{24,16},{1,9},{9,1},{17,25},{25,17},{2,10},{10... | collective-permute-start | bytes 215048 | tf_op jit(solution)/shard_map/ppermute | solution.py:433
  15.3 0.6 %collective-permute-done.8.refs_1_ = bf16[280,128]{1,0:T(8,128)(2,1)S(1)} collective-permute-done((bf16[280,128]{1,0:T(8,128)(2,1)S(1)}, bf16[280,128]{1,0:T(8,128)(2,1)S(1)}, u32[]{:S(2)}, u32[]{:S(2)}) %collective-permute-start.8) | collective-permute-done | bytes 71712 | tf_op jit(solution)/shard_map/ppermute | solution.py:433
  15.9 0.0 collective-permute-done.9.refs_2_
  15.9 0.4 %equalize.3.refs_0_ = bf16[2,256,256]{2,1,0:T(8,128)(2,1)S(1)} custom-call(bf16[280,128]{1,0:T(8,128)(2,1)S(1)} %collective-permute-done.refs_3_.refs_0_, bf16[280,128]{1,0:T(8,128)(2,1)S(1)} %collective-permute-done.8.refs_1_, bf16[280,128]{1,0:T(8,128)(2,1)S(1)} %collective-permute-done.9.refs_2_, bf16[280,128]{1,0:T(8,128)(2,1)S(1)} %get-tuple-element.40.refs_3_, ...), custom_call_target="tpu_custom_call" | custom-call | bytes 1024 | tf_op jit(solution)/shard_map/equalize/pallas_call | solution.py:273
  16.4 1.0 %collective-permute-start.10 = (bf16[2,256,256]{2,1,0:T(8,128)(2,1)S(1)}, bf16[2,256,256]{2,1,0:T(8,128)(2,1)S(1)}, u32[]{:S(2)}, u32[]{:S(2)}) collective-permute-start(bf16[2,256,256]{2,1,0:T(8,128)(2,1)S(1)} %equalize.3.refs_0_), channel_id=1, source_target_pairs={{0,2},{1,3},{2,0},{3,1},{4,6},{5,7},{6,4},{7,5},{8,10},{9,11},{10,... | collective-permute-start | bytes 786440 | tf_op jit(solution)/shard_map/ppermute | solution.py:476
  17.4 1.5 %collective-permute-start.13 = (bf16[2,256,256]{2,1,0:T(8,128)(2,1)S(1)}, bf16[2,256,256]{2,1,0:T(8,128)(2,1)S(1)}, u32[]{:S(2)}, u32[]{:S(2)}) collective-permute-start(bf16[2,256,256]{2,1,0:T(8,128)(2,1)S(1)} %equalize.3.refs_0_), channel_id=1, source_target_pairs={{0,4},{4,0},{1,5},{5,1},{2,6},{6,2},{3,7},{7,3},{8,12},{12,8},{9,1... | collective-permute-start | bytes 786440 | tf_op jit(solution)/shard_map/ppermute | solution.py:477
  18.9 0.0 collective-permute-done.1.refs_0_
  18.9 1.7 %collective-permute-done.2.refs_1_ = bf16[280,128]{1,0:T(8,128)(2,1)S(1)} collective-permute-done((bf16[280,128]{1,0:T(8,128)(2,1)S(1)}, bf16[280,128]{1,0:T(8,128)(2,1)S(1)}, u32[]{:S(2)}, u32[]{:S(2)}) %collective-permute-start.2) | collective-permute-done | bytes 71712 | tf_op jit(solution)/shard_map/ppermute | solution.py:433
  20.5 0.0 collective-permute-done.3.refs_2_
  20.5 0.5 %equalize.2 = (bf16[2,256,256]{2,1,0:T(8,128)(2,1)S(1)}, bf16[2,272,256]{2,1,0:T(8,128)(2,1)S(1)}) custom-call(bf16[280,128]{1,0:T(8,128)(2,1)S(1)} %collective-permute-done.1.refs_0_, bf16[280,128]{1,0:T(8,128)(2,1)S(1)} %collective-permute-done.2.refs_1_, bf16[280,128]{1,0:T(8,128)(2,1)S(1)} %collective-permute-done.3.refs_2_, ...), custom_call_target="tpu_custom_call" | custom-call | bytes 1024 | tf_op jit(solution)/shard_map/equalize/pallas_call | solution.py:273
  21.0 1.6 %collective-permute-start.4 = (bf16[2,256,256]{2,1,0:T(8,128)(2,1)S(1)}, bf16[2,256,256]{2,1,0:T(8,128)(2,1)S(1)}, u32[]{:S(2)}, u32[]{:S(2)}) collective-permute-start(bf16[2,256,256]{2,1,0:T(8,128)(2,1)S(1)} %get-tuple-element.36.refs_2_.refs_0_), channel_id=1, source_target_pairs={{0,2},{1,3},{2,0},{3,1},{4,6},{5,7},{6,4},{7,5},{8,10},{9,11},{10,... | collective-permute-start | bytes 786440 | tf_op jit(solution)/shard_map/ppermute | solution.py:476
  22.6 1.5 %collective-permute-start.7 = (bf16[2,272,256]{2,1,0:T(8,128)(2,1)S(1)}, bf16[2,272,256]{2,1,0:T(8,128)(2,1)S(1)}, u32[]{:S(2)}, u32[]{:S(2)}) collective-permute-start(bf16[2,272,256]{2,1,0:T(8,128)(2,1)S(1)} %get-tuple-element.37), channel_id=1, source_target_pairs={{0,4},{4,0},{1,5},{5,1},{2,6},{6,2},{3,7},{7,3},{8,12},{12,8},{9,1... | collective-permute-start | bytes 835592 | tf_op jit(solution)/shard_map/ppermute | solution.py:477
  24.1 0.4 %collective-permute-done.10.refs_1_ = bf16[2,256,256]{2,1,0:T(8,128)(2,1)S(1)} collective-permute-done((bf16[2,256,256]{2,1,0:T(8,128)(2,1)S(1)}, bf16[2,256,256]{2,1,0:T(8,128)(2,1)S(1)}, u32[]{:S(2)}, u32[]{:S(2)}) %collective-permute-start.10) | collective-permute-done | bytes 262176 | tf_op jit(solution)/shard_map/ppermute | solution.py:476
  24.6 0.1 collective-permute-start.11
  24.7 0.5 %collective-permute-start.12 = (bf16[2,256,256]{2,1,0:T(8,128)(2,1)S(1)}, bf16[2,256,256]{2,1,0:T(8,128)(2,1)S(1)}, u32[]{:S(2)}, u32[]{:S(2)}) collective-permute-start(bf16[2,256,256]{2,1,0:T(8,128)(2,1)S(1)} %get-tuple-element.41.refs_1_), channel_id=1, source_target_pairs={{0,1},{1,0},{2,3},{3,2},{4,5},{5,4},{6,7},{7,6},{8,9},{9,8},{10,11... | collective-permute-start | bytes 786440 | tf_op jit(solution)/shard_map/ppermute | solution.py:487
  25.1 0.0 collective-permute-done.13.refs_4_
  25.2 0.1 collective-permute-start.5
  25.2 3.2 %collective-permute-done.4.refs_1_ = bf16[2,256,256]{2,1,0:T(8,128)(2,1)S(1)} collective-permute-done((bf16[2,256,256]{2,1,0:T(8,128)(2,1)S(1)}, bf16[2,256,256]{2,1,0:T(8,128)(2,1)S(1)}, u32[]{:S(2)}, u32[]{:S(2)}) %collective-permute-start.4) | collective-permute-done | bytes 262176 | tf_op jit(solution)/shard_map/ppermute | solution.py:476
  28.4 0.0 collective-permute-start.6
  28.4 0.0 collective-permute-done.11.refs_2_
  28.5 0.0 collective-permute-done.12.refs_3_
  28.5 0.0 copy-done.2
  28.5 0.7 %correlate.2 = (f32[2,2,4,32,128]{4,3,2,1,0:T(8,128)S(1)}, f32[2,4,8,128]{3,2,1,0:T(8,128)S(1)}) custom-call(bf16[2,256,256]{2,1,0:T(8,128)(2,1)S(1)} %equalize.3.refs_0_, bf16[2,256,256]{2,1,0:T(8,128)(2,1)S(1)} %get-tuple-element.41.refs_1_, bf16[2,256,256]{2,1,0:T(8,128)(2,1)S(1)} %collective-permute-done.11.refs_2_, ...), custom_call_target="tpu_custom_call" | custom-call | bytes 1024 | tf_op jit(solution)/shard_map/correlate/pallas_call | solution.py:417
  29.2 0.5 %collective-permute-done.7.refs_0_ = bf16[2,272,256]{2,1,0:T(8,128)(2,1)S(1)} collective-permute-done((bf16[2,272,256]{2,1,0:T(8,128)(2,1)S(1)}, bf16[2,272,256]{2,1,0:T(8,128)(2,1)S(1)}, u32[]{:S(2)}, u32[]{:S(2)}) %collective-permute-start.7) | collective-permute-done | bytes 278560 | tf_op jit(solution)/shard_map/ppermute | solution.py:477
  29.7 0.0 collective-permute-done.5.refs_2_
  29.7 0.2 collective-permute-done.6.refs_3_
  30.0 1.6 %correlate.3 = f32[2,16,32,128]{3,2,1,0:T(8,128)} custom-call(bf16[2,256,256]{2,1,0:T(8,128)(2,1)S(1)} %get-tuple-element.36.refs_2_.refs_0_, bf16[2,256,256]{2,1,0:T(8,128)(2,1)S(1)} %collective-permute-done.4.refs_1_, bf16[2,256,256]{2,1,0:T(8,128)(2,1)S(1)} %collective-permute-done.5.refs_2_, bf16[2,256,256]{2,1,0:T(8,128)(2,1)S(1)} %collective-permute-done.6.refs_3_, ...), custom_call_target="tpu_custom_call" | custom-call | bytes 1024 | tf_op jit(solution)/shard_map/correlate/pallas_call | solution.py:417
  (3 shorter events, 0.1 us)
Async XLA Ops:
  0.0 8.3 %copy-start = (f32[128,128]{1,0:T(8,128)S(1)}, f32[128,128]{1,0:T(8,128)}, u32[]{:S(2)}) copy-start(f32[128,128]{1,0:T(8,128)} %constant.5.clone.pick_ref) | copy-start | bytes 196612
  0.0 8.3 %copy-start.1 = (f32[8,2,128]{2,1,0:T(2,128)S(1)}, f32[8,2,128]{2,1,0:T(2,128)}, u32[]{:S(2)}) copy-start(f32[8,2,128]{2,1,0:T(2,128)} %gains_ref.1) | copy-start | bytes 24580
  2.6 7.8 %collective-permute-start = (bf16[280,128]{1,0:T(8,128)(2,1)S(1)}, bf16[280,128]{1,0:T(8,128)(2,1)S(1)}, u32[]{:S(2)}, u32[]{:S(2)}) collective-permute-start(bf16[280,128]{1,0:T(8,128)(2,1)S(1)} %get-tuple-element.30), channel_id=1, source_target_pairs={{0,24},{8,16},{16,8},{24,0},{1,25},{9,17},{17,9},{25,1},{2,26},{10... | collective-permute-start | bytes 215048 | tf_op jit(solution)/shard_map/ppermute | solution.py:433
  7.7 8.2 %collective-permute-start.8 = (bf16[280,128]{1,0:T(8,128)(2,1)S(1)}, bf16[280,128]{1,0:T(8,128)(2,1)S(1)}, u32[]{:S(2)}, u32[]{:S(2)}) collective-permute-start(bf16[280,128]{1,0:T(8,128)(2,1)S(1)} %get-tuple-element.38), channel_id=1, source_target_pairs={{0,16},{8,24},{16,0},{24,8},{1,17},{9,25},{17,1},{25,9},{2,18},{10... | collective-permute-start | bytes 215048 | tf_op jit(solution)/shard_map/ppermute | solution.py:433
  7.7 8.2 %collective-permute-start.9 = (bf16[280,128]{1,0:T(8,128)(2,1)S(1)}, bf16[280,128]{1,0:T(8,128)(2,1)S(1)}, u32[]{:S(2)}, u32[]{:S(2)}) collective-permute-start(bf16[280,128]{1,0:T(8,128)(2,1)S(1)} %get-tuple-element.39), channel_id=1, source_target_pairs={{0,8},{8,0},{16,24},{24,16},{1,9},{9,1},{17,25},{25,17},{2,10},{10... | collective-permute-start | bytes 215048 | tf_op jit(solution)/shard_map/ppermute | solution.py:433
  8.3 20.1 %copy-start.2 = (s32[8,8]{1,0:T(8,128)S(1)}, s32[8,8]{1,0:T(8,128)}, u32[]{:S(2)}) copy-start(s32[8,8]{1,0:T(8,128)} %refs_5_.1) | copy-start | bytes 772
  10.4 8.5 %collective-permute-start.1 = (bf16[280,128]{1,0:T(8,128)(2,1)S(1)}, bf16[280,128]{1,0:T(8,128)(2,1)S(1)}, u32[]{:S(2)}, u32[]{:S(2)}) collective-permute-start(bf16[280,128]{1,0:T(8,128)(2,1)S(1)} %get-tuple-element.31), channel_id=1, source_target_pairs={{0,24},{8,16},{16,8},{24,0},{1,25},{9,17},{17,9},{25,1},{2,26},{10... | collective-permute-start | bytes 215048 | tf_op jit(solution)/shard_map/ppermute | solution.py:433
  14.7 5.8 %collective-permute-start.2 = (bf16[280,128]{1,0:T(8,128)(2,1)S(1)}, bf16[280,128]{1,0:T(8,128)(2,1)S(1)}, u32[]{:S(2)}, u32[]{:S(2)}) collective-permute-start(bf16[280,128]{1,0:T(8,128)(2,1)S(1)} %get-tuple-element.32), channel_id=1, source_target_pairs={{0,16},{8,24},{16,0},{24,8},{1,17},{9,25},{17,1},{25,9},{2,18},{10... | collective-permute-start | bytes 215048 | tf_op jit(solution)/shard_map/ppermute | solution.py:433
  15.0 5.6 %collective-permute-start.3 = (bf16[280,128]{1,0:T(8,128)(2,1)S(1)}, bf16[280,128]{1,0:T(8,128)(2,1)S(1)}, u32[]{:S(2)}, u32[]{:S(2)}) collective-permute-start(bf16[280,128]{1,0:T(8,128)(2,1)S(1)} %get-tuple-element.33), channel_id=1, source_target_pairs={{0,8},{8,0},{16,24},{24,16},{1,9},{9,1},{17,25},{25,17},{2,10},{10... | collective-permute-start | bytes 215048 | tf_op jit(solution)/shard_map/ppermute | solution.py:433
  16.4 8.1 %collective-permute-start.10 = (bf16[2,256,256]{2,1,0:T(8,128)(2,1)S(1)}, bf16[2,256,256]{2,1,0:T(8,128)(2,1)S(1)}, u32[]{:S(2)}, u32[]{:S(2)}) collective-permute-start(bf16[2,256,256]{2,1,0:T(8,128)(2,1)S(1)} %equalize.3.refs_0_), channel_id=1, source_target_pairs={{0,2},{1,3},{2,0},{3,1},{4,6},{5,7},{6,4},{7,5},{8,10},{9,11},{10,... | collective-permute-start | bytes 786440 | tf_op jit(solution)/shard_map/ppermute | solution.py:476
  17.4 7.8 %collective-permute-start.13 = (bf16[2,256,256]{2,1,0:T(8,128)(2,1)S(1)}, bf16[2,256,256]{2,1,0:T(8,128)(2,1)S(1)}, u32[]{:S(2)}, u32[]{:S(2)}) collective-permute-start(bf16[2,256,256]{2,1,0:T(8,128)(2,1)S(1)} %equalize.3.refs_0_), channel_id=1, source_target_pairs={{0,4},{4,0},{1,5},{5,1},{2,6},{6,2},{3,7},{7,3},{8,12},{12,8},{9,1... | collective-permute-start | bytes 786440 | tf_op jit(solution)/shard_map/ppermute | solution.py:477
  21.0 7.4 %collective-permute-start.4 = (bf16[2,256,256]{2,1,0:T(8,128)(2,1)S(1)}, bf16[2,256,256]{2,1,0:T(8,128)(2,1)S(1)}, u32[]{:S(2)}, u32[]{:S(2)}) collective-permute-start(bf16[2,256,256]{2,1,0:T(8,128)(2,1)S(1)} %get-tuple-element.36.refs_2_.refs_0_), channel_id=1, source_target_pairs={{0,2},{1,3},{2,0},{3,1},{4,6},{5,7},{6,4},{7,5},{8,10},{9,11},{10,... | collective-permute-start | bytes 786440 | tf_op jit(solution)/shard_map/ppermute | solution.py:476
  22.6 7.1 %collective-permute-start.7 = (bf16[2,272,256]{2,1,0:T(8,128)(2,1)S(1)}, bf16[2,272,256]{2,1,0:T(8,128)(2,1)S(1)}, u32[]{:S(2)}, u32[]{:S(2)}) collective-permute-start(bf16[2,272,256]{2,1,0:T(8,128)(2,1)S(1)} %get-tuple-element.37), channel_id=1, source_target_pairs={{0,4},{4,0},{1,5},{5,1},{2,6},{6,2},{3,7},{7,3},{8,12},{12,8},{9,1... | collective-permute-start | bytes 835592 | tf_op jit(solution)/shard_map/ppermute | solution.py:477
  24.6 3.9 %collective-permute-start.11 = (bf16[2,256,256]{2,1,0:T(8,128)(2,1)S(1)}, bf16[2,256,256]{2,1,0:T(8,128)(2,1)S(1)}, u32[]{:S(2)}, u32[]{:S(2)}) collective-permute-start(bf16[2,256,256]{2,1,0:T(8,128)(2,1)S(1)} %get-tuple-element.42), channel_id=1, source_target_pairs={{0,1},{1,0},{2,3},{3,2},{4,5},{5,4},{6,7},{7,6},{8,9},{9,8},{10,11... | collective-permute-start | bytes 786440 | tf_op jit(solution)/shard_map/ppermute | solution.py:486
  24.7 3.8 %collective-permute-start.12 = (bf16[2,256,256]{2,1,0:T(8,128)(2,1)S(1)}, bf16[2,256,256]{2,1,0:T(8,128)(2,1)S(1)}, u32[]{:S(2)}, u32[]{:S(2)}) collective-permute-start(bf16[2,256,256]{2,1,0:T(8,128)(2,1)S(1)} %get-tuple-element.41.refs_1_), channel_id=1, source_target_pairs={{0,1},{1,0},{2,3},{3,2},{4,5},{5,4},{6,7},{7,6},{8,9},{9,8},{10,11... | collective-permute-start | bytes 786440 | tf_op jit(solution)/shard_map/ppermute | solution.py:487
  25.2 4.6 %collective-permute-start.5 = (bf16[2,256,256]{2,1,0:T(8,128)(2,1)S(1)}, bf16[2,256,256]{2,1,0:T(8,128)(2,1)S(1)}, u32[]{:S(2)}, u32[]{:S(2)}) collective-permute-start(bf16[2,256,256]{2,1,0:T(8,128)(2,1)S(1)} %get-tuple-element.36.refs_2_.refs_0_), channel_id=1, source_target_pairs={{0,1},{1,0},{2,3},{3,2},{4,5},{5,4},{6,7},{7,6},{8,9},{9,8},{10,11... | collective-permute-start | bytes 786440 | tf_op jit(solution)/shard_map/ppermute | solution.py:486
  28.4 1.5 %collective-permute-start.6 = (bf16[2,256,256]{2,1,0:T(8,128)(2,1)S(1)}, bf16[2,256,256]{2,1,0:T(8,128)(2,1)S(1)}, u32[]{:S(2)}, u32[]{:S(2)}) collective-permute-start(bf16[2,256,256]{2,1,0:T(8,128)(2,1)S(1)} %collective-permute-done.4.refs_1_), channel_id=1, source_target_pairs={{0,1},{1,0},{2,3},{3,2},{4,5},{5,4},{6,7},{7,6},{8,9},{9,8},{10,11... | collective-permute-start | bytes 786440 | tf_op jit(solution)/shard_map/ppermute | solution.py:487

commit v19 on v18

--- a/solution.py
+++ b/solution.py
@@ -62,13 +62,15 @@
     return np.concatenate([tables.reshape(-1, lanes), terms, pad])
 
 
-def transform(filt, table, scale, stage, out_refs):
+def transform(filt, table, scale, stage, out_refs, table_copies=()):
     owners = len(out_refs)
     me = lax.axis_index("chan")
-    spectra = [
-        jnp.dot(filt[r], table[r * NCHAN : (r + 1) * NCHAN], preferred_element_type=jnp.float32) * scale
-        for r in range(2)
-    ]
+    spectra = []
+    for r in range(2):
+        for copy in table_copies[r : r + 1]:
+            copy.wait()
+        spectrum = jnp.dot(filt[r], table[r * NCHAN : (r + 1) * NCHAN], preferred_element_type=jnp.float32)
+        spectra.append(spectrum * scale)
     width = spectra[0].shape[1] // owners
     for owner in range(owners):
         here = slice(owner * width, (owner + 1) * width)
@@ -91,17 +93,23 @@
                 sems.at[piece],
             )
         )
-    table_copy = pltpu.make_async_copy(table_hbm.at[pl.ds(0, 2 * NCHAN)], table, sems.at[pieces])
+    table_copies = [
+        pltpu.make_async_copy(
+            table_hbm.at[pl.ds(r * NCHAN, NCHAN)], table.at[pl.ds(r * NCHAN, NCHAN)], sems.at[pieces + r]
+        )
+        for r in range(2)
+    ]
     coef_copy = pltpu.make_async_copy(
-        table_hbm.at[pl.ds(PARTS * 2 * NCHAN, terms.shape[0])], terms, sems.at[pieces + 1]
+        table_hbm.at[pl.ds(PARTS * 2 * NCHAN, terms.shape[0])], terms, sems.at[pieces + 2]
     )
     coef_copy.start()
     for copy in copies:
         copy.start()
     later_copy = pltpu.make_async_copy(
-        table_hbm.at[pl.ds(2 * NCHAN, (PARTS - 1) * 2 * NCHAN)], later, sems.at[pieces + 2]
+        table_hbm.at[pl.ds(2 * NCHAN, (PARTS - 1) * 2 * NCHAN)], later, sems.at[pieces + 3]
     )
-    table_copy.start()
+    for copy in table_copies:
+        copy.start()
     later_copy.start()
     tail = volt.shape[2] - (lead + frames) * NCHAN
     volt[:, :, : lead * NCHAN] = jnp.zeros((2, SIG, lead * NCHAN), jnp.int32)
@@ -140,8 +148,7 @@
         copies[piece].wait()
         filter_group(piece * per, per)
     filter_group(frames, GROUP)
-    table_copy.wait()
-    transform(filt, table, scale, stage, out_refs)
+    transform(filt, table, scale, stage, out_refs, table_copies)
     later_copy.wait()
 
 
@@ -189,7 +196,7 @@
             pltpu.VMEM((terms, across), jnp.bfloat16),
             pltpu.VMEM((TAPS * NCHAN // across, across), jnp.float32),
             pltpu.VMEM((owners, sent, lanes), jnp.bfloat16),
-            pltpu.SemaphoreType.DMA((pieces + 3,)),
+            pltpu.SemaphoreType.DMA((pieces + 4,)),
         ],
         compiler_params=pltpu.CompilerParams(vmem_limit_bytes=FILTER_VMEM_BYTES),
         cost_estimate=pl.CostEstimate(flops=1 << 29, bytes_accessed=4 << 20, transcendentals=0),

time: 31.8 us -> 32.2 us (1.013)
  Pallas kernels: 6.56 us -> 6.99 us
    pallas_call x1, Pallas kernels: 2.57 us -> 3 us  [filtered_and_first(): pl.pallas_call(functools.partial(filter_kernel, frames, pieces, spectrum_...]
where the time goes in v19:
time: 32.2 us; the launch traced here: 32 us
  starting transfers between devices  16.9 us (52%)
  waiting for transfers between devices  8.08 us (25%)
  Pallas kernels  6.99 us (22%)
    ppermute x6, starting transfers between devices, to_owners(): lax.ppermute(pieces[d], 'chan', [(i, i ^ d) for i in range(owners)])  10.7 us
    ppermute x6, waiting for transfers between devices, to_owners(): lax.ppermute(pieces[d], 'chan', [(i, i ^ d) for i in range(owners)])  3.68 us
    ppermute x2, waiting for transfers between devices, shards(): far = [lax.ppermute(own[part], 'bcol', across[d]) for d in range(1, chips)]  3.64 us
    ppermute x2, starting transfers between devices, shards(): lax.ppermute((longer or own)[-1], 'brow', along[d])  3.04 us
    pallas_call x1, Pallas kernels, filtered_and_first(): pl.pallas_call(functools.partial(filter_kernel, frames, pieces, spectrum_...  3 us
    ppermute x2, starting transfers between devices, shards(): far = [lax.ppermute(own[part], 'bcol', across[d]) for d in range(1, chips)]  2.52 us
    pallas_call x2, Pallas kernels, correlate(): pl.pallas_call(functools.partial(correlate_kernel, n_row, n_col, h, times...  2.36 us
    pallas_call x2, Pallas kernels, equalize(): pl.pallas_call(functools.partial(equalize_kernel, owners, frames, h, part...  0.93 us
  transfers between devices with their start and end apart: 14, of which 7 were waited for; matrix products, arithmetic and copies ran while one was open for 0% of the time, Pallas kernels for 7%

profile of v19, /device:TPU:0, one launch (start us, length us, event | category | flops | bytes accessed | tf_op | source)
XLA Modules:
  0.0 32.0 jit_solution(57210090328054013)
XLA Ops:
  0.0 0.0 copy-start
  0.0 0.0 copy-start.1
  0.0 3.0 %filter_and_transform.1 = (bf16[280,128]{1,0:T(8,128)(2,1)S(1)}, bf16[280,128]{1,0:T(8,128)(2,1)S(1)}, bf16[280,128]{1,0:T(8,128)(2,1)S(1)}, bf16[280,128]{1,0:T...) custom-call(s32[2,8,32768]{2,1,0:T(8,128)} %volt_hbm.1, ...), custom_call_target="tpu_custom_call" | custom-call | flops 536870912 | bytes 4194304 | tf_op jit(solution)/shard_map/filter_and_transform/pallas_call | solution.py:184
  3.0 5.1 %collective-permute-start = (bf16[280,128]{1,0:T(8,128)(2,1)S(1)}, bf16[280,128]{1,0:T(8,128)(2,1)S(1)}, u32[]{:S(2)}, u32[]{:S(2)}) collective-permute-start(bf16[280,128]{1,0:T(8,128)(2,1)S(1)} %get-tuple-element.30), channel_id=1, source_target_pairs={{0,24},{8,16},{16,8},{24,0},{1,25},{9,17},{17,9},{25,1},{2,26},{10... | collective-permute-start | bytes 215048 | tf_op jit(solution)/shard_map/ppermute | solution.py:440
  8.1 0.0 collective-permute-start.8
  8.1 0.6 %collective-permute-start.9 = (bf16[280,128]{1,0:T(8,128)(2,1)S(1)}, bf16[280,128]{1,0:T(8,128)(2,1)S(1)}, u32[]{:S(2)}, u32[]{:S(2)}) collective-permute-start(bf16[280,128]{1,0:T(8,128)(2,1)S(1)} %get-tuple-element.39), channel_id=1, source_target_pairs={{0,8},{8,0},{16,24},{24,16},{1,9},{9,1},{17,25},{25,17},{2,10},{10... | collective-permute-start | bytes 215048 | tf_op jit(solution)/shard_map/ppermute | solution.py:440
  8.8 0.0 copy-done
  8.8 0.0 copy-done.1
  8.8 0.0 copy-start.2
  8.8 0.6 %transform.1 = (bf16[280,128]{1,0:T(8,128)(2,1)S(1)}, bf16[280,128]{1,0:T(8,128)(2,1)S(1)}, bf16[280,128]{1,0:T(8,128)(2,1)S(1)}, bf16[280,128]{1,0:T(8,128)(2,1)S(1)}, f32[128,16]{1,0:T(8,128)S(1)}) custom-call(bf16[2,288,1024]{2,1,0:T(8,128)(2,1)S(1)} %get-tuple-element.25.filt, bf16[2048,256]{1,0:T(8,128)(2,1)S(1)} %get-tuple-element.26.later, ...), custom_call_target="tpu_custom_call" | custom-call | flops 536870912 | bytes 2097152 | tf_op jit(solution)/shard_map/transform/pallas_call | solution.py:220
  9.4 1.4 %collective-permute-done.refs_3_.refs_0_ = bf16[280,128]{1,0:T(8,128)(2,1)S(1)} collective-permute-done((bf16[280,128]{1,0:T(8,128)(2,1)S(1)}, bf16[280,128]{1,0:T(8,128)(2,1)S(1)}, u32[]{:S(2)}, u32[]{:S(2)}) %collective-permute-start) | collective-permute-done | bytes 71712 | tf_op jit(solution)/shard_map/ppermute | solution.py:440
  10.9 4.3 %collective-permute-start.1 = (bf16[280,128]{1,0:T(8,128)(2,1)S(1)}, bf16[280,128]{1,0:T(8,128)(2,1)S(1)}, u32[]{:S(2)}, u32[]{:S(2)}) collective-permute-start(bf16[280,128]{1,0:T(8,128)(2,1)S(1)} %get-tuple-element.31), channel_id=1, source_target_pairs={{0,24},{8,16},{16,8},{24,0},{1,25},{9,17},{17,9},{25,1},{2,26},{10... | collective-permute-start | bytes 215048 | tf_op jit(solution)/shard_map/ppermute | solution.py:440
  15.1 0.3 collective-permute-start.2
  15.4 0.4 %collective-permute-start.3 = (bf16[280,128]{1,0:T(8,128)(2,1)S(1)}, bf16[280,128]{1,0:T(8,128)(2,1)S(1)}, u32[]{:S(2)}, u32[]{:S(2)}) collective-permute-start(bf16[280,128]{1,0:T(8,128)(2,1)S(1)} %get-tuple-element.33), channel_id=1, source_target_pairs={{0,8},{8,0},{16,24},{24,16},{1,9},{9,1},{17,25},{25,17},{2,10},{10... | collective-permute-start | bytes 215048 | tf_op jit(solution)/shard_map/ppermute | solution.py:440
  15.8 0.6 %collective-permute-done.8.refs_1_ = bf16[280,128]{1,0:T(8,128)(2,1)S(1)} collective-permute-done((bf16[280,128]{1,0:T(8,128)(2,1)S(1)}, bf16[280,128]{1,0:T(8,128)(2,1)S(1)}, u32[]{:S(2)}, u32[]{:S(2)}) %collective-permute-start.8) | collective-permute-done | bytes 71712 | tf_op jit(solution)/shard_map/ppermute | solution.py:440
  16.4 0.0 collective-permute-done.9.refs_2_
  16.4 0.4 %equalize.3.refs_0_ = bf16[2,256,256]{2,1,0:T(8,128)(2,1)S(1)} custom-call(bf16[280,128]{1,0:T(8,128)(2,1)S(1)} %collective-permute-done.refs_3_.refs_0_, bf16[280,128]{1,0:T(8,128)(2,1)S(1)} %collective-permute-done.8.refs_1_, bf16[280,128]{1,0:T(8,128)(2,1)S(1)} %collective-permute-done.9.refs_2_, bf16[280,128]{1,0:T(8,128)(2,1)S(1)} %get-tuple-element.40.refs_3_, ...), custom_call_target="tpu_custom_call" | custom-call | bytes 1024 | tf_op jit(solution)/shard_map/equalize/pallas_call | solution.py:280
  16.8 1.0 %collective-permute-start.10 = (bf16[2,256,256]{2,1,0:T(8,128)(2,1)S(1)}, bf16[2,256,256]{2,1,0:T(8,128)(2,1)S(1)}, u32[]{:S(2)}, u32[]{:S(2)}) collective-permute-start(bf16[2,256,256]{2,1,0:T(8,128)(2,1)S(1)} %equalize.3.refs_0_), channel_id=1, source_target_pairs={{0,2},{1,3},{2,0},{3,1},{4,6},{5,7},{6,4},{7,5},{8,10},{9,11},{10,... | collective-permute-start | bytes 786440 | tf_op jit(solution)/shard_map/ppermute | solution.py:483
  17.8 1.5 %collective-permute-start.13 = (bf16[2,256,256]{2,1,0:T(8,128)(2,1)S(1)}, bf16[2,256,256]{2,1,0:T(8,128)(2,1)S(1)}, u32[]{:S(2)}, u32[]{:S(2)}) collective-permute-start(bf16[2,256,256]{2,1,0:T(8,128)(2,1)S(1)} %equalize.3.refs_0_), channel_id=1, source_target_pairs={{0,4},{4,0},{1,5},{5,1},{2,6},{6,2},{3,7},{7,3},{8,12},{12,8},{9,1... | collective-permute-start | bytes 786440 | tf_op jit(solution)/shard_map/ppermute | solution.py:484
  19.3 0.0 collective-permute-done.1.refs_0_
  19.3 1.7 %collective-permute-done.2.refs_1_ = bf16[280,128]{1,0:T(8,128)(2,1)S(1)} collective-permute-done((bf16[280,128]{1,0:T(8,128)(2,1)S(1)}, bf16[280,128]{1,0:T(8,128)(2,1)S(1)}, u32[]{:S(2)}, u32[]{:S(2)}) %collective-permute-start.2) | collective-permute-done | bytes 71712 | tf_op jit(solution)/shard_map/ppermute | solution.py:440
  21.0 0.0 collective-permute-done.3.refs_2_
  21.0 0.5 %equalize.2 = (bf16[2,256,256]{2,1,0:T(8,128)(2,1)S(1)}, bf16[2,272,256]{2,1,0:T(8,128)(2,1)S(1)}) custom-call(bf16[280,128]{1,0:T(8,128)(2,1)S(1)} %collective-permute-done.1.refs_0_, bf16[280,128]{1,0:T(8,128)(2,1)S(1)} %collective-permute-done.2.refs_1_, bf16[280,128]{1,0:T(8,128)(2,1)S(1)} %collective-permute-done.3.refs_2_, ...), custom_call_target="tpu_custom_call" | custom-call | bytes 1024 | tf_op jit(solution)/shard_map/equalize/pallas_call | solution.py:280
  21.5 1.6 %collective-permute-start.4 = (bf16[2,256,256]{2,1,0:T(8,128)(2,1)S(1)}, bf16[2,256,256]{2,1,0:T(8,128)(2,1)S(1)}, u32[]{:S(2)}, u32[]{:S(2)}) collective-permute-start(bf16[2,256,256]{2,1,0:T(8,128)(2,1)S(1)} %get-tuple-element.36.refs_2_.refs_0_), channel_id=1, source_target_pairs={{0,2},{1,3},{2,0},{3,1},{4,6},{5,7},{6,4},{7,5},{8,10},{9,11},{10,... | collective-permute-start | bytes 786440 | tf_op jit(solution)/shard_map/ppermute | solution.py:483
  23.0 1.5 %collective-permute-start.7 = (bf16[2,272,256]{2,1,0:T(8,128)(2,1)S(1)}, bf16[2,272,256]{2,1,0:T(8,128)(2,1)S(1)}, u32[]{:S(2)}, u32[]{:S(2)}) collective-permute-start(bf16[2,272,256]{2,1,0:T(8,128)(2,1)S(1)} %get-tuple-element.37), channel_id=1, source_target_pairs={{0,4},{4,0},{1,5},{5,1},{2,6},{6,2},{3,7},{7,3},{8,12},{12,8},{9,1... | collective-permute-start | bytes 835592 | tf_op jit(solution)/shard_map/ppermute | solution.py:484
  24.5 0.4 %collective-permute-done.10.refs_1_ = bf16[2,256,256]{2,1,0:T(8,128)(2,1)S(1)} collective-permute-done((bf16[2,256,256]{2,1,0:T(8,128)(2,1)S(1)}, bf16[2,256,256]{2,1,0:T(8,128)(2,1)S(1)}, u32[]{:S(2)}, u32[]{:S(2)}) %collective-permute-start.10) | collective-permute-done | bytes 262176 | tf_op jit(solution)/shard_map/ppermute | solution.py:483
  25.0 0.1 collective-permute-start.11
  25.1 0.5 %collective-permute-start.12 = (bf16[2,256,256]{2,1,0:T(8,128)(2,1)S(1)}, bf16[2,256,256]{2,1,0:T(8,128)(2,1)S(1)}, u32[]{:S(2)}, u32[]{:S(2)}) collective-permute-start(bf16[2,256,256]{2,1,0:T(8,128)(2,1)S(1)} %get-tuple-element.41.refs_1_), channel_id=1, source_target_pairs={{0,1},{1,0},{2,3},{3,2},{4,5},{5,4},{6,7},{7,6},{8,9},{9,8},{10,11... | collective-permute-start | bytes 786440 | tf_op jit(solution)/shard_map/ppermute | solution.py:494
  25.6 0.0 collective-permute-done.13.refs_4_
  25.6 0.1 collective-permute-start.5
  25.7 3.2 %collective-permute-done.4.refs_1_ = bf16[2,256,256]{2,1,0:T(8,128)(2,1)S(1)} collective-permute-done((bf16[2,256,256]{2,1,0:T(8,128)(2,1)S(1)}, bf16[2,256,256]{2,1,0:T(8,128)(2,1)S(1)}, u32[]{:S(2)}, u32[]{:S(2)}) %collective-permute-start.4) | collective-permute-done | bytes 262176 | tf_op jit(solution)/shard_map/ppermute | solution.py:483
  28.9 0.0 collective-permute-start.6
  28.9 0.0 collective-permute-done.11.refs_2_
  28.9 0.0 collective-permute-done.12.refs_3_
  28.9 0.0 copy-done.2
  28.9 0.7 %correlate.2 = (f32[2,2,4,32,128]{4,3,2,1,0:T(8,128)S(1)}, f32[2,4,8,128]{3,2,1,0:T(8,128)S(1)}) custom-call(bf16[2,256,256]{2,1,0:T(8,128)(2,1)S(1)} %equalize.3.refs_0_, bf16[2,256,256]{2,1,0:T(8,128)(2,1)S(1)} %get-tuple-element.41.refs_1_, bf16[2,256,256]{2,1,0:T(8,128)(2,1)S(1)} %collective-permute-done.11.refs_2_, ...), custom_call_target="tpu_custom_call" | custom-call | bytes 1024 | tf_op jit(solution)/shard_map/correlate/pallas_call | solution.py:424
  29.6 0.5 %collective-permute-done.7.refs_0_ = bf16[2,272,256]{2,1,0:T(8,128)(2,1)S(1)} collective-permute-done((bf16[2,272,256]{2,1,0:T(8,128)(2,1)S(1)}, bf16[2,272,256]{2,1,0:T(8,128)(2,1)S(1)}, u32[]{:S(2)}, u32[]{:S(2)}) %collective-permute-start.7) | collective-permute-done | bytes 278560 | tf_op jit(solution)/shard_map/ppermute | solution.py:484
  30.2 0.0 collective-permute-done.5.refs_2_
  30.2 0.2 collective-permute-done.6.refs_3_
  30.4 1.6 %correlate.3 = f32[2,16,32,128]{3,2,1,0:T(8,128)} custom-call(bf16[2,256,256]{2,1,0:T(8,128)(2,1)S(1)} %get-tuple-element.36.refs_2_.refs_0_, bf16[2,256,256]{2,1,0:T(8,128)(2,1)S(1)} %collective-permute-done.4.refs_1_, bf16[2,256,256]{2,1,0:T(8,128)(2,1)S(1)} %collective-permute-done.5.refs_2_, bf16[2,256,256]{2,1,0:T(8,128)(2,1)S(1)} %collective-permute-done.6.refs_3_, ...), custom_call_target="tpu_custom_call" | custom-call | bytes 1024 | tf_op jit(solution)/shard_map/correlate/pallas_call | solution.py:424
  (3 shorter events, 0.1 us)
Async XLA Ops:
  0.0 8.8 %copy-start = (f32[128,128]{1,0:T(8,128)S(1)}, f32[128,128]{1,0:T(8,128)}, u32[]{:S(2)}) copy-start(f32[128,128]{1,0:T(8,128)} %constant.5.clone.pick_ref) | copy-start | bytes 196612
  0.0 8.8 %copy-start.1 = (f32[8,2,128]{2,1,0:T(2,128)S(1)}, f32[8,2,128]{2,1,0:T(2,128)}, u32[]{:S(2)}) copy-start(f32[8,2,128]{2,1,0:T(2,128)} %gains_ref.1) | copy-start | bytes 24580
  3.0 7.8 %collective-permute-start = (bf16[280,128]{1,0:T(8,128)(2,1)S(1)}, bf16[280,128]{1,0:T(8,128)(2,1)S(1)}, u32[]{:S(2)}, u32[]{:S(2)}) collective-permute-start(bf16[280,128]{1,0:T(8,128)(2,1)S(1)} %get-tuple-element.30), channel_id=1, source_target_pairs={{0,24},{8,16},{16,8},{24,0},{1,25},{9,17},{17,9},{25,1},{2,26},{10... | collective-permute-start | bytes 215048 | tf_op jit(solution)/shard_map/ppermute | solution.py:440
  8.1 8.2 %collective-permute-start.8 = (bf16[280,128]{1,0:T(8,128)(2,1)S(1)}, bf16[280,128]{1,0:T(8,128)(2,1)S(1)}, u32[]{:S(2)}, u32[]{:S(2)}) collective-permute-start(bf16[280,128]{1,0:T(8,128)(2,1)S(1)} %get-tuple-element.38), channel_id=1, source_target_pairs={{0,16},{8,24},{16,0},{24,8},{1,17},{9,25},{17,1},{25,9},{2,18},{10... | collective-permute-start | bytes 215048 | tf_op jit(solution)/shard_map/ppermute | solution.py:440
  8.1 8.2 %collective-permute-start.9 = (bf16[280,128]{1,0:T(8,128)(2,1)S(1)}, bf16[280,128]{1,0:T(8,128)(2,1)S(1)}, u32[]{:S(2)}, u32[]{:S(2)}) collective-permute-start(bf16[280,128]{1,0:T(8,128)(2,1)S(1)} %get-tuple-element.39), channel_id=1, source_target_pairs={{0,8},{8,0},{16,24},{24,16},{1,9},{9,1},{17,25},{25,17},{2,10},{10... | collective-permute-start | bytes 215048 | tf_op jit(solution)/shard_map/ppermute | solution.py:440
  8.8 20.1 %copy-start.2 = (s32[8,8]{1,0:T(8,128)S(1)}, s32[8,8]{1,0:T(8,128)}, u32[]{:S(2)}) copy-start(s32[8,8]{1,0:T(8,128)} %refs_5_.1) | copy-start | bytes 772
  10.9 8.5 %collective-permute-start.1 = (bf16[280,128]{1,0:T(8,128)(2,1)S(1)}, bf16[280,128]{1,0:T(8,128)(2,1)S(1)}, u32[]{:S(2)}, u32[]{:S(2)}) collective-permute-start(bf16[280,128]{1,0:T(8,128)(2,1)S(1)} %get-tuple-element.31), channel_id=1, source_target_pairs={{0,24},{8,16},{16,8},{24,0},{1,25},{9,17},{17,9},{25,1},{2,26},{10... | collective-permute-start | bytes 215048 | tf_op jit(solution)/shard_map/ppermute | solution.py:440
  15.1 5.8 %collective-permute-start.2 = (bf16[280,128]{1,0:T(8,128)(2,1)S(1)}, bf16[280,128]{1,0:T(8,128)(2,1)S(1)}, u32[]{:S(2)}, u32[]{:S(2)}) collective-permute-start(bf16[280,128]{1,0:T(8,128)(2,1)S(1)} %get-tuple-element.32), channel_id=1, source_target_pairs={{0,16},{8,24},{16,0},{24,8},{1,17},{9,25},{17,1},{25,9},{2,18},{10... | collective-permute-start | bytes 215048 | tf_op jit(solution)/shard_map/ppermute | solution.py:440
  15.4 5.6 %collective-permute-start.3 = (bf16[280,128]{1,0:T(8,128)(2,1)S(1)}, bf16[280,128]{1,0:T(8,128)(2,1)S(1)}, u32[]{:S(2)}, u32[]{:S(2)}) collective-permute-start(bf16[280,128]{1,0:T(8,128)(2,1)S(1)} %get-tuple-element.33), channel_id=1, source_target_pairs={{0,8},{8,0},{16,24},{24,16},{1,9},{9,1},{17,25},{25,17},{2,10},{10... | collective-permute-start | bytes 215048 | tf_op jit(solution)/shard_map/ppermute | solution.py:440
  16.8 8.1 %collective-permute-start.10 = (bf16[2,256,256]{2,1,0:T(8,128)(2,1)S(1)}, bf16[2,256,256]{2,1,0:T(8,128)(2,1)S(1)}, u32[]{:S(2)}, u32[]{:S(2)}) collective-permute-start(bf16[2,256,256]{2,1,0:T(8,128)(2,1)S(1)} %equalize.3.refs_0_), channel_id=1, source_target_pairs={{0,2},{1,3},{2,0},{3,1},{4,6},{5,7},{6,4},{7,5},{8,10},{9,11},{10,... | collective-permute-start | bytes 786440 | tf_op jit(solution)/shard_map/ppermute | solution.py:483
  17.8 7.8 %collective-permute-start.13 = (bf16[2,256,256]{2,1,0:T(8,128)(2,1)S(1)}, bf16[2,256,256]{2,1,0:T(8,128)(2,1)S(1)}, u32[]{:S(2)}, u32[]{:S(2)}) collective-permute-start(bf16[2,256,256]{2,1,0:T(8,128)(2,1)S(1)} %equalize.3.refs_0_), channel_id=1, source_target_pairs={{0,4},{4,0},{1,5},{5,1},{2,6},{6,2},{3,7},{7,3},{8,12},{12,8},{9,1... | collective-permute-start | bytes 786440 | tf_op jit(solution)/shard_map/ppermute | solution.py:484
  21.5 7.4 %collective-permute-start.4 = (bf16[2,256,256]{2,1,0:T(8,128)(2,1)S(1)}, bf16[2,256,256]{2,1,0:T(8,128)(2,1)S(1)}, u32[]{:S(2)}, u32[]{:S(2)}) collective-permute-start(bf16[2,256,256]{2,1,0:T(8,128)(2,1)S(1)} %get-tuple-element.36.refs_2_.refs_0_), channel_id=1, source_target_pairs={{0,2},{1,3},{2,0},{3,1},{4,6},{5,7},{6,4},{7,5},{8,10},{9,11},{10,... | collective-permute-start | bytes 786440 | tf_op jit(solution)/shard_map/ppermute | solution.py:483
  23.0 7.1 %collective-permute-start.7 = (bf16[2,272,256]{2,1,0:T(8,128)(2,1)S(1)}, bf16[2,272,256]{2,1,0:T(8,128)(2,1)S(1)}, u32[]{:S(2)}, u32[]{:S(2)}) collective-permute-start(bf16[2,272,256]{2,1,0:T(8,128)(2,1)S(1)} %get-tuple-element.37), channel_id=1, source_target_pairs={{0,4},{4,0},{1,5},{5,1},{2,6},{6,2},{3,7},{7,3},{8,12},{12,8},{9,1... | collective-permute-start | bytes 835592 | tf_op jit(solution)/shard_map/ppermute | solution.py:484
  25.0 3.9 %collective-permute-start.11 = (bf16[2,256,256]{2,1,0:T(8,128)(2,1)S(1)}, bf16[2,256,256]{2,1,0:T(8,128)(2,1)S(1)}, u32[]{:S(2)}, u32[]{:S(2)}) collective-permute-start(bf16[2,256,256]{2,1,0:T(8,128)(2,1)S(1)} %get-tuple-element.42), channel_id=1, source_target_pairs={{0,1},{1,0},{2,3},{3,2},{4,5},{5,4},{6,7},{7,6},{8,9},{9,8},{10,11... | collective-permute-start | bytes 786440 | tf_op jit(solution)/shard_map/ppermute | solution.py:493
  25.1 3.8 %collective-permute-start.12 = (bf16[2,256,256]{2,1,0:T(8,128)(2,1)S(1)}, bf16[2,256,256]{2,1,0:T(8,128)(2,1)S(1)}, u32[]{:S(2)}, u32[]{:S(2)}) collective-permute-start(bf16[2,256,256]{2,1,0:T(8,128)(2,1)S(1)} %get-tuple-element.41.refs_1_), channel_id=1, source_target_pairs={{0,1},{1,0},{2,3},{3,2},{4,5},{5,4},{6,7},{7,6},{8,9},{9,8},{10,11... | collective-permute-start | bytes 786440 | tf_op jit(solution)/shard_map/ppermute | solution.py:494
  25.6 4.6 %collective-permute-start.5 = (bf16[2,256,256]{2,1,0:T(8,128)(2,1)S(1)}, bf16[2,256,256]{2,1,0:T(8,128)(2,1)S(1)}, u32[]{:S(2)}, u32[]{:S(2)}) collective-permute-start(bf16[2,256,256]{2,1,0:T(8,128)(2,1)S(1)} %get-tuple-element.36.refs_2_.refs_0_), channel_id=1, source_target_pairs={{0,1},{1,0},{2,3},{3,2},{4,5},{5,4},{6,7},{7,6},{8,9},{9,8},{10,11... | collective-permute-start | bytes 786440 | tf_op jit(solution)/shard_map/ppermute | solution.py:493
  28.9 1.5 %collective-permute-start.6 = (bf16[2,256,256]{2,1,0:T(8,128)(2,1)S(1)}, bf16[2,256,256]{2,1,0:T(8,128)(2,1)S(1)}, u32[]{:S(2)}, u32[]{:S(2)}) collective-permute-start(bf16[2,256,256]{2,1,0:T(8,128)(2,1)S(1)} %collective-permute-done.4.refs_1_), channel_id=1, source_target_pairs={{0,1},{1,0},{2,3},{3,2},{4,5},{5,4},{6,7},{7,6},{8,9},{9,8},{10,11... | collective-permute-start | bytes 786440 | tf_op jit(solution)/shard_map/ppermute | solution.py:494

commit v20 on v18

--- a/solution.py
+++ b/solution.py
@@ -170,7 +170,7 @@
     frames = voltages.shape[2] // NCHAN
     rows = (frames + GROUP) * SIG
     sent = (frames + TAPS - 1) * SIG
-    pieces = 4
+    pieces = 2
     across = table.shape[1]
     terms = table.shape[0] - PARTS * 2 * NCHAN
     lanes = 2 * CHANNELS // owners // PARTS

time: 31.8 us -> 31.9 us (level)
  no operation moved by 1% of the time
where the time goes in v20:
time: 31.9 us; the launch traced here: 31.8 us
  starting transfers between devices  16.9 us (53%)
  waiting for transfers between devices  8.08 us (25%)
  Pallas kernels  6.73 us (21%)
    ppermute x6, starting transfers between devices, to_owners(): lax.ppermute(pieces[d], 'chan', [(i, i ^ d) for i in range(owners)])  10.7 us
    ppermute x6, waiting for transfers between devices, to_owners(): lax.ppermute(pieces[d], 'chan', [(i, i ^ d) for i in range(owners)])  3.68 us
    ppermute x2, waiting for transfers between devices, shards(): far = [lax.ppermute(own[part], 'bcol', across[d]) for d in range(1, chips)]  3.64 us
    ppermute x2, starting transfers between devices, shards(): lax.ppermute((longer or own)[-1], 'brow', along[d])  3.04 us
    pallas_call x1, Pallas kernels, filtered_and_first(): pl.pallas_call(functools.partial(filter_kernel, frames, pieces, spectrum_...  2.75 us
    ppermute x2, starting transfers between devices, shards(): far = [lax.ppermute(own[part], 'bcol', across[d]) for d in range(1, chips)]  2.52 us
    pallas_call x2, Pallas kernels, correlate(): pl.pallas_call(functools.partial(correlate_kernel, n_row, n_col, h, times...  2.36 us
    pallas_call x2, Pallas kernels, equalize(): pl.pallas_call(functools.partial(equalize_kernel, owners, frames, h, part...  0.93 us
  transfers between devices with their start and end apart: 14, of which 7 were waited for; matrix products, arithmetic and copies ran while one was open for 0% of the time, Pallas kernels for 7%

profile of v20, /device:TPU:0, one launch (start us, length us, event | category | flops | bytes accessed | tf_op | source)
XLA Modules:
  0.0 31.8 jit_solution(14332279054785139135)
XLA Ops:
  0.0 0.0 copy-start
  0.0 0.0 copy-start.1
  0.0 2.7 %filter_and_transform.1 = (bf16[280,128]{1,0:T(8,128)(2,1)S(1)}, bf16[280,128]{1,0:T(8,128)(2,1)S(1)}, bf16[280,128]{1,0:T(8,128)(2,1)S(1)}, bf16[280,128]{1,0:T...) custom-call(s32[2,8,32768]{2,1,0:T(8,128)} %volt_hbm.1, ...), custom_call_target="tpu_custom_call" | custom-call | flops 536870912 | bytes 4194304 | tf_op jit(solution)/shard_map/filter_and_transform/pallas_call | solution.py:177
  2.8 5.1 %collective-permute-start = (bf16[280,128]{1,0:T(8,128)(2,1)S(1)}, bf16[280,128]{1,0:T(8,128)(2,1)S(1)}, u32[]{:S(2)}, u32[]{:S(2)}) collective-permute-start(bf16[280,128]{1,0:T(8,128)(2,1)S(1)} %get-tuple-element.30), channel_id=1, source_target_pairs={{0,24},{8,16},{16,8},{24,0},{1,25},{9,17},{17,9},{25,1},{2,26},{10... | collective-permute-start | bytes 215048 | tf_op jit(solution)/shard_map/ppermute | solution.py:433
  7.9 0.0 collective-permute-start.8
  7.9 0.6 %collective-permute-start.9 = (bf16[280,128]{1,0:T(8,128)(2,1)S(1)}, bf16[280,128]{1,0:T(8,128)(2,1)S(1)}, u32[]{:S(2)}, u32[]{:S(2)}) collective-permute-start(bf16[280,128]{1,0:T(8,128)(2,1)S(1)} %get-tuple-element.39), channel_id=1, source_target_pairs={{0,8},{8,0},{16,24},{24,16},{1,9},{9,1},{17,25},{25,17},{2,10},{10... | collective-permute-start | bytes 215048 | tf_op jit(solution)/shard_map/ppermute | solution.py:433
  8.5 0.0 copy-done
  8.5 0.0 copy-done.1
  8.5 0.0 copy-start.2
  8.5 0.6 %transform.1 = (bf16[280,128]{1,0:T(8,128)(2,1)S(1)}, bf16[280,128]{1,0:T(8,128)(2,1)S(1)}, bf16[280,128]{1,0:T(8,128)(2,1)S(1)}, bf16[280,128]{1,0:T(8,128)(2,1)S(1)}, f32[128,16]{1,0:T(8,128)S(1)}) custom-call(bf16[2,288,1024]{2,1,0:T(8,128)(2,1)S(1)} %get-tuple-element.25.filt, bf16[2048,256]{1,0:T(8,128)(2,1)S(1)} %get-tuple-element.26.later, ...), custom_call_target="tpu_custom_call" | custom-call | flops 536870912 | bytes 2097152 | tf_op jit(solution)/shard_map/transform/pallas_call | solution.py:213
  9.2 1.4 %collective-permute-done.refs_3_.refs_0_ = bf16[280,128]{1,0:T(8,128)(2,1)S(1)} collective-permute-done((bf16[280,128]{1,0:T(8,128)(2,1)S(1)}, bf16[280,128]{1,0:T(8,128)(2,1)S(1)}, u32[]{:S(2)}, u32[]{:S(2)}) %collective-permute-start) | collective-permute-done | bytes 71712 | tf_op jit(solution)/shard_map/ppermute | solution.py:433
  10.6 4.3 %collective-permute-start.1 = (bf16[280,128]{1,0:T(8,128)(2,1)S(1)}, bf16[280,128]{1,0:T(8,128)(2,1)S(1)}, u32[]{:S(2)}, u32[]{:S(2)}) collective-permute-start(bf16[280,128]{1,0:T(8,128)(2,1)S(1)} %get-tuple-element.31), channel_id=1, source_target_pairs={{0,24},{8,16},{16,8},{24,0},{1,25},{9,17},{17,9},{25,1},{2,26},{10... | collective-permute-start | bytes 215048 | tf_op jit(solution)/shard_map/ppermute | solution.py:433
  14.9 0.3 collective-permute-start.2
  15.1 0.4 %collective-permute-start.3 = (bf16[280,128]{1,0:T(8,128)(2,1)S(1)}, bf16[280,128]{1,0:T(8,128)(2,1)S(1)}, u32[]{:S(2)}, u32[]{:S(2)}) collective-permute-start(bf16[280,128]{1,0:T(8,128)(2,1)S(1)} %get-tuple-element.33), channel_id=1, source_target_pairs={{0,8},{8,0},{16,24},{24,16},{1,9},{9,1},{17,25},{25,17},{2,10},{10... | collective-permute-start | bytes 215048 | tf_op jit(solution)/shard_map/ppermute | solution.py:433
  15.5 0.6 %collective-permute-done.8.refs_1_ = bf16[280,128]{1,0:T(8,128)(2,1)S(1)} collective-permute-done((bf16[280,128]{1,0:T(8,128)(2,1)S(1)}, bf16[280,128]{1,0:T(8,128)(2,1)S(1)}, u32[]{:S(2)}, u32[]{:S(2)}) %collective-permute-start.8) | collective-permute-done | bytes 71712 | tf_op jit(solution)/shard_map/ppermute | solution.py:433
  16.1 0.0 collective-permute-done.9.refs_2_
  16.1 0.4 %equalize.3.refs_0_ = bf16[2,256,256]{2,1,0:T(8,128)(2,1)S(1)} custom-call(bf16[280,128]{1,0:T(8,128)(2,1)S(1)} %collective-permute-done.refs_3_.refs_0_, bf16[280,128]{1,0:T(8,128)(2,1)S(1)} %collective-permute-done.8.refs_1_, bf16[280,128]{1,0:T(8,128)(2,1)S(1)} %collective-permute-done.9.refs_2_, bf16[280,128]{1,0:T(8,128)(2,1)S(1)} %get-tuple-element.40.refs_3_, ...), custom_call_target="tpu_custom_call" | custom-call | bytes 1024 | tf_op jit(solution)/shard_map/equalize/pallas_call | solution.py:273
  16.6 1.0 %collective-permute-start.10 = (bf16[2,256,256]{2,1,0:T(8,128)(2,1)S(1)}, bf16[2,256,256]{2,1,0:T(8,128)(2,1)S(1)}, u32[]{:S(2)}, u32[]{:S(2)}) collective-permute-start(bf16[2,256,256]{2,1,0:T(8,128)(2,1)S(1)} %equalize.3.refs_0_), channel_id=1, source_target_pairs={{0,2},{1,3},{2,0},{3,1},{4,6},{5,7},{6,4},{7,5},{8,10},{9,11},{10,... | collective-permute-start | bytes 786440 | tf_op jit(solution)/shard_map/ppermute | solution.py:476
  17.5 1.5 %collective-permute-start.13 = (bf16[2,256,256]{2,1,0:T(8,128)(2,1)S(1)}, bf16[2,256,256]{2,1,0:T(8,128)(2,1)S(1)}, u32[]{:S(2)}, u32[]{:S(2)}) collective-permute-start(bf16[2,256,256]{2,1,0:T(8,128)(2,1)S(1)} %equalize.3.refs_0_), channel_id=1, source_target_pairs={{0,4},{4,0},{1,5},{5,1},{2,6},{6,2},{3,7},{7,3},{8,12},{12,8},{9,1... | collective-permute-start | bytes 786440 | tf_op jit(solution)/shard_map/ppermute | solution.py:477
  19.1 0.0 collective-permute-done.1.refs_0_
  19.1 1.7 %collective-permute-done.2.refs_1_ = bf16[280,128]{1,0:T(8,128)(2,1)S(1)} collective-permute-done((bf16[280,128]{1,0:T(8,128)(2,1)S(1)}, bf16[280,128]{1,0:T(8,128)(2,1)S(1)}, u32[]{:S(2)}, u32[]{:S(2)}) %collective-permute-start.2) | collective-permute-done | bytes 71712 | tf_op jit(solution)/shard_map/ppermute | solution.py:433
  20.7 0.0 collective-permute-done.3.refs_2_
  20.7 0.5 %equalize.2 = (bf16[2,256,256]{2,1,0:T(8,128)(2,1)S(1)}, bf16[2,272,256]{2,1,0:T(8,128)(2,1)S(1)}) custom-call(bf16[280,128]{1,0:T(8,128)(2,1)S(1)} %collective-permute-done.1.refs_0_, bf16[280,128]{1,0:T(8,128)(2,1)S(1)} %collective-permute-done.2.refs_1_, bf16[280,128]{1,0:T(8,128)(2,1)S(1)} %collective-permute-done.3.refs_2_, ...), custom_call_target="tpu_custom_call" | custom-call | bytes 1024 | tf_op jit(solution)/shard_map/equalize/pallas_call | solution.py:273
  21.2 1.6 %collective-permute-start.4 = (bf16[2,256,256]{2,1,0:T(8,128)(2,1)S(1)}, bf16[2,256,256]{2,1,0:T(8,128)(2,1)S(1)}, u32[]{:S(2)}, u32[]{:S(2)}) collective-permute-start(bf16[2,256,256]{2,1,0:T(8,128)(2,1)S(1)} %get-tuple-element.36.refs_2_.refs_0_), channel_id=1, source_target_pairs={{0,2},{1,3},{2,0},{3,1},{4,6},{5,7},{6,4},{7,5},{8,10},{9,11},{10,... | collective-permute-start | bytes 786440 | tf_op jit(solution)/shard_map/ppermute | solution.py:476
  22.8 1.5 %collective-permute-start.7 = (bf16[2,272,256]{2,1,0:T(8,128)(2,1)S(1)}, bf16[2,272,256]{2,1,0:T(8,128)(2,1)S(1)}, u32[]{:S(2)}, u32[]{:S(2)}) collective-permute-start(bf16[2,272,256]{2,1,0:T(8,128)(2,1)S(1)} %get-tuple-element.37), channel_id=1, source_target_pairs={{0,4},{4,0},{1,5},{5,1},{2,6},{6,2},{3,7},{7,3},{8,12},{12,8},{9,1... | collective-permute-start | bytes 835592 | tf_op jit(solution)/shard_map/ppermute | solution.py:477
  24.3 0.4 %collective-permute-done.10.refs_1_ = bf16[2,256,256]{2,1,0:T(8,128)(2,1)S(1)} collective-permute-done((bf16[2,256,256]{2,1,0:T(8,128)(2,1)S(1)}, bf16[2,256,256]{2,1,0:T(8,128)(2,1)S(1)}, u32[]{:S(2)}, u32[]{:S(2)}) %collective-permute-start.10) | collective-permute-done | bytes 262176 | tf_op jit(solution)/shard_map/ppermute | solution.py:476
  24.8 0.1 collective-permute-start.11
  24.8 0.5 %collective-permute-start.12 = (bf16[2,256,256]{2,1,0:T(8,128)(2,1)S(1)}, bf16[2,256,256]{2,1,0:T(8,128)(2,1)S(1)}, u32[]{:S(2)}, u32[]{:S(2)}) collective-permute-start(bf16[2,256,256]{2,1,0:T(8,128)(2,1)S(1)} %get-tuple-element.41.refs_1_), channel_id=1, source_target_pairs={{0,1},{1,0},{2,3},{3,2},{4,5},{5,4},{6,7},{7,6},{8,9},{9,8},{10,11... | collective-permute-start | bytes 786440 | tf_op jit(solution)/shard_map/ppermute | solution.py:487
  25.3 0.0 collective-permute-done.13.refs_4_
  25.3 0.1 collective-permute-start.5
  25.4 3.2 %collective-permute-done.4.refs_1_ = bf16[2,256,256]{2,1,0:T(8,128)(2,1)S(1)} collective-permute-done((bf16[2,256,256]{2,1,0:T(8,128)(2,1)S(1)}, bf16[2,256,256]{2,1,0:T(8,128)(2,1)S(1)}, u32[]{:S(2)}, u32[]{:S(2)}) %collective-permute-start.4) | collective-permute-done | bytes 262176 | tf_op jit(solution)/shard_map/ppermute | solution.py:476
  28.6 0.0 collective-permute-start.6
  28.6 0.0 collective-permute-done.11.refs_2_
  28.6 0.0 collective-permute-done.12.refs_3_
  28.6 0.0 copy-done.2
  28.6 0.7 %correlate.2 = (f32[2,2,4,32,128]{4,3,2,1,0:T(8,128)S(1)}, f32[2,4,8,128]{3,2,1,0:T(8,128)S(1)}) custom-call(bf16[2,256,256]{2,1,0:T(8,128)(2,1)S(1)} %equalize.3.refs_0_, bf16[2,256,256]{2,1,0:T(8,128)(2,1)S(1)} %get-tuple-element.41.refs_1_, bf16[2,256,256]{2,1,0:T(8,128)(2,1)S(1)} %collective-permute-done.11.refs_2_, ...), custom_call_target="tpu_custom_call" | custom-call | bytes 1024 | tf_op jit(solution)/shard_map/correlate/pallas_call | solution.py:417
  29.4 0.5 %collective-permute-done.7.refs_0_ = bf16[2,272,256]{2,1,0:T(8,128)(2,1)S(1)} collective-permute-done((bf16[2,272,256]{2,1,0:T(8,128)(2,1)S(1)}, bf16[2,272,256]{2,1,0:T(8,128)(2,1)S(1)}, u32[]{:S(2)}, u32[]{:S(2)}) %collective-permute-start.7) | collective-permute-done | bytes 278560 | tf_op jit(solution)/shard_map/ppermute | solution.py:477
  29.9 0.0 collective-permute-done.5.refs_2_
  29.9 0.2 collective-permute-done.6.refs_3_
  30.2 1.6 %correlate.3 = f32[2,16,32,128]{3,2,1,0:T(8,128)} custom-call(bf16[2,256,256]{2,1,0:T(8,128)(2,1)S(1)} %get-tuple-element.36.refs_2_.refs_0_, bf16[2,256,256]{2,1,0:T(8,128)(2,1)S(1)} %collective-permute-done.4.refs_1_, bf16[2,256,256]{2,1,0:T(8,128)(2,1)S(1)} %collective-permute-done.5.refs_2_, bf16[2,256,256]{2,1,0:T(8,128)(2,1)S(1)} %collective-permute-done.6.refs_3_, ...), custom_call_target="tpu_custom_call" | custom-call | bytes 1024 | tf_op jit(solution)/shard_map/correlate/pallas_call | solution.py:417
  (3 shorter events, 0.1 us)
Async XLA Ops:
  0.0 8.5 %copy-start = (f32[128,128]{1,0:T(8,128)S(1)}, f32[128,128]{1,0:T(8,128)}, u32[]{:S(2)}) copy-start(f32[128,128]{1,0:T(8,128)} %constant.5.clone.pick_ref) | copy-start | bytes 196612
  0.0 8.5 %copy-start.1 = (f32[8,2,128]{2,1,0:T(2,128)S(1)}, f32[8,2,128]{2,1,0:T(2,128)}, u32[]{:S(2)}) copy-start(f32[8,2,128]{2,1,0:T(2,128)} %gains_ref.1) | copy-start | bytes 24580
  2.8 7.8 %collective-permute-start = (bf16[280,128]{1,0:T(8,128)(2,1)S(1)}, bf16[280,128]{1,0:T(8,128)(2,1)S(1)}, u32[]{:S(2)}, u32[]{:S(2)}) collective-permute-start(bf16[280,128]{1,0:T(8,128)(2,1)S(1)} %get-tuple-element.30), channel_id=1, source_target_pairs={{0,24},{8,16},{16,8},{24,0},{1,25},{9,17},{17,9},{25,1},{2,26},{10... | collective-permute-start | bytes 215048 | tf_op jit(solution)/shard_map/ppermute | solution.py:433
  7.9 8.2 %collective-permute-start.8 = (bf16[280,128]{1,0:T(8,128)(2,1)S(1)}, bf16[280,128]{1,0:T(8,128)(2,1)S(1)}, u32[]{:S(2)}, u32[]{:S(2)}) collective-permute-start(bf16[280,128]{1,0:T(8,128)(2,1)S(1)} %get-tuple-element.38), channel_id=1, source_target_pairs={{0,16},{8,24},{16,0},{24,8},{1,17},{9,25},{17,1},{25,9},{2,18},{10... | collective-permute-start | bytes 215048 | tf_op jit(solution)/shard_map/ppermute | solution.py:433
  7.9 8.2 %collective-permute-start.9 = (bf16[280,128]{1,0:T(8,128)(2,1)S(1)}, bf16[280,128]{1,0:T(8,128)(2,1)S(1)}, u32[]{:S(2)}, u32[]{:S(2)}) collective-permute-start(bf16[280,128]{1,0:T(8,128)(2,1)S(1)} %get-tuple-element.39), channel_id=1, source_target_pairs={{0,8},{8,0},{16,24},{24,16},{1,9},{9,1},{17,25},{25,17},{2,10},{10... | collective-permute-start | bytes 215048 | tf_op jit(solution)/shard_map/ppermute | solution.py:433
  8.5 20.1 %copy-start.2 = (s32[8,8]{1,0:T(8,128)S(1)}, s32[8,8]{1,0:T(8,128)}, u32[]{:S(2)}) copy-start(s32[8,8]{1,0:T(8,128)} %refs_5_.1) | copy-start | bytes 772
  10.6 8.5 %collective-permute-start.1 = (bf16[280,128]{1,0:T(8,128)(2,1)S(1)}, bf16[280,128]{1,0:T(8,128)(2,1)S(1)}, u32[]{:S(2)}, u32[]{:S(2)}) collective-permute-start(bf16[280,128]{1,0:T(8,128)(2,1)S(1)} %get-tuple-element.31), channel_id=1, source_target_pairs={{0,24},{8,16},{16,8},{24,0},{1,25},{9,17},{17,9},{25,1},{2,26},{10... | collective-permute-start | bytes 215048 | tf_op jit(solution)/shard_map/ppermute | solution.py:433
  14.9 5.8 %collective-permute-start.2 = (bf16[280,128]{1,0:T(8,128)(2,1)S(1)}, bf16[280,128]{1,0:T(8,128)(2,1)S(1)}, u32[]{:S(2)}, u32[]{:S(2)}) collective-permute-start(bf16[280,128]{1,0:T(8,128)(2,1)S(1)} %get-tuple-element.32), channel_id=1, source_target_pairs={{0,16},{8,24},{16,0},{24,8},{1,17},{9,25},{17,1},{25,9},{2,18},{10... | collective-permute-start | bytes 215048 | tf_op jit(solution)/shard_map/ppermute | solution.py:433
  15.1 5.6 %collective-permute-start.3 = (bf16[280,128]{1,0:T(8,128)(2,1)S(1)}, bf16[280,128]{1,0:T(8,128)(2,1)S(1)}, u32[]{:S(2)}, u32[]{:S(2)}) collective-permute-start(bf16[280,128]{1,0:T(8,128)(2,1)S(1)} %get-tuple-element.33), channel_id=1, source_target_pairs={{0,8},{8,0},{16,24},{24,16},{1,9},{9,1},{17,25},{25,17},{2,10},{10... | collective-permute-start | bytes 215048 | tf_op jit(solution)/shard_map/ppermute | solution.py:433
  16.6 8.1 %collective-permute-start.10 = (bf16[2,256,256]{2,1,0:T(8,128)(2,1)S(1)}, bf16[2,256,256]{2,1,0:T(8,128)(2,1)S(1)}, u32[]{:S(2)}, u32[]{:S(2)}) collective-permute-start(bf16[2,256,256]{2,1,0:T(8,128)(2,1)S(1)} %equalize.3.refs_0_), channel_id=1, source_target_pairs={{0,2},{1,3},{2,0},{3,1},{4,6},{5,7},{6,4},{7,5},{8,10},{9,11},{10,... | collective-permute-start | bytes 786440 | tf_op jit(solution)/shard_map/ppermute | solution.py:476
  17.5 7.8 %collective-permute-start.13 = (bf16[2,256,256]{2,1,0:T(8,128)(2,1)S(1)}, bf16[2,256,256]{2,1,0:T(8,128)(2,1)S(1)}, u32[]{:S(2)}, u32[]{:S(2)}) collective-permute-start(bf16[2,256,256]{2,1,0:T(8,128)(2,1)S(1)} %equalize.3.refs_0_), channel_id=1, source_target_pairs={{0,4},{4,0},{1,5},{5,1},{2,6},{6,2},{3,7},{7,3},{8,12},{12,8},{9,1... | collective-permute-start | bytes 786440 | tf_op jit(solution)/shard_map/ppermute | solution.py:477
  21.2 7.4 %collective-permute-start.4 = (bf16[2,256,256]{2,1,0:T(8,128)(2,1)S(1)}, bf16[2,256,256]{2,1,0:T(8,128)(2,1)S(1)}, u32[]{:S(2)}, u32[]{:S(2)}) collective-permute-start(bf16[2,256,256]{2,1,0:T(8,128)(2,1)S(1)} %get-tuple-element.36.refs_2_.refs_0_), channel_id=1, source_target_pairs={{0,2},{1,3},{2,0},{3,1},{4,6},{5,7},{6,4},{7,5},{8,10},{9,11},{10,... | collective-permute-start | bytes 786440 | tf_op jit(solution)/shard_map/ppermute | solution.py:476
  22.8 7.1 %collective-permute-start.7 = (bf16[2,272,256]{2,1,0:T(8,128)(2,1)S(1)}, bf16[2,272,256]{2,1,0:T(8,128)(2,1)S(1)}, u32[]{:S(2)}, u32[]{:S(2)}) collective-permute-start(bf16[2,272,256]{2,1,0:T(8,128)(2,1)S(1)} %get-tuple-element.37), channel_id=1, source_target_pairs={{0,4},{4,0},{1,5},{5,1},{2,6},{6,2},{3,7},{7,3},{8,12},{12,8},{9,1... | collective-permute-start | bytes 835592 | tf_op jit(solution)/shard_map/ppermute | solution.py:477
  24.8 3.9 %collective-permute-start.11 = (bf16[2,256,256]{2,1,0:T(8,128)(2,1)S(1)}, bf16[2,256,256]{2,1,0:T(8,128)(2,1)S(1)}, u32[]{:S(2)}, u32[]{:S(2)}) collective-permute-start(bf16[2,256,256]{2,1,0:T(8,128)(2,1)S(1)} %get-tuple-element.42), channel_id=1, source_target_pairs={{0,1},{1,0},{2,3},{3,2},{4,5},{5,4},{6,7},{7,6},{8,9},{9,8},{10,11... | collective-permute-start | bytes 786440 | tf_op jit(solution)/shard_map/ppermute | solution.py:486
  24.8 3.8 %collective-permute-start.12 = (bf16[2,256,256]{2,1,0:T(8,128)(2,1)S(1)}, bf16[2,256,256]{2,1,0:T(8,128)(2,1)S(1)}, u32[]{:S(2)}, u32[]{:S(2)}) collective-permute-start(bf16[2,256,256]{2,1,0:T(8,128)(2,1)S(1)} %get-tuple-element.41.refs_1_), channel_id=1, source_target_pairs={{0,1},{1,0},{2,3},{3,2},{4,5},{5,4},{6,7},{7,6},{8,9},{9,8},{10,11... | collective-permute-start | bytes 786440 | tf_op jit(solution)/shard_map/ppermute | solution.py:487
  25.3 4.6 %collective-permute-start.5 = (bf16[2,256,256]{2,1,0:T(8,128)(2,1)S(1)}, bf16[2,256,256]{2,1,0:T(8,128)(2,1)S(1)}, u32[]{:S(2)}, u32[]{:S(2)}) collective-permute-start(bf16[2,256,256]{2,1,0:T(8,128)(2,1)S(1)} %get-tuple-element.36.refs_2_.refs_0_), channel_id=1, source_target_pairs={{0,1},{1,0},{2,3},{3,2},{4,5},{5,4},{6,7},{7,6},{8,9},{9,8},{10,11... | collective-permute-start | bytes 786440 | tf_op jit(solution)/shard_map/ppermute | solution.py:486
  28.6 1.5 %collective-permute-start.6 = (bf16[2,256,256]{2,1,0:T(8,128)(2,1)S(1)}, bf16[2,256,256]{2,1,0:T(8,128)(2,1)S(1)}, u32[]{:S(2)}, u32[]{:S(2)}) collective-permute-start(bf16[2,256,256]{2,1,0:T(8,128)(2,1)S(1)} %collective-permute-done.4.refs_1_), channel_id=1, source_target_pairs={{0,1},{1,0},{2,3},{3,2},{4,5},{5,4},{6,7},{7,6},{8,9},{9,8},{10,11... | collective-permute-start | bytes 786440 | tf_op jit(solution)/shard_map/ppermute | solution.py:487

commit v21 on v18

--- a/solution.py
+++ b/solution.py
@@ -470,7 +470,7 @@
             pieces = next_part(part + 1, filt, tables, antenna_gains, owners)
             if part == 0:
                 *pieces, gains = pieces
-            later = to_owners([pieces[0], *held_back(pieces[1:], arrived[-1:])])
+            later = to_owners([pieces[0], *held_back(pieces[1:], arrived[owners // 2 : owners // 2 + 1])])
         block, *longer = equalize(arrived, gains, part, frames)
         own.append(block)
         far = [lax.ppermute(own[part], "bcol", across[d]) for d in range(1, chips)]

time: 31.8 us -> 33.3 us (1.047)
  waiting for transfers between devices: 8.07 us -> 8.84 us
  starting transfers between devices: 16.9 us -> 17.6 us
    ppermute x2, starting transfers between devices: 2.52 us -> 3.11 us  [shards(): far = [lax.ppermute(own[part], 'bcol', across[d]) for d in range(1, chips)]]
    ppermute x6, waiting for transfers between devices: 3.68 us -> 4.22 us  [to_owners(): lax.ppermute(pieces[d], 'chan', [(i, i ^ d) for i in range(owners)])]
  transfers between devices with their start and end apart: 14 -> 14, of which waited for: 7 -> 5; matrix products, arithmetic and copies ran while one was open for 0% -> 0% of each run, Pallas kernels for 7% -> 7%
where the time goes in v21:
time: 33.3 us; the launch traced here: 33.1 us
  starting transfers between devices  17.6 us (53%)
  waiting for transfers between devices  8.84 us (27%)
  Pallas kernels  6.56 us (20%)
    ppermute x6, starting transfers between devices, to_owners(): lax.ppermute(pieces[d], 'chan', [(i, i ^ d) for i in range(owners)])  10.8 us
    ppermute x6, waiting for transfers between devices, to_owners(): lax.ppermute(pieces[d], 'chan', [(i, i ^ d) for i in range(owners)])  4.22 us
    ppermute x2, waiting for transfers between devices, shards(): far = [lax.ppermute(own[part], 'bcol', across[d]) for d in range(1, chips)]  3.81 us
    ppermute x2, starting transfers between devices, shards(): far = [lax.ppermute(own[part], 'bcol', across[d]) for d in range(1, chips)]  3.11 us
    ppermute x2, starting transfers between devices, shards(): lax.ppermute((longer or own)[-1], 'brow', along[d])  3.04 us
    pallas_call x1, Pallas kernels, filtered_and_first(): pl.pallas_call(functools.partial(filter_kernel, frames, pieces, spectrum_...  2.57 us
    pallas_call x2, Pallas kernels, correlate(): pl.pallas_call(functools.partial(correlate_kernel, n_row, n_col, h, times...  2.37 us
    pallas_call x2, Pallas kernels, equalize(): pl.pallas_call(functools.partial(equalize_kernel, owners, frames, h, part...  0.93 us
  transfers between devices with their start and end apart: 14, of which 5 were waited for; matrix products, arithmetic and copies ran while one was open for 0% of the time, Pallas kernels for 7%

profile of v21, /device:TPU:0, one launch (start us, length us, event | category | flops | bytes accessed | tf_op | source)
XLA Modules:
  0.0 33.1 jit_solution(11789997785316766688)
XLA Ops:
  0.0 0.0 copy-start
  0.0 0.0 copy-start.1
  0.0 2.6 %filter_and_transform.1 = (bf16[280,128]{1,0:T(8,128)(2,1)S(1)}, bf16[280,128]{1,0:T(8,128)(2,1)S(1)}, bf16[280,128]{1,0:T(8,128)(2,1)S(1)}, bf16[280,128]{1,0:T...) custom-call(s32[2,8,32768]{2,1,0:T(8,128)} %volt_hbm.1, ...), custom_call_target="tpu_custom_call" | custom-call | flops 536870912 | bytes 4194304 | tf_op jit(solution)/shard_map/filter_and_transform/pallas_call | solution.py:177
  2.6 4.1 %collective-permute-start = (bf16[280,128]{1,0:T(8,128)(2,1)S(1)}, bf16[280,128]{1,0:T(8,128)(2,1)S(1)}, u32[]{:S(2)}, u32[]{:S(2)}) collective-permute-start(bf16[280,128]{1,0:T(8,128)(2,1)S(1)} %get-tuple-element.30), channel_id=1, source_target_pairs={{0,16},{8,24},{16,0},{24,8},{1,17},{9,25},{17,1},{25,9},{2,18},{10... | collective-permute-start | bytes 215048 | tf_op jit(solution)/shard_map/ppermute | solution.py:433
  6.7 1.3 %collective-permute-start.8 = (bf16[280,128]{1,0:T(8,128)(2,1)S(1)}, bf16[280,128]{1,0:T(8,128)(2,1)S(1)}, u32[]{:S(2)}, u32[]{:S(2)}) collective-permute-start(bf16[280,128]{1,0:T(8,128)(2,1)S(1)} %get-tuple-element.38), channel_id=1, source_target_pairs={{0,24},{8,16},{16,8},{24,0},{1,25},{9,17},{17,9},{25,1},{2,26},{10... | collective-permute-start | bytes 215048 | tf_op jit(solution)/shard_map/ppermute | solution.py:433
  8.0 0.2 collective-permute-start.9
  8.3 0.0 copy-done
  8.3 0.0 copy-done.1
  8.3 0.0 copy-start.2
  8.3 0.6 %transform.1 = (bf16[280,128]{1,0:T(8,128)(2,1)S(1)}, bf16[280,128]{1,0:T(8,128)(2,1)S(1)}, bf16[280,128]{1,0:T(8,128)(2,1)S(1)}, bf16[280,128]{1,0:T(8,128)(2,1)S(1)}, f32[128,16]{1,0:T(8,128)S(1)}) custom-call(bf16[2,288,1024]{2,1,0:T(8,128)(2,1)S(1)} %get-tuple-element.25.filt, bf16[2048,256]{1,0:T(8,128)(2,1)S(1)} %get-tuple-element.26.later, ...), custom_call_target="tpu_custom_call" | custom-call | flops 536870912 | bytes 2097152 | tf_op jit(solution)/shard_map/transform/pallas_call | solution.py:213
  8.9 2.6 %collective-permute-done.refs_3_.refs_1_ = bf16[280,128]{1,0:T(8,128)(2,1)S(1)} collective-permute-done((bf16[280,128]{1,0:T(8,128)(2,1)S(1)}, bf16[280,128]{1,0:T(8,128)(2,1)S(1)}, u32[]{:S(2)}, u32[]{:S(2)}) %collective-permute-start) | collective-permute-done | bytes 71712 | tf_op jit(solution)/shard_map/ppermute | solution.py:433
  11.5 4.5 %collective-permute-start.1 = (bf16[280,128]{1,0:T(8,128)(2,1)S(1)}, bf16[280,128]{1,0:T(8,128)(2,1)S(1)}, u32[]{:S(2)}, u32[]{:S(2)}) collective-permute-start(bf16[280,128]{1,0:T(8,128)(2,1)S(1)} %get-tuple-element.31), channel_id=1, source_target_pairs={{0,24},{8,16},{16,8},{24,0},{1,25},{9,17},{17,9},{25,1},{2,26},{10... | collective-permute-start | bytes 215048 | tf_op jit(solution)/shard_map/ppermute | solution.py:433
  16.0 0.0 collective-permute-start.2
  16.0 0.6 %collective-permute-start.3 = (bf16[280,128]{1,0:T(8,128)(2,1)S(1)}, bf16[280,128]{1,0:T(8,128)(2,1)S(1)}, u32[]{:S(2)}, u32[]{:S(2)}) collective-permute-start(bf16[280,128]{1,0:T(8,128)(2,1)S(1)} %get-tuple-element.33), channel_id=1, source_target_pairs={{0,8},{8,0},{16,24},{24,16},{1,9},{9,1},{17,25},{25,17},{2,10},{10... | collective-permute-start | bytes 215048 | tf_op jit(solution)/shard_map/ppermute | solution.py:433
  16.6 0.0 collective-permute-done.8.refs_0_
  16.6 0.0 collective-permute-done.9.refs_2_
  16.6 0.5 %equalize.3.refs_0_ = bf16[2,256,256]{2,1,0:T(8,128)(2,1)S(1)} custom-call(bf16[280,128]{1,0:T(8,128)(2,1)S(1)} %collective-permute-done.8.refs_0_, bf16[280,128]{1,0:T(8,128)(2,1)S(1)} %collective-permute-done.refs_3_.refs_1_, bf16[280,128]{1,0:T(8,128)(2,1)S(1)} %collective-permute-done.9.refs_2_, bf16[280,128]{1,0:T(8,128)(2,1)S(1)} %get-tuple-element.40.refs_3_, ...), custom_call_target="tpu_custom_call" | custom-call | bytes 1024 | tf_op jit(solution)/shard_map/equalize/pallas_call | solution.py:273
  17.1 1.6 %collective-permute-start.10 = (bf16[2,256,256]{2,1,0:T(8,128)(2,1)S(1)}, bf16[2,256,256]{2,1,0:T(8,128)(2,1)S(1)}, u32[]{:S(2)}, u32[]{:S(2)}) collective-permute-start(bf16[2,256,256]{2,1,0:T(8,128)(2,1)S(1)} %equalize.3.refs_0_), channel_id=1, source_target_pairs={{0,2},{1,3},{2,0},{3,1},{4,6},{5,7},{6,4},{7,5},{8,10},{9,11},{10,... | collective-permute-start | bytes 786440 | tf_op jit(solution)/shard_map/ppermute | solution.py:476
  18.6 1.5 %collective-permute-start.13 = (bf16[2,256,256]{2,1,0:T(8,128)(2,1)S(1)}, bf16[2,256,256]{2,1,0:T(8,128)(2,1)S(1)}, u32[]{:S(2)}, u32[]{:S(2)}) collective-permute-start(bf16[2,256,256]{2,1,0:T(8,128)(2,1)S(1)} %equalize.3.refs_0_), channel_id=1, source_target_pairs={{0,4},{4,0},{1,5},{5,1},{2,6},{6,2},{3,7},{7,3},{8,12},{12,8},{9,1... | collective-permute-start | bytes 786440 | tf_op jit(solution)/shard_map/ppermute | solution.py:477
  20.2 0.0 collective-permute-done.1.refs_0_
  20.2 1.5 %collective-permute-done.2.refs_1_ = bf16[280,128]{1,0:T(8,128)(2,1)S(1)} collective-permute-done((bf16[280,128]{1,0:T(8,128)(2,1)S(1)}, bf16[280,128]{1,0:T(8,128)(2,1)S(1)}, u32[]{:S(2)}, u32[]{:S(2)}) %collective-permute-start.2) | collective-permute-done | bytes 71712 | tf_op jit(solution)/shard_map/ppermute | solution.py:433
  21.6 0.2 collective-permute-done.3.refs_2_
  21.8 0.5 %equalize.2 = (bf16[2,256,256]{2,1,0:T(8,128)(2,1)S(1)}, bf16[2,272,256]{2,1,0:T(8,128)(2,1)S(1)}) custom-call(bf16[280,128]{1,0:T(8,128)(2,1)S(1)} %collective-permute-done.1.refs_0_, bf16[280,128]{1,0:T(8,128)(2,1)S(1)} %collective-permute-done.2.refs_1_, bf16[280,128]{1,0:T(8,128)(2,1)S(1)} %collective-permute-done.3.refs_2_, ...), custom_call_target="tpu_custom_call" | custom-call | bytes 1024 | tf_op jit(solution)/shard_map/equalize/pallas_call | solution.py:273
  22.3 1.6 %collective-permute-start.4 = (bf16[2,256,256]{2,1,0:T(8,128)(2,1)S(1)}, bf16[2,256,256]{2,1,0:T(8,128)(2,1)S(1)}, u32[]{:S(2)}, u32[]{:S(2)}) collective-permute-start(bf16[2,256,256]{2,1,0:T(8,128)(2,1)S(1)} %get-tuple-element.36.refs_2_.refs_0_), channel_id=1, source_target_pairs={{0,2},{1,3},{2,0},{3,1},{4,6},{5,7},{6,4},{7,5},{8,10},{9,11},{10,... | collective-permute-start | bytes 786440 | tf_op jit(solution)/shard_map/ppermute | solution.py:476
  23.9 1.5 %collective-permute-start.7 = (bf16[2,272,256]{2,1,0:T(8,128)(2,1)S(1)}, bf16[2,272,256]{2,1,0:T(8,128)(2,1)S(1)}, u32[]{:S(2)}, u32[]{:S(2)}) collective-permute-start(bf16[2,272,256]{2,1,0:T(8,128)(2,1)S(1)} %get-tuple-element.37), channel_id=1, source_target_pairs={{0,4},{4,0},{1,5},{5,1},{2,6},{6,2},{3,7},{7,3},{8,12},{12,8},{9,1... | collective-permute-start | bytes 835592 | tf_op jit(solution)/shard_map/ppermute | solution.py:477
  25.4 0.0 collective-permute-done.10.refs_1_
  25.4 0.1 collective-permute-start.11
  25.5 0.5 %collective-permute-start.12 = (bf16[2,256,256]{2,1,0:T(8,128)(2,1)S(1)}, bf16[2,256,256]{2,1,0:T(8,128)(2,1)S(1)}, u32[]{:S(2)}, u32[]{:S(2)}) collective-permute-start(bf16[2,256,256]{2,1,0:T(8,128)(2,1)S(1)} %get-tuple-element.41.refs_1_), channel_id=1, source_target_pairs={{0,1},{1,0},{2,3},{3,2},{4,5},{5,4},{6,7},{7,6},{8,9},{9,8},{10,11... | collective-permute-start | bytes 786440 | tf_op jit(solution)/shard_map/ppermute | solution.py:487
  26.0 0.0 collective-permute-done.13.refs_4_
  26.0 0.1 collective-permute-start.5
  26.1 3.8 %collective-permute-done.4.refs_1_ = bf16[2,256,256]{2,1,0:T(8,128)(2,1)S(1)} collective-permute-done((bf16[2,256,256]{2,1,0:T(8,128)(2,1)S(1)}, bf16[2,256,256]{2,1,0:T(8,128)(2,1)S(1)}, u32[]{:S(2)}, u32[]{:S(2)}) %collective-permute-start.4) | collective-permute-done | bytes 262176 | tf_op jit(solution)/shard_map/ppermute | solution.py:476
  29.9 0.0 collective-permute-start.6
  29.9 0.0 collective-permute-done.11.refs_2_
  29.9 0.0 collective-permute-done.12.refs_3_
  29.9 0.0 copy-done.2
  29.9 0.7 %correlate.2 = (f32[2,2,4,32,128]{4,3,2,1,0:T(8,128)S(1)}, f32[2,4,8,128]{3,2,1,0:T(8,128)S(1)}) custom-call(bf16[2,256,256]{2,1,0:T(8,128)(2,1)S(1)} %equalize.3.refs_0_, bf16[2,256,256]{2,1,0:T(8,128)(2,1)S(1)} %get-tuple-element.41.refs_1_, bf16[2,256,256]{2,1,0:T(8,128)(2,1)S(1)} %collective-permute-done.11.refs_2_, ...), custom_call_target="tpu_custom_call" | custom-call | bytes 1024 | tf_op jit(solution)/shard_map/correlate/pallas_call | solution.py:417
  30.6 0.8 %collective-permute-done.7.refs_0_ = bf16[2,272,256]{2,1,0:T(8,128)(2,1)S(1)} collective-permute-done((bf16[2,272,256]{2,1,0:T(8,128)(2,1)S(1)}, bf16[2,272,256]{2,1,0:T(8,128)(2,1)S(1)}, u32[]{:S(2)}, u32[]{:S(2)}) %collective-permute-start.7) | collective-permute-done | bytes 278560 | tf_op jit(solution)/shard_map/ppermute | solution.py:477
  31.5 0.0 collective-permute-done.5.refs_2_
  31.5 0.0 collective-permute-done.6.refs_3_
  31.5 1.6 %correlate.3 = f32[2,16,32,128]{3,2,1,0:T(8,128)} custom-call(bf16[2,256,256]{2,1,0:T(8,128)(2,1)S(1)} %get-tuple-element.36.refs_2_.refs_0_, bf16[2,256,256]{2,1,0:T(8,128)(2,1)S(1)} %collective-permute-done.4.refs_1_, bf16[2,256,256]{2,1,0:T(8,128)(2,1)S(1)} %collective-permute-done.5.refs_2_, bf16[2,256,256]{2,1,0:T(8,128)(2,1)S(1)} %collective-permute-done.6.refs_3_, ...), custom_call_target="tpu_custom_call" | custom-call | bytes 1024 | tf_op jit(solution)/shard_map/correlate/pallas_call | solution.py:417
  (3 shorter events, 0.1 us)
Async XLA Ops:
  0.0 8.3 %copy-start = (f32[128,128]{1,0:T(8,128)S(1)}, f32[128,128]{1,0:T(8,128)}, u32[]{:S(2)}) copy-start(f32[128,128]{1,0:T(8,128)} %constant.5.clone.pick_ref) | copy-start | bytes 196612
  0.0 8.3 %copy-start.1 = (f32[8,2,128]{2,1,0:T(2,128)S(1)}, f32[8,2,128]{2,1,0:T(2,128)}, u32[]{:S(2)}) copy-start(f32[8,2,128]{2,1,0:T(2,128)} %gains_ref.1) | copy-start | bytes 24580
  2.6 8.9 %collective-permute-start = (bf16[280,128]{1,0:T(8,128)(2,1)S(1)}, bf16[280,128]{1,0:T(8,128)(2,1)S(1)}, u32[]{:S(2)}, u32[]{:S(2)}) collective-permute-start(bf16[280,128]{1,0:T(8,128)(2,1)S(1)} %get-tuple-element.30), channel_id=1, source_target_pairs={{0,16},{8,24},{16,0},{24,8},{1,17},{9,25},{17,1},{25,9},{2,18},{10... | collective-permute-start | bytes 215048 | tf_op jit(solution)/shard_map/ppermute | solution.py:433
  6.7 9.9 %collective-permute-start.8 = (bf16[280,128]{1,0:T(8,128)(2,1)S(1)}, bf16[280,128]{1,0:T(8,128)(2,1)S(1)}, u32[]{:S(2)}, u32[]{:S(2)}) collective-permute-start(bf16[280,128]{1,0:T(8,128)(2,1)S(1)} %get-tuple-element.38), channel_id=1, source_target_pairs={{0,24},{8,16},{16,8},{24,0},{1,25},{9,17},{17,9},{25,1},{2,26},{10... | collective-permute-start | bytes 215048 | tf_op jit(solution)/shard_map/ppermute | solution.py:433
  8.0 8.6 %collective-permute-start.9 = (bf16[280,128]{1,0:T(8,128)(2,1)S(1)}, bf16[280,128]{1,0:T(8,128)(2,1)S(1)}, u32[]{:S(2)}, u32[]{:S(2)}) collective-permute-start(bf16[280,128]{1,0:T(8,128)(2,1)S(1)} %get-tuple-element.39), channel_id=1, source_target_pairs={{0,8},{8,0},{16,24},{24,16},{1,9},{9,1},{17,25},{25,17},{2,10},{10... | collective-permute-start | bytes 215048 | tf_op jit(solution)/shard_map/ppermute | solution.py:433
  8.3 21.6 %copy-start.2 = (s32[8,8]{1,0:T(8,128)S(1)}, s32[8,8]{1,0:T(8,128)}, u32[]{:S(2)}) copy-start(s32[8,8]{1,0:T(8,128)} %refs_5_.1) | copy-start | bytes 772
  11.5 8.7 %collective-permute-start.1 = (bf16[280,128]{1,0:T(8,128)(2,1)S(1)}, bf16[280,128]{1,0:T(8,128)(2,1)S(1)}, u32[]{:S(2)}, u32[]{:S(2)}) collective-permute-start(bf16[280,128]{1,0:T(8,128)(2,1)S(1)} %get-tuple-element.31), channel_id=1, source_target_pairs={{0,24},{8,16},{16,8},{24,0},{1,25},{9,17},{17,9},{25,1},{2,26},{10... | collective-permute-start | bytes 215048 | tf_op jit(solution)/shard_map/ppermute | solution.py:433
  16.0 5.7 %collective-permute-start.2 = (bf16[280,128]{1,0:T(8,128)(2,1)S(1)}, bf16[280,128]{1,0:T(8,128)(2,1)S(1)}, u32[]{:S(2)}, u32[]{:S(2)}) collective-permute-start(bf16[280,128]{1,0:T(8,128)(2,1)S(1)} %get-tuple-element.32), channel_id=1, source_target_pairs={{0,16},{8,24},{16,0},{24,8},{1,17},{9,25},{17,1},{25,9},{2,18},{10... | collective-permute-start | bytes 215048 | tf_op jit(solution)/shard_map/ppermute | solution.py:433
  16.0 5.8 %collective-permute-start.3 = (bf16[280,128]{1,0:T(8,128)(2,1)S(1)}, bf16[280,128]{1,0:T(8,128)(2,1)S(1)}, u32[]{:S(2)}, u32[]{:S(2)}) collective-permute-start(bf16[280,128]{1,0:T(8,128)(2,1)S(1)} %get-tuple-element.33), channel_id=1, source_target_pairs={{0,8},{8,0},{16,24},{24,16},{1,9},{9,1},{17,25},{25,17},{2,10},{10... | collective-permute-start | bytes 215048 | tf_op jit(solution)/shard_map/ppermute | solution.py:433
  17.1 8.3 %collective-permute-start.10 = (bf16[2,256,256]{2,1,0:T(8,128)(2,1)S(1)}, bf16[2,256,256]{2,1,0:T(8,128)(2,1)S(1)}, u32[]{:S(2)}, u32[]{:S(2)}) collective-permute-start(bf16[2,256,256]{2,1,0:T(8,128)(2,1)S(1)} %equalize.3.refs_0_), channel_id=1, source_target_pairs={{0,2},{1,3},{2,0},{3,1},{4,6},{5,7},{6,4},{7,5},{8,10},{9,11},{10,... | collective-permute-start | bytes 786440 | tf_op jit(solution)/shard_map/ppermute | solution.py:476
  18.6 7.4 %collective-permute-start.13 = (bf16[2,256,256]{2,1,0:T(8,128)(2,1)S(1)}, bf16[2,256,256]{2,1,0:T(8,128)(2,1)S(1)}, u32[]{:S(2)}, u32[]{:S(2)}) collective-permute-start(bf16[2,256,256]{2,1,0:T(8,128)(2,1)S(1)} %equalize.3.refs_0_), channel_id=1, source_target_pairs={{0,4},{4,0},{1,5},{5,1},{2,6},{6,2},{3,7},{7,3},{8,12},{12,8},{9,1... | collective-permute-start | bytes 786440 | tf_op jit(solution)/shard_map/ppermute | solution.py:477
  22.3 7.6 %collective-permute-start.4 = (bf16[2,256,256]{2,1,0:T(8,128)(2,1)S(1)}, bf16[2,256,256]{2,1,0:T(8,128)(2,1)S(1)}, u32[]{:S(2)}, u32[]{:S(2)}) collective-permute-start(bf16[2,256,256]{2,1,0:T(8,128)(2,1)S(1)} %get-tuple-element.36.refs_2_.refs_0_), channel_id=1, source_target_pairs={{0,2},{1,3},{2,0},{3,1},{4,6},{5,7},{6,4},{7,5},{8,10},{9,11},{10,... | collective-permute-start | bytes 786440 | tf_op jit(solution)/shard_map/ppermute | solution.py:476
  23.9 7.6 %collective-permute-start.7 = (bf16[2,272,256]{2,1,0:T(8,128)(2,1)S(1)}, bf16[2,272,256]{2,1,0:T(8,128)(2,1)S(1)}, u32[]{:S(2)}, u32[]{:S(2)}) collective-permute-start(bf16[2,272,256]{2,1,0:T(8,128)(2,1)S(1)} %get-tuple-element.37), channel_id=1, source_target_pairs={{0,4},{4,0},{1,5},{5,1},{2,6},{6,2},{3,7},{7,3},{8,12},{12,8},{9,1... | collective-permute-start | bytes 835592 | tf_op jit(solution)/shard_map/ppermute | solution.py:477
  25.4 4.5 %collective-permute-start.11 = (bf16[2,256,256]{2,1,0:T(8,128)(2,1)S(1)}, bf16[2,256,256]{2,1,0:T(8,128)(2,1)S(1)}, u32[]{:S(2)}, u32[]{:S(2)}) collective-permute-start(bf16[2,256,256]{2,1,0:T(8,128)(2,1)S(1)} %get-tuple-element.42), channel_id=1, source_target_pairs={{0,1},{1,0},{2,3},{3,2},{4,5},{5,4},{6,7},{7,6},{8,9},{9,8},{10,11... | collective-permute-start | bytes 786440 | tf_op jit(solution)/shard_map/ppermute | solution.py:486
  25.5 4.4 %collective-permute-start.12 = (bf16[2,256,256]{2,1,0:T(8,128)(2,1)S(1)}, bf16[2,256,256]{2,1,0:T(8,128)(2,1)S(1)}, u32[]{:S(2)}, u32[]{:S(2)}) collective-permute-start(bf16[2,256,256]{2,1,0:T(8,128)(2,1)S(1)} %get-tuple-element.41.refs_1_), channel_id=1, source_target_pairs={{0,1},{1,0},{2,3},{3,2},{4,5},{5,4},{6,7},{7,6},{8,9},{9,8},{10,11... | collective-permute-start | bytes 786440 | tf_op jit(solution)/shard_map/ppermute | solution.py:487
  26.0 5.5 %collective-permute-start.5 = (bf16[2,256,256]{2,1,0:T(8,128)(2,1)S(1)}, bf16[2,256,256]{2,1,0:T(8,128)(2,1)S(1)}, u32[]{:S(2)}, u32[]{:S(2)}) collective-permute-start(bf16[2,256,256]{2,1,0:T(8,128)(2,1)S(1)} %get-tuple-element.36.refs_2_.refs_0_), channel_id=1, source_target_pairs={{0,1},{1,0},{2,3},{3,2},{4,5},{5,4},{6,7},{7,6},{8,9},{9,8},{10,11... | collective-permute-start | bytes 786440 | tf_op jit(solution)/shard_map/ppermute | solution.py:486
  29.9 1.6 %collective-permute-start.6 = (bf16[2,256,256]{2,1,0:T(8,128)(2,1)S(1)}, bf16[2,256,256]{2,1,0:T(8,128)(2,1)S(1)}, u32[]{:S(2)}, u32[]{:S(2)}) collective-permute-start(bf16[2,256,256]{2,1,0:T(8,128)(2,1)S(1)} %collective-permute-done.4.refs_1_), channel_id=1, source_target_pairs={{0,1},{1,0},{2,3},{3,2},{4,5},{5,4},{6,7},{7,6},{8,9},{9,8},{10,11... | collective-permute-start | bytes 786440 | tf_op jit(solution)/shard_map/ppermute | solution.py:487

commit v22 on v18

--- a/solution.py
+++ b/solution.py
@@ -95,8 +95,9 @@
     coef_copy = pltpu.make_async_copy(
         table_hbm.at[pl.ds(PARTS * 2 * NCHAN, terms.shape[0])], terms, sems.at[pieces + 1]
     )
+    copies[0].start()
     coef_copy.start()
-    for copy in copies:
+    for copy in copies[1:]:
         copy.start()
     later_copy = pltpu.make_async_copy(
         table_hbm.at[pl.ds(2 * NCHAN, (PARTS - 1) * 2 * NCHAN)], later, sems.at[pieces + 2]

time: 31.8 us -> 31.7 us (level)
  no operation moved by 1% of the time
where the time goes in v22:
time: 31.7 us; the launch traced here: 31.6 us
  starting transfers between devices  16.9 us (53%)
  waiting for transfers between devices  8.07 us (25%)
  Pallas kernels  6.54 us (21%)
    ppermute x6, starting transfers between devices, to_owners(): lax.ppermute(pieces[d], 'chan', [(i, i ^ d) for i in range(owners)])  10.7 us
    ppermute x6, waiting for transfers between devices, to_owners(): lax.ppermute(pieces[d], 'chan', [(i, i ^ d) for i in range(owners)])  3.68 us
    ppermute x2, waiting for transfers between devices, shards(): far = [lax.ppermute(own[part], 'bcol', across[d]) for d in range(1, chips)]  3.64 us
    ppermute x2, starting transfers between devices, shards(): lax.ppermute((longer or own)[-1], 'brow', along[d])  3.04 us
    pallas_call x1, Pallas kernels, filtered_and_first(): pl.pallas_call(functools.partial(filter_kernel, frames, pieces, spectrum_...  2.55 us
    ppermute x2, starting transfers between devices, shards(): far = [lax.ppermute(own[part], 'bcol', across[d]) for d in range(1, chips)]  2.52 us
    pallas_call x2, Pallas kernels, correlate(): pl.pallas_call(functools.partial(correlate_kernel, n_row, n_col, h, times...  2.36 us
    pallas_call x2, Pallas kernels, equalize(): pl.pallas_call(functools.partial(equalize_kernel, owners, frames, h, part...  0.93 us
  transfers between devices with their start and end apart: 14, of which 7 were waited for; matrix products, arithmetic and copies ran while one was open for 0% of the time, Pallas kernels for 7%

profile of v22, /device:TPU:0, one launch (start us, length us, event | category | flops | bytes accessed | tf_op | source)
XLA Modules:
  0.0 31.6 jit_solution(17667595845704089288)
XLA Ops:
  0.0 0.0 copy-start
  0.0 0.0 copy-start.1
  0.0 2.6 %filter_and_transform.1 = (bf16[280,128]{1,0:T(8,128)(2,1)S(1)}, bf16[280,128]{1,0:T(8,128)(2,1)S(1)}, bf16[280,128]{1,0:T(8,128)(2,1)S(1)}, bf16[280,128]{1,0:T...) custom-call(s32[2,8,32768]{2,1,0:T(8,128)} %volt_hbm.1, ...), custom_call_target="tpu_custom_call" | custom-call | flops 536870912 | bytes 4194304 | tf_op jit(solution)/shard_map/filter_and_transform/pallas_call | solution.py:178
  2.6 5.1 %collective-permute-start = (bf16[280,128]{1,0:T(8,128)(2,1)S(1)}, bf16[280,128]{1,0:T(8,128)(2,1)S(1)}, u32[]{:S(2)}, u32[]{:S(2)}) collective-permute-start(bf16[280,128]{1,0:T(8,128)(2,1)S(1)} %get-tuple-element.30), channel_id=1, source_target_pairs={{0,24},{8,16},{16,8},{24,0},{1,25},{9,17},{17,9},{25,1},{2,26},{10... | collective-permute-start | bytes 215048 | tf_op jit(solution)/shard_map/ppermute | solution.py:434
  7.7 0.0 collective-permute-start.8
  7.7 0.6 %collective-permute-start.9 = (bf16[280,128]{1,0:T(8,128)(2,1)S(1)}, bf16[280,128]{1,0:T(8,128)(2,1)S(1)}, u32[]{:S(2)}, u32[]{:S(2)}) collective-permute-start(bf16[280,128]{1,0:T(8,128)(2,1)S(1)} %get-tuple-element.39), channel_id=1, source_target_pairs={{0,8},{8,0},{16,24},{24,16},{1,9},{9,1},{17,25},{25,17},{2,10},{10... | collective-permute-start | bytes 215048 | tf_op jit(solution)/shard_map/ppermute | solution.py:434
  8.3 0.0 copy-done
  8.3 0.0 copy-done.1
  8.3 0.0 copy-start.2
  8.3 0.6 %transform.1 = (bf16[280,128]{1,0:T(8,128)(2,1)S(1)}, bf16[280,128]{1,0:T(8,128)(2,1)S(1)}, bf16[280,128]{1,0:T(8,128)(2,1)S(1)}, bf16[280,128]{1,0:T(8,128)(2,1)S(1)}, f32[128,16]{1,0:T(8,128)S(1)}) custom-call(bf16[2,288,1024]{2,1,0:T(8,128)(2,1)S(1)} %get-tuple-element.25.filt, bf16[2048,256]{1,0:T(8,128)(2,1)S(1)} %get-tuple-element.26.later, ...), custom_call_target="tpu_custom_call" | custom-call | flops 536870912 | bytes 2097152 | tf_op jit(solution)/shard_map/transform/pallas_call | solution.py:214
  9.0 1.4 %collective-permute-done.refs_3_.refs_0_ = bf16[280,128]{1,0:T(8,128)(2,1)S(1)} collective-permute-done((bf16[280,128]{1,0:T(8,128)(2,1)S(1)}, bf16[280,128]{1,0:T(8,128)(2,1)S(1)}, u32[]{:S(2)}, u32[]{:S(2)}) %collective-permute-start) | collective-permute-done | bytes 71712 | tf_op jit(solution)/shard_map/ppermute | solution.py:434
  10.4 4.3 %collective-permute-start.1 = (bf16[280,128]{1,0:T(8,128)(2,1)S(1)}, bf16[280,128]{1,0:T(8,128)(2,1)S(1)}, u32[]{:S(2)}, u32[]{:S(2)}) collective-permute-start(bf16[280,128]{1,0:T(8,128)(2,1)S(1)} %get-tuple-element.31), channel_id=1, source_target_pairs={{0,24},{8,16},{16,8},{24,0},{1,25},{9,17},{17,9},{25,1},{2,26},{10... | collective-permute-start | bytes 215048 | tf_op jit(solution)/shard_map/ppermute | solution.py:434
  14.7 0.3 collective-permute-start.2
  15.0 0.4 %collective-permute-start.3 = (bf16[280,128]{1,0:T(8,128)(2,1)S(1)}, bf16[280,128]{1,0:T(8,128)(2,1)S(1)}, u32[]{:S(2)}, u32[]{:S(2)}) collective-permute-start(bf16[280,128]{1,0:T(8,128)(2,1)S(1)} %get-tuple-element.33), channel_id=1, source_target_pairs={{0,8},{8,0},{16,24},{24,16},{1,9},{9,1},{17,25},{25,17},{2,10},{10... | collective-permute-start | bytes 215048 | tf_op jit(solution)/shard_map/ppermute | solution.py:434
  15.3 0.6 %collective-permute-done.8.refs_1_ = bf16[280,128]{1,0:T(8,128)(2,1)S(1)} collective-permute-done((bf16[280,128]{1,0:T(8,128)(2,1)S(1)}, bf16[280,128]{1,0:T(8,128)(2,1)S(1)}, u32[]{:S(2)}, u32[]{:S(2)}) %collective-permute-start.8) | collective-permute-done | bytes 71712 | tf_op jit(solution)/shard_map/ppermute | solution.py:434
  15.9 0.0 collective-permute-done.9.refs_2_
  15.9 0.4 %equalize.3.refs_0_ = bf16[2,256,256]{2,1,0:T(8,128)(2,1)S(1)} custom-call(bf16[280,128]{1,0:T(8,128)(2,1)S(1)} %collective-permute-done.refs_3_.refs_0_, bf16[280,128]{1,0:T(8,128)(2,1)S(1)} %collective-permute-done.8.refs_1_, bf16[280,128]{1,0:T(8,128)(2,1)S(1)} %collective-permute-done.9.refs_2_, bf16[280,128]{1,0:T(8,128)(2,1)S(1)} %get-tuple-element.40.refs_3_, ...), custom_call_target="tpu_custom_call" | custom-call | bytes 1024 | tf_op jit(solution)/shard_map/equalize/pallas_call | solution.py:274
  16.4 1.0 %collective-permute-start.10 = (bf16[2,256,256]{2,1,0:T(8,128)(2,1)S(1)}, bf16[2,256,256]{2,1,0:T(8,128)(2,1)S(1)}, u32[]{:S(2)}, u32[]{:S(2)}) collective-permute-start(bf16[2,256,256]{2,1,0:T(8,128)(2,1)S(1)} %equalize.3.refs_0_), channel_id=1, source_target_pairs={{0,2},{1,3},{2,0},{3,1},{4,6},{5,7},{6,4},{7,5},{8,10},{9,11},{10,... | collective-permute-start | bytes 786440 | tf_op jit(solution)/shard_map/ppermute | solution.py:477
  17.3 1.5 %collective-permute-start.13 = (bf16[2,256,256]{2,1,0:T(8,128)(2,1)S(1)}, bf16[2,256,256]{2,1,0:T(8,128)(2,1)S(1)}, u32[]{:S(2)}, u32[]{:S(2)}) collective-permute-start(bf16[2,256,256]{2,1,0:T(8,128)(2,1)S(1)} %equalize.3.refs_0_), channel_id=1, source_target_pairs={{0,4},{4,0},{1,5},{5,1},{2,6},{6,2},{3,7},{7,3},{8,12},{12,8},{9,1... | collective-permute-start | bytes 786440 | tf_op jit(solution)/shard_map/ppermute | solution.py:478
  18.9 0.0 collective-permute-done.1.refs_0_
  18.9 1.7 %collective-permute-done.2.refs_1_ = bf16[280,128]{1,0:T(8,128)(2,1)S(1)} collective-permute-done((bf16[280,128]{1,0:T(8,128)(2,1)S(1)}, bf16[280,128]{1,0:T(8,128)(2,1)S(1)}, u32[]{:S(2)}, u32[]{:S(2)}) %collective-permute-start.2) | collective-permute-done | bytes 71712 | tf_op jit(solution)/shard_map/ppermute | solution.py:434
  20.5 0.0 collective-permute-done.3.refs_2_
  20.5 0.5 %equalize.2 = (bf16[2,256,256]{2,1,0:T(8,128)(2,1)S(1)}, bf16[2,272,256]{2,1,0:T(8,128)(2,1)S(1)}) custom-call(bf16[280,128]{1,0:T(8,128)(2,1)S(1)} %collective-permute-done.1.refs_0_, bf16[280,128]{1,0:T(8,128)(2,1)S(1)} %collective-permute-done.2.refs_1_, bf16[280,128]{1,0:T(8,128)(2,1)S(1)} %collective-permute-done.3.refs_2_, ...), custom_call_target="tpu_custom_call" | custom-call | bytes 1024 | tf_op jit(solution)/shard_map/equalize/pallas_call | solution.py:274
  21.0 1.6 %collective-permute-start.4 = (bf16[2,256,256]{2,1,0:T(8,128)(2,1)S(1)}, bf16[2,256,256]{2,1,0:T(8,128)(2,1)S(1)}, u32[]{:S(2)}, u32[]{:S(2)}) collective-permute-start(bf16[2,256,256]{2,1,0:T(8,128)(2,1)S(1)} %get-tuple-element.36.refs_2_.refs_0_), channel_id=1, source_target_pairs={{0,2},{1,3},{2,0},{3,1},{4,6},{5,7},{6,4},{7,5},{8,10},{9,11},{10,... | collective-permute-start | bytes 786440 | tf_op jit(solution)/shard_map/ppermute | solution.py:477
  22.6 1.5 %collective-permute-start.7 = (bf16[2,272,256]{2,1,0:T(8,128)(2,1)S(1)}, bf16[2,272,256]{2,1,0:T(8,128)(2,1)S(1)}, u32[]{:S(2)}, u32[]{:S(2)}) collective-permute-start(bf16[2,272,256]{2,1,0:T(8,128)(2,1)S(1)} %get-tuple-element.37), channel_id=1, source_target_pairs={{0,4},{4,0},{1,5},{5,1},{2,6},{6,2},{3,7},{7,3},{8,12},{12,8},{9,1... | collective-permute-start | bytes 835592 | tf_op jit(solution)/shard_map/ppermute | solution.py:478
  24.1 0.4 %collective-permute-done.10.refs_1_ = bf16[2,256,256]{2,1,0:T(8,128)(2,1)S(1)} collective-permute-done((bf16[2,256,256]{2,1,0:T(8,128)(2,1)S(1)}, bf16[2,256,256]{2,1,0:T(8,128)(2,1)S(1)}, u32[]{:S(2)}, u32[]{:S(2)}) %collective-permute-start.10) | collective-permute-done | bytes 262176 | tf_op jit(solution)/shard_map/ppermute | solution.py:477
  24.6 0.1 collective-permute-start.11
  24.6 0.5 %collective-permute-start.12 = (bf16[2,256,256]{2,1,0:T(8,128)(2,1)S(1)}, bf16[2,256,256]{2,1,0:T(8,128)(2,1)S(1)}, u32[]{:S(2)}, u32[]{:S(2)}) collective-permute-start(bf16[2,256,256]{2,1,0:T(8,128)(2,1)S(1)} %get-tuple-element.41.refs_1_), channel_id=1, source_target_pairs={{0,1},{1,0},{2,3},{3,2},{4,5},{5,4},{6,7},{7,6},{8,9},{9,8},{10,11... | collective-permute-start | bytes 786440 | tf_op jit(solution)/shard_map/ppermute | solution.py:488
  25.1 0.0 collective-permute-done.13.refs_4_
  25.1 0.1 collective-permute-start.5
  25.2 3.2 %collective-permute-done.4.refs_1_ = bf16[2,256,256]{2,1,0:T(8,128)(2,1)S(1)} collective-permute-done((bf16[2,256,256]{2,1,0:T(8,128)(2,1)S(1)}, bf16[2,256,256]{2,1,0:T(8,128)(2,1)S(1)}, u32[]{:S(2)}, u32[]{:S(2)}) %collective-permute-start.4) | collective-permute-done | bytes 262176 | tf_op jit(solution)/shard_map/ppermute | solution.py:477
  28.4 0.0 collective-permute-start.6
  28.4 0.0 collective-permute-done.11.refs_2_
  28.4 0.0 collective-permute-done.12.refs_3_
  28.4 0.0 copy-done.2
  28.5 0.7 %correlate.2 = (f32[2,2,4,32,128]{4,3,2,1,0:T(8,128)S(1)}, f32[2,4,8,128]{3,2,1,0:T(8,128)S(1)}) custom-call(bf16[2,256,256]{2,1,0:T(8,128)(2,1)S(1)} %equalize.3.refs_0_, bf16[2,256,256]{2,1,0:T(8,128)(2,1)S(1)} %get-tuple-element.41.refs_1_, bf16[2,256,256]{2,1,0:T(8,128)(2,1)S(1)} %collective-permute-done.11.refs_2_, ...), custom_call_target="tpu_custom_call" | custom-call | bytes 1024 | tf_op jit(solution)/shard_map/correlate/pallas_call | solution.py:418
  29.2 0.5 %collective-permute-done.7.refs_0_ = bf16[2,272,256]{2,1,0:T(8,128)(2,1)S(1)} collective-permute-done((bf16[2,272,256]{2,1,0:T(8,128)(2,1)S(1)}, bf16[2,272,256]{2,1,0:T(8,128)(2,1)S(1)}, u32[]{:S(2)}, u32[]{:S(2)}) %collective-permute-start.7) | collective-permute-done | bytes 278560 | tf_op jit(solution)/shard_map/ppermute | solution.py:478
  29.7 0.0 collective-permute-done.5.refs_2_
  29.7 0.2 collective-permute-done.6.refs_3_
  30.0 1.6 %correlate.3 = f32[2,16,32,128]{3,2,1,0:T(8,128)} custom-call(bf16[2,256,256]{2,1,0:T(8,128)(2,1)S(1)} %get-tuple-element.36.refs_2_.refs_0_, bf16[2,256,256]{2,1,0:T(8,128)(2,1)S(1)} %collective-permute-done.4.refs_1_, bf16[2,256,256]{2,1,0:T(8,128)(2,1)S(1)} %collective-permute-done.5.refs_2_, bf16[2,256,256]{2,1,0:T(8,128)(2,1)S(1)} %collective-permute-done.6.refs_3_, ...), custom_call_target="tpu_custom_call" | custom-call | bytes 1024 | tf_op jit(solution)/shard_map/correlate/pallas_call | solution.py:418
  (3 shorter events, 0.1 us)
Async XLA Ops:
  0.0 8.3 %copy-start = (f32[128,128]{1,0:T(8,128)S(1)}, f32[128,128]{1,0:T(8,128)}, u32[]{:S(2)}) copy-start(f32[128,128]{1,0:T(8,128)} %constant.5.clone.pick_ref) | copy-start | bytes 196612
  0.0 8.3 %copy-start.1 = (f32[8,2,128]{2,1,0:T(2,128)S(1)}, f32[8,2,128]{2,1,0:T(2,128)}, u32[]{:S(2)}) copy-start(f32[8,2,128]{2,1,0:T(2,128)} %gains_ref.1) | copy-start | bytes 24580
  2.6 7.8 %collective-permute-start = (bf16[280,128]{1,0:T(8,128)(2,1)S(1)}, bf16[280,128]{1,0:T(8,128)(2,1)S(1)}, u32[]{:S(2)}, u32[]{:S(2)}) collective-permute-start(bf16[280,128]{1,0:T(8,128)(2,1)S(1)} %get-tuple-element.30), channel_id=1, source_target_pairs={{0,24},{8,16},{16,8},{24,0},{1,25},{9,17},{17,9},{25,1},{2,26},{10... | collective-permute-start | bytes 215048 | tf_op jit(solution)/shard_map/ppermute | solution.py:434
  7.7 8.2 %collective-permute-start.8 = (bf16[280,128]{1,0:T(8,128)(2,1)S(1)}, bf16[280,128]{1,0:T(8,128)(2,1)S(1)}, u32[]{:S(2)}, u32[]{:S(2)}) collective-permute-start(bf16[280,128]{1,0:T(8,128)(2,1)S(1)} %get-tuple-element.38), channel_id=1, source_target_pairs={{0,16},{8,24},{16,0},{24,8},{1,17},{9,25},{17,1},{25,9},{2,18},{10... | collective-permute-start | bytes 215048 | tf_op jit(solution)/shard_map/ppermute | solution.py:434
  7.7 8.2 %collective-permute-start.9 = (bf16[280,128]{1,0:T(8,128)(2,1)S(1)}, bf16[280,128]{1,0:T(8,128)(2,1)S(1)}, u32[]{:S(2)}, u32[]{:S(2)}) collective-permute-start(bf16[280,128]{1,0:T(8,128)(2,1)S(1)} %get-tuple-element.39), channel_id=1, source_target_pairs={{0,8},{8,0},{16,24},{24,16},{1,9},{9,1},{17,25},{25,17},{2,10},{10... | collective-permute-start | bytes 215048 | tf_op jit(solution)/shard_map/ppermute | solution.py:434
  8.3 20.1 %copy-start.2 = (s32[8,8]{1,0:T(8,128)S(1)}, s32[8,8]{1,0:T(8,128)}, u32[]{:S(2)}) copy-start(s32[8,8]{1,0:T(8,128)} %refs_5_.1) | copy-start | bytes 772
  10.4 8.5 %collective-permute-start.1 = (bf16[280,128]{1,0:T(8,128)(2,1)S(1)}, bf16[280,128]{1,0:T(8,128)(2,1)S(1)}, u32[]{:S(2)}, u32[]{:S(2)}) collective-permute-start(bf16[280,128]{1,0:T(8,128)(2,1)S(1)} %get-tuple-element.31), channel_id=1, source_target_pairs={{0,24},{8,16},{16,8},{24,0},{1,25},{9,17},{17,9},{25,1},{2,26},{10... | collective-permute-start | bytes 215048 | tf_op jit(solution)/shard_map/ppermute | solution.py:434
  14.7 5.8 %collective-permute-start.2 = (bf16[280,128]{1,0:T(8,128)(2,1)S(1)}, bf16[280,128]{1,0:T(8,128)(2,1)S(1)}, u32[]{:S(2)}, u32[]{:S(2)}) collective-permute-start(bf16[280,128]{1,0:T(8,128)(2,1)S(1)} %get-tuple-element.32), channel_id=1, source_target_pairs={{0,16},{8,24},{16,0},{24,8},{1,17},{9,25},{17,1},{25,9},{2,18},{10... | collective-permute-start | bytes 215048 | tf_op jit(solution)/shard_map/ppermute | solution.py:434
  15.0 5.6 %collective-permute-start.3 = (bf16[280,128]{1,0:T(8,128)(2,1)S(1)}, bf16[280,128]{1,0:T(8,128)(2,1)S(1)}, u32[]{:S(2)}, u32[]{:S(2)}) collective-permute-start(bf16[280,128]{1,0:T(8,128)(2,1)S(1)} %get-tuple-element.33), channel_id=1, source_target_pairs={{0,8},{8,0},{16,24},{24,16},{1,9},{9,1},{17,25},{25,17},{2,10},{10... | collective-permute-start | bytes 215048 | tf_op jit(solution)/shard_map/ppermute | solution.py:434
  16.4 8.1 %collective-permute-start.10 = (bf16[2,256,256]{2,1,0:T(8,128)(2,1)S(1)}, bf16[2,256,256]{2,1,0:T(8,128)(2,1)S(1)}, u32[]{:S(2)}, u32[]{:S(2)}) collective-permute-start(bf16[2,256,256]{2,1,0:T(8,128)(2,1)S(1)} %equalize.3.refs_0_), channel_id=1, source_target_pairs={{0,2},{1,3},{2,0},{3,1},{4,6},{5,7},{6,4},{7,5},{8,10},{9,11},{10,... | collective-permute-start | bytes 786440 | tf_op jit(solution)/shard_map/ppermute | solution.py:477
  17.3 7.8 %collective-permute-start.13 = (bf16[2,256,256]{2,1,0:T(8,128)(2,1)S(1)}, bf16[2,256,256]{2,1,0:T(8,128)(2,1)S(1)}, u32[]{:S(2)}, u32[]{:S(2)}) collective-permute-start(bf16[2,256,256]{2,1,0:T(8,128)(2,1)S(1)} %equalize.3.refs_0_), channel_id=1, source_target_pairs={{0,4},{4,0},{1,5},{5,1},{2,6},{6,2},{3,7},{7,3},{8,12},{12,8},{9,1... | collective-permute-start | bytes 786440 | tf_op jit(solution)/shard_map/ppermute | solution.py:478
  21.0 7.4 %collective-permute-start.4 = (bf16[2,256,256]{2,1,0:T(8,128)(2,1)S(1)}, bf16[2,256,256]{2,1,0:T(8,128)(2,1)S(1)}, u32[]{:S(2)}, u32[]{:S(2)}) collective-permute-start(bf16[2,256,256]{2,1,0:T(8,128)(2,1)S(1)} %get-tuple-element.36.refs_2_.refs_0_), channel_id=1, source_target_pairs={{0,2},{1,3},{2,0},{3,1},{4,6},{5,7},{6,4},{7,5},{8,10},{9,11},{10,... | collective-permute-start | bytes 786440 | tf_op jit(solution)/shard_map/ppermute | solution.py:477
  22.6 7.1 %collective-permute-start.7 = (bf16[2,272,256]{2,1,0:T(8,128)(2,1)S(1)}, bf16[2,272,256]{2,1,0:T(8,128)(2,1)S(1)}, u32[]{:S(2)}, u32[]{:S(2)}) collective-permute-start(bf16[2,272,256]{2,1,0:T(8,128)(2,1)S(1)} %get-tuple-element.37), channel_id=1, source_target_pairs={{0,4},{4,0},{1,5},{5,1},{2,6},{6,2},{3,7},{7,3},{8,12},{12,8},{9,1... | collective-permute-start | bytes 835592 | tf_op jit(solution)/shard_map/ppermute | solution.py:478
  24.6 3.9 %collective-permute-start.11 = (bf16[2,256,256]{2,1,0:T(8,128)(2,1)S(1)}, bf16[2,256,256]{2,1,0:T(8,128)(2,1)S(1)}, u32[]{:S(2)}, u32[]{:S(2)}) collective-permute-start(bf16[2,256,256]{2,1,0:T(8,128)(2,1)S(1)} %get-tuple-element.42), channel_id=1, source_target_pairs={{0,1},{1,0},{2,3},{3,2},{4,5},{5,4},{6,7},{7,6},{8,9},{9,8},{10,11... | collective-permute-start | bytes 786440 | tf_op jit(solution)/shard_map/ppermute | solution.py:487
  24.6 3.8 %collective-permute-start.12 = (bf16[2,256,256]{2,1,0:T(8,128)(2,1)S(1)}, bf16[2,256,256]{2,1,0:T(8,128)(2,1)S(1)}, u32[]{:S(2)}, u32[]{:S(2)}) collective-permute-start(bf16[2,256,256]{2,1,0:T(8,128)(2,1)S(1)} %get-tuple-element.41.refs_1_), channel_id=1, source_target_pairs={{0,1},{1,0},{2,3},{3,2},{4,5},{5,4},{6,7},{7,6},{8,9},{9,8},{10,11... | collective-permute-start | bytes 786440 | tf_op jit(solution)/shard_map/ppermute | solution.py:488
  25.1 4.6 %collective-permute-start.5 = (bf16[2,256,256]{2,1,0:T(8,128)(2,1)S(1)}, bf16[2,256,256]{2,1,0:T(8,128)(2,1)S(1)}, u32[]{:S(2)}, u32[]{:S(2)}) collective-permute-start(bf16[2,256,256]{2,1,0:T(8,128)(2,1)S(1)} %get-tuple-element.36.refs_2_.refs_0_), channel_id=1, source_target_pairs={{0,1},{1,0},{2,3},{3,2},{4,5},{5,4},{6,7},{7,6},{8,9},{9,8},{10,11... | collective-permute-start | bytes 786440 | tf_op jit(solution)/shard_map/ppermute | solution.py:487
  28.4 1.5 %collective-permute-start.6 = (bf16[2,256,256]{2,1,0:T(8,128)(2,1)S(1)}, bf16[2,256,256]{2,1,0:T(8,128)(2,1)S(1)}, u32[]{:S(2)}, u32[]{:S(2)}) collective-permute-start(bf16[2,256,256]{2,1,0:T(8,128)(2,1)S(1)} %collective-permute-done.4.refs_1_), channel_id=1, source_target_pairs={{0,1},{1,0},{2,3},{3,2},{4,5},{5,4},{6,7},{7,6},{8,9},{9,8},{10,11... | collective-permute-start | bytes 786440 | tf_op jit(solution)/shard_map/ppermute | solution.py:488
